TPU v7x, 32 devices: a whole 2x2x4 slice. The times are simulated.
32 devices in a mesh: rows: 4 (over x, core), seq: 8 (over z, y).
Axes of the slice: x: 2, y: 2, z: 4, core: 2. Of those that a mesh axis runs over, the one named last changes fastest.
Arguments:
- tokens: bfloat16 [2, 4, 1152, 512], P(None, 'rows', 'seq'), may hold values from -6 to 6
- segments: int32 [2, 4, 1152], P(None, 'rows', 'seq'), may hold values from 0 to 24, as said below
- cotangent: bfloat16 [2, 4, 1152, 512], P(None, 'rows', 'seq'), may hold values from -6 to 6
- gain_attn: bfloat16 [512], replicated, may hold values from 0.5 to 1.5
- w_query: bfloat16 [512, 512], replicated, may hold values from -0.25 to 0.25
- w_key: bfloat16 [512, 512], replicated, may hold values from -0.25 to 0.25
- w_value: bfloat16 [512, 512], replicated, may hold values from -0.25 to 0.25
- conv_key: bfloat16 [1536, 512], replicated, may hold values from -0.15625 to 0.15625
- conv_value: bfloat16 [1536, 512], replicated, may hold values from -0.15625 to 0.15625
- w_out: bfloat16 [512, 512], replicated, may hold values from -1 to 1
- gain_ffn: bfloat16 [512], replicated, may hold values from 0.5 to 1.5
- w_up: bfloat16 [512, 2048], replicated, may hold values from -0.25 to 0.25
- w_down: bfloat16 [2048, 512], replicated, may hold values from -0.125 to 0.125
Outputs:
- layer_out: bfloat16 [2, 4, 1152, 512], P(None, 'rows', 'seq')
- grad_tokens: bfloat16 [2, 4, 1152, 512], P(None, 'rows', 'seq')
- grad_gain_attn: float32 [512], replicated
- grad_w_query: float32 [512, 512], replicated
- grad_w_key: float32 [512, 512], replicated
- grad_w_value: float32 [512, 512], replicated
- grad_conv_key: float32 [1536, 512], replicated
- grad_conv_value: float32 [1536, 512], replicated
- grad_w_out: float32 [512, 512], replicated
- grad_gain_ffn: float32 [512], replicated
- grad_w_up: float32 [512, 2048], replicated
- grad_w_down: float32 [2048, 512], replicated
Inputs may be any that keep to these rules, and one draw needn't show every extreme that they name: `segments`: along each row document numbers start at 0 at the first position, never fall and rise by at most one from a position to the next; a document may begin at any position.
All inputs are finite; a program needn't handle non-finite values.
Results may differ from a plain program's by a relative error of at most 0.015.
Values may be sent and summed in bfloat16 or wider, within the bound.
No kernel may reach another device: no remote copies, remote signals or barrier semaphores. Data moves between devices by JAX's collectives and lax.ppermute only.
A program may use at most 192 MiB of HBM per device.

v0:
```python
import math

import jax
import jax.numpy as jnp
from jax import lax
from jax.sharding import PartitionSpec as P

HEADS = 8
HEAD_DIM = 64


EPSILON = 1e-05
MASKED_OUT = -1e30


def normalize(values):
    average = jnp.mean(values, axis=-1, keepdims=True)
    centred = values - average
    variance = jnp.mean(centred * centred, axis=-1, keepdims=True)
    inverse_dev = lax.rsqrt(variance + EPSILON)
    return (centred * inverse_dev, inverse_dev)


def normalize_back(grad_normed, centred_unit, inverse_dev, gain_value):
    gain_grad = jnp.sum(grad_normed * centred_unit, axis=(0, 1))
    grad_unit = grad_normed * gain_value
    first_mean = jnp.mean(grad_unit, axis=-1, keepdims=True)
    second_mean = jnp.mean(grad_unit * centred_unit, axis=-1, keepdims=True)
    return (inverse_dev * (grad_unit - first_mean - centred_unit * second_mean), gain_grad)


def project(operand, matrix):
    return jnp.einsum("rsc,cd->rsd", operand, matrix, preferred_element_type=jnp.float32)


def project_back(gradient, matrix):
    return jnp.einsum("rsd,cd->rsc", gradient, matrix, preferred_element_type=jnp.float32)


def weight_grad(operand, gradient):
    return jnp.einsum("rsc,rsd->cd", operand, gradient, preferred_element_type=jnp.float32)


def split_heads(values):
    return values.reshape(values.shape[0], values.shape[1], HEADS, HEAD_DIM)


def merge_heads(values):
    return values.reshape(values.shape[0], values.shape[1], HEADS * HEAD_DIM)


def block_rows(total_rows):
    return math.gcd(total_rows, 512)


def window_mask(segment_rows):
    row_count, shard_len = segment_rows.shape
    grouped = segment_rows.reshape(row_count, shard_len // 3, 3)
    return (grouped == grouped[:, :, 2:3]).astype(jnp.bfloat16)[..., None]


def windows(vectors, in_window):
    row_count, shard_len, model_dim = vectors.shape
    grouped = vectors.reshape(row_count, shard_len // 3, 3, model_dim) * in_window
    return grouped.reshape(row_count, shard_len // 3, 3 * model_dim)


def unwind(gradient, in_window):
    row_count, slot_count, wide_dim = gradient.shape
    model_dim = wide_dim // 3
    grouped = gradient.reshape(row_count, slot_count, 3, model_dim) * in_window.astype(jnp.float32)
    return grouped.reshape(row_count, slot_count * 3, model_dim)


def visible(query_place, query_segment, slot_first, slot_count, slot_segment):
    slot_end = 3 * (slot_first + jnp.arange(slot_count, dtype=jnp.int32)) + 2
    causal = slot_end[None, None, :] <= query_place[None, :, None]
    matching = slot_segment[:, None, :] == query_segment[:, :, None]
    return (causal & matching)[:, None]


def key_block(query_heads, all_keys, query_place, query_segment, slot_segment, number, block_size):
    offset = number * block_size
    key_heads = split_heads(lax.dynamic_slice_in_dim(all_keys, offset, block_size, 1))
    segment_part = lax.dynamic_slice_in_dim(slot_segment, offset, block_size, 1)
    visible_now = visible(query_place, query_segment, offset, block_size, segment_part)
    scores = jnp.einsum(
        "rqhe,rjhe->rhqj", query_heads, key_heads, preferred_element_type=jnp.float32
    ) * HEAD_DIM ** (-0.5)
    return (jnp.where(visible_now, scores, MASKED_OUT), key_heads, offset)


def attend_forward(
    queries, key_rows, value_rows, all_keys, all_values, query_place, segment_rows, slot_segment
):
    query_heads = split_heads(queries)
    key_heads = split_heads(key_rows)
    value_heads = split_heads(value_rows)
    total_slots = all_keys.shape[1]
    block_size = block_rows(total_slots)
    own_score = jnp.einsum(
        "rqhe,rqhe->rhq", query_heads, key_heads, preferred_element_type=jnp.float32
    ) * HEAD_DIM ** (-0.5)

    def statistics(number, carried):
        running_max, running_sum = carried
        scores, block_keys, offset = key_block(
            query_heads, all_keys, query_place, segment_rows, slot_segment, number, block_size
        )
        new_max = jnp.maximum(running_max, jnp.max(scores, axis=-1))
        running_sum = running_sum * jnp.exp(running_max - new_max) + jnp.sum(
            jnp.exp(scores - new_max[..., None]), axis=-1
        )
        return (new_max, running_sum)

    running_max, running_sum = lax.fori_loop(
        0, total_slots // block_size, statistics, (own_score, jnp.ones_like(own_score))
    )
    log_total = running_max + jnp.log(running_sum)
    own_weight = jnp.exp(own_score - log_total)
    initial = jnp.einsum(
        "rhq,rqhe->rqhe",
        own_weight.astype(jnp.bfloat16),
        value_heads,
        preferred_element_type=jnp.float32,
    )

    def weigh_values(number, accumulated):
        scores, block_keys, offset = key_block(
            query_heads, all_keys, query_place, segment_rows, slot_segment, number, block_size
        )
        weight = jnp.exp(scores - log_total[..., None]).astype(jnp.bfloat16)
        block_values = split_heads(lax.dynamic_slice_in_dim(all_values, offset, block_size, 1))
        return accumulated + jnp.einsum(
            "rhqj,rjhe->rqhe", weight, block_values, preferred_element_type=jnp.float32
        )

    accumulated = lax.fori_loop(0, total_slots // block_size, weigh_values, initial)
    return (merge_heads(accumulated).astype(jnp.bfloat16), log_total, own_weight)


def forward(tokens_in, segment_rows, segment_all, query_place, weights):
    gain_attn, w_query, w_key, w_value, conv_key, conv_value, w_out, gain_ffn, w_up, w_down = (
        weights
    )
    residual = tokens_in.astype(jnp.float32)
    unit_attn, invdev_attn = normalize(residual)
    normed = (unit_attn * gain_attn.astype(jnp.float32)).astype(jnp.bfloat16)
    queries = project(normed, w_query).astype(jnp.bfloat16)
    key_rows = project(normed, w_key).astype(jnp.bfloat16)
    value_rows = project(normed, w_value).astype(jnp.bfloat16)
    in_window = window_mask(segment_rows)
    key_window = windows(key_rows, in_window)
    value_window = windows(value_rows, in_window)
    packed_key = project(key_window, conv_key).astype(jnp.bfloat16)
    packed_value = project(value_window, conv_value).astype(jnp.bfloat16)
    all_keys, all_values = (
        lax.all_gather(packed_key, "seq", axis=1, tiled=True),
        lax.all_gather(packed_value, "seq", axis=1, tiled=True),
    )
    slot_segment = segment_all[:, 2::3]
    attended, log_total, own_weight = attend_forward(
        queries, key_rows, value_rows, all_keys, all_values, query_place, segment_rows, slot_segment
    )
    hidden = residual + project(attended, w_out)
    unit_ffn, invdev_ffn = normalize(hidden)
    normed_ffn = (unit_ffn * gain_ffn.astype(jnp.float32)).astype(jnp.bfloat16)
    expanded = project(normed_ffn, w_up)
    activated = jax.nn.gelu(expanded).astype(jnp.bfloat16)
    layer_out = (hidden + project(activated, w_down)).astype(jnp.bfloat16)
    return {
        "unit_attn": unit_attn,
        "invdev_attn": invdev_attn,
        "normed": normed,
        "queries": queries,
        "key_rows": key_rows,
        "value_rows": value_rows,
        "in_window": in_window,
        "key_window": key_window,
        "value_window": value_window,
        "packed_key": packed_key,
        "packed_value": packed_value,
        "all_keys": all_keys,
        "all_values": all_values,
        "attended": attended,
        "log_total": log_total,
        "own_weight": own_weight,
        "unit_ffn": unit_ffn,
        "invdev_ffn": invdev_ffn,
        "normed_ffn": normed_ffn,
        "expanded": expanded,
        "activated": activated,
        "layer_out": layer_out,
        "segment_rows": segment_rows,
    }


def ffn_back(stored, cotangent_rows, weights):
    gain_attn, w_query, w_key, w_value, conv_key, conv_value, w_out, gain_ffn, w_up, w_down = (
        weights
    )
    grad_w_down = weight_grad(stored["activated"], cotangent_rows)
    d_activated = project_back(cotangent_rows, w_down)
    gelu_value, gelu_back = jax.vjp(jax.nn.gelu, stored["expanded"])
    d_expanded = gelu_back(d_activated)[0].astype(jnp.bfloat16)
    grad_w_up = weight_grad(stored["normed_ffn"], d_expanded)
    d_normed_ffn = project_back(d_expanded, w_up)
    d_input, grad_gain_ffn = normalize_back(
        d_normed_ffn, stored["unit_ffn"], stored["invdev_ffn"], gain_ffn.astype(jnp.float32)
    )
    return (cotangent_rows.astype(jnp.float32) + d_input, (grad_gain_ffn, grad_w_up, grad_w_down))


def attention_back(stored, d_hidden, weights, query_place, segment_all):
    gain_attn, w_query, w_key, w_value, conv_key, conv_value, w_out, gain_ffn, w_up, w_down = (
        weights
    )
    d_branch = d_hidden.astype(jnp.bfloat16)
    grad_w_out = weight_grad(stored["attended"], d_branch)
    d_attended = project_back(d_branch, w_out).astype(jnp.bfloat16)
    query_heads = split_heads(stored["queries"])
    key_heads = split_heads(stored["key_rows"])
    value_heads = split_heads(stored["value_rows"])
    grad_heads = split_heads(d_attended)
    all_keys = stored["all_keys"]
    all_values = stored["all_values"]
    log_total = stored["log_total"]
    own_weight = stored["own_weight"]
    segment_rows = stored["segment_rows"]
    slot_segment = segment_all[:, 2::3]
    total_slots = all_keys.shape[1]
    block_size = block_rows(total_slots)
    step_count = total_slots // block_size
    score_scale = HEAD_DIM ** (-0.5)
    own_prob_grad = jnp.einsum(
        "rqhe,rqhe->rhq", grad_heads, value_heads, preferred_element_type=jnp.float32
    )

    def block_terms(number):
        scores, block_keys, offset = key_block(
            query_heads, all_keys, query_place, segment_rows, slot_segment, number, block_size
        )
        exact_prob = jnp.exp(scores - log_total[..., None])
        block_values = split_heads(lax.dynamic_slice_in_dim(all_values, offset, block_size, 1))
        prob_grad = jnp.einsum(
            "rqhe,rjhe->rhqj", grad_heads, block_values, preferred_element_type=jnp.float32
        )
        return (exact_prob, prob_grad, block_keys, offset)

    def add_delta(number, delta_sum):
        exact_prob, prob_grad, block_keys, offset = block_terms(number)
        return delta_sum + jnp.sum(exact_prob * prob_grad, axis=-1)

    delta_sum = lax.fori_loop(0, step_count, add_delta, own_weight * own_prob_grad)

    def query_step(number, carried):
        exact_prob, prob_grad, block_keys, offset = block_terms(number)
        score_grad = (exact_prob * (prob_grad - delta_sum[..., None])).astype(jnp.bfloat16)
        query_sum = carried[0] + jnp.einsum(
            "rhqj,rjhe->rqhe", score_grad, block_keys, preferred_element_type=jnp.float32
        )
        return (query_sum,)

    query_zero = jnp.zeros(query_heads.shape, jnp.float32)
    query_sum = lax.fori_loop(0, step_count, query_step, (query_zero,))[0]
    all_queries, all_grads = (
        lax.all_gather(stored["queries"], "seq", axis=1, tiled=True),
        lax.all_gather(d_attended, "seq", axis=1, tiled=True),
    )
    all_log, all_delta = (
        lax.all_gather(log_total, "seq", axis=2, tiled=True),
        lax.all_gather(delta_sum, "seq", axis=2, tiled=True),
    )
    own_keys = split_heads(stored["packed_key"])
    own_values = split_heads(stored["packed_value"])
    slot_count = own_keys.shape[1]
    slot_first = lax.axis_index("seq") * slot_count
    own_slot_segment = segment_rows[:, 2::3]
    length = all_queries.shape[1]
    query_block = block_rows(length)

    def owner_step(number, carried):
        offset = number * query_block
        part_queries = split_heads(lax.dynamic_slice_in_dim(all_queries, offset, query_block, 1))
        part_grads = split_heads(lax.dynamic_slice_in_dim(all_grads, offset, query_block, 1))
        part_log = lax.dynamic_slice_in_dim(all_log, offset, query_block, 2)
        part_delta = lax.dynamic_slice_in_dim(all_delta, offset, query_block, 2)
        part_segment = lax.dynamic_slice_in_dim(segment_all, offset, query_block, 1)
        part_place = offset + jnp.arange(query_block, dtype=jnp.int32)
        visible_now = visible(part_place, part_segment, slot_first, slot_count, own_slot_segment)
        scores = (
            jnp.einsum(
                "rqhe,rjhe->rhqj", part_queries, own_keys, preferred_element_type=jnp.float32
            )
            * score_scale
        )
        exact_prob = jnp.exp(jnp.where(visible_now, scores, MASKED_OUT) - part_log[..., None])
        prob_grad = jnp.einsum(
            "rqhe,rjhe->rhqj", part_grads, own_values, preferred_element_type=jnp.float32
        )
        score_grad = (exact_prob * (prob_grad - part_delta[..., None])).astype(jnp.bfloat16)
        key_sums = carried[0] + jnp.einsum(
            "rhqj,rqhe->rjhe", score_grad, part_queries, preferred_element_type=jnp.float32
        )
        value_sums = carried[1] + jnp.einsum(
            "rhqj,rqhe->rjhe",
            exact_prob.astype(jnp.bfloat16),
            part_grads,
            preferred_element_type=jnp.float32,
        )
        return (key_sums, value_sums)

    slot_zero = jnp.zeros(own_keys.shape, jnp.float32)
    key_sums, value_sums = lax.fori_loop(
        0, length // query_block, owner_step, (slot_zero, slot_zero)
    )
    d_packed_key = merge_heads(key_sums * score_scale).astype(jnp.bfloat16)
    d_packed_value = merge_heads(value_sums).astype(jnp.bfloat16)
    own_score_grad = (own_weight * (own_prob_grad - delta_sum)).astype(jnp.bfloat16)
    own_query = jnp.einsum(
        "rhq,rqhe->rqhe", own_score_grad, key_heads, preferred_element_type=jnp.float32
    )
    d_queries = merge_heads((query_sum + own_query) * score_scale).astype(jnp.bfloat16)
    key_self = (
        jnp.einsum(
            "rhq,rqhe->rqhe", own_score_grad, query_heads, preferred_element_type=jnp.float32
        )
        * score_scale
    )
    value_self = jnp.einsum(
        "rhq,rqhe->rqhe",
        own_weight.astype(jnp.bfloat16),
        grad_heads,
        preferred_element_type=jnp.float32,
    )
    grad_conv_key = weight_grad(stored["key_window"], d_packed_key)
    grad_conv_value = weight_grad(stored["value_window"], d_packed_value)
    key_from = unwind(project_back(d_packed_key, conv_key), stored["in_window"])
    value_from = unwind(project_back(d_packed_value, conv_value), stored["in_window"])
    d_keys = (key_from + merge_heads(key_self)).astype(jnp.bfloat16)
    d_values = (value_from + merge_heads(value_self)).astype(jnp.bfloat16)
    normed = stored["normed"]
    grad_w_query = weight_grad(normed, d_queries)
    grad_w_key = weight_grad(normed, d_keys)
    grad_w_value = weight_grad(normed, d_values)
    d_normed = (
        project_back(d_queries, w_query)
        + project_back(d_keys, w_key)
        + project_back(d_values, w_value)
    )
    d_input, grad_gain_attn = normalize_back(
        d_normed, stored["unit_attn"], stored["invdev_attn"], gain_attn.astype(jnp.float32)
    )
    return (
        (d_hidden + d_input).astype(jnp.bfloat16),
        (
            grad_gain_attn,
            grad_w_query,
            grad_w_key,
            grad_w_value,
            grad_conv_key,
            grad_conv_value,
            grad_w_out,
        ),
    )


def add_up(running, parts):
    if running is None:
        return parts
    return tuple((first_term + second_term for first_term, second_term in zip(running, parts)))


def body(
    tokens,
    segments,
    cotangent,
    gain_attn,
    w_query,
    w_key,
    w_value,
    conv_key,
    conv_value,
    w_out,
    gain_ffn,
    w_up,
    w_down,
):
    weights = (
        gain_attn,
        w_query,
        w_key,
        w_value,
        conv_key,
        conv_value,
        w_out,
        gain_ffn,
        w_up,
        w_down,
    )
    batch_count = tokens.shape[0]
    shard_len = tokens.shape[2]
    segment_all = lax.all_gather(segments, "seq", axis=2, tiled=True)
    query_place = lax.axis_index("seq") * shard_len + jnp.arange(shard_len, dtype=jnp.int32)
    states = []
    layer_outputs = []
    token_grads = []
    ffn_total = None
    attn_total = None
    for number in range(batch_count):
        stored = forward(
            tokens[number], segments[number], segment_all[number], query_place, weights
        )
        layer_outputs.append(stored["layer_out"])
        d_hidden, ffn_parts = ffn_back(stored, cotangent[number], weights)
        ffn_total = add_up(ffn_total, ffn_parts)
        d_tokens, attn_parts = attention_back(
            stored, d_hidden, weights, query_place, segment_all[number]
        )
        attn_total = add_up(attn_total, attn_parts)
        token_grads.append(d_tokens)
    g_gain_attn, g_query, g_key, g_value, g_conv_key, g_conv_value, g_out = attn_total
    g_gain_ffn, g_up, g_down = ffn_total
    summed = lax.psum(
        (
            g_gain_attn,
            g_query,
            g_key,
            g_value,
            g_conv_key,
            g_conv_value,
            g_out,
            g_gain_ffn,
            g_up,
            g_down,
        ),
        ("rows", "seq"),
    )
    summed_attn = summed[:7]
    summed_ffn = summed[7:]
    return (
        (jnp.stack(layer_outputs, axis=0), jnp.stack(token_grads, axis=0))
        + tuple(summed_attn)
        + tuple(summed_ffn)
    )


def solution(mesh):
    in_specs = (
        P(None, "rows", "seq", None),
        P(None, "rows", "seq"),
        P(None, "rows", "seq", None),
        P(),
        P(),
        P(),
        P(),
        P(),
        P(),
        P(),
        P(),
        P(),
        P(),
    )
    out_specs = (
        P(None, "rows", "seq", None),
        P(None, "rows", "seq", None),
        P(),
        P(),
        P(),
        P(),
        P(),
        P(),
        P(),
        P(),
        P(),
        P(),
    )
    return jax.shard_map(body, mesh=mesh, in_specs=in_specs, out_specs=out_specs, check_vma=False)
```

profile of v0, /device:TPU:0, one launch (start us, length us, event | category | flops | bytes accessed | tf_op | source)
XLA Modules:
  0.0 1011.0 jit_solution(13655968369815020077)
XLA Ops:
  10.6 2.1 convolution_convert_fusion.7
  21.6 1.9 reshape.2776
  28.0 2.0 broadcast_multiply_fusion.2
  35.1 1.8 reshape.2777
  38.8 2.0 broadcast_multiply_fusion
  51.8 2.6 convolution_convert_fusion.11
  57.2 32.8 %all-gather.3 = bf16[384,512]{1,0:T(8,128)(2,1)S(1)} all-gather(bf16[48,512]{1,0:T(8,128)(2,1)S(1)} %convolution_convert_fusion.8), channel_id=5, replica_groups=mesh['rows'=4,'seq'=8] {'seq'}, dimensions={0}, use_global_device_ids=true | all-gather | bytes 442368 | tf_op jit(solution)/shard_map/all_gather | solution.py:159
  90.9 31.0 %all-gather.1 = bf16[384,512]{1,0:T(8,128)(2,1)S(1)} all-gather(bf16[48,512]{1,0:T(8,128)(2,1)S(1)} %convolution_convert_fusion.10), channel_id=3, replica_groups=mesh['rows'=4,'seq'=8] {'seq'}, dimensions={0}, use_global_device_ids=true | all-gather | bytes 442368 | tf_op jit(solution)/shard_map/all_gather | solution.py:159
  122.8 31.1 %all-gather.2 = bf16[384,512]{1,0:T(8,128)(2,1)S(1)} all-gather(bf16[48,512]{1,0:T(8,128)(2,1)S(1)} %convolution_convert_fusion.9), channel_id=4, replica_groups=mesh['rows'=4,'seq'=8] {'seq'}, dimensions={0}, use_global_device_ids=true | all-gather | bytes 442368 | tf_op jit(solution)/shard_map/all_gather | solution.py:158
  154.1 33.5 %all-gather = bf16[384,512]{1,0:T(8,128)(2,1)} all-gather(bf16[48,512]{1,0:T(8,128)(2,1)} %convolution_convert_fusion.11), channel_id=2, replica_groups=mesh['rows'=4,'seq'=8] {'seq'}, dimensions={0}, use_global_device_ids=true | all-gather | bytes 442368 | tf_op jit(solution)/shard_map/all_gather | solution.py:158
  188.8 31.5 %all_gather.39 = s32[2,1,1152]{0,1,2:T(1,128)S(1)} all-gather(s32[2,1,144]{0,1,2:T(1,128)} %copy.253), channel_id=1, replica_groups=mesh['rows'=4,'seq'=8] {'seq'}, dimensions={2}, use_global_device_ids=true | all-gather | bytes 10368 | tf_op jit(solution)/shard_map/all_gather | solution.py:403
  220.3 42.9 %slice_reduce_fusion.1 = (s32[1152]{0:T(1024)S(1)}, s32[1152]{0:T(1024)}) fusion(s32[2,1,1152]{0,1,2:T(1,128)S(1)} %all_gather.39), kind=kLoop, calls=%fused_computation.271 | loop fusion | bytes 18432 | tf_op jit(solution)/shard_map/slice | solution.py:412
  265.2 9.7 while.152
  279.0 9.9 while.153
  301.1 2.0 multiply_bitcast_fusion.1
  304.5 15.7 %while.148 = (s32[]{:T(128)}, f32[1,144,8,64]{1,3,2,0:T(8,128)S(1)}, bf16[1,384,512]{1,2,0:T(8,128)(2,1)}, s32[1,384]{1,0:T(1,128)}, s32[1,1,144]{2,1,0:T(1,128)...) while((s32[]{:T(128)}, f32[1,144,8,64]{1,3,2,0:T(8,128)S(1)}, ...), condition=%wide.region_7.8_spmd.clone, body=%wide.region_6.7_spmd.clone.sunk | while | flops 38468116 | bytes 1569659 | solution.py:138
  325.8 16.0 %while.149 = (s32[]{:T(128)}, f32[1,144,8,64]{1,3,2,0:T(8,128)S(1)}, bf16[1,384,512]{1,2,0:T(8,128)(2,1)}, s32[1,384]{1,0:T(1,128)}, s32[1,1,144]{2,1,0:T(1,128)...) while((s32[]{:T(128)}, f32[1,144,8,64]{1,3,2,0:T(8,128)S(1)}, ...), condition=%wide.region_17.18_spmd.clone, body=%wide.region_16.17_spmd.clone.sunk | while | flops 38468116 | bytes 1569659 | solution.py:138
  360.0 34.1 %all_gather.45 = f32[1,8,1152]{1,0,2:T(1,128)} all-gather(f32[1,8,144]{1,0,2:T(1,128)S(1)} %copy-done.83), channel_id=1, replica_groups=mesh['rows'=4,'seq'=8] {'seq'}, dimensions={2}, use_global_device_ids=true | all-gather | bytes 41472 | tf_op jit(solution)/shard_map/all_gather | solution.py:271
  395.3 10.2 %while.151 = (s32[]{:T(128)}, f32[1,8,144]{2,1,0:T(8,128)S(1)}, s32[1,384]{1,0:T(1,128)}, s32[1,1,144]{2,1,0:T(1,128)}, bf16[1,384,512]{1,2,0:T(8,128)(2,1)S(1)}...) while((s32[]{:T(128)}, f32[1,8,144]{2,1,0:T(8,128)S(1)}, ...), condition=%wide.region_35.36_spmd.clone, body=%wide.region_33.35_spmd.clone.sunk | while | flops 38541844 | bytes 2325379 | solution.py:254
  409.7 2.0 convert_multiply_fusion.5
  412.6 3.4 while.150
  418.0 34.5 %all_gather.47 = f32[1,8,1152]{1,0,2:T(1,128)} all-gather(f32[1,8,144]{1,0,2:T(1,128)S(1)} %copy.285), channel_id=1, replica_groups=mesh['rows'=4,'seq'=8] {'seq'}, dimensions={2}, use_global_device_ids=true | all-gather | bytes 41472 | tf_op jit(solution)/shard_map/all_gather | solution.py:272
  453.8 2.8 fusion.209
  456.7 2.8 fusion.231
  473.8 31.9 %all_gather.49 = f32[1,8,1152]{1,0,2:T(1,128)S(1)} all-gather(f32[1,8,144]{1,0,2:T(1,128)S(1)} %bitcast.884), channel_id=1, replica_groups=mesh['rows'=4,'seq'=8] {'seq'}, dimensions={2}, use_global_device_ids=true | all-gather | bytes 41472 | tf_op jit(solution)/shard_map/all_gather | solution.py:271
  506.8 14.4 %while.156 = (s32[]{:T(128)}, f32[1,144,8,64]{1,3,2,0:T(8,128)}, bf16[1,384,512]{1,2,0:T(8,128)(2,1)S(1)}, s32[1,384]{1,0:T(1,128)}, s32[1,1,144]{2,1,0:T(1,128)...) while((s32[]{:T(128)}, f32[1,144,8,64]{1,3,2,0:T(8,128)}, ...), condition=%wide.region_37.38_spmd.clone, body=%wide.region_36.37_spmd.clone.sunk | while | flops 57711124 | bytes 2901405 | solution.py:265
  513.6 2.4 fusion.463
  518.8 2.4 fusion.463
  521.2 2.2 copy.311
  525.8 3.5 while.154
  537.5 31.3 %all_gather.51 = f32[1,8,1152]{1,0,2:T(1,128)S(1)} all-gather(f32[1,8,144]{1,0,2:T(1,128)S(1)} %copy-done.131), channel_id=1, replica_groups=mesh['rows'=4,'seq'=8] {'seq'}, dimensions={2}, use_global_device_ids=true | all-gather | bytes 41472 | tf_op jit(solution)/shard_map/all_gather | solution.py:272
  572.5 5.2 convolution_add_fusion.2
  577.7 2.9 convolution_add_fusion.3
  582.1 31.2 %while.155 = (s32[]{:T(128)}, f32[1,48,8,64]{3,1,2,0:T(8,128)S(1)}, f32[1,48,8,64]{3,1,2,0:T(8,128)S(1)}, bf16[1,1152,512]{2,1,0:T(8,128)(2,1)}, s32[]{:T(128)},...) while((s32[]{:T(128)}, f32[1,48,8,64]{3,1,2,0:T(8,128)S(1)}, ...), condition=%wide.region_28.29_spmd.clone, body=%wide.region_27.28_spmd.clone.sunk | while | flops 25626904 | bytes 2694442 | solution.py:314
  616.5 31.6 %while.157 = (s32[]{:T(128)}, f32[1,48,8,64]{3,1,2,0:T(8,128)S(1)}, f32[1,48,8,64]{3,1,2,0:T(8,128)S(1)}, bf16[1,1152,512]{2,1,0:T(8,128)(2,1)}, s32[]{:T(128)},...) while((s32[]{:T(128)}, f32[1,48,8,64]{3,1,2,0:T(8,128)S(1)}, ...), condition=%wide.region_39.40_spmd.clone, body=%wide.region_38.39_spmd.clone.sunk | while | flops 25626904 | bytes 2694442 | solution.py:314
  651.2 2.4 fusion.197
  654.5 2.7 fusion.199
  658.2 2.4 fusion.196
  660.8 2.8 fusion.198
  669.6 2.3 convolution_add_fusion.1
  671.8 2.3 convolution_add_fusion
  675.4 2.0 reshape.2789
  678.5 2.7 fusion.148
  692.5 41.3 %all-reduce = (f32[512]{0:T(512)}, f32[512]{0:T(512)}) all-reduce(f32[512]{0:T(512)S(1)} %add.882, f32[512]{0:T(512)S(1)} %add.893), channel_id=1, replica_groups=mesh['rows'=4,'seq'=8] {'rows','seq'}, use_global_device_ids=true, to_apply=%region_44.45 | all-reduce | flops 1024 | bytes 8192 | tf_op jit(solution)/shard_map/psum | solution.py:424
  734.8 250.5 %all-reduce.4.cloned.1.call-done = (f32[512,512]{1,0:T(8,128)}, f32[512,512]{1,0:T(8,128)}, f32[512,512]{1,0:T(8,128)}, f32[1536,512]{1,0:T(8,128)}, f32[1536,51...) async-done(((f32[512,512]{1,0:T(8,128)}, f32[512,512]{1,0:T(8,128)}, f32[512,512]{1,0:T(8,128)}, f32[1536,512]{1,0:T(8,128)}, ...) | async-done | bytes 18874384 | tf_op jit(solution)/shard_map/psum | solution.py:424
  985.3 2.4 copy.471
  997.4 2.1 copy.477
  1001.1 2.1 copy.478
  (996 shorter events, 302.5 us)
Async XLA Ops:
  7.2 336.5 %copy-start = (bf16[512,2048]{1,0:T(8,128)(2,1)S(1)}, bf16[512,2048]{1,0:T(8,128)(2,1)}, u32[]{:S(2)}) copy-start(bf16[512,2048]{1,0:T(8,128)(2,1)} %param.44) | copy-start | bytes 6291460
  7.2 7.5 copy-start.7
  7.2 7.5 copy-start.75
  7.2 574.8 %all-gather.13.cloned.1.call-start = ((), (), s32[]{:S(2)}) async-start(), calls=%async_computation | async-start | bytes 1327104 | tf_op jit(solution)/shard_map/all_gather | solution.py:267
  8.1 30.7 %copy-start.136 = (f32[512]{0:T(512)}, f32[512]{0:T(512)S(1)}, u32[]{:S(2)}) copy-start(f32[512]{0:T(512)S(1)} %convert_element_type.518) | copy-start | bytes 6148
  9.3 18.7 %copy-start.151 = (f32[144]{0:T(256)}, f32[144]{0:T(256)S(1)}, u32[]{:S(2)}) copy-start(f32[144]{0:T(256)S(1)} %get-tuple-element.2816) | copy-start | bytes 1732
  9.3 29.5 %copy-start.149 = (f32[144]{0:T(256)}, f32[144]{0:T(256)S(1)}, u32[]{:S(2)}) copy-start(f32[144]{0:T(256)S(1)} %get-tuple-element.2815) | copy-start | bytes 1732
  9.3 6.4 copy-start.73
  10.6 17.4 %copy-start.155 = (f32[144]{0:T(256)}, f32[144]{0:T(256)S(1)}, u32[]{:S(2)}) copy-start(f32[144]{0:T(256)S(1)} %add_rsqrt_fusion.3) | copy-start | bytes 1732
  12.7 569.3 %all-gather.15.cloned.1.call-start = ((), (), s32[]{:S(2)}) async-start(), calls=%async_computation.1 | async-start | bytes 1327104 | tf_op jit(solution)/shard_map/all_gather | solution.py:268
  13.9 14.0 %copy-start.121 = (s32[1,1,144]{2,1,0:T(1,128)}, s32[1,1,144]{2,1,0:T(1,128)S(1)}, u32[]{:S(2)}) copy-start(s32[1,1,144]{2,1,0:T(1,128)S(1)} %get-tuple-element.3806) | copy-start | bytes 1732
  14.7 24.1 %copy-start.153 = (f32[144]{0:T(256)}, f32[144]{0:T(256)S(1)}, u32[]{:S(2)}) copy-start(f32[144]{0:T(256)S(1)} %add_rsqrt_fusion.1) | copy-start | bytes 1732
  17.6 10.4 %copy-start.17 = (bf16[512,512]{1,0:T(8,128)(2,1)S(1)}, bf16[512,512]{1,0:T(8,128)(2,1)}, u32[]{:S(2)}) copy-start(bf16[512,512]{1,0:T(8,128)(2,1)} %param.39) | copy-start | bytes 1572868
  35.1 9.2 copy-start.176
  40.8 8.2 copy-start.50
  40.8 8.2 copy-start.54
  49.2 249.2 %copy-start.77 = (f32[8,144]{0,1:T(8,128)}, f32[8,144]{0,1:T(8,128)S(1)}, u32[]{:S(2)}) copy-start(f32[8,144]{0,1:T(8,128)S(1)} %broadcast_multiply_fusion.4) | copy-start | bytes 13828
  51.1 243.3 %copy-start.79 = (f32[8,144]{0,1:T(8,128)}, f32[8,144]{0,1:T(8,128)S(1)}, u32[]{:S(2)}) copy-start(f32[8,144]{0,1:T(8,128)S(1)} %fusion.156) | copy-start | bytes 13828
  55.8 66.9 %copy-start.128 = (bf16[48,512]{1,0:T(8,128)(2,1)}, bf16[48,512]{1,0:T(8,128)(2,1)S(1)}, u32[]{:S(2)}) copy-start(bf16[48,512]{1,0:T(8,128)(2,1)S(1)} %convolution_convert_fusion.9) | copy-start | bytes 147460
  56.8 34.1 %copy-start.123 = (bf16[48,512]{1,0:T(8,128)(2,1)}, bf16[48,512]{1,0:T(8,128)(2,1)S(1)}, u32[]{:S(2)}) copy-start(bf16[48,512]{1,0:T(8,128)(2,1)S(1)} %convolution_convert_fusion.10) | copy-start | bytes 147460
  57.1 65.6 %copy-start.125 = (bf16[48,512]{1,0:T(8,128)(2,1)}, bf16[48,512]{1,0:T(8,128)(2,1)S(1)}, u32[]{:S(2)}) copy-start(bf16[48,512]{1,0:T(8,128)(2,1)S(1)} %convolution_convert_fusion.8) | copy-start | bytes 147460
  288.8 12.3 %copy-start.5 = (bf16[1,384,512]{1,2,0:T(8,128)(2,1)}, bf16[1,384,512]{1,2,0:T(8,128)(2,1)S(1)}, u32[]{:S(2)}) copy-start(bf16[1,384,512]{1,2,0:T(8,128)(2,1)S(1)} %get-tuple-element.3938) | copy-start | bytes 1179652
  343.5 8.1 copy-start.15
  343.5 8.1 copy-start.157
  343.7 7.9 copy-start.162
  353.6 6.3 copy-start.83
  353.6 262.8 %all-gather.17.cloned.1.call-start = ((), (), s32[]{:S(2)}) async-start(), calls=%async_computation.2 | async-start | bytes 1327104 | tf_op jit(solution)/shard_map/all_gather | solution.py:267
  354.4 262.1 %all-gather.19.cloned.1.call-start = ((), (), s32[]{:S(2)}) async-start(), calls=%async_computation.3 | async-start | bytes 1327104 | tf_op jit(solution)/shard_map/all_gather | solution.py:268
  355.4 38.6 %copy-start.67 = (bf16[144,512]{1,0:T(8,128)(2,1)S(1)}, bf16[144,512]{1,0:T(8,128)(2,1)}, u32[]{:S(2)}) copy-start(bf16[144,512]{1,0:T(8,128)(2,1)} %convolution_convert_fusion) | copy-start | bytes 442372
  355.4 38.9 %copy-start.59 = (bf16[144,8,64]{2,1,0:T(8,128)(2,1)S(1)}, bf16[144,8,64]{2,1,0:T(8,128)(2,1)}, u32[]{:S(2)}) copy-start(bf16[144,8,64]{2,1,0:T(8,128)(2,1)} %reshape.2781) | copy-start | bytes 442372
  355.5 629.8 %all-reduce.4.cloned.1.call-start = ((), (), s32[]{:S(2)}) async-start(), calls=%async_computation.4 | async-start | bytes 37748736 | tf_op jit(solution)/shard_map/psum | solution.py:424
  359.2 36.1 %copy-start.80 = (f32[8,144]{0,1:T(8,128)S(1)}, f32[8,144]{0,1:T(8,128)}, u32[]{:S(2)}) copy-start(f32[8,144]{0,1:T(8,128)} %copy-done.79) | copy-start | bytes 13828
  359.2 36.1 %copy-start.81 = (f32[1,8,144]{1,2,0:T(8,128)S(1)}, f32[1,8,144]{1,2,0:T(8,128)}, u32[]{:S(2)}) copy-start(f32[1,8,144]{1,2,0:T(8,128)} %get-tuple-element.2759) | copy-start | bytes 13828
  359.9 35.4 %copy-start.6 = (bf16[1,384,512]{1,2,0:T(8,128)(2,1)S(1)}, bf16[1,384,512]{1,2,0:T(8,128)(2,1)}, u32[]{:S(2)}) copy-start(bf16[1,384,512]{1,2,0:T(8,128)(2,1)} %get-tuple-element.3939) | copy-start | bytes 1179652
  395.3 11.7 %copy-start.111 = (f32[144,8]{1,0:T(8,128)S(1)}, f32[144,8]{1,0:T(8,128)}, u32[]{:S(2)}) copy-start(f32[144,8]{1,0:T(8,128)} %get-tuple-element.2758) | copy-start | bytes 13828
  416.0 36.5 %copy-start.33 = (f32[144,512]{1,0:T(8,128)S(1)}, f32[144,512]{1,0:T(8,128)}, u32[]{:S(2)}) copy-start(f32[144,512]{1,0:T(8,128)} %copy-done.32) | copy-start | bytes 884740
  416.0 36.5 %copy-start.64 = (bf16[1,144,8,64]{1,3,2,0:T(8,128)(2,1)S(1)}, bf16[1,144,8,64]{1,3,2,0:T(8,128)(2,1)}, u32[]{:S(2)}) copy-start(bf16[1,144,8,64]{1,3,2,0:T(8,128)(2,1)} %copy-done.63) | copy-start | bytes 442372
  417.9 35.8 %copy-start.39 = (f32[144,2048]{1,0:T(8,128)S(1)}, f32[144,2048]{1,0:T(8,128)}, u32[]{:S(2)}) copy-start(f32[144,2048]{1,0:T(8,128)} %copy-done.38) | copy-start | bytes 3538948
  418.0 35.8 %copy-start.96 = (bf16[2,1,144,512]{3,2,1,0:T(8,128)(2,1)S(1)}, bf16[2,1,144,512]{3,2,1,0:T(8,128)(2,1)}, u32[]{:S(2)}) copy-start(bf16[2,1,144,512]{3,2,1,0:T(8,128)(2,1)} %param.35) | copy-start | bytes 884740
  459.5 13.2 %copy-start.66 = (f32[1,8,1152]{1,0,2:T(1,128)S(1)}, f32[1,8,1152]{1,0,2:T(1,128)}, u32[]{:S(2)}) copy-start(f32[1,8,1152]{1,0,2:T(1,128)} %all_gather.45) | copy-start | bytes 110596
  461.5 12.3 %copy-start.82 = (f32[1,8,144]{1,2,0:T(8,128)S(1)}, f32[1,8,144]{1,2,0:T(8,128)}, u32[]{:S(2)}) copy-start(f32[1,8,144]{1,2,0:T(8,128)} %get-tuple-element.2759) | copy-start | bytes 13828
  524.7 11.3 %copy-start.27 = (f32[144,8,64]{2,1,0:T(8,128)}, f32[144,8,64]{2,1,0:T(8,128)S(1)}, u32[]{:S(2)}) copy-start(f32[144,8,64]{2,1,0:T(8,128)S(1)} %multiply_multiply_fusion.4) | copy-start | bytes 884740
  533.0 38.2 %copy-start.85 = (bf16[144,512]{1,0:T(8,128)(2,1)}, bf16[144,512]{1,0:T(8,128)(2,1)S(1)}, u32[]{:S(2)}) copy-start(bf16[144,512]{1,0:T(8,128)(2,1)S(1)} %convert_element_type.560) | copy-start | bytes 442372
  537.0 32.8 %copy-start.36 = (f32[144,512]{1,0:T(8,128)S(1)}, f32[144,512]{1,0:T(8,128)}, u32[]{:S(2)}) copy-start(f32[144,512]{1,0:T(8,128)} %copy-done.35) | copy-start | bytes 884740
  537.0 32.8 %copy-start.43 = (f32[512,512]{1,0:T(8,128)S(1)}, f32[512,512]{1,0:T(8,128)}, u32[]{:S(2)}) copy-start(f32[512,512]{1,0:T(8,128)} %fusion.227) | copy-start | bytes 3145732
  537.0 32.8 %copy-start.72 = (bf16[1,144,8,64]{1,3,2,0:T(8,128)(2,1)S(1)}, bf16[1,144,8,64]{1,3,2,0:T(8,128)(2,1)}, u32[]{:S(2)}) copy-start(bf16[1,144,8,64]{1,3,2,0:T(8,128)(2,1)} %copy-done.71) | copy-start | bytes 442372
  691.9 41.8 %copy-start.34 = (f32[144,512]{1,0:T(8,128)S(1)}, f32[144,512]{1,0:T(8,128)}, u32[]{:S(2)}) copy-start(f32[144,512]{1,0:T(8,128)} %copy-done.32) | copy-start | bytes 884740
  691.9 41.8 %copy-start.37 = (f32[144,512]{1,0:T(8,128)S(1)}, f32[144,512]{1,0:T(8,128)}, u32[]{:S(2)}) copy-start(f32[144,512]{1,0:T(8,128)} %copy-done.35) | copy-start | bytes 884740
  (150 other events, 364.5 us)
Sparse Core Ops, SparseCore 0:
  12.8 43.7 all-gather.12
  353.8 44.4 all-gather.14
  400.5 43.7 all-gather.16
  446.3 39.2 all-gather.18
  674.2 311.0 all-reduce.3
where the time goes:
time: 1030 us; the launch traced here: 1010 us
  blocking collectives  333 us (32%)
  waiting for transfers between devices  251 us (24%)
  local copies, waits for them, and re-layouts  247 us (24%)
  matrix products  110 us (11%)
  other arithmetic  50.6 us (5%)
  between operations  16 us (2%)
    psum x1, waiting for transfers between devices, body(): lax.psum((g_gain_attn, g_query, g_key, g_value, g_conv_key, g_conv_value,...  250 us
    all_gather x2, blocking collectives, attention_back(): lax.all_gather(log_total, 'seq', axis=2, tiled=True)  66 us
    all_gather x2, blocking collectives, attention_back(): lax.all_gather(delta_sum, 'seq', axis=2, tiled=True)  65.8 us
    all_gather x2, blocking collectives, forward(): lax.all_gather(packed_key, 'seq', axis=1, tiled=True)  64.6 us
    all_gather x2, blocking collectives, forward(): lax.all_gather(packed_value, 'seq', axis=1, tiled=True)  63.8 us
    unnamed x385, local copies, waits for them, and re-layouts  53.3 us
    slice x1, local copies, waits for them, and re-layouts, body(): segment_all[number]  42.9 us
    psum x1, blocking collectives, body(): lax.psum((g_gain_attn, g_query, g_key, g_value, g_conv_key, g_conv_value,...  41.3 us
  transfers between devices with their start and end apart: 5, of which 1 were waited for; matrix products, arithmetic and copies ran while one was open for 31% of the time, Pallas kernels for 0%

commit v1 on v0

v1 whole, which is shorter than its diff:
```python
import functools

import jax
import jax.numpy as jnp
from jax import lax
from jax.experimental import pallas as pl
from jax.experimental.pallas import tpu as pltpu
from jax.sharding import PartitionSpec as P

HEADS = 8
HEAD_DIM = 64
LANES = 128
GROUPS = HEADS * HEAD_DIM // LANES
EPSILON = 1e-05
MASKED_OUT = -1e30
SCALE = HEAD_DIM ** (-0.5)
GELU_SCALE = 0.7978845608028654
GELU_CUBIC = 0.044715
SCATTER_BITS = 5
EXTRA_ROWS = 16
VMEM_LIMIT = 60 * 1024 * 1024

BF16 = jnp.bfloat16
F32 = jnp.float32


def dot(left, right):
    return jnp.dot(left, right, preferred_element_type=F32)


def dot_nt(left, right):
    return lax.dot_general(left, right, (((1,), (1,)), ((), ())), preferred_element_type=F32)


def dot_tn(left, right):
    return lax.dot_general(left, right, (((0,), (0,)), ((), ())), preferred_element_type=F32)


def normalize(values):
    average = jnp.mean(values, axis=-1, keepdims=True)
    centred = values - average
    variance = jnp.mean(centred * centred, axis=-1, keepdims=True)
    inverse_dev = lax.rsqrt(variance + EPSILON)
    return centred * inverse_dev, inverse_dev


def normalize_back(grad_normed, unit, inverse_dev, gain):
    grad_unit = grad_normed * gain
    first_mean = jnp.mean(grad_unit, axis=-1, keepdims=True)
    second_mean = jnp.mean(grad_unit * unit, axis=-1, keepdims=True)
    return inverse_dev * (grad_unit - first_mean - unit * second_mean)


class Plan:
    def __init__(self, mesh):
        self.n_rows = mesh.shape["rows"]
        self.n_seq = mesh.shape["seq"]
        rows = [("rows", 1 << i) for i in range(self.n_rows.bit_length() - 1)]
        seq = [("seq", 1 << i) for i in range(self.n_seq.bit_length() - 1)]
        kept = max(0, min(len(seq), SCATTER_BITS - len(rows)))
        self.seq_block = 1 << kept
        self.blocks = self.n_rows * self.seq_block
        core, others = rows[:1], rows[1:]
        low, high = seq[:1], seq[1:kept] if kept else []
        low = low[:kept]
        self.core = core[0]
        self.first = others + low
        self.second = low + others
        self.tail = high
        self.rest = seq[kept:]
        bits = [1 << i for i in range(len(seq))]
        self.key_order = bits[::-1]
        self.value_order = bits[:1] + bits[:0:-1]

    def mask(self, bit):
        axis, value = bit
        return value * self.seq_block if axis == "rows" else value

    def relative(self, order, position):
        result = 0
        for number, bit in enumerate(order):
            if position >> (len(order) - 1 - number) & 1:
                result |= self.mask(bit)
        return result

    def seq_relative(self, order, position):
        result = 0
        for number, bit in enumerate(order):
            if position >> number & 1:
                result |= bit
        return result

    def swap(self, array, bit):
        axis, value = bit
        size = self.n_rows if axis == "rows" else self.n_seq
        return lax.ppermute(array, axis, [(i, i ^ value) for i in range(size)])


def order_matrix(length, transposed):
    slots = length // 3
    rows = lax.broadcasted_iota(jnp.int32, (length, length), 1 if transposed else 0)
    columns = lax.broadcasted_iota(jnp.int32, (length, length), 0 if transposed else 1)
    tap = (rows >= slots).astype(jnp.int32) + (rows >= 2 * slots).astype(jnp.int32)
    return (columns == 3 * (rows - tap * slots) + tap).astype(BF16)


def window_masks(segment_column, slots):
    last = segment_column[2 * slots :]
    return [(segment_column[i * slots : (i + 1) * slots] == last).astype(F32) for i in range(3)]


def call(kernel, name, outs, scratch=(), flops=0, bytes_accessed=0, smem=0, anywhere=()):
    def space(number):
        if number < smem:
            return pltpu.SMEM
        return pl.ANY if number in anywhere else pltpu.VMEM

    def specs(count):
        return [pl.BlockSpec(memory_space=space(number)) for number in range(count)]

    def run(*operands):
        return pl.pallas_call(
            kernel,
            name=name,
            out_shape=[jax.ShapeDtypeStruct(shape, dtype) for shape, dtype in outs],
            in_specs=specs(len(operands)),
            out_specs=[pl.BlockSpec(memory_space=pltpu.VMEM)] * len(outs),
            scratch_shapes=list(scratch),
            compiler_params=pltpu.CompilerParams(vmem_limit_bytes=VMEM_LIMIT),
            cost_estimate=pl.CostEstimate(
                flops=flops, bytes_accessed=bytes_accessed, transcendentals=0
            ),
        )(*operands)

    return run


def project_kernel(
    tokens, gain, w_query, w_key, w_value, conv_key, conv_value, segment_column, extra,
    x_out, normed_out, query_out, key_out, value_out, packed_key, packed_value,
):
    batch, length, width = tokens.shape
    slots = length // 3
    order = order_matrix(length, False)
    rows = [dot(order, tokens[b]) for b in range(batch)]
    x = jnp.concatenate(rows, axis=0)
    x_out[...] = x
    unit, _ = normalize(x)
    normed = (unit * gain[...].astype(F32)).astype(BF16)
    normed_out[...] = normed
    query_out[...] = dot(normed, w_query[...]).astype(BF16)
    for matrix, conv, flat_out, packed_out in (
        (w_key, conv_key, key_out, packed_key),
        (w_value, conv_value, value_out, packed_value),
    ):
        flat = dot(normed, matrix[...]).astype(BF16)
        flat_out[...] = flat
        taps = [[], [], []]
        for b in range(batch):
            masks = window_masks(segment_column[b], slots)
            for i in range(3):
                start = b * length + i * slots
                part = flat[start : start + slots].astype(F32) * masks[i]
                taps[i].append(part.astype(BF16))
        total = None
        for i in range(3):
            term = dot(jnp.concatenate(taps[i], axis=0), conv[i * width : (i + 1) * width, :])
            total = term if total is None else total + term
        packed_out[0 : batch * slots, :] = total.astype(BF16)
    packed_key[batch * slots :, :] = extra[...]


def layer_kernel(
    plan, keep_prob,
    place, x_in, cotangent, query_in, key_in, value_in, keys_near, keys_far, values_near, values_far,
    segment_column, w_out, gain_ffn, w_up, w_down,
    layer_out, d_hidden_out, normed_ffn_out, activated_out, d_expanded_out, cotangent_out,
    attended_out, d_branch_out, d_query_out, d_key_own, d_value_own, d_packed_key, d_packed_value,
    gain_grad,
    all_keys, all_values, all_extra, bias, statistics, prob_keep, expanded_sum, d_normed_sum,
    d_attended, copied,
):
    batch, length, width = cotangent.shape
    slots = length // 3
    n_seq = plan.n_seq
    half = n_seq // 2
    total_slots = slots * n_seq
    own_place = place[0]
    key_position = {plan.seq_relative(plan.key_order, p): p for p in range(n_seq)}
    copies = []

    def fetch(source, target):
        copies.append(pltpu.make_async_copy(source, target, copied.at[len(copies)]))
        copies[-1].start()

    for p in range(n_seq):
        keys = keys_near.at[p] if p < half else keys_far.at[p - half]
        values = values_near.at[p] if p < half else values_far.at[p - half]
        q = key_position[plan.seq_relative(plan.value_order, p)]
        fetch(keys.at[pl.ds(batch * slots, EXTRA_ROWS), :], all_extra.at[p])
        for b in range(batch):
            rows = pl.ds(b * slots, slots)
            fetch(keys.at[rows, :], all_keys.at[b, pl.ds(p * slots, slots), :])
            fetch(values.at[rows, :], all_values.at[b, pl.ds(q * slots, slots), :])
    for copy in copies:
        copy.wait()

    segment_rows = jnp.zeros((EXTRA_ROWS, total_slots), F32)
    slot_lane = lax.broadcasted_iota(jnp.int32, (1, total_slots), 1)
    slot_end = jnp.zeros((1, total_slots), jnp.int32)
    select_row = lax.broadcasted_iota(jnp.int32, (LANES, total_slots), 0)
    select_lane = lax.broadcasted_iota(jnp.int32, (LANES, total_slots), 1)
    for p in range(n_seq):
        selected = (select_lane == select_row + p * slots) & (select_row < slots)
        segment_rows += dot(all_extra[p, :, 0:LANES], selected.astype(BF16))
        owner = plan.seq_relative(plan.key_order, p) ^ own_place
        here = (slot_lane >= p * slots) & (slot_lane < (p + 1) * slots)
        slot_end = jnp.where(here, length * owner - length * p + 3 * slot_lane + 2, slot_end)
    row = lax.broadcasted_iota(jnp.int32, (length, 1), 0)
    tap = (row >= slots).astype(jnp.int32) + (row >= 2 * slots).astype(jnp.int32)
    query_place = length * own_place + 3 * (row - tap * slots) + tap
    causal = slot_end <= query_place
    for b in range(batch):
        matching = segment_rows[b : b + 1, :] == segment_column[b]
        bias[b] = jnp.where(causal & matching, 0.0, MASKED_OUT)

    low_lane = lax.broadcasted_iota(jnp.int32, (length, LANES), 1) < HEAD_DIM

    def stacked(part):
        zero = jnp.zeros_like(part)
        return jnp.concatenate(
            [jnp.where(low_lane, part, zero), jnp.where(low_lane, zero, part)], axis=0
        )

    def twice(part):
        return jnp.concatenate([part, part], axis=0)

    def merged(part):
        return jnp.where(low_lane, part[:length], part[length:])

    def rows_of(b):
        return pl.ds(pl.multiple_of(b * length, 16), length)

    def lanes_of(g):
        return pl.ds(pl.multiple_of(g * LANES, LANES), LANES)

    def scaled_queries(b, g):
        part = query_in[rows_of(b), lanes_of(g)].astype(F32) * SCALE
        return stacked(part).astype(BF16)

    def attend(number, carry):
        b, g = number // GROUPS, number % GROUPS
        rows, lanes = rows_of(b), lanes_of(g)
        queries = scaled_queries(b, g)
        own_key = twice(key_in[rows, lanes].astype(F32))
        scores = dot_nt(queries, all_keys[b, :, lanes]) + twice(bias[b])
        own_score = jnp.sum(queries.astype(F32) * own_key, axis=-1, keepdims=True)
        top = jnp.maximum(own_score, jnp.max(scores, axis=-1, keepdims=True))
        raised = jnp.exp(scores - top)
        own_raised = jnp.exp(own_score - top)
        inverse = 1.0 / (own_raised + jnp.sum(raised, axis=-1, keepdims=True))
        prob = raised * inverse
        own_prob = own_raised * inverse
        if keep_prob:
            prob_keep[number] = prob
        statistics[number, :, 0:1] = own_prob
        statistics[number, :, 1:2] = top - jnp.log(inverse)
        result = dot(prob.astype(BF16), all_values[b, :, lanes])
        own_value = twice(value_in[rows, lanes].astype(F32))
        result += own_prob.astype(BF16).astype(F32) * own_value
        attended_out[rows, lanes] = merged(result).astype(BF16)
        return carry

    lax.fori_loop(0, batch * GROUPS, attend, 0)

    x = x_in[...]
    hidden = x + dot(attended_out[...], w_out[...])
    unit, inverse_dev = normalize(hidden)
    gain = gain_ffn[...].astype(F32)
    normed_ffn_out[...] = (unit * gain).astype(BF16)
    order = order_matrix(length, False)
    for b in range(batch):
        cotangent_out[b * length : (b + 1) * length, :] = dot(order, cotangent[b]).astype(BF16)
    expanded_sum[...] = hidden
    d_normed_sum[...] = jnp.zeros_like(d_normed_sum)
    chunk = width
    total_width = w_up.shape[1]

    def feed(number, carry):
        columns = pl.ds(pl.multiple_of(number * chunk, chunk), chunk)
        expanded = dot(normed_ffn_out[...], w_up[:, columns])
        square = expanded * expanded
        curve = jnp.tanh(GELU_SCALE * expanded * (1.0 + GELU_CUBIC * square))
        activated = (0.5 * expanded * (1.0 + curve)).astype(BF16)
        activated_out[:, columns] = activated
        slope = 0.5 * (1.0 + curve) + 0.5 * expanded * (1.0 - curve * curve) * (
            GELU_SCALE * (1.0 + 3.0 * GELU_CUBIC * square)
        )
        expanded_sum[...] += dot(activated, w_down[columns, :])
        d_activated = dot_nt(cotangent_out[...], w_down[columns, :])
        d_expanded = (d_activated * slope).astype(BF16)
        d_expanded_out[:, columns] = d_expanded
        d_normed_sum[...] += dot_nt(d_expanded, w_up[:, columns])
        return carry

    lax.fori_loop(0, total_width // chunk, feed, 0)

    unorder = order_matrix(length, True)
    for b in range(batch):
        part = expanded_sum[b * length : (b + 1) * length, :].astype(BF16)
        layer_out[b] = dot(unorder, part).astype(BF16)
    d_normed = d_normed_sum[...]
    gain_grad[...] = jnp.sum(d_normed * unit, axis=0, keepdims=True)
    d_hidden = cotangent_out[...].astype(F32) + normalize_back(d_normed, unit, inverse_dev, gain)
    d_hidden_out[...] = d_hidden
    d_branch = d_hidden.astype(BF16)
    d_branch_out[...] = d_branch
    d_attended[...] = dot_nt(d_branch, w_out[...]).astype(BF16)

    value_spot = [key_position[plan.seq_relative(plan.value_order, p)] for p in range(n_seq)]

    def attend_back(number, carry):
        b, g = number // GROUPS, number % GROUPS
        rows, lanes = rows_of(b), lanes_of(g)
        queries = scaled_queries(b, g)
        own_prob = statistics[number, :, 0:1]
        if keep_prob:
            prob = prob_keep[number]
        else:
            scores = dot_nt(queries, all_keys[b, :, lanes]) + twice(bias[b])
            prob = jnp.exp(scores - statistics[number, :, 1:2])
        grads = stacked(d_attended[rows, lanes])
        own_value = twice(value_in[rows, lanes].astype(F32))
        own_key = twice(key_in[rows, lanes].astype(F32))
        prob_grad = dot_nt(grads, all_values[b, :, lanes])
        own_prob_grad = jnp.sum(grads.astype(F32) * own_value, axis=-1, keepdims=True)
        delta = own_prob * own_prob_grad + jnp.sum(prob * prob_grad, axis=-1, keepdims=True)
        d_score = (prob * (prob_grad - delta)).astype(BF16)
        d_own = (own_prob * (own_prob_grad - delta)).astype(BF16).astype(F32)
        own_low = own_prob.astype(BF16).astype(F32)
        d_query = merged(dot(d_score, all_keys[b, :, lanes]) + d_own * own_key) * SCALE
        d_query_out[rows, lanes] = d_query.astype(BF16)
        d_key_own[rows, lanes] = merged(d_own * queries.astype(F32))
        d_value_own[rows, lanes] = merged(own_low * grads.astype(F32))
        key_sums = dot_tn(d_score, queries).astype(BF16)
        value_sums = dot_tn(prob.astype(BF16), grads).astype(BF16)
        for p in range(n_seq):
            d_packed_key[p, pl.ds(pl.multiple_of(b * slots, 16), slots), lanes] = key_sums[
                p * slots : (p + 1) * slots
            ]
            q = value_spot[p]
            d_packed_value[p, pl.ds(pl.multiple_of(b * slots, 16), slots), lanes] = value_sums[
                q * slots : (q + 1) * slots
            ]
        return carry

    lax.fori_loop(0, batch * GROUPS, attend_back, 0)


def spread(plan, place, order, parts, send, keep, offset):
    rows_block = sum(rows for _, rows in parts)
    half = plan.blocks // 2
    for target, core in ((send, 1), (keep, 0)):
        for p in range(half):
            block = plan.relative(order, core * half + p) ^ place
            start = offset + p * rows_block
            for source, rows in parts:
                target[start : start + rows, :] = source[
                    pl.ds(pl.multiple_of(block * rows, 16), rows), :
                ]
                start += rows


def ffn_grad_kernel(
    plan, order_a, order_b,
    place, activated, cotangent, normed_ffn, d_expanded, attended, d_branch,
    send, keep,
    down_rows, up_rows, out_rows,
):
    width = cotangent.shape[1]
    chunk = 512
    for c in range(activated.shape[1] // chunk):
        columns = slice(c * chunk, (c + 1) * chunk)
        down_rows[columns, :] = dot_tn(activated[:, columns], cotangent[...]).astype(BF16)
        up_rows[c] = dot_tn(normed_ffn[...], d_expanded[:, columns]).astype(BF16)
    out_rows[...] = dot_tn(attended[...], d_branch[...]).astype(BF16)
    mine = place[1]
    down_block = activated.shape[1] // plan.blocks
    thin = width // plan.blocks
    rows_a = down_block + thin
    spread(plan, mine, order_a, ((down_rows, down_block), (out_rows, thin)), send, keep, 0)
    ups = tuple((up_rows.at[c], thin) for c in range(activated.shape[1] // chunk))
    spread(plan, mine, order_b, ups, send, keep, rows_a * plan.blocks // 2)


def tail_kernel(
    plan, order_a, order_b,
    place, d_packed_key, d_packed_value, x_in, normed, d_query, key_in, value_in,
    d_key_own, d_value_own, d_hidden, segment_column, gain, w_query, w_key, w_value,
    conv_key, conv_value, gain_ffn_grad,
    send, keep, grad_tokens,
    key_conv_rows, value_conv_rows, key_rows, value_rows, query_rows, gain_rows,
):
    batch, length, width = grad_tokens.shape
    slots = length // 3
    masks = [window_masks(segment_column[b], slots) for b in range(batch)]
    grads = []
    for d_packed, flat, conv, own, conv_rows, rows_out in (
        (d_packed_key, key_in, conv_key, d_key_own, key_conv_rows, key_rows),
        (d_packed_value, value_in, conv_value, d_value_own, value_conv_rows, value_rows),
    ):
        back = d_packed[...]
        pieces = [[None] * 3 for _ in range(batch)]
        for i in range(3):
            taps = []
            from_tap = dot_nt(back, conv[i * width : (i + 1) * width, :])
            for b in range(batch):
                start = b * length + i * slots
                part = flat[start : start + slots, :].astype(F32) * masks[b][i]
                taps.append(part.astype(BF16))
                pieces[b][i] = from_tap[b * slots : (b + 1) * slots] * masks[b][i]
            window = jnp.concatenate(taps, axis=0)
            conv_rows[i * width : (i + 1) * width, :] = dot_tn(window, back).astype(BF16)
        whole = jnp.concatenate([piece for row in pieces for piece in row], axis=0)
        d_flat = (whole + own[...]).astype(BF16)
        grads.append(d_flat)
        rows_out[...] = dot_tn(normed[...], d_flat).astype(BF16)
    query_rows[...] = dot_tn(normed[...], d_query[...]).astype(BF16)
    d_normed = (
        dot_nt(d_query[...], w_query[...])
        + dot_nt(grads[0], w_key[...])
        + dot_nt(grads[1], w_value[...])
    )
    unit, inverse_dev = normalize(x_in[...])
    gain_grad = jnp.sum(d_normed * unit, axis=0, keepdims=True)
    d_input = normalize_back(d_normed, unit, inverse_dev, gain[...].astype(F32))
    result = (d_hidden[...] + d_input).astype(BF16)
    unorder = order_matrix(length, True)
    for b in range(batch):
        part = result[b * length : (b + 1) * length, :]
        grad_tokens[b] = dot(unorder, part).astype(BF16)
    row = lax.broadcasted_iota(jnp.int32, (EXTRA_ROWS, width), 0)
    gains = jnp.where(row == 0, gain_grad, jnp.where(row == 1, gain_ffn_grad[...], 0.0))
    for p in range(plan.blocks):
        gain_rows[p * EXTRA_ROWS : (p + 1) * EXTRA_ROWS, :] = gains.astype(BF16)
    mine = place[1]
    conv_block = 3 * width // plan.blocks
    thin = width // plan.blocks
    rows_a = conv_block + 2 * thin
    spread(
        plan, mine, order_a,
        ((key_conv_rows, conv_block), (key_rows, thin), (query_rows, thin)), send, keep, 0,
    )
    spread(
        plan, mine, order_b,
        ((value_conv_rows, conv_block), (value_rows, thin), (gain_rows, EXTRA_ROWS)),
        send, keep, rows_a * plan.blocks // 2,
    )


def unspread(plan, place, order, parts, near, far, offset):
    rows_block = sum(rows for _, rows, _ in parts)
    half = plan.blocks // 2
    for source, core in ((near, 0), (far, 1)):
        for p in range(half):
            block = plan.relative(order, core * half + p) ^ place
            start = offset + p * rows_block
            for target, rows, columns in parts:
                part = source[start : start + rows, :].astype(F32)
                spot = pl.ds(pl.multiple_of(block * rows, 16), rows)
                target[spot, columns] = part
                start += rows


def ffn_finish_kernel(plan, order_a, order_b, place, near, far, grad_down, grad_up, grad_out):
    width = grad_out.shape[1]
    down_block = grad_down.shape[0] // plan.blocks
    thin = width // plan.blocks
    everything = slice(None)
    unspread(
        plan, place[1], order_a,
        ((grad_down, down_block, everything), (grad_out, thin, everything)), near, far, 0,
    )
    ups = tuple(
        (grad_up, thin, slice(c * width, (c + 1) * width)) for c in range(grad_up.shape[1] // width)
    )
    unspread(plan, place[1], order_b, ups, near, far, (down_block + thin) * plan.blocks // 2)


def tail_finish_kernel(
    plan, order_a, order_b, place, near, far,
    grad_conv_key, grad_key, grad_query, grad_conv_value, grad_value, grad_gains,
):
    width = grad_key.shape[1]
    conv_block = grad_conv_key.shape[0] // plan.blocks
    thin = width // plan.blocks
    everything = slice(None)
    unspread(
        plan, place[1], order_a,
        (
            (grad_conv_key, conv_block, everything),
            (grad_key, thin, everything),
            (grad_query, thin, everything),
        ),
        near, far, 0,
    )
    offset = (conv_block + 2 * thin) * plan.blocks // 2
    rows_block = conv_block + thin + EXTRA_ROWS
    half = plan.blocks // 2
    for source, core in ((near, 0), (far, 1)):
        for p in range(half):
            block = plan.relative(order_b, core * half + p) ^ place[1]
            start = offset + p * rows_block
            grad_conv_value[pl.ds(pl.multiple_of(block * conv_block, 16), conv_block), :] = source[
                start : start + conv_block, :
            ].astype(F32)
            start += conv_block
            grad_value[pl.ds(pl.multiple_of(block * thin, 16), thin), :] = source[
                start : start + thin, :
            ].astype(F32)
    start = offset + conv_block + thin
    grad_gains[...] = near[start : start + EXTRA_ROWS, :].astype(F32)


def add(left, right):
    return (left.astype(F32) + right.astype(F32)).astype(BF16)


def gather_row(plan, array, order):
    held = array[None]
    for number, bit in enumerate(order):
        arrived = plan.swap(held, ("seq", bit))
        if number == len(order) - 1:
            return held, arrived
        held = jnp.concatenate([held, arrived], axis=0)


def scatter_row(plan, array, order):
    held = array
    for bit in reversed(order):
        half = held.shape[0] // 2
        held = add(held[:half], plan.swap(held[half:], ("seq", bit)))
    return held[0]


def halve(plan, array, bit):
    half = array.shape[0] // 2
    return add(array[:half], plan.swap(array[half:], bit))


def reduce_blocks(plan, send, keep, split, first_a, first_b):
    total = add(keep, plan.swap(send, plan.core))
    part_a, part_b = total[:split], total[split:]
    for bit_a, bit_b in zip(first_a, first_b):
        part_a = halve(plan, part_a, bit_a)
        part_b = halve(plan, part_b, bit_b)
    for bit in plan.tail:
        half_a, half_b = part_a.shape[0] // 2, part_b.shape[0] // 2
        arrived = plan.swap(jnp.concatenate([part_a[half_a:], part_b[half_b:]], axis=0), bit)
        part_a = add(part_a[:half_a], arrived[:half_a])
        part_b = add(part_b[:half_b], arrived[half_a:])
    for bit in plan.rest:
        arrived = plan.swap(jnp.concatenate([part_a, part_b], axis=0), bit)
        part_a = add(part_a, arrived[: part_a.shape[0]])
        part_b = add(part_b, arrived[part_a.shape[0] :])
    return part_a, part_b


def gather_blocks(plan, part_a, part_b, first_a, first_b):
    for bit in reversed(plan.tail):
        arrived = plan.swap(jnp.concatenate([part_a, part_b], axis=0), bit)
        rows = part_a.shape[0]
        part_a = jnp.concatenate([part_a, arrived[:rows]], axis=0)
        part_b = jnp.concatenate([part_b, arrived[rows:]], axis=0)
    for bit_a, bit_b in zip(reversed(first_a), reversed(first_b)):
        far_a, far_b = plan.swap(part_a, bit_a), plan.swap(part_b, bit_b)
        part_a = jnp.concatenate([part_a, far_a], axis=0)
        part_b = jnp.concatenate([part_b, far_b], axis=0)
    near = jnp.concatenate([part_a, part_b], axis=0)
    return near, plan.swap(near, plan.core)


def body(
    plan, tokens, segments, cotangent, gain_attn, w_query, w_key, w_value, conv_key, conv_value,
    w_out, gain_ffn, w_up, w_down,
):
    batch, _, length, width = tokens.shape
    slots = length // 3
    positions = batch * length
    tokens, segments, cotangent = tokens[:, 0], segments[:, 0], cotangent[:, 0]
    gain_attn, gain_ffn = gain_attn[None], gain_ffn[None]
    seq_place = lax.axis_index("seq").astype(jnp.int32)
    block_place = lax.axis_index("rows").astype(jnp.int32) * plan.seq_block + lax.rem(
        seq_place, jnp.int32(plan.seq_block)
    )
    place = jnp.stack([seq_place, block_place])
    grouped = segments.reshape(batch, slots, 3)
    segment_column = grouped.transpose(0, 2, 1).reshape(batch, length, 1).astype(F32)
    extra = jnp.pad(
        grouped[:, :, 2].astype(BF16), ((0, EXTRA_ROWS - batch), (0, width - slots))
    )
    flat = ((positions, width), BF16)
    flat32 = ((positions, width), F32)
    x, normed, queries, key_rows, value_rows, packed_key, packed_value = call(
        project_kernel,
        "project",
        [flat32] + [flat] * 4
        + [((batch * slots + EXTRA_ROWS, width), BF16), ((batch * slots, width), BF16)],
        flops=2 * positions * width * width * 5,
        bytes_accessed=2 * width * width * 9,
    )(
        tokens, gain_attn, w_query, w_key, w_value, conv_key, conv_value, segment_column, extra
    )
    keys_near, keys_far = gather_row(plan, packed_key, plan.key_order)
    values_near, values_far = gather_row(plan, packed_value, plan.value_order)

    total_slots = slots * plan.n_seq
    keep_prob = total_slots <= 768
    wide = ((positions, w_up.shape[1]), BF16)
    steps = batch * GROUPS
    packed_shape = ((plan.n_seq, batch * slots, width), BF16)
    (
        layer_out, d_hidden, normed_ffn, activated, d_expanded, cotangent_rows, attended, d_branch,
        d_query, d_key_own, d_value_own, d_packed_key, d_packed_value, gain_ffn_grad,
    ) = call(
        functools.partial(layer_kernel, plan, keep_prob),
        "layer",
        [
            ((batch, length, width), BF16), flat32, flat, wide, wide, flat, flat, flat,
            flat, flat32, flat32, packed_shape, packed_shape, ((1, width), F32),
        ],
        scratch=[
            pltpu.VMEM((batch, total_slots, width), BF16),
            pltpu.VMEM((batch, total_slots, width), BF16),
            pltpu.VMEM((plan.n_seq, EXTRA_ROWS, width), BF16),
            pltpu.VMEM((batch, length, total_slots), F32),
            pltpu.VMEM((steps, 2 * length, LANES), F32),
            pltpu.VMEM((steps if keep_prob else 1, 2 * length, total_slots), F32),
            pltpu.VMEM((positions, width), F32),
            pltpu.VMEM((positions, width), F32),
            pltpu.VMEM((positions, width), BF16),
            pltpu.SemaphoreType.DMA((plan.n_seq * (1 + 2 * batch),)),
        ],
        flops=2 * positions * width * width * 24,
        bytes_accessed=2 * width * width * 20,
        smem=1,
        anywhere=(6, 7, 8, 9),
    )(
        place, x, cotangent, queries, key_rows, value_rows, keys_near, keys_far, values_near,
        values_far, segment_column, w_out, gain_ffn, w_up, w_down,
    )

    core = [plan.core]
    order_a, order_b = core + plan.first + plan.tail, core + plan.second + plan.tail
    half = plan.blocks // 2
    thin = width // plan.blocks
    down_block = w_down.shape[0] // plan.blocks
    chunks = w_up.shape[1] // width
    rows_a, rows_b = down_block + thin, chunks * thin
    buffer = ((half * (rows_a + rows_b), width), BF16)
    ffn_send, ffn_keep = call(
        functools.partial(ffn_grad_kernel, plan, order_a, order_b),
        "ffn_grads",
        [buffer, buffer],
        scratch=[
            pltpu.VMEM((w_down.shape[0], width), BF16),
            pltpu.VMEM((chunks, width, width), BF16),
            pltpu.VMEM((width, width), BF16),
        ],
        flops=2 * positions * width * width * 9,
        bytes_accessed=2 * width * width * 18,
        smem=1,
    )(place, activated, cotangent_rows, normed_ffn, d_expanded, attended, d_branch)
    own_key_grad = scatter_row(plan, d_packed_key, plan.key_order)
    own_value_grad = scatter_row(plan, d_packed_value, plan.value_order)
    ffn_a, ffn_b = reduce_blocks(
        plan, ffn_send, ffn_keep, half * rows_a, plan.first, plan.second
    )

    conv_block = conv_key.shape[0] // plan.blocks
    tail_a, tail_b = conv_block + 2 * thin, conv_block + thin + EXTRA_ROWS
    tail_buffer = ((half * (tail_a + tail_b), width), BF16)
    square = pltpu.VMEM((width, width), BF16)
    tail_send, tail_keep, grad_tokens = call(
        functools.partial(tail_kernel, plan, order_b, order_a),
        "tail",
        [tail_buffer, tail_buffer, ((batch, length, width), BF16)],
        scratch=[
            pltpu.VMEM(conv_key.shape, BF16), pltpu.VMEM(conv_value.shape, BF16),
            square, square, square, pltpu.VMEM((plan.blocks * EXTRA_ROWS, width), BF16),
        ],
        flops=2 * positions * width * width * 10,
        bytes_accessed=2 * width * width * 18,
        smem=1,
    )(
        place, own_key_grad, own_value_grad, x, normed, d_query, key_rows, value_rows,
        d_key_own, d_value_own, d_hidden, segment_column, gain_attn, w_query, w_key, w_value,
        conv_key, conv_value, gain_ffn_grad,
    )
    ffn_near, ffn_far = gather_blocks(plan, ffn_a, ffn_b, plan.first, plan.second)
    tail_first, tail_second = reduce_blocks(
        plan, tail_send, tail_keep, half * tail_a, plan.second, plan.first
    )
    tail_near, tail_far = gather_blocks(
        plan, tail_first, tail_second, plan.second, plan.first
    )
    matrix = ((width, width), F32)
    grad_down, grad_up, grad_out = call(
        functools.partial(ffn_finish_kernel, plan, order_a, order_b),
        "ffn_finish",
        [(w_down.shape, F32), (w_up.shape, F32), matrix],
        bytes_accessed=6 * width * width * 9,
        smem=1,
    )(place, ffn_near, ffn_far)
    grad_conv_key, grad_key, grad_query, grad_conv_value, grad_value, grad_gains = call(
        functools.partial(tail_finish_kernel, plan, order_b, order_a),
        "tail_finish",
        [(conv_key.shape, F32), matrix, matrix, (conv_value.shape, F32), matrix]
        + [((EXTRA_ROWS, width), F32)],
        bytes_accessed=6 * width * width * 9,
        smem=1,
    )(place, tail_near, tail_far)
    return (
        layer_out[:, None], grad_tokens[:, None], grad_gains[0], grad_query, grad_key, grad_value,
        grad_conv_key, grad_conv_value, grad_out, grad_gains[1], grad_up, grad_down,
    )


def solution(mesh):
    packed = P(None, "rows", "seq", None)
    in_specs = (packed, P(None, "rows", "seq"), packed) + (P(),) * 10
    out_specs = (packed, packed) + (P(),) * 10
    return jax.shard_map(
        functools.partial(body, Plan(mesh)),
        mesh=mesh, in_specs=in_specs, out_specs=out_specs, check_vma=False,
    )
```

time: 1030 us -> 277 us (0.27); the launches traced: 1010 us -> 276 us
  blocking collectives: 333 us -> 0 us
  local copies, waits for them, and re-layouts: 247 us -> 8.42 us
  matrix products: 110 us -> 0 us
  waiting for transfers between devices: 251 us -> 150 us
  Pallas kernels: 0 us -> 58.4 us
  starting transfers between devices: 0.2 us -> 46 us
  other arithmetic: 50.6 us -> 12.2 us
  between operations: 16 us -> 1.38 us
    all_gather x9 -> x0, blocking collectives: 292 us -> none  [the longest x2 66 us: attention_back(): lax.all_gather(log_total, 'seq', axis=2, tiled=True)]
    psum x1 -> x0, waiting for transfers between devices: 250 us -> none  [body(): lax.psum((g_gain_attn, g_query, g_key, g_value, g_conv_key, g_conv_value,...]
    ppermute x0 -> x40, waiting for transfers between devices: none -> 150 us  [swap(): return lax.ppermute(array, axis, [(i, i ^ value) for i in range(size)])]
    dot_general x138 -> x0, matrix products: 110 us -> none  [the longest x16 27.3 us: weight_grad(): jnp.einsum('rsc,rsd->cd', operand, gradient, preferred_element_type=jnp.f...]
    pallas_call x0 -> x6, Pallas kernels: none -> 58.4 us  [run(): pl.pallas_call(kernel, name=name, out_shape=[jax.ShapeDtypeStruct(shape,...]
    unnamed x385 -> x33, local copies, waits for them, and re-layouts: 53.3 us -> 2.67 us
    dynamic_slice x102 -> x0, local copies, waits for them, and re-layouts: 49.9 us -> none  [the longest x36 19.9 us: owner_step(): lax.dynamic_slice_in_dim(all_grads, offset, query_block, 1)]
    slice x8 -> x29, local copies, waits for them, and re-layouts: 48.6 us -> 2.08 us  [the longest x1 1.38 us: body(): grad_gains[1]]
  transfers between devices with their start and end apart: 5 -> 40, of which waited for: 1 -> 26; matrix products, arithmetic and copies ran while one was open for 31% -> 4% of each run, Pallas kernels for 0% -> 6%
where the time goes in v1:
time: 277 us; the launch traced here: 276 us
  waiting for transfers between devices  150 us (54%)
  Pallas kernels  58.4 us (21%)
  starting transfers between devices  46 us (17%)
  other arithmetic  12.2 us (4%)
  local copies, waits for them, and re-layouts  8.42 us (3%)
    ppermute x40, waiting for transfers between devices, swap(): return lax.ppermute(array, axis, [(i, i ^ value) for i in range(size)])  150 us
    pallas_call x6, Pallas kernels, run(): pl.pallas_call(kernel, name=name, out_shape=[jax.ShapeDtypeStruct(shape,...  58.4 us
    ppermute x40, starting transfers between devices, swap(): return lax.ppermute(array, axis, [(i, i ^ value) for i in range(size)])  46 us
  transfers between devices with their start and end apart: 40, of which 26 were waited for; matrix products, arithmetic and copies ran while one was open for 4% of the time, Pallas kernels for 6%

profile of v1, /device:TPU:0, one launch (start us, length us, event | category | flops | bytes accessed | tf_op | source)
XLA Modules:
  0.0 276.2 jit_solution(6610888482494634979)
XLA Ops:
  5.2 4.8 %project.1 = (f32[288,512]{1,0:T(8,128)}, bf16[288,512]{1,0:T(8,128)(2,1)}, bf16[288,512]{1,0:T(8,128)(2,1)}, bf16[288,512]{1,0:T(8,128)(2,1)}, bf16[288,512]{1,...) custom-call(bf16[2,144,512]{2,1,0:T(8,128)(2,1)} %bitcast.25, bf16[1,512]{1,0:T(2,128)(2,1)} %broadcast_in_dim.18.gain, ...), custom_call_target="tpu_custom_call" | custom-call | flops 754974720 | bytes 4718592 | tf_op jit(solution)/shard_map/project/pallas_call | solution.py:122
  10.1 4.0 %collective-permute-start = (bf16[1,112,512]{2,1,0:T(8,128)(2,1)}, bf16[1,112,512]{2,1,0:T(8,128)(2,1)S(1)}, u32[]{:S(2)}, u32[]{:S(2)}) collective-permute-start(bf16[1,112,512]{2,1,0:T(8,128)(2,1)} %bitcast.19), channel_id=1, source_target_pairs={{0,4},{1,5},{2,6},{3,7},{4,0},{5,1},{6,2},{7,3},{8,12},{9,13},{10,... | collective-permute-start | bytes 344072 | tf_op jit(solution)/shard_map/ppermute | solution.py:96
  14.1 1.5 collective-permute-start.3
  15.6 4.3 %collective-permute-done = bf16[1,112,512]{2,1,0:T(8,128)(2,1)S(1)} collective-permute-done((bf16[1,112,512]{2,1,0:T(8,128)(2,1)}, bf16[1,112,512]{2,1,0:T(8,128)(2,1)S(1)}, u32[]{:S(2)}, u32[]{:S(2)}) %collective-permute-start) | collective-permute-done | bytes 114720 | tf_op jit(solution)/shard_map/ppermute | solution.py:96
  22.6 3.3 %collective-permute-start.4 = (bf16[2,96,512]{2,1,0:T(8,128)(2,1)S(1)}, bf16[2,96,512]{2,1,0:T(8,128)(2,1)S(1)}, u32[]{:S(2)}, u32[]{:S(2)}) collective-permute-start(bf16[2,96,512]{2,1,0:T(8,128)(2,1)S(1)} %pad_maximum_fusion.16), channel_id=1, source_target_pairs={{0,4},{1,5},{2,6},{3,7},{4,0},{5,1},{6,2},{7,3},{8,12},{9,13},{10,... | collective-permute-start | bytes 589832 | tf_op jit(solution)/shard_map/ppermute | solution.py:96
  26.0 5.4 %collective-permute-done.1 = bf16[2,112,512]{2,1,0:T(8,128)(2,1)S(1)} collective-permute-done((bf16[2,112,512]{2,1,0:T(8,128)(2,1)S(1)}, bf16[2,112,512]{2,1,0:T(8,128)(2,1)S(1)}, u32[]{:S(2)}, u32[]{:S(2)}) %collective-permute-start.1) | collective-permute-done | bytes 229408 | tf_op jit(solution)/shard_map/ppermute | solution.py:96
  32.3 1.4 collective-permute-start.2
  37.3 7.5 %collective-permute-done.5.values_far = bf16[4,96,512]{2,1,0:T(8,128)(2,1)S(1)} collective-permute-done((bf16[4,96,512]{2,1,0:T(8,128)(2,1)S(1)}, bf16[4,96,512]{2,1,0:T(8,128)(2,1)S(1)}, u32[]{:S(2)}, u32[]{:S(2)}) %collective-permute-start.5) | collective-permute-done | bytes 393248 | tf_op jit(solution)/shard_map/ppermute | solution.py:96
  45.7 23.8 %layer.1 = (bf16[2,144,512]{2,1,0:T(8,128)(2,1)}, f32[288,512]{1,0:T(8,128)}, bf16[288,512]{1,0:T(8,128)(2,1)}, bf16[288,2048]{1,0:T(8,128)(2,1)}, bf16[288,2048...) custom-call(s32[2]{0:T(128)} %pad_add_fusion.place, ...), custom_call_target="tpu_custom_call" | custom-call | flops 3623878656 | bytes 10485760 | tf_op jit(solution)/shard_map/layer/pallas_call | solution.py:122
  69.5 7.0 %ffn_grads.1 = (bf16[2304,512]{1,0:T(8,128)(2,1)}, bf16[2304,512]{1,0:T(8,128)(2,1)}) custom-call(s32[2]{0:T(128)} %pad_add_fusion.place, bf16[288,2048]{1,0:T(8,128)(2,1)} %get-tuple-element.71.activated, bf16[288,512]{1,0:T(8,128)(2,1)} %get-tuple-element.72.cotangent, bf16[288,512]{1,0:T(8,128)(2,1)} %get-tuple-element.73.normed_ffn, ...), custom_call_target="tpu_custom_call" | custom-call | flops 1358954496 | bytes 9437184 | tf_op jit(solution)/shard_map/ffn_grads/pallas_call | solution.py:122
  76.6 1.8 collective-permute-start.9
  78.4 1.6 collective-permute-start.6
  80.0 8.2 %collective-permute-done.9 = bf16[4,96,512]{2,1,0:T(8,128)(2,1)S(1)} collective-permute-done((bf16[4,96,512]{2,1,0:T(8,128)(2,1)S(1)}, bf16[4,96,512]{2,1,0:T(8,128)(2,1)S(1)}, u32[]{:S(2)}, u32[]{:S(2)}) %collective-permute-start.9) | collective-permute-done | bytes 393248 | tf_op jit(solution)/shard_map/ppermute | solution.py:96
  88.3 2.7 collective-permute-start.10
  91.1 1.8 collective-permute-start.7
  92.9 7.2 %collective-permute-done.10 = bf16[2,96,512]{2,1,0:T(8,128)(2,1)S(1)} collective-permute-done((bf16[2,96,512]{2,1,0:T(8,128)(2,1)S(1)}, bf16[2,96,512]{2,1,0:T(8,128)(2,1)S(1)}, u32[]{:S(2)}, u32[]{:S(2)}) %collective-permute-start.10) | collective-permute-done | bytes 196640 | tf_op jit(solution)/shard_map/ppermute | solution.py:96
  100.2 1.6 collective-permute-start.11
  101.9 2.9 %collective-permute-done.11 = bf16[1,96,512]{2,1,0:T(8,128)(2,1)S(1)} collective-permute-done((bf16[1,96,512]{2,1,0:T(8,128)(2,1)S(1)}, bf16[1,96,512]{2,1,0:T(8,128)(2,1)S(1)}, u32[]{:S(2)}, u32[]{:S(2)}) %collective-permute-start.11) | collective-permute-done | bytes 98336 | tf_op jit(solution)/shard_map/ppermute | solution.py:96
  105.5 3.5 %collective-permute-done.8 = bf16[1,96,512]{2,1,0:T(8,128)(2,1)S(1)} collective-permute-done((bf16[1,96,512]{2,1,0:T(8,128)(2,1)S(1)}, bf16[1,96,512]{2,1,0:T(8,128)(2,1)S(1)}, u32[]{:S(2)}, u32[]{:S(2)}) %collective-permute-start.8) | collective-permute-done | bytes 98336 | tf_op jit(solution)/shard_map/ppermute | solution.py:96
  109.7 9.4 %tail.1 = (bf16[2560,512]{1,0:T(8,128)(2,1)}, bf16[2560,512]{1,0:T(8,128)(2,1)}, bf16[2,144,512]{2,1,0:T(8,128)(2,1)}) custom-call(s32[2]{0:T(128)} %pad_add_fusion.place, bf16[96,512]{1,0:T(8,128)(2,1)} %fusion.d_packed_key, bf16[96,512]{1,0:T(8,128)(2,1)} %fusion.1.d_packed_value, f32[288,512]{1,0:T(8,128)} %get-tuple-element.47.x_in, ...), custom_call_target="tpu_custom_call" | custom-call | flops 1509949440 | bytes 9437184 | tf_op jit(solution)/shard_map/tail/pallas_call | solution.py:122
  119.2 2.3 add_convert_fusion.1
  122.2 1.6 collective-permute-start.27
  123.8 12.2 %collective-permute-done.29 = bf16[512,512]{1,0:T(8,128)(2,1)S(1)} collective-permute-done((bf16[512,512]{1,0:T(8,128)(2,1)S(1)}, bf16[512,512]{1,0:T(8,128)(2,1)S(1)}, u32[]{:S(2)}, u32[]{:S(2)}) %collective-permute-start.29) | collective-permute-done | bytes 524320 | tf_op jit(solution)/shard_map/ppermute | solution.py:96
  136.1 1.6 collective-permute-start.30
  137.7 1.9 collective-permute-done.27
  139.9 1.8 collective-permute-start.28
  141.6 3.1 %collective-permute-done.30 = bf16[256,512]{1,0:T(8,128)(2,1)S(1)} collective-permute-done((bf16[256,512]{1,0:T(8,128)(2,1)S(1)}, bf16[256,512]{1,0:T(8,128)(2,1)S(1)}, u32[]{:S(2)}, u32[]{:S(2)}) %collective-permute-start.30) | collective-permute-done | bytes 262176 | tf_op jit(solution)/shard_map/ppermute | solution.py:96
  144.8 3.6 %collective-permute-done.28 = bf16[320,512]{1,0:T(8,128)(2,1)S(1)} collective-permute-done((bf16[320,512]{1,0:T(8,128)(2,1)S(1)}, bf16[320,512]{1,0:T(8,128)(2,1)S(1)}, u32[]{:S(2)}, u32[]{:S(2)}) %collective-permute-start.28) | collective-permute-done | bytes 327712 | tf_op jit(solution)/shard_map/ppermute | solution.py:96
  149.5 5.9 %collective-permute-done.31 = bf16[288,512]{1,0:T(8,128)(2,1)S(1)} collective-permute-done((bf16[288,512]{1,0:T(8,128)(2,1)S(1)}, bf16[288,512]{1,0:T(8,128)(2,1)S(1)}, u32[]{:S(2)}, u32[]{:S(2)}) %collective-permute-start.31) | collective-permute-done | bytes 294944 | tf_op jit(solution)/shard_map/ppermute | solution.py:96
  157.7 1.5 collective-permute-start.15
  159.2 6.3 %collective-permute-done.32 = bf16[144,512]{1,0:T(8,128)(2,1)S(1)} collective-permute-done((bf16[144,512]{1,0:T(8,128)(2,1)S(1)}, bf16[144,512]{1,0:T(8,128)(2,1)S(1)}, u32[]{:S(2)}, u32[]{:S(2)}) %collective-permute-start.32) | collective-permute-done | bytes 147488 | tf_op jit(solution)/shard_map/ppermute | solution.py:96
  165.7 7.2 %collective-permute-done.33 = bf16[144,512]{1,0:T(8,128)(2,1)S(1)} collective-permute-done((bf16[144,512]{1,0:T(8,128)(2,1)S(1)}, bf16[144,512]{1,0:T(8,128)(2,1)S(1)}, u32[]{:S(2)}, u32[]{:S(2)}) %collective-permute-start.33) | collective-permute-done | bytes 147488 | tf_op jit(solution)/shard_map/ppermute | solution.py:96
  174.2 1.6 collective-permute-start.14
  176.5 5.9 %collective-permute-done.16 = bf16[320,512]{1,0:T(8,128)(2,1)S(1)} collective-permute-done((bf16[320,512]{1,0:T(8,128)(2,1)S(1)}, bf16[320,512]{1,0:T(8,128)(2,1)S(1)}, u32[]{:S(2)}, u32[]{:S(2)}) %collective-permute-start.16) | collective-permute-done | bytes 327712 | tf_op jit(solution)/shard_map/ppermute | solution.py:96
  184.9 5.8 %collective-permute-done.17 = bf16[320,512]{1,0:T(8,128)(2,1)S(1)} collective-permute-done((bf16[320,512]{1,0:T(8,128)(2,1)S(1)}, bf16[320,512]{1,0:T(8,128)(2,1)S(1)}, u32[]{:S(2)}, u32[]{:S(2)}) %collective-permute-start.17) | collective-permute-done | bytes 327712 | tf_op jit(solution)/shard_map/ppermute | solution.py:96
  191.7 1.9 collective-permute-start.36
  193.6 5.8 %collective-permute-done.18 = bf16[160,512]{1,0:T(8,128)(2,1)S(1)} collective-permute-done((bf16[160,512]{1,0:T(8,128)(2,1)S(1)}, bf16[160,512]{1,0:T(8,128)(2,1)S(1)}, u32[]{:S(2)}, u32[]{:S(2)}) %collective-permute-start.18) | collective-permute-done | bytes 163872 | tf_op jit(solution)/shard_map/ppermute | solution.py:96
  199.6 7.1 %collective-permute-done.19 = bf16[160,512]{1,0:T(8,128)(2,1)S(1)} collective-permute-done((bf16[160,512]{1,0:T(8,128)(2,1)S(1)}, bf16[160,512]{1,0:T(8,128)(2,1)S(1)}, u32[]{:S(2)}, u32[]{:S(2)}) %collective-permute-start.19) | collective-permute-done | bytes 163872 | tf_op jit(solution)/shard_map/ppermute | solution.py:96
  206.9 7.0 %collective-permute-done.20 = bf16[320,512]{1,0:T(8,128)(2,1)S(1)} collective-permute-done((bf16[320,512]{1,0:T(8,128)(2,1)S(1)}, bf16[320,512]{1,0:T(8,128)(2,1)S(1)}, u32[]{:S(2)}, u32[]{:S(2)}) %collective-permute-start.20) | collective-permute-done | bytes 327712 | tf_op jit(solution)/shard_map/ppermute | solution.py:96
  214.0 3.0 %collective-permute-start.21 = (bf16[320,512]{1,0:T(8,128)(2,1)S(1)}, bf16[320,512]{1,0:T(8,128)(2,1)S(1)}, u32[]{:S(2)}, u32[]{:S(2)}) collective-permute-start(bf16[320,512]{1,0:T(8,128)(2,1)S(1)} %pad_maximum_fusion.9), channel_id=1, source_target_pairs={{0,16},{8,24},{16,0},{24,8},{1,17},{9,25},{17,1},{25,9},{2,18},{10... | collective-permute-start | bytes 983048 | tf_op jit(solution)/shard_map/ppermute | solution.py:96
  217.1 4.9 %collective-permute-done.21 = bf16[320,512]{1,0:T(8,128)(2,1)S(1)} collective-permute-done((bf16[320,512]{1,0:T(8,128)(2,1)S(1)}, bf16[320,512]{1,0:T(8,128)(2,1)S(1)}, u32[]{:S(2)}, u32[]{:S(2)}) %collective-permute-start.21) | collective-permute-done | bytes 327712 | tf_op jit(solution)/shard_map/ppermute | solution.py:96
  226.1 16.1 %collective-permute-done.23 = bf16[320,512]{1,0:T(8,128)(2,1)S(1)} collective-permute-done((bf16[320,512]{1,0:T(8,128)(2,1)S(1)}, bf16[320,512]{1,0:T(8,128)(2,1)S(1)}, u32[]{:S(2)}, u32[]{:S(2)}) %collective-permute-start.23) | collective-permute-done | bytes 327712 | tf_op jit(solution)/shard_map/ppermute | solution.py:96
  242.3 1.8 collective-permute-start.24
  244.3 8.7 %collective-permute-done.24 = bf16[640,512]{1,0:T(8,128)(2,1)S(1)} collective-permute-done((bf16[640,512]{1,0:T(8,128)(2,1)S(1)}, bf16[640,512]{1,0:T(8,128)(2,1)S(1)}, u32[]{:S(2)}, u32[]{:S(2)}) %collective-permute-start.24) | collective-permute-done | bytes 655392 | tf_op jit(solution)/shard_map/ppermute | solution.py:96
  253.2 1.5 copy-done.2
  255.1 6.4 %collective-permute-done.39.far = bf16[2304,512]{1,0:T(8,128)(2,1)} collective-permute-done((bf16[2304,512]{1,0:T(8,128)(2,1)S(1)}, bf16[2304,512]{1,0:T(8,128)(2,1)}, u32[]{:S(2)}, u32[]{:S(2)}) %collective-permute-start.39) | collective-permute-done | bytes 2359328 | tf_op jit(solution)/shard_map/ppermute | solution.py:96
  261.5 6.6 %ffn_finish.1 = (f32[2048,512]{1,0:T(8,128)}, f32[512,2048]{1,0:T(8,128)}, f32[512,512]{1,0:T(8,128)}) custom-call(s32[2]{0:T(128)} %pad_add_fusion.place, bf16[2304,512]{1,0:T(8,128)(2,1)} %copy-done.2, bf16[2304,512]{1,0:T(8,128)(2,1)} %collective-permute-done.39.far), custom_call_target="tpu_custom_call" | custom-call | bytes 14155776 | tf_op jit(solution)/shard_map/ffn_finish/pallas_call | solution.py:122
  268.1 6.7 %tail_finish.1 = (f32[1536,512]{1,0:T(8,128)}, f32[512,512]{1,0:T(8,128)}, f32[512,512]{1,0:T(8,128)}, f32[1536,512]{1,0:T(8,128)}, f32[512,512]{1,0:T(8,128)}, /*index=5*/f32[16,512]{1,0:T(8,128)}) custom-call(s32[2]{0:T(128)} %pad_add_fusion.place, bf16[2560,512]{1,0:T(8,128)(2,1)} %copy-done, bf16[2560,512]{1,0:T(8,128)(2,1)} %collective-permute-done.25.far), custom_call_target="tpu_custom_call" | custom-call | bytes 14155776 | tf_op jit(solution)/shard_map/tail_finish/pallas_call | solution.py:122
  (154 shorter events, 31.1 us)
Async XLA Ops:
  10.1 26.1 %copy-start.8 = (bf16[512]{0:T(512)(128)(2,1)S(1)}, bf16[512]{0:T(512)(128)(2,1)}, u32[]{:S(2)}) copy-start(bf16[512]{0:T(512)(128)(2,1)} %param.23) | copy-start | bytes 3076
  10.1 9.8 %collective-permute-start = (bf16[1,112,512]{2,1,0:T(8,128)(2,1)}, bf16[1,112,512]{2,1,0:T(8,128)(2,1)S(1)}, u32[]{:S(2)}, u32[]{:S(2)}) collective-permute-start(bf16[1,112,512]{2,1,0:T(8,128)(2,1)} %bitcast.19), channel_id=1, source_target_pairs={{0,4},{1,5},{2,6},{3,7},{4,0},{5,1},{6,2},{7,3},{8,12},{9,13},{10,... | collective-permute-start | bytes 344072 | tf_op jit(solution)/shard_map/ppermute | solution.py:96
  14.1 7.6 %collective-permute-start.3 = (bf16[1,96,512]{2,1,0:T(8,128)(2,1)}, bf16[1,96,512]{2,1,0:T(8,128)(2,1)S(1)}, u32[]{:S(2)}, u32[]{:S(2)}) collective-permute-start(bf16[1,96,512]{2,1,0:T(8,128)(2,1)} %bitcast.22), channel_id=1, source_target_pairs={{0,1},{1,0},{2,3},{3,2},{4,5},{5,4},{6,7},{7,6},{8,9},{9,8},{10,11... | collective-permute-start | bytes 294920 | tf_op jit(solution)/shard_map/ppermute | solution.py:96
  20.8 10.6 %collective-permute-start.1 = (bf16[2,112,512]{2,1,0:T(8,128)(2,1)S(1)}, bf16[2,112,512]{2,1,0:T(8,128)(2,1)S(1)}, u32[]{:S(2)}, u32[]{:S(2)}) collective-permute-start(bf16[2,112,512]{2,1,0:T(8,128)(2,1)S(1)} %pad_maximum_fusion.15), channel_id=1, source_target_pairs={{0,2},{1,3},{2,0},{3,1},{4,6},{5,7},{6,4},{7,5},{8,10},{9,11},{10,... | collective-permute-start | bytes 688136 | tf_op jit(solution)/shard_map/ppermute | solution.py:96
  22.6 12.4 %collective-permute-start.4 = (bf16[2,96,512]{2,1,0:T(8,128)(2,1)S(1)}, bf16[2,96,512]{2,1,0:T(8,128)(2,1)S(1)}, u32[]{:S(2)}, u32[]{:S(2)}) collective-permute-start(bf16[2,96,512]{2,1,0:T(8,128)(2,1)S(1)} %pad_maximum_fusion.16), channel_id=1, source_target_pairs={{0,4},{1,5},{2,6},{3,7},{4,0},{5,1},{6,2},{7,3},{8,12},{9,13},{10,... | collective-permute-start | bytes 589832 | tf_op jit(solution)/shard_map/ppermute | solution.py:96
  32.3 12.5 %copy-start.6 = (bf16[4,112,512]{2,1,0:T(8,128)(2,1)}, bf16[4,112,512]{2,1,0:T(8,128)(2,1)S(1)}, u32[]{:S(2)}) copy-start(bf16[4,112,512]{2,1,0:T(8,128)(2,1)S(1)} %pad_maximum_fusion.4.keys_near) | copy-start | bytes 1376260
  32.3 12.5 %collective-permute-start.2 = (bf16[4,112,512]{2,1,0:T(8,128)(2,1)S(1)}, bf16[4,112,512]{2,1,0:T(8,128)(2,1)S(1)}, u32[]{:S(2)}, u32[]{:S(2)}) collective-permute-start(bf16[4,112,512]{2,1,0:T(8,128)(2,1)S(1)} %pad_maximum_fusion.4.keys_near), channel_id=1, source_target_pairs={{0,1},{1,0},{2,3},{3,2},{4,5},{5,4},{6,7},{7,6},{8,9},{9,8},{10,11... | collective-permute-start | bytes 1376264 | tf_op jit(solution)/shard_map/ppermute | solution.py:96
  36.0 8.9 %copy-start.7 = (bf16[4,96,512]{2,1,0:T(8,128)(2,1)}, bf16[4,96,512]{2,1,0:T(8,128)(2,1)S(1)}, u32[]{:S(2)}) copy-start(bf16[4,96,512]{2,1,0:T(8,128)(2,1)S(1)} %pad_maximum_fusion.5.values_near) | copy-start | bytes 1179652
  36.0 8.8 %collective-permute-start.5 = (bf16[4,96,512]{2,1,0:T(8,128)(2,1)S(1)}, bf16[4,96,512]{2,1,0:T(8,128)(2,1)S(1)}, u32[]{:S(2)}, u32[]{:S(2)}) collective-permute-start(bf16[4,96,512]{2,1,0:T(8,128)(2,1)S(1)} %pad_maximum_fusion.5.values_near), channel_id=1, source_target_pairs={{0,2},{1,3},{2,0},{3,1},{4,6},{5,7},{6,4},{7,5},{8,10},{9,11},{10,... | collective-permute-start | bytes 1179656 | tf_op jit(solution)/shard_map/ppermute | solution.py:96
  69.5 7.0 %copy-start.5 = (bf16[8,96,512]{2,1,0:T(8,128)(2,1)S(1)}, bf16[8,96,512]{2,1,0:T(8,128)(2,1)}, u32[]{:S(2)}) copy-start(bf16[8,96,512]{2,1,0:T(8,128)(2,1)} %get-tuple-element.55) | copy-start | bytes 2359300
  69.5 8.8 %copy-start.4 = (bf16[8,96,512]{2,1,0:T(8,128)(2,1)S(1)}, bf16[8,96,512]{2,1,0:T(8,128)(2,1)}, u32[]{:S(2)}) copy-start(bf16[8,96,512]{2,1,0:T(8,128)(2,1)} %get-tuple-element.54) | copy-start | bytes 2359300
  76.5 42.7 %collective-permute-start.26 = (bf16[2304,512]{1,0:T(8,128)(2,1)}, bf16[2304,512]{1,0:T(8,128)(2,1)}, u32[]{:S(2)}, u32[]{:S(2)}) collective-permute-start(bf16[2304,512]{1,0:T(8,128)(2,1)} %get-tuple-element.78), channel_id=1, source_target_pairs={{0,8},{8,0},{16,24},{24,16},{1,9},{9,1},{17,25},{25,17},{2,10},{10... | collective-permute-start | bytes 7077896 | tf_op jit(solution)/shard_map/ppermute | solution.py:96
  76.6 11.6 %collective-permute-start.9 = (bf16[4,96,512]{2,1,0:T(8,128)(2,1)S(1)}, bf16[4,96,512]{2,1,0:T(8,128)(2,1)S(1)}, u32[]{:S(2)}, u32[]{:S(2)}) collective-permute-start(bf16[4,96,512]{2,1,0:T(8,128)(2,1)S(1)} %slice.210), channel_id=1, source_target_pairs={{0,2},{1,3},{2,0},{3,1},{4,6},{5,7},{6,4},{7,5},{8,10},{9,11},{10,... | collective-permute-start | bytes 1179656 | tf_op jit(solution)/shard_map/ppermute | solution.py:96
  78.4 12.6 %collective-permute-start.6 = (bf16[4,96,512]{2,1,0:T(8,128)(2,1)S(1)}, bf16[4,96,512]{2,1,0:T(8,128)(2,1)S(1)}, u32[]{:S(2)}, u32[]{:S(2)}) collective-permute-start(bf16[4,96,512]{2,1,0:T(8,128)(2,1)S(1)} %slice.204), channel_id=1, source_target_pairs={{0,1},{1,0},{2,3},{3,2},{4,5},{5,4},{6,7},{7,6},{8,9},{9,8},{10,11... | collective-permute-start | bytes 1179656 | tf_op jit(solution)/shard_map/ppermute | solution.py:96
  88.3 11.8 %collective-permute-start.10 = (bf16[2,96,512]{2,1,0:T(8,128)(2,1)S(1)}, bf16[2,96,512]{2,1,0:T(8,128)(2,1)S(1)}, u32[]{:S(2)}, u32[]{:S(2)}) collective-permute-start(bf16[2,96,512]{2,1,0:T(8,128)(2,1)S(1)} %slice.271), channel_id=1, source_target_pairs={{0,4},{1,5},{2,6},{3,7},{4,0},{5,1},{6,2},{7,3},{8,12},{9,13},{10,... | collective-permute-start | bytes 589832 | tf_op jit(solution)/shard_map/ppermute | solution.py:96
  91.1 10.7 %collective-permute-start.7 = (bf16[2,96,512]{2,1,0:T(8,128)(2,1)S(1)}, bf16[2,96,512]{2,1,0:T(8,128)(2,1)S(1)}, u32[]{:S(2)}, u32[]{:S(2)}) collective-permute-start(bf16[2,96,512]{2,1,0:T(8,128)(2,1)S(1)} %slice.267), channel_id=1, source_target_pairs={{0,2},{1,3},{2,0},{3,1},{4,6},{5,7},{6,4},{7,5},{8,10},{9,11},{10,... | collective-permute-start | bytes 589832 | tf_op jit(solution)/shard_map/ppermute | solution.py:96
  100.2 4.7 %collective-permute-start.11 = (bf16[1,96,512]{2,1,0:T(8,128)(2,1)S(1)}, bf16[1,96,512]{2,1,0:T(8,128)(2,1)S(1)}, u32[]{:S(2)}, u32[]{:S(2)}) collective-permute-start(bf16[1,96,512]{2,1,0:T(8,128)(2,1)S(1)} %slice.273), channel_id=1, source_target_pairs={{0,1},{1,0},{2,3},{3,2},{4,5},{5,4},{6,7},{7,6},{8,9},{9,8},{10,11... | collective-permute-start | bytes 294920 | tf_op jit(solution)/shard_map/ppermute | solution.py:96
  101.8 7.2 %collective-permute-start.8 = (bf16[1,96,512]{2,1,0:T(8,128)(2,1)S(1)}, bf16[1,96,512]{2,1,0:T(8,128)(2,1)S(1)}, u32[]{:S(2)}, u32[]{:S(2)}) collective-permute-start(bf16[1,96,512]{2,1,0:T(8,128)(2,1)S(1)} %slice.269), channel_id=1, source_target_pairs={{0,4},{1,5},{2,6},{3,7},{4,0},{5,1},{6,2},{7,3},{8,12},{9,13},{10,... | collective-permute-start | bytes 294920 | tf_op jit(solution)/shard_map/ppermute | solution.py:96
  109.7 9.5 %copy-start.3 = (bf16[2304,512]{1,0:T(8,128)(2,1)S(1)}, bf16[2304,512]{1,0:T(8,128)(2,1)}, u32[]{:S(2)}) copy-start(bf16[2304,512]{1,0:T(8,128)(2,1)} %get-tuple-element.77) | copy-start | bytes 7077892
  119.2 29.4 %collective-permute-start.12 = (bf16[2560,512]{1,0:T(8,128)(2,1)}, bf16[2560,512]{1,0:T(8,128)(2,1)S(1)}, u32[]{:S(2)}, u32[]{:S(2)}) collective-permute-start(bf16[2560,512]{1,0:T(8,128)(2,1)} %get-tuple-element.64), channel_id=1, source_target_pairs={{0,8},{8,0},{16,24},{24,16},{1,9},{9,1},{17,25},{25,17},{2,10},{10... | collective-permute-start | bytes 7864328 | tf_op jit(solution)/shard_map/ppermute | solution.py:96
  121.6 14.4 %collective-permute-start.29 = (bf16[512,512]{1,0:T(8,128)(2,1)S(1)}, bf16[512,512]{1,0:T(8,128)(2,1)S(1)}, u32[]{:S(2)}, u32[]{:S(2)}) collective-permute-start(bf16[512,512]{1,0:T(8,128)(2,1)S(1)} %slice.305), channel_id=1, source_target_pairs={{0,1},{1,0},{2,3},{3,2},{4,5},{5,4},{6,7},{7,6},{8,9},{9,8},{10,11... | collective-permute-start | bytes 1572872 | tf_op jit(solution)/shard_map/ppermute | solution.py:96
  122.2 17.4 %collective-permute-start.27 = (bf16[640,512]{1,0:T(8,128)(2,1)S(1)}, bf16[640,512]{1,0:T(8,128)(2,1)S(1)}, u32[]{:S(2)}, u32[]{:S(2)}) collective-permute-start(bf16[640,512]{1,0:T(8,128)(2,1)S(1)} %slice.299), channel_id=1, source_target_pairs={{0,16},{8,24},{16,0},{24,8},{1,17},{9,25},{17,1},{25,9},{2,18},{10... | collective-permute-start | bytes 1966088 | tf_op jit(solution)/shard_map/ppermute | solution.py:96
  136.1 12.5 %copy-start.1 = (bf16[2560,512]{1,0:T(8,128)(2,1)S(1)}, bf16[2560,512]{1,0:T(8,128)(2,1)}, u32[]{:S(2)}) copy-start(bf16[2560,512]{1,0:T(8,128)(2,1)} %get-tuple-element.63) | copy-start | bytes 7864324
  136.1 8.6 %collective-permute-start.30 = (bf16[256,512]{1,0:T(8,128)(2,1)S(1)}, bf16[256,512]{1,0:T(8,128)(2,1)S(1)}, u32[]{:S(2)}, u32[]{:S(2)}) collective-permute-start(bf16[256,512]{1,0:T(8,128)(2,1)S(1)} %slice.307), channel_id=1, source_target_pairs={{0,16},{8,24},{16,0},{24,8},{1,17},{9,25},{17,1},{25,9},{2,18},{10... | collective-permute-start | bytes 786440 | tf_op jit(solution)/shard_map/ppermute | solution.py:96
  139.9 8.5 %collective-permute-start.28 = (bf16[320,512]{1,0:T(8,128)(2,1)S(1)}, bf16[320,512]{1,0:T(8,128)(2,1)S(1)}, u32[]{:S(2)}, u32[]{:S(2)}) collective-permute-start(bf16[320,512]{1,0:T(8,128)(2,1)S(1)} %slice.301), channel_id=1, source_target_pairs={{0,1},{1,0},{2,3},{3,2},{4,5},{5,4},{6,7},{7,6},{8,9},{9,8},{10,11... | collective-permute-start | bytes 983048 | tf_op jit(solution)/shard_map/ppermute | solution.py:96
  148.5 6.9 %collective-permute-start.31 = (bf16[288,512]{1,0:T(8,128)(2,1)S(1)}, bf16[288,512]{1,0:T(8,128)(2,1)S(1)}, u32[]{:S(2)}, u32[]{:S(2)}) collective-permute-start(bf16[288,512]{1,0:T(8,128)(2,1)S(1)} %pad_maximum_fusion.12), channel_id=1, source_target_pairs={{0,2},{1,3},{2,0},{3,1},{4,6},{5,7},{6,4},{7,5},{8,10},{9,11},{10,... | collective-permute-start | bytes 884744 | tf_op jit(solution)/shard_map/ppermute | solution.py:96
  155.6 10.0 %collective-permute-start.32 = (bf16[144,512]{1,0:T(8,128)(2,1)S(1)}, bf16[144,512]{1,0:T(8,128)(2,1)S(1)}, u32[]{:S(2)}, u32[]{:S(2)}) collective-permute-start(bf16[144,512]{1,0:T(8,128)(2,1)S(1)} %pad_maximum_fusion.19), channel_id=1, source_target_pairs={{0,4},{1,5},{2,6},{3,7},{4,0},{5,1},{6,2},{7,3},{8,12},{9,13},{10,... | collective-permute-start | bytes 442376 | tf_op jit(solution)/shard_map/ppermute | solution.py:96
  156.7 16.1 %collective-permute-start.13 = (bf16[640,512]{1,0:T(8,128)(2,1)S(1)}, bf16[640,512]{1,0:T(8,128)(2,1)S(1)}, u32[]{:S(2)}, u32[]{:S(2)}) collective-permute-start(bf16[640,512]{1,0:T(8,128)(2,1)S(1)} %get-tuple-element.124), channel_id=1, source_target_pairs={{0,1},{1,0},{2,3},{3,2},{4,5},{5,4},{6,7},{7,6},{8,9},{9,8},{10,11... | collective-permute-start | bytes 1966088 | tf_op jit(solution)/shard_map/ppermute | solution.py:96
  157.7 15.2 %collective-permute-start.15 = (bf16[640,512]{1,0:T(8,128)(2,1)S(1)}, bf16[640,512]{1,0:T(8,128)(2,1)S(1)}, u32[]{:S(2)}, u32[]{:S(2)}) collective-permute-start(bf16[640,512]{1,0:T(8,128)(2,1)S(1)} %get-tuple-element.125), channel_id=1, source_target_pairs={{0,16},{8,24},{16,0},{24,8},{1,17},{9,25},{17,1},{25,9},{2,18},{10... | collective-permute-start | bytes 1966088 | tf_op jit(solution)/shard_map/ppermute | solution.py:96
  165.6 7.2 %collective-permute-start.33 = (bf16[144,512]{1,0:T(8,128)(2,1)S(1)}, bf16[144,512]{1,0:T(8,128)(2,1)S(1)}, u32[]{:S(2)}, u32[]{:S(2)}) collective-permute-start(bf16[144,512]{1,0:T(8,128)(2,1)S(1)} %pad_maximum_fusion.20), channel_id=1, source_target_pairs={{0,4},{1,5},{2,6},{3,7},{4,0},{5,1},{6,2},{7,3},{8,12},{9,13},{10,... | collective-permute-start | bytes 442376 | tf_op jit(solution)/shard_map/ppermute | solution.py:96
  173.3 9.1 %collective-permute-start.16 = (bf16[320,512]{1,0:T(8,128)(2,1)S(1)}, bf16[320,512]{1,0:T(8,128)(2,1)S(1)}, u32[]{:S(2)}, u32[]{:S(2)}) collective-permute-start(bf16[320,512]{1,0:T(8,128)(2,1)S(1)} %slice.283), channel_id=1, source_target_pairs={{0,1},{1,0},{2,3},{3,2},{4,5},{5,4},{6,7},{7,6},{8,9},{9,8},{10,11... | collective-permute-start | bytes 983048 | tf_op jit(solution)/shard_map/ppermute | solution.py:96
  174.2 8.2 %collective-permute-start.14 = (bf16[320,512]{1,0:T(8,128)(2,1)S(1)}, bf16[320,512]{1,0:T(8,128)(2,1)S(1)}, u32[]{:S(2)}, u32[]{:S(2)}) collective-permute-start(bf16[320,512]{1,0:T(8,128)(2,1)S(1)} %slice.277), channel_id=1, source_target_pairs={{0,16},{8,24},{16,0},{24,8},{1,17},{9,25},{17,1},{25,9},{2,18},{10... | collective-permute-start | bytes 983048 | tf_op jit(solution)/shard_map/ppermute | solution.py:96
  175.8 7.8 %collective-permute-start.34 = (bf16[288,512]{1,0:T(8,128)(2,1)S(1)}, bf16[288,512]{1,0:T(8,128)(2,1)S(1)}, u32[]{:S(2)}, u32[]{:S(2)}) collective-permute-start(bf16[288,512]{1,0:T(8,128)(2,1)S(1)} %pad_maximum_fusion.13), channel_id=1, source_target_pairs={{0,2},{1,3},{2,0},{3,1},{4,6},{5,7},{6,4},{7,5},{8,10},{9,11},{10,... | collective-permute-start | bytes 884744 | tf_op jit(solution)/shard_map/ppermute | solution.py:96
  182.6 8.1 %collective-permute-start.17 = (bf16[320,512]{1,0:T(8,128)(2,1)S(1)}, bf16[320,512]{1,0:T(8,128)(2,1)S(1)}, u32[]{:S(2)}, u32[]{:S(2)}) collective-permute-start(bf16[320,512]{1,0:T(8,128)(2,1)S(1)} %pad_maximum_fusion.6), channel_id=1, source_target_pairs={{0,2},{1,3},{2,0},{3,1},{4,6},{5,7},{6,4},{7,5},{8,10},{9,11},{10,... | collective-permute-start | bytes 983048 | tf_op jit(solution)/shard_map/ppermute | solution.py:96
  183.7 7.9 %collective-permute-start.35 = (bf16[320,512]{1,0:T(8,128)(2,1)S(1)}, bf16[320,512]{1,0:T(8,128)(2,1)S(1)}, u32[]{:S(2)}, u32[]{:S(2)}) collective-permute-start(bf16[320,512]{1,0:T(8,128)(2,1)S(1)} %pad_maximum_fusion.11), channel_id=1, source_target_pairs={{0,1},{1,0},{2,3},{3,2},{4,5},{5,4},{6,7},{7,6},{8,9},{9,8},{10,11... | collective-permute-start | bytes 983048 | tf_op jit(solution)/shard_map/ppermute | solution.py:96
  190.8 8.6 %collective-permute-start.18 = (bf16[160,512]{1,0:T(8,128)(2,1)S(1)}, bf16[160,512]{1,0:T(8,128)(2,1)S(1)}, u32[]{:S(2)}, u32[]{:S(2)}) collective-permute-start(bf16[160,512]{1,0:T(8,128)(2,1)S(1)} %pad_maximum_fusion.17), channel_id=1, source_target_pairs={{0,4},{1,5},{2,6},{3,7},{4,0},{5,1},{6,2},{7,3},{8,12},{9,13},{10,... | collective-permute-start | bytes 491528 | tf_op jit(solution)/shard_map/ppermute | solution.py:96
  191.7 15.1 %collective-permute-start.36 = (bf16[640,512]{1,0:T(8,128)(2,1)S(1)}, bf16[640,512]{1,0:T(8,128)(2,1)S(1)}, u32[]{:S(2)}, u32[]{:S(2)}) collective-permute-start(bf16[640,512]{1,0:T(8,128)(2,1)S(1)} %pad_maximum_fusion.2), channel_id=1, source_target_pairs={{0,16},{8,24},{16,0},{24,8},{1,17},{9,25},{17,1},{25,9},{2,18},{10... | collective-permute-start | bytes 1966088 | tf_op jit(solution)/shard_map/ppermute | solution.py:96
  199.5 7.2 %collective-permute-start.19 = (bf16[160,512]{1,0:T(8,128)(2,1)S(1)}, bf16[160,512]{1,0:T(8,128)(2,1)S(1)}, u32[]{:S(2)}, u32[]{:S(2)}) collective-permute-start(bf16[160,512]{1,0:T(8,128)(2,1)S(1)} %pad_maximum_fusion.18), channel_id=1, source_target_pairs={{0,4},{1,5},{2,6},{3,7},{4,0},{5,1},{6,2},{7,3},{8,12},{9,13},{10,... | collective-permute-start | bytes 491528 | tf_op jit(solution)/shard_map/ppermute | solution.py:96
  206.8 7.1 %collective-permute-start.20 = (bf16[320,512]{1,0:T(8,128)(2,1)S(1)}, bf16[320,512]{1,0:T(8,128)(2,1)S(1)}, u32[]{:S(2)}, u32[]{:S(2)}) collective-permute-start(bf16[320,512]{1,0:T(8,128)(2,1)S(1)} %pad_maximum_fusion.7), channel_id=1, source_target_pairs={{0,2},{1,3},{2,0},{3,1},{4,6},{5,7},{6,4},{7,5},{8,10},{9,11},{10,... | collective-permute-start | bytes 983048 | tf_op jit(solution)/shard_map/ppermute | solution.py:96
  214.0 8.1 %collective-permute-start.21 = (bf16[320,512]{1,0:T(8,128)(2,1)S(1)}, bf16[320,512]{1,0:T(8,128)(2,1)S(1)}, u32[]{:S(2)}, u32[]{:S(2)}) collective-permute-start(bf16[320,512]{1,0:T(8,128)(2,1)S(1)} %pad_maximum_fusion.9), channel_id=1, source_target_pairs={{0,16},{8,24},{16,0},{24,8},{1,17},{9,25},{17,1},{25,9},{2,18},{10... | collective-permute-start | bytes 983048 | tf_op jit(solution)/shard_map/ppermute | solution.py:96
  217.0 7.8 %collective-permute-start.37 = (bf16[256,512]{1,0:T(8,128)(2,1)S(1)}, bf16[256,512]{1,0:T(8,128)(2,1)S(1)}, u32[]{:S(2)}, u32[]{:S(2)}) collective-permute-start(bf16[256,512]{1,0:T(8,128)(2,1)S(1)} %pad_maximum_fusion.14), channel_id=1, source_target_pairs={{0,16},{8,24},{16,0},{24,8},{1,17},{9,25},{17,1},{25,9},{2,18},{10... | collective-permute-start | bytes 786440 | tf_op jit(solution)/shard_map/ppermute | solution.py:96
  222.1 22.0 %collective-permute-start.22 = (bf16[640,512]{1,0:T(8,128)(2,1)S(1)}, bf16[640,512]{1,0:T(8,128)(2,1)S(1)}, u32[]{:S(2)}, u32[]{:S(2)}) collective-permute-start(bf16[640,512]{1,0:T(8,128)(2,1)S(1)} %pad_maximum_fusion), channel_id=1, source_target_pairs={{0,1},{1,0},{2,3},{3,2},{4,5},{5,4},{6,7},{7,6},{8,9},{9,8},{10,11... | collective-permute-start | bytes 1966088 | tf_op jit(solution)/shard_map/ppermute | solution.py:96
  223.3 18.9 %collective-permute-start.23 = (bf16[320,512]{1,0:T(8,128)(2,1)S(1)}, bf16[320,512]{1,0:T(8,128)(2,1)S(1)}, u32[]{:S(2)}, u32[]{:S(2)}) collective-permute-start(bf16[320,512]{1,0:T(8,128)(2,1)S(1)} %pad_maximum_fusion.10), channel_id=1, source_target_pairs={{0,1},{1,0},{2,3},{3,2},{4,5},{5,4},{6,7},{7,6},{8,9},{9,8},{10,11... | collective-permute-start | bytes 983048 | tf_op jit(solution)/shard_map/ppermute | solution.py:96
  224.9 28.2 %collective-permute-start.38 = (bf16[512,512]{1,0:T(8,128)(2,1)S(1)}, bf16[512,512]{1,0:T(8,128)(2,1)S(1)}, u32[]{:S(2)}, u32[]{:S(2)}) collective-permute-start(bf16[512,512]{1,0:T(8,128)(2,1)S(1)} %pad_maximum_fusion.3), channel_id=1, source_target_pairs={{0,1},{1,0},{2,3},{3,2},{4,5},{5,4},{6,7},{7,6},{8,9},{9,8},{10,11... | collective-permute-start | bytes 1572872 | tf_op jit(solution)/shard_map/ppermute | solution.py:96
  242.3 10.7 %collective-permute-start.24 = (bf16[640,512]{1,0:T(8,128)(2,1)S(1)}, bf16[640,512]{1,0:T(8,128)(2,1)S(1)}, u32[]{:S(2)}, u32[]{:S(2)}) collective-permute-start(bf16[640,512]{1,0:T(8,128)(2,1)S(1)} %pad_maximum_fusion.1), channel_id=1, source_target_pairs={{0,16},{8,24},{16,0},{24,8},{1,17},{9,25},{17,1},{25,9},{2,18},{10... | collective-permute-start | bytes 1966088 | tf_op jit(solution)/shard_map/ppermute | solution.py:96
  253.0 15.1 %copy-start = (bf16[2560,512]{1,0:T(8,128)(2,1)}, bf16[2560,512]{1,0:T(8,128)(2,1)S(1)}, u32[]{:S(2)}) copy-start(bf16[2560,512]{1,0:T(8,128)(2,1)S(1)} %constant_dynamic-update-slice_fusion.near) | copy-start | bytes 7864324
  253.0 15.1 %collective-permute-start.25 = (bf16[2560,512]{1,0:T(8,128)(2,1)S(1)}, bf16[2560,512]{1,0:T(8,128)(2,1)}, u32[]{:S(2)}, u32[]{:S(2)}) collective-permute-start(bf16[2560,512]{1,0:T(8,128)(2,1)S(1)} %constant_dynamic-update-slice_fusion.near), channel_id=1, source_target_pairs={{0,8},{8,0},{16,24},{24,16},{1,9},{9,1},{17,25},{25,17},{2,10},{10... | collective-permute-start | bytes 7864328 | tf_op jit(solution)/shard_map/ppermute | solution.py:96
  254.7 6.8 %collective-permute-start.39 = (bf16[2304,512]{1,0:T(8,128)(2,1)S(1)}, bf16[2304,512]{1,0:T(8,128)(2,1)}, u32[]{:S(2)}, u32[]{:S(2)}) collective-permute-start(bf16[2304,512]{1,0:T(8,128)(2,1)S(1)} %constant_dynamic-update-slice_fusion.10.near), channel_id=1, source_target_pairs={{0,8},{8,0},{16,24},{24,16},{1,9},{9,1},{17,25},{25,17},{2,10},{10... | collective-permute-start | bytes 7077896 | tf_op jit(solution)/shard_map/ppermute | solution.py:96
  (3 other events, 3.2 us)

commit v2 on v1

v2 whole, which is shorter than its diff:
```python
import functools

import jax
import jax.numpy as jnp
from jax import lax
from jax.experimental import pallas as pl
from jax.experimental.pallas import tpu as pltpu
from jax.sharding import PartitionSpec as P

HEADS = 8
HEAD_DIM = 64
LANES = 128
GROUPS = HEADS * HEAD_DIM // LANES
EPSILON = 1e-05
MASKED_OUT = -1e30
SCALE = HEAD_DIM ** (-0.5)
GELU_SCALE = 0.7978845608028654
GELU_CUBIC = 0.044715
SCATTER_BITS = 5
EXTRA_ROWS = 16
VMEM_SMALL = 28 * 1024 * 1024
VMEM_LARGE = 60 * 1024 * 1024
SHORT_ROW = 768

BF16 = jnp.bfloat16
F32 = jnp.float32


def dot(left, right):
    return jnp.dot(left, right, preferred_element_type=F32)


def dot_nt(left, right):
    return lax.dot_general(left, right, (((1,), (1,)), ((), ())), preferred_element_type=F32)


def dot_tn(left, right):
    return lax.dot_general(left, right, (((0,), (0,)), ((), ())), preferred_element_type=F32)


def normalize(values):
    average = jnp.mean(values, axis=-1, keepdims=True)
    centred = values - average
    variance = jnp.mean(centred * centred, axis=-1, keepdims=True)
    inverse_dev = lax.rsqrt(variance + EPSILON)
    return centred * inverse_dev, inverse_dev


def normalize_back(grad_normed, unit, inverse_dev, gain):
    grad_unit = grad_normed * gain
    first_mean = jnp.mean(grad_unit, axis=-1, keepdims=True)
    second_mean = jnp.mean(grad_unit * unit, axis=-1, keepdims=True)
    return inverse_dev * (grad_unit - first_mean - unit * second_mean)


class Plan:
    def __init__(self, mesh):
        self.n_rows = mesh.shape["rows"]
        self.n_seq = mesh.shape["seq"]
        rows = [("rows", 1 << i) for i in range(self.n_rows.bit_length() - 1)]
        seq = [("seq", 1 << i) for i in range(self.n_seq.bit_length() - 1)]
        kept = max(0, min(len(seq), SCATTER_BITS - len(rows)))
        self.seq_block = 1 << kept
        self.blocks = self.n_rows * self.seq_block
        core, others = rows[:1], rows[1:]
        low, high = seq[:1], seq[1:kept] if kept else []
        low = low[:kept]
        self.core = core[0]
        self.first = others + low
        self.second = low + others
        self.tail = high
        self.rest = seq[kept:]
        bits = [1 << i for i in range(len(seq))]
        self.key_order = bits[::-1]
        self.value_order = bits[:1] + bits[:0:-1]

    def mask(self, bit):
        axis, value = bit
        return value * self.seq_block if axis == "rows" else value

    def relative(self, order, position):
        result = 0
        for number, bit in enumerate(order):
            if position >> (len(order) - 1 - number) & 1:
                result |= self.mask(bit)
        return result

    def seq_relative(self, order, position):
        result = 0
        for number, bit in enumerate(order):
            if position >> number & 1:
                result |= bit
        return result

    def swap(self, array, bit):
        axis, value = bit
        size = self.n_rows if axis == "rows" else self.n_seq
        return lax.ppermute(array, axis, [(i, i ^ value) for i in range(size)])


def order_matrix(length, transposed):
    slots = length // 3
    rows = lax.broadcasted_iota(jnp.int32, (length, length), 1 if transposed else 0)
    columns = lax.broadcasted_iota(jnp.int32, (length, length), 0 if transposed else 1)
    tap = (rows >= slots).astype(jnp.int32) + (rows >= 2 * slots).astype(jnp.int32)
    return (columns == 3 * (rows - tap * slots) + tap).astype(BF16)


def window_masks(segment_column, slots):
    last = segment_column[2 * slots :]
    return [(segment_column[i * slots : (i + 1) * slots] == last).astype(F32) for i in range(3)]


def fetch_all(pairs, arrived):
    copies = [
        pltpu.make_async_copy(source, target, arrived.at[number])
        for number, (source, target) in enumerate(pairs)
    ]
    for copy in copies:
        copy.start()

    def ready(number):
        copies[number].wait()
        return pairs[number][1]

    return ready


def call(
    kernel, name, outs, scratch=(), flops=0, bytes_accessed=0, anywhere=(), out_anywhere=(), aliases=None,
    vmem=VMEM_SMALL,
):
    def spec(number, places):
        return pl.BlockSpec(memory_space=pltpu.HBM if number in places else pltpu.VMEM)

    def run(*operands):
        operands = [
            pltpu.with_memory_space_constraint(operand, pltpu.HBM) if number in anywhere else operand
            for number, operand in enumerate(operands)
        ]
        return pl.pallas_call(
            kernel,
            name=name,
            out_shape=[jax.ShapeDtypeStruct(shape, dtype) for shape, dtype in outs],
            in_specs=[spec(number, anywhere) for number in range(len(operands))],
            out_specs=[spec(number, out_anywhere) for number in range(len(outs))],
            scratch_shapes=list(scratch),
            input_output_aliases=aliases or {},
            compiler_params=pltpu.CompilerParams(vmem_limit_bytes=vmem),
            cost_estimate=pl.CostEstimate(
                flops=flops, bytes_accessed=bytes_accessed, transcendentals=0
            ),
        )(*operands)

    return run


def own_places(plan):
    seq = lax.axis_index("seq")
    return seq, lax.axis_index("rows") * plan.seq_block + lax.rem(seq, plan.seq_block)


def read_segments(order, segments, batch):
    length = order.shape[0]
    rows = [segments[b].astype(F32) for b in range(batch)]
    rows = jnp.concatenate(rows + [jnp.zeros((EXTRA_ROWS - batch, length), F32)], axis=0)
    columns = dot_nt(order, rows.astype(BF16))
    return rows, [columns[:, b : b + 1] for b in range(batch)]


def project_kernel(
    tokens_far, gain_far, segments_far, w_query, w_key, w_value, conv_key, conv_value,
    x_out, normed_out, query_out, key_out, value_out, packed_key, packed_value, segment_out,
    query_here, key_here, value_here, conv_key_here, conv_value_here, tokens, gain, segments,
    arrived,
):
    ready = fetch_all(
        [
            (tokens_far, tokens), (segments_far, segments), (gain_far, gain), (w_key, key_here), (conv_key, conv_key_here), (w_value, value_here),
            (conv_value, conv_value_here), (w_query, query_here),
        ],
        arrived,
    )
    batch, _, length, width = tokens.shape
    slots = length // 3
    order = order_matrix(length, False)
    for number in range(3):
        ready(number)
    rows = [dot(order, tokens[b, 0]) for b in range(batch)]
    segment_rows, segment_columns = read_segments(order, segments, batch)
    for b in range(batch):
        x_out[b] = rows[b]
        segment_out[b] = segment_columns[b]
    last = lax.broadcasted_iota(jnp.int32, (length, width), 0)
    slot = lax.broadcasted_iota(jnp.int32, (length, width), 1)
    extra = dot(segment_rows.astype(BF16), (last == 3 * slot + 2).astype(BF16)).astype(BF16)
    unit, _ = normalize(jnp.concatenate(rows, axis=0))
    normed = (unit * gain[...].astype(F32).reshape(1, width)).astype(BF16)

    def put(target, values):
        for b in range(batch):
            target[b] = values[b * length : (b + 1) * length]

    put(normed_out, normed)
    for number, flat_out, packed_out in ((3, key_out, packed_key), (5, value_out, packed_value)):
        flat = dot(normed, ready(number)[...]).astype(BF16)
        put(flat_out, flat)
        taps = [[], [], []]
        for b in range(batch):
            masks = window_masks(segment_columns[b], slots)
            for i in range(3):
                start = b * length + i * slots
                part = flat[start : start + slots].astype(F32) * masks[i]
                taps[i].append(part.astype(BF16))
        conv = ready(number + 1)
        total = None
        for i in range(3):
            term = dot(jnp.concatenate(taps[i], axis=0), conv[i * width : (i + 1) * width, :])
            total = term if total is None else total + term
        for b in range(batch):
            packed_out[b, 0:slots, :] = total[b * slots : (b + 1) * slots].astype(BF16)
            if number == 3:
                packed_out[b, slots:, :] = extra
    put(query_out, dot(normed, ready(7)[...]).astype(BF16))


def layer_kernel(
    plan, short, number_mb,
    x_in, cotangent, query_in, key_in, value_in, segment_column, gain_ffn,
    keys_near, keys_far, values_near, values_far, w_out, w_up, w_down,
    layer_out, d_hidden_out, normed_ffn_out, activated_out, d_expanded_out, cotangent_out,
    attended_out, d_branch_out, d_query_out, d_key_own, d_value_own, d_packed_key, d_packed_value,
    gain_grad,
    all_keys, all_values, all_extra, bias, statistics, prob_keep, expanded_sum, d_normed_sum,
    d_attended,
):
    _, _, length, width = cotangent.shape
    x_in, query_in, key_in, value_in = (
        ref.at[number_mb] for ref in (x_in, query_in, key_in, value_in)
    )
    slots = length // 3
    n_seq = plan.n_seq
    half = n_seq // 2
    total_slots = slots * n_seq
    own_place = lax.axis_index("seq")
    key_position = {plan.seq_relative(plan.key_order, p): p for p in range(n_seq)}
    for p in range(n_seq):
        keys = keys_near.at[p] if p < half else keys_far.at[p - half]
        values = values_near.at[p] if p < half else values_far.at[p - half]
        q = key_position[plan.seq_relative(plan.value_order, p)]
        all_keys[p * slots : (p + 1) * slots, :] = keys[0:slots, :]
        all_extra[p] = keys[slots:, 0:LANES]
        all_values[q * slots : (q + 1) * slots, :] = values[...]

    segment_rows = jnp.zeros((EXTRA_ROWS, total_slots), F32)
    slot_lane = lax.broadcasted_iota(jnp.int32, (1, total_slots), 1)
    slot_end = jnp.zeros((1, total_slots), jnp.int32)
    select_row = lax.broadcasted_iota(jnp.int32, (LANES, total_slots), 0)
    select_lane = lax.broadcasted_iota(jnp.int32, (LANES, total_slots), 1)
    for p in range(n_seq):
        selected = (select_lane == select_row + p * slots) & (select_row < slots)
        segment_rows += dot(all_extra[p], selected.astype(BF16))
        owner = plan.seq_relative(plan.key_order, p) ^ own_place
        here = (slot_lane >= p * slots) & (slot_lane < (p + 1) * slots)
        slot_end = jnp.where(here, length * owner - length * p + 3 * slot_lane + 2, slot_end)
    row = lax.broadcasted_iota(jnp.int32, (length, 1), 0)
    tap = (row >= slots).astype(jnp.int32) + (row >= 2 * slots).astype(jnp.int32)
    query_place = length * own_place + 3 * (row - tap * slots) + tap
    matching = segment_rows[number_mb : number_mb + 1, :] == segment_column[number_mb]
    bias[...] = jnp.where((slot_end <= query_place) & matching, 0.0, MASKED_OUT)

    low_lane = lax.broadcasted_iota(jnp.int32, (length, LANES), 1) < HEAD_DIM

    def stacked(part):
        zero = jnp.zeros_like(part)
        return jnp.concatenate(
            [jnp.where(low_lane, part, zero), jnp.where(low_lane, zero, part)], axis=0
        )

    def twice(part):
        return jnp.concatenate([part, part], axis=0)

    def merged(part):
        return jnp.where(low_lane, part[:length], part[length:])

    def lanes_of(g):
        return pl.ds(pl.multiple_of(g * LANES, LANES), LANES)

    def scaled_queries(g):
        part = query_in[:, lanes_of(g)].astype(F32) * SCALE
        return stacked(part).astype(BF16)

    def attend(number, carry):
        lanes = lanes_of(number)
        queries = scaled_queries(number)
        own_key = twice(key_in[:, lanes].astype(F32))
        scores = dot_nt(queries, all_keys[:, lanes]) + twice(bias[...])
        own_score = jnp.sum(queries.astype(F32) * own_key, axis=-1, keepdims=True)
        top = jnp.maximum(own_score, jnp.max(scores, axis=-1, keepdims=True))
        raised = jnp.exp(scores - top)
        own_raised = jnp.exp(own_score - top)
        inverse = 1.0 / (own_raised + jnp.sum(raised, axis=-1, keepdims=True))
        prob = raised * inverse
        own_prob = own_raised * inverse
        if short:
            prob_keep[number] = prob
        statistics[number, :, 0:1] = own_prob
        statistics[number, :, 1:2] = top - jnp.log(inverse)
        result = dot(prob.astype(BF16), all_values[:, lanes])
        own_value = twice(value_in[:, lanes].astype(F32))
        result += own_prob.astype(BF16).astype(F32) * own_value
        attended_out[:, lanes] = merged(result).astype(BF16)
        return carry

    lax.fori_loop(0, GROUPS, attend, 0, unroll=short)

    x = x_in[...]
    hidden = x + dot(attended_out[...], w_out[...])
    unit, inverse_dev = normalize(hidden)
    gain = gain_ffn[...].astype(F32).reshape(1, width)
    normed_ffn_out[...] = (unit * gain).astype(BF16)
    order = order_matrix(length, False)
    cotangent_out[...] = dot(order, cotangent[number_mb, 0]).astype(BF16)
    expanded_sum[...] = hidden
    d_normed_sum[...] = jnp.zeros_like(d_normed_sum)
    chunk = width
    total_width = w_up.shape[1]

    def feed(number, carry):
        columns = pl.ds(pl.multiple_of(number * chunk, chunk), chunk)
        expanded = dot(normed_ffn_out[...], w_up[:, columns])
        square = expanded * expanded
        curve = jnp.tanh(GELU_SCALE * expanded * (1.0 + GELU_CUBIC * square))
        activated = (0.5 * expanded * (1.0 + curve)).astype(BF16)
        activated_out[:, columns] = activated
        slope = 0.5 * (1.0 + curve) + 0.5 * expanded * (1.0 - curve * curve) * (
            GELU_SCALE * (1.0 + 3.0 * GELU_CUBIC * square)
        )
        expanded_sum[...] += dot(activated, w_down[columns, :])
        d_activated = dot_nt(cotangent_out[...], w_down[columns, :])
        d_expanded = (d_activated * slope).astype(BF16)
        d_expanded_out[:, columns] = d_expanded
        d_normed_sum[...] += dot_nt(d_expanded, w_up[:, columns])
        return carry

    lax.fori_loop(0, total_width // chunk, feed, 0, unroll=True)

    unorder = order_matrix(length, True)
    layer_out[...] = dot(unorder, expanded_sum[...].astype(BF16)).astype(BF16)
    d_normed = d_normed_sum[...]
    gain_grad[...] = jnp.sum(d_normed * unit, axis=0, keepdims=True)
    d_hidden = cotangent_out[...].astype(F32) + normalize_back(d_normed, unit, inverse_dev, gain)
    d_hidden_out[...] = d_hidden
    d_branch = d_hidden.astype(BF16)
    d_branch_out[...] = d_branch
    d_attended[...] = dot_nt(d_branch, w_out[...]).astype(BF16)

    value_spot = [key_position[plan.seq_relative(plan.value_order, p)] for p in range(n_seq)]

    def attend_back(number, carry):
        lanes = lanes_of(number)
        queries = scaled_queries(number)
        own_prob = statistics[number, :, 0:1]
        if short:
            prob = prob_keep[number]
        else:
            scores = dot_nt(queries, all_keys[:, lanes]) + twice(bias[...])
            prob = jnp.exp(scores - statistics[number, :, 1:2])
        grads = stacked(d_attended[:, lanes])
        own_value = twice(value_in[:, lanes].astype(F32))
        own_key = twice(key_in[:, lanes].astype(F32))
        prob_grad = dot_nt(grads, all_values[:, lanes])
        own_prob_grad = jnp.sum(grads.astype(F32) * own_value, axis=-1, keepdims=True)
        delta = own_prob * own_prob_grad + jnp.sum(prob * prob_grad, axis=-1, keepdims=True)
        d_score = (prob * (prob_grad - delta)).astype(BF16)
        d_own = (own_prob * (own_prob_grad - delta)).astype(BF16).astype(F32)
        own_low = own_prob.astype(BF16).astype(F32)
        d_query = merged(dot(d_score, all_keys[:, lanes]) + d_own * own_key) * SCALE
        d_query_out[:, lanes] = d_query.astype(BF16)
        d_key_own[:, lanes] = merged(d_own * queries.astype(F32))
        d_value_own[:, lanes] = merged(own_low * grads.astype(F32))
        key_sums = dot_tn(d_score, queries).astype(BF16)
        value_sums = dot_tn(prob.astype(BF16), grads).astype(BF16)
        for p in range(n_seq):
            d_packed_key[p, :, lanes] = key_sums[p * slots : (p + 1) * slots]
            q = value_spot[p]
            d_packed_value[p, :, lanes] = value_sums[q * slots : (q + 1) * slots]
        return carry

    lax.fori_loop(0, GROUPS, attend_back, 0, unroll=short)


def spread(plan, place, order, parts, send, keep, offset):
    rows_block = sum(rows for _, rows in parts)
    half = plan.blocks // 2
    for target, core in ((send, 1), (keep, 0)):
        for p in range(half):
            block = plan.relative(order, core * half + p) ^ place
            start = offset + p * rows_block
            for source, rows in parts:
                target[start : start + rows, :] = source[
                    pl.ds(pl.multiple_of(block * rows, 16), rows), :
                ]
                start += rows


def ffn_grad_kernel(
    plan, order_a, order_b, batch, *refs,
):
    operands, refs = refs[: 7 * batch], refs[7 * batch :]
    activated, cotangent, normed_ffn, d_expanded, attended, d_branch, d_query = (
        operands[i * batch : (i + 1) * batch] for i in range(7)
    )
    normed_in, send, keep, down_rows, up_rows, out_rows, query_rows = refs
    width = cotangent[0].shape[1]
    wide = activated[0].shape[1]
    chunk = 512

    def joined(parts, columns=slice(None)):
        return jnp.concatenate([part[:, columns] for part in parts], axis=0)

    for c in range(wide // chunk):
        columns = slice(c * chunk, (c + 1) * chunk)
        down_rows[columns, :] = dot_tn(joined(activated, columns), joined(cotangent)).astype(BF16)
        up_rows[c] = dot_tn(joined(normed_ffn), joined(d_expanded, columns)).astype(BF16)
    out_rows[...] = dot_tn(joined(attended), joined(d_branch)).astype(BF16)
    normed = [normed_in.at[b] for b in range(batch)]
    query_rows[...] = dot_tn(joined(normed), joined(d_query)).astype(BF16)
    _, mine = own_places(plan)
    down_block = wide // plan.blocks
    thin = width // plan.blocks
    rows_a = down_block + thin
    spread(plan, mine, order_a, ((down_rows, down_block), (out_rows, thin)), send, keep, 0)
    ups = tuple((up_rows.at[c], thin) for c in range(wide // chunk)) + ((query_rows, thin),)
    spread(plan, mine, order_b, ups, send, keep, rows_a * plan.blocks // 2)


def tail_kernel(
    plan, order_a, order_b, batch,
    x_in, normed_in, key_in, value_in, segment_column, gain, *refs,
):
    per_batch, refs = refs[: 7 * batch], refs[7 * batch :]
    d_packed_key, d_packed_value, d_query, d_key_own, d_value_own, d_hidden, gain_ffn_grad = (
        per_batch[i * batch : (i + 1) * batch] for i in range(7)
    )
    (
        w_query, w_key, w_value, conv_key, conv_value,
        send, keep, grad_tokens,
        key_conv_rows, value_conv_rows, key_rows, value_rows,
    ) = refs
    _, length, width = x_in.shape
    slots = length // 3

    def joined(parts):
        return jnp.concatenate([parts[b][...] for b in range(batch)], axis=0)

    masks = [window_masks(segment_column[b], slots) for b in range(batch)]
    normed = joined(normed_in)
    d_queries = joined(d_query)
    grads = []
    for conv, d_packed, flat, own, conv_rows, rows_out in (
        (conv_key, d_packed_key, key_in, d_key_own, key_conv_rows, key_rows),
        (conv_value, d_packed_value, value_in, d_value_own, value_conv_rows, value_rows),
    ):
        back = joined(d_packed)
        pieces = [[None] * 3 for _ in range(batch)]
        for i in range(3):
            taps = []
            from_tap = dot_nt(back, conv[i * width : (i + 1) * width, :])
            for b in range(batch):
                part = flat[b, i * slots : (i + 1) * slots, :].astype(F32) * masks[b][i]
                taps.append(part.astype(BF16))
                pieces[b][i] = from_tap[b * slots : (b + 1) * slots] * masks[b][i]
            window = jnp.concatenate(taps, axis=0)
            conv_rows[i * width : (i + 1) * width, :] = dot_tn(window, back).astype(BF16)
        whole = jnp.concatenate([piece for row in pieces for piece in row], axis=0)
        d_flat = (whole + joined(own)).astype(BF16)
        grads.append(d_flat)
        rows_out[...] = dot_tn(normed, d_flat).astype(BF16)
    d_normed = (
        dot_nt(d_queries, w_query[...])
        + dot_nt(grads[0], w_key[...])
        + dot_nt(grads[1], w_value[...])
    )
    unit, inverse_dev = normalize(joined(x_in))
    gain_grad = jnp.sum(d_normed * unit, axis=0, keepdims=True)
    d_input = normalize_back(d_normed, unit, inverse_dev, gain[...].astype(F32).reshape(1, width))
    result = (joined(d_hidden) + d_input).astype(BF16)
    unorder = order_matrix(length, True)
    for b in range(batch):
        part = result[b * length : (b + 1) * length, :]
        grad_tokens[b, 0] = dot(unorder, part).astype(BF16)
    ffn_grad = sum(part[...] for part in gain_ffn_grad)
    row = lax.broadcasted_iota(jnp.int32, (EXTRA_ROWS, width), 0)
    gains = jnp.where(row == 0, gain_grad, jnp.where(row == 1, ffn_grad, 0.0))
    _, mine = own_places(plan)
    conv_block = 3 * width // plan.blocks
    thin = width // plan.blocks
    rows_a = conv_block + thin
    spread(
        plan, mine, order_a, ((key_conv_rows, conv_block), (key_rows, thin)), send, keep, 0
    )
    spread(
        plan, mine, order_b, ((value_conv_rows, conv_block), (value_rows, thin)), send, keep,
        rows_a * plan.blocks // 2,
    )
    keep[rows_a * plan.blocks :, :] = gains.astype(BF16)
    send[rows_a * plan.blocks :, :] = gains.astype(BF16)


def finish_kernel(plan, layouts, core, count, *refs):
    blocks, refs = refs[0], refs[1 + core * count :]
    targets, (stage, sent) = refs[:count], refs[count:]
    _, mine = own_places(plan)
    half = plan.blocks // 2
    copies = []
    start = 0
    for order, parts in layouts:
        for p in range(half):
            block = plan.relative(order, core * half + p) ^ mine
            for rows, target, columns in parts:
                stage[start : start + rows, :] = blocks[start : start + rows, :].astype(F32)
                spot = pl.ds(pl.multiple_of(block * rows, 16), rows)
                copy = pltpu.make_async_copy(
                    stage.at[pl.ds(start, rows), :],
                    targets[target].at[spot, columns],
                    sent.at[len(copies)],
                )
                copy.start()
                copies.append(copy)
                start += rows
    for copy in copies:
        copy.wait()


def finish(plan, name, layouts, near, far, shapes):
    count = len(shapes)
    copies = plan.blocks // 2 * sum(len(parts) for _, parts in layouts)
    outs = [(shape, F32) for shape in shapes]
    scratch = [pltpu.VMEM(near.shape, F32), pltpu.SemaphoreType.DMA((copies,))]
    everywhere = tuple(range(count))
    targets = call(
        functools.partial(finish_kernel, plan, layouts, 0, count),
        name + "_near", outs, scratch, bytes_accessed=6 * near.size, out_anywhere=everywhere,
    )(near)
    return call(
        functools.partial(finish_kernel, plan, layouts, 1, count),
        name + "_far", outs, scratch, bytes_accessed=6 * near.size,
        anywhere=tuple(range(1, count + 1)), out_anywhere=everywhere,
        aliases={1 + number: number for number in everywhere},
    )(far, *targets)


def add(left, right):
    return (left.astype(F32) + right.astype(F32)).astype(BF16)


def gather_row(plan, array, order):
    held = array[None]
    for number, bit in enumerate(order):
        arrived = plan.swap(held, ("seq", bit))
        if number == len(order) - 1:
            return held, arrived
        held = jnp.concatenate([held, arrived], axis=0)


class Order:
    def __init__(self):
        self.last = ()

    def turn(self, array):
        return after(array, *self.last) if self.last else array

    def done(self, *arrays):
        self.last = arrays


class RowScatter:
    def __init__(self, plan, order, array, bits):
        self.plan, self.order, self.held, self.bits = plan, order, array, list(bits)

    def step(self):
        half = self.held.shape[0] // 2
        arrived = self.plan.swap(self.held[half:], ("seq", self.bits.pop()))
        self.held = add(self.held[:half], self.order.turn(arrived))
        self.order.done(self.held)


def after(value, *earlier):
    return lax.optimization_barrier((value, *earlier))[0]


class Reduction:
    def __init__(self, plan, order, send, keep, split, first_a, first_b, extra=0):
        self.plan, self.order, self.split, self.extra = plan, order, split, extra
        self.send, self.keep = send, keep
        self.bits = list(zip(first_a, first_b))

    def swap(self, array, bit):
        return self.order.turn(self.plan.swap(array, bit))

    def halve(self, array, bit, extra):
        half = (array.shape[0] - extra) // 2
        arrived = self.swap(array[half:], bit)
        total = add(array[:half], arrived[:half])
        if extra:
            total = jnp.concatenate([total, add(array[2 * half :], arrived[half:])], axis=0)
        self.order.done(total)
        return total

    def core(self):
        total = add(self.keep, self.swap(self.send, self.plan.core))
        self.part_a, self.part_b = total[: self.split], total[self.split :]
        self.order.done(self.part_a, self.part_b)

    def scatter_a(self, number):
        self.part_a = self.halve(self.part_a, self.bits[number][0], 0)

    def scatter_b(self, number):
        self.part_b = self.halve(self.part_b, self.bits[number][1], self.extra)

    def scatter_tail(self, number):
        part_a, part_b = self.part_a, self.part_b
        half_a, half_b = part_a.shape[0] // 2, (part_b.shape[0] - self.extra) // 2
        sent = jnp.concatenate([part_a[half_a:], part_b[half_b:]], axis=0)
        arrived = self.swap(sent, self.plan.tail[number])
        self.part_a = add(part_a[:half_a], arrived[:half_a])
        kept = jnp.concatenate([part_b[:half_b], part_b[2 * half_b :]], axis=0)
        self.part_b = add(kept, arrived[half_a:])
        self.order.done(self.part_a, self.part_b)

    def rest(self):
        rows = self.part_a.shape[0]
        for bit in self.plan.rest:
            arrived = self.plan.swap(jnp.concatenate([self.part_a, self.part_b], axis=0), bit)
            self.part_a = add(self.part_a, arrived[:rows])
            self.part_b = add(self.part_b, arrived[rows:])
        kept = self.part_b.shape[0] - self.extra
        self.part_b, extra = self.part_b[:kept], self.part_b[kept:]
        return extra

    def gather_tail(self, number):
        rows = self.part_a.shape[0]
        sent = jnp.concatenate([self.part_a, self.part_b], axis=0)
        arrived = self.swap(sent, self.plan.tail[number])
        self.part_a = jnp.concatenate([self.part_a, arrived[:rows]], axis=0)
        self.part_b = jnp.concatenate([self.part_b, arrived[rows:]], axis=0)
        self.order.done(self.part_a, self.part_b)

    def gather_a(self, number):
        far = self.swap(self.part_a, self.bits[number][0])
        self.part_a = jnp.concatenate([self.part_a, far], axis=0)
        self.order.done(self.part_a)

    def gather_b(self, number):
        far = self.swap(self.part_b, self.bits[number][1])
        self.part_b = jnp.concatenate([self.part_b, far], axis=0)
        self.order.done(self.part_b)

    def last(self):
        near = jnp.concatenate([self.part_a, self.part_b], axis=0)
        return near, self.plan.swap(near, self.plan.core)


def body(
    plan, tokens, segments, cotangent, gain_attn, w_query, w_key, w_value, conv_key, conv_value,
    w_out, gain_ffn, w_up, w_down,
):
    batch, _, length, width = tokens.shape
    slots = length // 3
    square = (width, width)
    flat = ((batch, length, width), BF16)
    flat32 = ((batch, length, width), F32)
    square_here = pltpu.VMEM(square, BF16)
    conv_here = pltpu.VMEM(conv_key.shape, BF16)
    x, normed, queries, key_rows, value_rows, packed_key, packed_value, segment_column = call(
        project_kernel,
        "project",
        [flat32] + [flat] * 4
        + [
            ((batch, slots + EXTRA_ROWS, width), BF16), ((batch, slots, width), BF16),
            ((batch, length, 1), F32),
        ],
        scratch=[square_here] * 3 + [conv_here] * 2
        + [
            pltpu.VMEM(tokens.shape, BF16), pltpu.VMEM(gain_attn.shape, BF16),
            pltpu.VMEM(segments.shape, jnp.int32), pltpu.SemaphoreType.DMA((8,)),
        ],
        flops=2 * batch * length * width * width * 5,
        bytes_accessed=2 * width * width * 9,
        anywhere=tuple(range(8)),
    )(tokens, gain_attn, segments, w_query, w_key, w_value, conv_key, conv_value)

    total_slots = slots * plan.n_seq
    short = total_slots <= SHORT_ROW
    one, one32 = ((length, width), BF16), ((length, width), F32)
    wide = ((length, w_up.shape[1]), BF16)
    packed_shape = ((plan.n_seq, slots, width), BF16)
    layers = []
    for b in range(batch):
        keys = gather_row(plan, packed_key[b], plan.key_order)
        values = gather_row(plan, packed_value[b], plan.value_order)
        layers.append(
            call(
                functools.partial(layer_kernel, plan, short, b),
                "layer",
                [one, one32, one, wide, wide, one, one, one]
                + [one, one32, one32, packed_shape, packed_shape, ((1, width), F32)],
                scratch=[
                    pltpu.VMEM((total_slots, width), BF16),
                    pltpu.VMEM((total_slots, width), BF16),
                    pltpu.VMEM((plan.n_seq, EXTRA_ROWS, LANES), BF16),
                    pltpu.VMEM((length, total_slots), F32),
                    pltpu.VMEM((GROUPS, 2 * length, LANES), F32),
                    pltpu.VMEM((GROUPS if short else 1, 2 * length, total_slots), F32),
                    pltpu.VMEM((length, width), F32),
                    pltpu.VMEM((length, width), F32),
                    pltpu.VMEM((length, width), BF16),
                ],
                flops=2 * length * width * width * 24,
                bytes_accessed=2 * width * width * 20,
                vmem=VMEM_SMALL if short else VMEM_LARGE,
            )(
                x, cotangent, queries, key_rows, value_rows, segment_column, gain_ffn,
                *keys, *values, w_out, w_up, w_down,
            )
        )
    (
        layer_out, d_hidden, normed_ffn, activated, d_expanded, cotangent_rows, attended, d_branch,
        d_query, d_key_own, d_value_own, d_packed_key, d_packed_value, gain_ffn_grad,
    ) = zip(*layers)
    order = Order()
    rows = [
        RowScatter(plan, order, part, bits)
        for b in range(batch)
        for part, bits in ((d_packed_key[b], plan.key_order), (d_packed_value[b], plan.value_order))
    ]
    steps = len(plan.key_order)
    for row in rows[:2]:
        row.step()

    core = [plan.core]
    order_a, order_b = core + plan.first + plan.tail, core + plan.second + plan.tail
    half = plan.blocks // 2
    thin = width // plan.blocks
    down_block = w_down.shape[0] // plan.blocks
    chunks = w_up.shape[1] // width
    rows_a, rows_b = down_block + thin, (chunks + 1) * thin
    buffer = ((half * (rows_a + rows_b), width), BF16)
    ffn_send, ffn_keep = call(
        functools.partial(ffn_grad_kernel, plan, order_a, order_b, batch),
        "ffn_grads",
        [buffer, buffer],
        scratch=[
            pltpu.VMEM((w_down.shape[0], width), BF16),
            pltpu.VMEM((chunks, width, width), BF16),
            square_here,
            square_here,
        ],
        flops=2 * batch * length * width * width * 10,
        bytes_accessed=2 * width * width * 18,
    )(order.turn(activated[0]), *activated[1:], *cotangent_rows, *normed_ffn, *d_expanded, *attended, *d_branch, *d_query, normed)
    ffn = Reduction(plan, order, ffn_send, ffn_keep, half * rows_a, plan.first, plan.second)
    stages, tails = range(len(plan.first)), range(len(plan.tail))
    for row in rows[2:]:
        row.step()
    ffn.core()
    for number in range(1, steps):
        for row in rows:
            row.step()
    own_key_grad, own_value_grad = (
        [row.held[0] for row in rows[kind::2]] for kind in range(2)
    )
    conv_block = conv_key.shape[0] // plan.blocks
    tail_rows = conv_block + thin
    tail_buffer = ((plan.blocks * tail_rows + EXTRA_ROWS, width), BF16)
    tail_send, tail_keep, grad_tokens = call(
        functools.partial(tail_kernel, plan, order_b, order_a, batch),
        "tail",
        [tail_buffer, tail_buffer, (tokens.shape, BF16)],
        scratch=[conv_here, conv_here, square_here, square_here],
        flops=2 * batch * length * width * width * 10,
        bytes_accessed=2 * width * width * 18,
    )(
        x, normed, key_rows, value_rows, segment_column, gain_attn,
        *own_key_grad, *own_value_grad, order.turn(d_query[0]), *d_query[1:], *d_key_own, *d_value_own, *d_hidden,
        *gain_ffn_grad, w_query, w_key, w_value, conv_key, conv_value,
    )
    tail = Reduction(
        plan, order, tail_send, tail_keep, half * tail_rows, plan.second, plan.first, EXTRA_ROWS
    )
    for number in stages[:1]:
        ffn.scatter_a(number)
        ffn.scatter_b(number)
    tail.core()
    for number in stages[1:]:
        ffn.scatter_a(number)
        ffn.scatter_b(number)
    for number in tails[:1]:
        ffn.scatter_tail(number)
    for number in stages[:1]:
        tail.scatter_a(number)
        tail.scatter_b(number)
    for number in tails[1:]:
        ffn.scatter_tail(number)
    for number in stages[1:]:
        tail.scatter_a(number)
        tail.scatter_b(number)
    ffn.rest()
    for number in tails:
        ffn.gather_tail(tails[-1 - number])
        tail.scatter_tail(number)
    gains = tail.rest().astype(F32)
    for number in stages[1:]:
        ffn.gather_a(number)
        ffn.gather_b(number)
    for number in tails:
        tail.gather_tail(tails[-1 - number])
    for number in stages[:1]:
        ffn.gather_a(number)
        ffn.gather_b(number)
    ffn_near, ffn_far = ffn.last()
    for number in stages[1:]:
        tail.gather_a(number)
        tail.gather_b(number)
    for number in stages[:1]:
        tail.gather_a(number)
        tail.gather_b(number)
    tail_near, tail_far = tail.last()
    everything = slice(None)
    ups = [(thin, 2, slice(c * width, (c + 1) * width)) for c in range(chunks)]
    grad_down, grad_out, grad_up, grad_query = finish(
        plan, "ffn_finish",
        [
            (order_a, [(down_block, 0, everything), (thin, 1, everything)]),
            (order_b, ups + [(thin, 3, everything)]),
        ],
        ffn_near, ffn_far, [w_down.shape, square, w_up.shape, square],
    )
    grad_conv_key, grad_key, grad_conv_value, grad_value = finish(
        plan, "tail_finish",
        [
            (order_b, [(conv_block, 0, everything), (thin, 1, everything)]),
            (order_a, [(conv_block, 2, everything), (thin, 3, everything)]),
        ],
        tail_near, tail_far, [conv_key.shape, square, conv_value.shape, square],
    )
    return (
        jnp.stack(layer_out)[:, None], grad_tokens, gains[0], grad_query, grad_key, grad_value,
        grad_conv_key, grad_conv_value, grad_out, gains[1], grad_up, grad_down,
    )


def solution(mesh):
    packed = P(None, "rows", "seq", None)
    in_specs = (packed, P(None, "rows", "seq"), packed) + (P(),) * 10
    out_specs = (packed, packed) + (P(),) * 10
    return jax.shard_map(
        functools.partial(body, Plan(mesh)),
        mesh=mesh, in_specs=in_specs, out_specs=out_specs, check_vma=False,
    )
```

time: 277 us -> 230 us (0.83)
  waiting for transfers between devices: 150 us -> 128 us
  Pallas kernels: 58.4 us -> 39 us
  starting transfers between devices: 46 us -> 54.8 us
  other arithmetic: 12.2 us -> 4.56 us
  local copies, waits for them, and re-layouts: 8.42 us -> 1.48 us
    ppermute x40 -> x52, waiting for transfers between devices: 150 us -> 128 us  [swap(): return lax.ppermute(array, axis, [(i, i ^ value) for i in range(size)])]
    pallas_call x6 -> x9, Pallas kernels: 58.4 us -> 39 us  [run(): pl.pallas_call(kernel, name=name, out_shape=[jax.ShapeDtypeStruct(shape,...]
    ppermute x40 -> x52, starting transfers between devices: 46 us -> 54.8 us  [swap(): return lax.ppermute(array, axis, [(i, i ^ value) for i in range(size)])]
    concatenate x4 -> x8, other arithmetic: 3.71 us -> 0.15 us  [gather_row(): held = jnp.concatenate([held, arrived], axis=0)]
  transfers between devices with their start and end apart: 40 -> 52, of which waited for: 26 -> 29; matrix products, arithmetic and copies ran while one was open for 4% -> 2% of each run, Pallas kernels for 6% -> 14%
where the time goes in v2:
time: 230 us
  waiting for transfers between devices  128 us (56%)
  starting transfers between devices  54.8 us (24%)
  Pallas kernels  39 us (17%)
  other arithmetic  4.56 us (2%)
    ppermute x52, waiting for transfers between devices, swap(): return lax.ppermute(array, axis, [(i, i ^ value) for i in range(size)])  128 us
    ppermute x52, starting transfers between devices, swap(): return lax.ppermute(array, axis, [(i, i ^ value) for i in range(size)])  54.8 us
    pallas_call x9, Pallas kernels, run(): pl.pallas_call(kernel, name=name, out_shape=[jax.ShapeDtypeStruct(shape,...  39 us
  transfers between devices with their start and end apart: 52, of which 29 were waited for; matrix products, arithmetic and copies ran while one was open for 2% of the time, Pallas kernels for 14%

profile of v2, /device:TPU:0, one launch (start us, length us, event | category | flops | bytes accessed | tf_op | source)
XLA Modules:
  0.0 229.8 jit_solution(9704109673051369266)
XLA Ops:
  0.7 3.5 %project.1 = (f32[2,144,512]{2,1,0:T(8,128)S(1)}, bf16[2,144,512]{2,1,0:T(8,128)(2,1)S(1)}, bf16[2,144,512]{2,1,0:T(8,128)(2,1)S(1)}, bf16[2,144,512]{2,1,0:T(8,...) custom-call(bf16[2,1,144,512]{3,2,1,0:T(8,128)(2,1)} %tokens_far.1, ...), custom_call_target="tpu_custom_call" | custom-call | flops 754974720 | bytes 4718592 | tf_op jit(solution)/shard_map/project/pallas_call | solution.py:141
  4.2 3.0 %collective-permute-start.9 = (bf16[1,48,512]{2,1,0:T(8,128)(2,1)S(1)}, bf16[1,48,512]{2,1,0:T(8,128)(2,1)S(1)}, u32[]{:S(2)}, u32[]{:S(2)}) collective-permute-start(bf16[1,48,512]{2,1,0:T(8,128)(2,1)S(1)} %get-tuple-element.225), channel_id=1, source_target_pairs={{0,1},{1,0},{2,3},{3,2},{4,5},{5,4},{6,7},{7,6},{8,9},{9,8},{10,11... | collective-permute-start | bytes 147464 | tf_op jit(solution)/shard_map/ppermute | solution.py:98
  7.3 2.7 %collective-permute-start.6 = (bf16[1,64,512]{2,1,0:T(8,128)(2,1)S(1)}, bf16[1,64,512]{2,1,0:T(8,128)(2,1)S(1)}, u32[]{:S(2)}, u32[]{:S(2)}) collective-permute-start(bf16[1,64,512]{2,1,0:T(8,128)(2,1)S(1)} %get-tuple-element.223), channel_id=1, source_target_pairs={{0,4},{1,5},{2,6},{3,7},{4,0},{5,1},{6,2},{7,3},{8,12},{9,13},{10,... | collective-permute-start | bytes 196616 | tf_op jit(solution)/shard_map/ppermute | solution.py:98
  10.5 2.9 %collective-permute-start.10 = (bf16[2,48,512]{2,1,0:T(8,128)(2,1)S(1)}, bf16[2,48,512]{2,1,0:T(8,128)(2,1)S(1)}, u32[]{:S(2)}, u32[]{:S(2)}) collective-permute-start(bf16[2,48,512]{2,1,0:T(8,128)(2,1)S(1)} %pad_maximum_fusion.27), channel_id=1, source_target_pairs={{0,4},{1,5},{2,6},{3,7},{4,0},{5,1},{6,2},{7,3},{8,12},{9,13},{10,... | collective-permute-start | bytes 294920 | tf_op jit(solution)/shard_map/ppermute | solution.py:98
  13.4 5.2 %collective-permute-done = bf16[1,64,512]{2,1,0:T(8,128)(2,1)S(1)} collective-permute-done((bf16[1,64,512]{2,1,0:T(8,128)(2,1)S(1)}, bf16[1,64,512]{2,1,0:T(8,128)(2,1)S(1)}, u32[]{:S(2)}, u32[]{:S(2)}) %collective-permute-start) | collective-permute-done | bytes 65568 | tf_op jit(solution)/shard_map/ppermute | solution.py:98
  19.0 3.4 %collective-permute-start.4 = (bf16[2,48,512]{2,1,0:T(8,128)(2,1)S(1)}, bf16[2,48,512]{2,1,0:T(8,128)(2,1)S(1)}, u32[]{:S(2)}, u32[]{:S(2)}) collective-permute-start(bf16[2,48,512]{2,1,0:T(8,128)(2,1)S(1)} %pad_maximum_fusion.26), channel_id=1, source_target_pairs={{0,4},{1,5},{2,6},{3,7},{4,0},{5,1},{6,2},{7,3},{8,12},{9,13},{10,... | collective-permute-start | bytes 294920 | tf_op jit(solution)/shard_map/ppermute | solution.py:98
  22.5 4.1 %collective-permute-done.1 = bf16[2,64,512]{2,1,0:T(8,128)(2,1)S(1)} collective-permute-done((bf16[2,64,512]{2,1,0:T(8,128)(2,1)S(1)}, bf16[2,64,512]{2,1,0:T(8,128)(2,1)S(1)}, u32[]{:S(2)}, u32[]{:S(2)}) %collective-permute-start.1) | collective-permute-done | bytes 131104 | tf_op jit(solution)/shard_map/ppermute | solution.py:98
  27.0 1.8 collective-permute-start.5
  29.5 1.6 collective-permute-start.11
  31.1 3.7 %collective-permute-done.5.values_far = bf16[4,48,512]{2,1,0:T(8,128)(2,1)S(1)} collective-permute-done((bf16[4,48,512]{2,1,0:T(8,128)(2,1)S(1)}, bf16[4,48,512]{2,1,0:T(8,128)(2,1)S(1)}, u32[]{:S(2)}, u32[]{:S(2)}) %collective-permute-start.5) | collective-permute-done | bytes 196640 | tf_op jit(solution)/shard_map/ppermute | solution.py:98
  35.6 8.1 %layer.2 = (bf16[144,512]{1,0:T(8,128)(2,1)S(1)}, f32[144,512]{1,0:T(8,128)S(1)}, bf16[144,512]{1,0:T(8,128)(2,1)S(1)}, bf16[144,2048]{1,0:T(8,128)(2,1)S(1)}, b...) custom-call(f32[2,144,512]{2,1,0:T(8,128)S(1)} %get-tuple-element.10, ...), custom_call_target="tpu_custom_call" | custom-call | flops 1811939328 | bytes 10485760 | tf_op jit(solution)/shard_map/layer/pallas_call | solution.py:141
  44.8 8.3 %layer.3 = (bf16[144,512]{1,0:T(8,128)(2,1)S(1)}, f32[144,512]{1,0:T(8,128)S(1)}, bf16[144,512]{1,0:T(8,128)(2,1)S(1)}, bf16[144,2048]{1,0:T(8,128)(2,1)S(1)}, b...) custom-call(f32[2,144,512]{2,1,0:T(8,128)S(1)} %get-tuple-element.10, ...), custom_call_target="tpu_custom_call" | custom-call | flops 1811939328 | bytes 10485760 | tf_op jit(solution)/shard_map/layer/pallas_call | solution.py:141
  55.2 4.8 %collective-permute-done.17 = bf16[4,48,512]{2,1,0:T(8,128)(2,1)S(1)} collective-permute-done((bf16[4,48,512]{2,1,0:T(8,128)(2,1)S(1)}, bf16[4,48,512]{2,1,0:T(8,128)(2,1)S(1)}, u32[]{:S(2)}, u32[]{:S(2)}) %collective-permute-start.17) | collective-permute-done | bytes 196640 | tf_op jit(solution)/shard_map/ppermute | solution.py:98
  60.0 3.3 %ffn_grads.1 = (bf16[2560,512]{1,0:T(8,128)(2,1)S(1)}, bf16[2560,512]{1,0:T(8,128)(2,1)S(1)}) custom-call(bf16[144,2048]{1,0:T(8,128)(2,1)S(1)} %get-tuple-element.140.refs_0_, bf16[144,2048]{1,0:T(8,128)(2,1)S(1)} %get-tuple-element.141.refs_1_, bf16[144,512]{1,0:T(8,128)(2,1)S(1)} %get-tuple-element.142.refs_2_, ...), custom_call_target="tpu_custom_call" | custom-call | flops 1509949440 | bytes 9437184 | tf_op jit(solution)/shard_map/ffn_grads/pallas_call | solution.py:141
  64.5 1.2 collective-permute-start.13
  65.7 5.6 %collective-permute-done.15 = bf16[4,48,512]{2,1,0:T(8,128)(2,1)S(1)} collective-permute-done((bf16[4,48,512]{2,1,0:T(8,128)(2,1)S(1)}, bf16[4,48,512]{2,1,0:T(8,128)(2,1)S(1)}, u32[]{:S(2)}, u32[]{:S(2)}) %collective-permute-start.15) | collective-permute-done | bytes 196640 | tf_op jit(solution)/shard_map/ppermute | solution.py:98
  71.4 2.5 %collective-permute-start.18 = (bf16[2,48,512]{2,1,0:T(8,128)(2,1)S(1)}, bf16[2,48,512]{2,1,0:T(8,128)(2,1)S(1)}, u32[]{:S(2)}, u32[]{:S(2)}) collective-permute-start(bf16[2,48,512]{2,1,0:T(8,128)(2,1)S(1)} %slice.362), channel_id=1, source_target_pairs={{0,4},{1,5},{2,6},{3,7},{4,0},{5,1},{6,2},{7,3},{8,12},{9,13},{10,... | collective-permute-start | bytes 294920 | tf_op jit(solution)/shard_map/ppermute | solution.py:98
  73.9 1.9 collective-permute-start.19
  76.0 2.9 %collective-permute-start.14 = (bf16[1,48,512]{2,1,0:T(8,128)(2,1)S(1)}, bf16[1,48,512]{2,1,0:T(8,128)(2,1)S(1)}, u32[]{:S(2)}, u32[]{:S(2)}) collective-permute-start(bf16[1,48,512]{2,1,0:T(8,128)(2,1)S(1)} %slice.360), channel_id=1, source_target_pairs={{0,4},{1,5},{2,6},{3,7},{4,0},{5,1},{6,2},{7,3},{8,12},{9,13},{10,... | collective-permute-start | bytes 147464 | tf_op jit(solution)/shard_map/ppermute | solution.py:98
  78.9 5.6 %collective-permute-done.20 = bf16[2,48,512]{2,1,0:T(8,128)(2,1)S(1)} collective-permute-done((bf16[2,48,512]{2,1,0:T(8,128)(2,1)S(1)}, bf16[2,48,512]{2,1,0:T(8,128)(2,1)S(1)}, u32[]{:S(2)}, u32[]{:S(2)}) %collective-permute-start.20) | collective-permute-done | bytes 98336 | tf_op jit(solution)/shard_map/ppermute | solution.py:98
  85.4 1.3 collective-permute-start.23
  86.8 2.0 collective-permute-done.22
  89.8 4.0 %tail.1 = (bf16[2064,512]{1,0:T(8,128)(2,1)S(1)}, bf16[2064,512]{1,0:T(8,128)(2,1)S(1)}, bf16[2,1,144,512]{3,2,1,0:T(8,128)(2,1)}) custom-call(f32[2,144,512]{2,1,0:T(8,128)S(1)} %get-tuple-element.101.x_in, bf16[2,144,512]{2,1,0:T(8,128)(2,1)S(1)} %get-tuple-element.110.normed_in.refs_14_, bf16[2,144,512]{2,1,0:T(8,128)(2,1)S(1)} %get-tuple-element.103.key_in, ...), custom_call_target="tpu_custom_call" | custom-call | flops 1509949440 | bytes 9437184 | tf_op jit(solution)/shard_map/tail/pallas_call | solution.py:141
  94.7 1.6 collective-permute-start.27
  97.4 14.5 %collective-permute-done.27 = bf16[640,512]{1,0:T(8,128)(2,1)S(1)} collective-permute-done((bf16[640,512]{1,0:T(8,128)(2,1)S(1)}, bf16[640,512]{1,0:T(8,128)(2,1)S(1)}, u32[]{:S(2)}, u32[]{:S(2)}) %collective-permute-start.27) | collective-permute-done | bytes 655392 | tf_op jit(solution)/shard_map/ppermute | solution.py:98
  115.1 7.0 %collective-permute-done.30 = bf16[320,512]{1,0:T(8,128)(2,1)S(1)} collective-permute-done((bf16[320,512]{1,0:T(8,128)(2,1)S(1)}, bf16[320,512]{1,0:T(8,128)(2,1)S(1)}, u32[]{:S(2)}, u32[]{:S(2)}) %collective-permute-start.30) | collective-permute-done | bytes 327712 | tf_op jit(solution)/shard_map/ppermute | solution.py:98
  123.4 4.1 %collective-permute-start.32 = (bf16[320,512]{1,0:T(8,128)(2,1)S(1)}, bf16[320,512]{1,0:T(8,128)(2,1)S(1)}, u32[]{:S(2)}, u32[]{:S(2)}) collective-permute-start(bf16[320,512]{1,0:T(8,128)(2,1)S(1)} %pad_maximum_fusion.6), channel_id=1, source_target_pairs={{0,2},{1,3},{2,0},{3,1},{4,6},{5,7},{6,4},{7,5},{8,10},{9,11},{10,... | collective-permute-start | bytes 983048 | tf_op jit(solution)/shard_map/ppermute | solution.py:98
  130.1 3.5 %collective-permute-done.32 = bf16[320,512]{1,0:T(8,128)(2,1)S(1)} collective-permute-done((bf16[320,512]{1,0:T(8,128)(2,1)S(1)}, bf16[320,512]{1,0:T(8,128)(2,1)S(1)}, u32[]{:S(2)}, u32[]{:S(2)}) %collective-permute-start.32) | collective-permute-done | bytes 327712 | tf_op jit(solution)/shard_map/ppermute | solution.py:98
  133.7 6.6 %collective-permute-done.29 = bf16[512,512]{1,0:T(8,128)(2,1)S(1)} collective-permute-done((bf16[512,512]{1,0:T(8,128)(2,1)S(1)}, bf16[512,512]{1,0:T(8,128)(2,1)S(1)}, u32[]{:S(2)}, u32[]{:S(2)}) %collective-permute-start.29) | collective-permute-done | bytes 524320 | tf_op jit(solution)/shard_map/ppermute | solution.py:98
  141.7 1.2 collective-permute-start.33
  144.1 8.3 %collective-permute-done.35 = bf16[160,512]{1,0:T(8,128)(2,1)S(1)} collective-permute-done((bf16[160,512]{1,0:T(8,128)(2,1)S(1)}, bf16[160,512]{1,0:T(8,128)(2,1)S(1)}, u32[]{:S(2)}, u32[]{:S(2)}) %collective-permute-start.35) | collective-permute-done | bytes 163872 | tf_op jit(solution)/shard_map/ppermute | solution.py:98
  153.2 7.2 %collective-permute-done.38 = bf16[160,512]{1,0:T(8,128)(2,1)S(1)} collective-permute-done((bf16[160,512]{1,0:T(8,128)(2,1)S(1)}, bf16[160,512]{1,0:T(8,128)(2,1)S(1)}, u32[]{:S(2)}, u32[]{:S(2)}) %collective-permute-start.38) | collective-permute-done | bytes 163872 | tf_op jit(solution)/shard_map/ppermute | solution.py:98
  160.6 4.5 %collective-permute-done.36 = bf16[272,512]{1,0:T(8,128)(2,1)S(1)} collective-permute-done((bf16[272,512]{1,0:T(8,128)(2,1)S(1)}, bf16[272,512]{1,0:T(8,128)(2,1)S(1)}, u32[]{:S(2)}, u32[]{:S(2)}) %collective-permute-start.36) | collective-permute-done | bytes 278560 | tf_op jit(solution)/shard_map/ppermute | solution.py:98
  165.3 3.3 %collective-permute-done.39 = bf16[320,512]{1,0:T(8,128)(2,1)S(1)} collective-permute-done((bf16[320,512]{1,0:T(8,128)(2,1)S(1)}, bf16[320,512]{1,0:T(8,128)(2,1)S(1)}, u32[]{:S(2)}, u32[]{:S(2)}) %collective-permute-start.39) | collective-permute-done | bytes 327712 | tf_op jit(solution)/shard_map/ppermute | solution.py:98
  168.6 1.6 collective-permute-start.40
  170.2 1.9 collective-permute-start.43
  172.2 3.3 %collective-permute-done.37 = bf16[144,512]{1,0:T(8,128)(2,1)S(1)} collective-permute-done((bf16[144,512]{1,0:T(8,128)(2,1)S(1)}, bf16[144,512]{1,0:T(8,128)(2,1)S(1)}, u32[]{:S(2)}, u32[]{:S(2)}) %collective-permute-start.37) | collective-permute-done | bytes 147488 | tf_op jit(solution)/shard_map/ppermute | solution.py:98
  175.8 1.6 collective-permute-done.43
  177.4 4.4 %collective-permute-done.42 = bf16[128,512]{1,0:T(8,128)(2,1)S(1)} collective-permute-done((bf16[128,512]{1,0:T(8,128)(2,1)S(1)}, bf16[128,512]{1,0:T(8,128)(2,1)S(1)}, u32[]{:S(2)}, u32[]{:S(2)}) %collective-permute-start.42) | collective-permute-done | bytes 131104 | tf_op jit(solution)/shard_map/ppermute | solution.py:98
  183.0 5.3 %collective-permute-done.44 = bf16[256,512]{1,0:T(8,128)(2,1)S(1)} collective-permute-done((bf16[256,512]{1,0:T(8,128)(2,1)S(1)}, bf16[256,512]{1,0:T(8,128)(2,1)S(1)}, u32[]{:S(2)}, u32[]{:S(2)}) %collective-permute-start.44) | collective-permute-done | bytes 262176 | tf_op jit(solution)/shard_map/ppermute | solution.py:98
  190.1 1.5 collective-permute-start.45
  191.6 10.7 %collective-permute-done.47 = bf16[256,512]{1,0:T(8,128)(2,1)S(1)} collective-permute-done((bf16[256,512]{1,0:T(8,128)(2,1)S(1)}, bf16[256,512]{1,0:T(8,128)(2,1)S(1)}, u32[]{:S(2)}, u32[]{:S(2)}) %collective-permute-start.47) | collective-permute-done | bytes 262176 | tf_op jit(solution)/shard_map/ppermute | solution.py:98
  203.6 7.0 %collective-permute-done.45 = bf16[640,512]{1,0:T(8,128)(2,1)S(1)} collective-permute-done((bf16[640,512]{1,0:T(8,128)(2,1)S(1)}, bf16[640,512]{1,0:T(8,128)(2,1)S(1)}, u32[]{:S(2)}, u32[]{:S(2)}) %collective-permute-start.45) | collective-permute-done | bytes 655392 | tf_op jit(solution)/shard_map/ppermute | solution.py:98
  210.9 5.4 %collective-permute-done.48 = bf16[512,512]{1,0:T(8,128)(2,1)S(1)} collective-permute-done((bf16[512,512]{1,0:T(8,128)(2,1)S(1)}, bf16[512,512]{1,0:T(8,128)(2,1)S(1)}, u32[]{:S(2)}, u32[]{:S(2)}) %collective-permute-start.48) | collective-permute-done | bytes 524320 | tf_op jit(solution)/shard_map/ppermute | solution.py:98
  217.9 3.3 %ffn_finish_near.1 = (f32[2048,512]{1,0:T(8,128)}, f32[512,512]{1,0:T(8,128)}, f32[512,2048]{1,0:T(8,128)}, f32[512,512]{1,0:T(8,128)}) custom-call(bf16[2560,512]{1,0:T(8,128)(2,1)S(1)} %constant_dynamic-update-slice_fusion.refs_0_), custom_call_target="tpu_custom_call" | custom-call | bytes 7864320 | tf_op jit(solution)/shard_map/ffn_finish_near/pallas_call | solution.py:141
  221.2 2.6 %tail_finish_near.1 = (f32[1536,512]{1,0:T(8,128)}, f32[512,512]{1,0:T(8,128)}, f32[1536,512]{1,0:T(8,128)}, f32[512,512]{1,0:T(8,128)}) custom-call(bf16[2048,512]{1,0:T(8,128)(2,1)S(1)} %constant_dynamic-update-slice_fusion.10.refs_0_), custom_call_target="tpu_custom_call" | custom-call | bytes 6291456 | tf_op jit(solution)/shard_map/tail_finish_near/pallas_call | solution.py:141
  223.8 2.6 %tail_finish_far.1 = (f32[1536,512]{1,0:T(8,128)}, f32[512,512]{1,0:T(8,128)}, f32[1536,512]{1,0:T(8,128)}, f32[512,512]{1,0:T(8,128)}) custom-call(bf16[2048,512]{1,0:T(8,128)(2,1)S(1)} %collective-permute-done.51.refs_0_, f32[1536,512]{1,0:T(8,128)} %get-tuple-element.179.refs_1_, ...), custom_call_target="tpu_custom_call", output_to_operand_aliasing={{0}: (1, {}), {1}: (2, {}), {2}: (3, {}), {3}: (4, {})} | custom-call | bytes 6291456 | tf_op jit(solution)/shard_map/tail_finish_far/pallas_call | solution.py:141
  226.4 3.3 %ffn_finish_far.1 = (f32[2048,512]{1,0:T(8,128)}, f32[512,512]{1,0:T(8,128)}, f32[512,2048]{1,0:T(8,128)}, f32[512,512]{1,0:T(8,128)}) custom-call(bf16[2560,512]{1,0:T(8,128)(2,1)S(1)} %collective-permute-done.46.refs_0_, f32[2048,512]{1,0:T(8,128)} %get-tuple-element.172.refs_1_, ...), custom_call_target="tpu_custom_call", output_to_operand_aliasing={{0}: (1, {}), {1}: (2, {}), {2}: (3, {}), {3}: (4, {})} | custom-call | bytes 7864320 | tf_op jit(solution)/shard_map/ffn_finish_far/pallas_call | solution.py:141
  (196 shorter events, 28.2 us)
Async XLA Ops:
  4.2 6.3 %collective-permute-start.9 = (bf16[1,48,512]{2,1,0:T(8,128)(2,1)S(1)}, bf16[1,48,512]{2,1,0:T(8,128)(2,1)S(1)}, u32[]{:S(2)}, u32[]{:S(2)}) collective-permute-start(bf16[1,48,512]{2,1,0:T(8,128)(2,1)S(1)} %get-tuple-element.225), channel_id=1, source_target_pairs={{0,1},{1,0},{2,3},{3,2},{4,5},{5,4},{6,7},{7,6},{8,9},{9,8},{10,11... | collective-permute-start | bytes 147464 | tf_op jit(solution)/shard_map/ppermute | solution.py:98
  7.3 15.2 %collective-permute-start.6 = (bf16[1,64,512]{2,1,0:T(8,128)(2,1)S(1)}, bf16[1,64,512]{2,1,0:T(8,128)(2,1)S(1)}, u32[]{:S(2)}, u32[]{:S(2)}) collective-permute-start(bf16[1,64,512]{2,1,0:T(8,128)(2,1)S(1)} %get-tuple-element.223), channel_id=1, source_target_pairs={{0,4},{1,5},{2,6},{3,7},{4,0},{5,1},{6,2},{7,3},{8,12},{9,13},{10,... | collective-permute-start | bytes 196616 | tf_op jit(solution)/shard_map/ppermute | solution.py:98
  9.9 8.7 %collective-permute-start = (bf16[1,64,512]{2,1,0:T(8,128)(2,1)S(1)}, bf16[1,64,512]{2,1,0:T(8,128)(2,1)S(1)}, u32[]{:S(2)}, u32[]{:S(2)}) collective-permute-start(bf16[1,64,512]{2,1,0:T(8,128)(2,1)S(1)} %get-tuple-element.222), channel_id=1, source_target_pairs={{0,4},{1,5},{2,6},{3,7},{4,0},{5,1},{6,2},{7,3},{8,12},{9,13},{10,... | collective-permute-start | bytes 196616 | tf_op jit(solution)/shard_map/ppermute | solution.py:98
  10.2 8.7 %collective-permute-start.3 = (bf16[1,48,512]{2,1,0:T(8,128)(2,1)S(1)}, bf16[1,48,512]{2,1,0:T(8,128)(2,1)S(1)}, u32[]{:S(2)}, u32[]{:S(2)}) collective-permute-start(bf16[1,48,512]{2,1,0:T(8,128)(2,1)S(1)} %get-tuple-element.224), channel_id=1, source_target_pairs={{0,1},{1,0},{2,3},{3,2},{4,5},{5,4},{6,7},{7,6},{8,9},{9,8},{10,11... | collective-permute-start | bytes 147464 | tf_op jit(solution)/shard_map/ppermute | solution.py:98
  10.5 18.9 %collective-permute-start.10 = (bf16[2,48,512]{2,1,0:T(8,128)(2,1)S(1)}, bf16[2,48,512]{2,1,0:T(8,128)(2,1)S(1)}, u32[]{:S(2)}, u32[]{:S(2)}) collective-permute-start(bf16[2,48,512]{2,1,0:T(8,128)(2,1)S(1)} %pad_maximum_fusion.27), channel_id=1, source_target_pairs={{0,4},{1,5},{2,6},{3,7},{4,0},{5,1},{6,2},{7,3},{8,12},{9,13},{10,... | collective-permute-start | bytes 294920 | tf_op jit(solution)/shard_map/ppermute | solution.py:98
  18.6 8.0 %collective-permute-start.1 = (bf16[2,64,512]{2,1,0:T(8,128)(2,1)S(1)}, bf16[2,64,512]{2,1,0:T(8,128)(2,1)S(1)}, u32[]{:S(2)}, u32[]{:S(2)}) collective-permute-start(bf16[2,64,512]{2,1,0:T(8,128)(2,1)S(1)} %pad_maximum_fusion.23), channel_id=1, source_target_pairs={{0,2},{1,3},{2,0},{3,1},{4,6},{5,7},{6,4},{7,5},{8,10},{9,11},{10,... | collective-permute-start | bytes 393224 | tf_op jit(solution)/shard_map/ppermute | solution.py:98
  19.0 8.0 %collective-permute-start.4 = (bf16[2,48,512]{2,1,0:T(8,128)(2,1)S(1)}, bf16[2,48,512]{2,1,0:T(8,128)(2,1)S(1)}, u32[]{:S(2)}, u32[]{:S(2)}) collective-permute-start(bf16[2,48,512]{2,1,0:T(8,128)(2,1)S(1)} %pad_maximum_fusion.26), channel_id=1, source_target_pairs={{0,4},{1,5},{2,6},{3,7},{4,0},{5,1},{6,2},{7,3},{8,12},{9,13},{10,... | collective-permute-start | bytes 294920 | tf_op jit(solution)/shard_map/ppermute | solution.py:98
  22.4 6.6 %collective-permute-start.7 = (bf16[2,64,512]{2,1,0:T(8,128)(2,1)S(1)}, bf16[2,64,512]{2,1,0:T(8,128)(2,1)S(1)}, u32[]{:S(2)}, u32[]{:S(2)}) collective-permute-start(bf16[2,64,512]{2,1,0:T(8,128)(2,1)S(1)} %pad_maximum_fusion.24), channel_id=1, source_target_pairs={{0,2},{1,3},{2,0},{3,1},{4,6},{5,7},{6,4},{7,5},{8,10},{9,11},{10,... | collective-permute-start | bytes 393224 | tf_op jit(solution)/shard_map/ppermute | solution.py:98
  26.7 8.9 %collective-permute-start.2 = (bf16[4,64,512]{2,1,0:T(8,128)(2,1)S(1)}, bf16[4,64,512]{2,1,0:T(8,128)(2,1)S(1)}, u32[]{:S(2)}, u32[]{:S(2)}) collective-permute-start(bf16[4,64,512]{2,1,0:T(8,128)(2,1)S(1)} %pad_maximum_fusion.12.keys_near), channel_id=1, source_target_pairs={{0,1},{1,0},{2,3},{3,2},{4,5},{5,4},{6,7},{7,6},{8,9},{9,8},{10,11... | collective-permute-start | bytes 786440 | tf_op jit(solution)/shard_map/ppermute | solution.py:98
  27.0 7.8 %collective-permute-start.5 = (bf16[4,48,512]{2,1,0:T(8,128)(2,1)S(1)}, bf16[4,48,512]{2,1,0:T(8,128)(2,1)S(1)}, u32[]{:S(2)}, u32[]{:S(2)}) collective-permute-start(bf16[4,48,512]{2,1,0:T(8,128)(2,1)S(1)} %pad_maximum_fusion.18.values_near), channel_id=1, source_target_pairs={{0,2},{1,3},{2,0},{3,1},{4,6},{5,7},{6,4},{7,5},{8,10},{9,11},{10,... | collective-permute-start | bytes 589832 | tf_op jit(solution)/shard_map/ppermute | solution.py:98
  29.1 15.7 %collective-permute-start.8 = (bf16[4,64,512]{2,1,0:T(8,128)(2,1)S(1)}, bf16[4,64,512]{2,1,0:T(8,128)(2,1)S(1)}, u32[]{:S(2)}, u32[]{:S(2)}) collective-permute-start(bf16[4,64,512]{2,1,0:T(8,128)(2,1)S(1)} %pad_maximum_fusion.13.keys_near), channel_id=1, source_target_pairs={{0,1},{1,0},{2,3},{3,2},{4,5},{5,4},{6,7},{7,6},{8,9},{9,8},{10,11... | collective-permute-start | bytes 786440 | tf_op jit(solution)/shard_map/ppermute | solution.py:98
  29.5 15.3 %collective-permute-start.11 = (bf16[4,48,512]{2,1,0:T(8,128)(2,1)S(1)}, bf16[4,48,512]{2,1,0:T(8,128)(2,1)S(1)}, u32[]{:S(2)}, u32[]{:S(2)}) collective-permute-start(bf16[4,48,512]{2,1,0:T(8,128)(2,1)S(1)} %pad_maximum_fusion.19.values_near), channel_id=1, source_target_pairs={{0,2},{1,3},{2,0},{3,1},{4,6},{5,7},{6,4},{7,5},{8,10},{9,11},{10,... | collective-permute-start | bytes 589832 | tf_op jit(solution)/shard_map/ppermute | solution.py:98
  43.7 11.4 %collective-permute-start.12 = (bf16[4,48,512]{2,1,0:T(8,128)(2,1)S(1)}, bf16[4,48,512]{2,1,0:T(8,128)(2,1)S(1)}, u32[]{:S(2)}, u32[]{:S(2)}) collective-permute-start(bf16[4,48,512]{2,1,0:T(8,128)(2,1)S(1)} %slice.276), channel_id=1, source_target_pairs={{0,1},{1,0},{2,3},{3,2},{4,5},{5,4},{6,7},{7,6},{8,9},{9,8},{10,11... | collective-permute-start | bytes 589832 | tf_op jit(solution)/shard_map/ppermute | solution.py:98
  53.1 12.6 %collective-permute-start.16 = (bf16[4,48,512]{2,1,0:T(8,128)(2,1)S(1)}, bf16[4,48,512]{2,1,0:T(8,128)(2,1)S(1)}, u32[]{:S(2)}, u32[]{:S(2)}) collective-permute-start(bf16[4,48,512]{2,1,0:T(8,128)(2,1)S(1)} %slice.284), channel_id=1, source_target_pairs={{0,1},{1,0},{2,3},{3,2},{4,5},{5,4},{6,7},{7,6},{8,9},{9,8},{10,11... | collective-permute-start | bytes 589832 | tf_op jit(solution)/shard_map/ppermute | solution.py:98
  63.4 30.4 %collective-permute-start.25 = (bf16[2560,512]{1,0:T(8,128)(2,1)S(1)}, bf16[2560,512]{1,0:T(8,128)(2,1)S(1)}, u32[]{:S(2)}, u32[]{:S(2)}) collective-permute-start(bf16[2560,512]{1,0:T(8,128)(2,1)S(1)} %get-tuple-element.153), channel_id=1, source_target_pairs={{0,8},{8,0},{16,24},{24,16},{1,9},{9,1},{17,25},{25,17},{2,10},{10... | collective-permute-start | bytes 7864328 | tf_op jit(solution)/shard_map/ppermute | solution.py:98
  63.5 7.8 %collective-permute-start.15 = (bf16[4,48,512]{2,1,0:T(8,128)(2,1)S(1)}, bf16[4,48,512]{2,1,0:T(8,128)(2,1)S(1)}, u32[]{:S(2)}, u32[]{:S(2)}) collective-permute-start(bf16[4,48,512]{2,1,0:T(8,128)(2,1)S(1)} %slice.282), channel_id=1, source_target_pairs={{0,2},{1,3},{2,0},{3,1},{4,6},{5,7},{6,4},{7,5},{8,10},{9,11},{10,... | collective-permute-start | bytes 589832 | tf_op jit(solution)/shard_map/ppermute | solution.py:98
  64.5 11.5 %collective-permute-start.13 = (bf16[2,48,512]{2,1,0:T(8,128)(2,1)S(1)}, bf16[2,48,512]{2,1,0:T(8,128)(2,1)S(1)}, u32[]{:S(2)}, u32[]{:S(2)}) collective-permute-start(bf16[2,48,512]{2,1,0:T(8,128)(2,1)S(1)} %slice.358), channel_id=1, source_target_pairs={{0,2},{1,3},{2,0},{3,1},{4,6},{5,7},{6,4},{7,5},{8,10},{9,11},{10,... | collective-permute-start | bytes 294920 | tf_op jit(solution)/shard_map/ppermute | solution.py:98
  71.4 13.1 %collective-permute-start.18 = (bf16[2,48,512]{2,1,0:T(8,128)(2,1)S(1)}, bf16[2,48,512]{2,1,0:T(8,128)(2,1)S(1)}, u32[]{:S(2)}, u32[]{:S(2)}) collective-permute-start(bf16[2,48,512]{2,1,0:T(8,128)(2,1)S(1)} %slice.362), channel_id=1, source_target_pairs={{0,4},{1,5},{2,6},{3,7},{4,0},{5,1},{6,2},{7,3},{8,12},{9,13},{10,... | collective-permute-start | bytes 294920 | tf_op jit(solution)/shard_map/ppermute | solution.py:98
  73.9 10.6 %collective-permute-start.19 = (bf16[2,48,512]{2,1,0:T(8,128)(2,1)S(1)}, bf16[2,48,512]{2,1,0:T(8,128)(2,1)S(1)}, u32[]{:S(2)}, u32[]{:S(2)}) collective-permute-start(bf16[2,48,512]{2,1,0:T(8,128)(2,1)S(1)} %slice.364), channel_id=1, source_target_pairs={{0,2},{1,3},{2,0},{3,1},{4,6},{5,7},{6,4},{7,5},{8,10},{9,11},{10,... | collective-permute-start | bytes 294920 | tf_op jit(solution)/shard_map/ppermute | solution.py:98
  75.8 8.6 %collective-permute-start.20 = (bf16[2,48,512]{2,1,0:T(8,128)(2,1)S(1)}, bf16[2,48,512]{2,1,0:T(8,128)(2,1)S(1)}, u32[]{:S(2)}, u32[]{:S(2)}) collective-permute-start(bf16[2,48,512]{2,1,0:T(8,128)(2,1)S(1)} %slice.366), channel_id=1, source_target_pairs={{0,4},{1,5},{2,6},{3,7},{4,0},{5,1},{6,2},{7,3},{8,12},{9,13},{10,... | collective-permute-start | bytes 294920 | tf_op jit(solution)/shard_map/ppermute | solution.py:98
  76.0 10.8 %collective-permute-start.14 = (bf16[1,48,512]{2,1,0:T(8,128)(2,1)S(1)}, bf16[1,48,512]{2,1,0:T(8,128)(2,1)S(1)}, u32[]{:S(2)}, u32[]{:S(2)}) collective-permute-start(bf16[1,48,512]{2,1,0:T(8,128)(2,1)S(1)} %slice.360), channel_id=1, source_target_pairs={{0,4},{1,5},{2,6},{3,7},{4,0},{5,1},{6,2},{7,3},{8,12},{9,13},{10,... | collective-permute-start | bytes 147464 | tf_op jit(solution)/shard_map/ppermute | solution.py:98
  93.8 21.3 %collective-permute-start.24 = (bf16[2064,512]{1,0:T(8,128)(2,1)S(1)}, bf16[2064,512]{1,0:T(8,128)(2,1)S(1)}, u32[]{:S(2)}, u32[]{:S(2)}) collective-permute-start(bf16[2064,512]{1,0:T(8,128)(2,1)S(1)} %get-tuple-element.138), channel_id=1, source_target_pairs={{0,8},{8,0},{16,24},{24,16},{1,9},{9,1},{17,25},{25,17},{2,10},{10... | collective-permute-start | bytes 6340616 | tf_op jit(solution)/shard_map/ppermute | solution.py:98
  94.7 17.2 %collective-permute-start.27 = (bf16[640,512]{1,0:T(8,128)(2,1)S(1)}, bf16[640,512]{1,0:T(8,128)(2,1)S(1)}, u32[]{:S(2)}, u32[]{:S(2)}) collective-permute-start(bf16[640,512]{1,0:T(8,128)(2,1)S(1)} %get-tuple-element.206), channel_id=1, source_target_pairs={{0,16},{8,24},{16,0},{24,8},{1,17},{9,25},{17,1},{25,9},{2,18},{10... | collective-permute-start | bytes 1966088 | tf_op jit(solution)/shard_map/ppermute | solution.py:98
  96.2 16.9 %collective-permute-start.26 = (bf16[640,512]{1,0:T(8,128)(2,1)S(1)}, bf16[640,512]{1,0:T(8,128)(2,1)S(1)}, u32[]{:S(2)}, u32[]{:S(2)}) collective-permute-start(bf16[640,512]{1,0:T(8,128)(2,1)S(1)} %get-tuple-element.207), channel_id=1, source_target_pairs={{0,1},{1,0},{2,3},{3,2},{4,5},{5,4},{6,7},{7,6},{8,9},{9,8},{10,11... | collective-permute-start | bytes 1966088 | tf_op jit(solution)/shard_map/ppermute | solution.py:98
  113.1 9.0 %collective-permute-start.30 = (bf16[320,512]{1,0:T(8,128)(2,1)S(1)}, bf16[320,512]{1,0:T(8,128)(2,1)S(1)}, u32[]{:S(2)}, u32[]{:S(2)}) collective-permute-start(bf16[320,512]{1,0:T(8,128)(2,1)S(1)} %slice.382), channel_id=1, source_target_pairs={{0,1},{1,0},{2,3},{3,2},{4,5},{5,4},{6,7},{7,6},{8,9},{9,8},{10,11... | collective-permute-start | bytes 983048 | tf_op jit(solution)/shard_map/ppermute | solution.py:98
  114.5 8.8 %collective-permute-start.31 = (bf16[320,512]{1,0:T(8,128)(2,1)S(1)}, bf16[320,512]{1,0:T(8,128)(2,1)S(1)}, u32[]{:S(2)}, u32[]{:S(2)}) collective-permute-start(bf16[320,512]{1,0:T(8,128)(2,1)S(1)} %slice.386), channel_id=1, source_target_pairs={{0,16},{8,24},{16,0},{24,8},{1,17},{9,25},{17,1},{25,9},{2,18},{10... | collective-permute-start | bytes 983048 | tf_op jit(solution)/shard_map/ppermute | solution.py:98
  123.4 10.2 %collective-permute-start.32 = (bf16[320,512]{1,0:T(8,128)(2,1)S(1)}, bf16[320,512]{1,0:T(8,128)(2,1)S(1)}, u32[]{:S(2)}, u32[]{:S(2)}) collective-permute-start(bf16[320,512]{1,0:T(8,128)(2,1)S(1)} %pad_maximum_fusion.6), channel_id=1, source_target_pairs={{0,2},{1,3},{2,0},{3,1},{4,6},{5,7},{6,4},{7,5},{8,10},{9,11},{10,... | collective-permute-start | bytes 983048 | tf_op jit(solution)/shard_map/ppermute | solution.py:98
  128.5 11.8 %collective-permute-start.29 = (bf16[512,512]{1,0:T(8,128)(2,1)S(1)}, bf16[512,512]{1,0:T(8,128)(2,1)S(1)}, u32[]{:S(2)}, u32[]{:S(2)}) collective-permute-start(bf16[512,512]{1,0:T(8,128)(2,1)S(1)} %slice.380), channel_id=1, source_target_pairs={{0,1},{1,0},{2,3},{3,2},{4,5},{5,4},{6,7},{7,6},{8,9},{9,8},{10,11... | collective-permute-start | bytes 1572872 | tf_op jit(solution)/shard_map/ppermute | solution.py:98
  129.1 11.9 %collective-permute-start.28 = (bf16[528,512]{1,0:T(8,128)(2,1)S(1)}, bf16[528,512]{1,0:T(8,128)(2,1)S(1)}, u32[]{:S(2)}, u32[]{:S(2)}) collective-permute-start(bf16[528,512]{1,0:T(8,128)(2,1)S(1)} %slice.378), channel_id=1, source_target_pairs={{0,16},{8,24},{16,0},{24,8},{1,17},{9,25},{17,1},{25,9},{2,18},{10... | collective-permute-start | bytes 1622024 | tf_op jit(solution)/shard_map/ppermute | solution.py:98
  141.2 11.3 %collective-permute-start.35 = (bf16[160,512]{1,0:T(8,128)(2,1)S(1)}, bf16[160,512]{1,0:T(8,128)(2,1)S(1)}, u32[]{:S(2)}, u32[]{:S(2)}) collective-permute-start(bf16[160,512]{1,0:T(8,128)(2,1)S(1)} %pad_maximum_fusion.20), channel_id=1, source_target_pairs={{0,4},{1,5},{2,6},{3,7},{4,0},{5,1},{6,2},{7,3},{8,12},{9,13},{10,... | collective-permute-start | bytes 491528 | tf_op jit(solution)/shard_map/ppermute | solution.py:98
  141.7 11.0 %collective-permute-start.33 = (bf16[272,512]{1,0:T(8,128)(2,1)S(1)}, bf16[272,512]{1,0:T(8,128)(2,1)S(1)}, u32[]{:S(2)}, u32[]{:S(2)}) collective-permute-start(bf16[272,512]{1,0:T(8,128)(2,1)S(1)} %fusion), channel_id=1, source_target_pairs={{0,1},{1,0},{2,3},{3,2},{4,5},{5,4},{6,7},{7,6},{8,9},{9,8},{10,11... | collective-permute-start | bytes 835592 | tf_op jit(solution)/shard_map/ppermute | solution.py:98
  142.9 9.7 %collective-permute-start.34 = (bf16[256,512]{1,0:T(8,128)(2,1)S(1)}, bf16[256,512]{1,0:T(8,128)(2,1)S(1)}, u32[]{:S(2)}, u32[]{:S(2)}) collective-permute-start(bf16[256,512]{1,0:T(8,128)(2,1)S(1)} %slice.394), channel_id=1, source_target_pairs={{0,16},{8,24},{16,0},{24,8},{1,17},{9,25},{17,1},{25,9},{2,18},{10... | collective-permute-start | bytes 786440 | tf_op jit(solution)/shard_map/ppermute | solution.py:98
  152.5 7.9 %collective-permute-start.38 = (bf16[160,512]{1,0:T(8,128)(2,1)S(1)}, bf16[160,512]{1,0:T(8,128)(2,1)S(1)}, u32[]{:S(2)}, u32[]{:S(2)}) collective-permute-start(bf16[160,512]{1,0:T(8,128)(2,1)S(1)} %pad_maximum_fusion.21), channel_id=1, source_target_pairs={{0,4},{1,5},{2,6},{3,7},{4,0},{5,1},{6,2},{7,3},{8,12},{9,13},{10,... | collective-permute-start | bytes 491528 | tf_op jit(solution)/shard_map/ppermute | solution.py:98
  152.9 12.2 %collective-permute-start.36 = (bf16[272,512]{1,0:T(8,128)(2,1)S(1)}, bf16[272,512]{1,0:T(8,128)(2,1)S(1)}, u32[]{:S(2)}, u32[]{:S(2)}) collective-permute-start(bf16[272,512]{1,0:T(8,128)(2,1)S(1)} %pad_maximum_fusion.11), channel_id=1, source_target_pairs={{0,2},{1,3},{2,0},{3,1},{4,6},{5,7},{6,4},{7,5},{8,10},{9,11},{10,... | collective-permute-start | bytes 835592 | tf_op jit(solution)/shard_map/ppermute | solution.py:98
  160.5 8.1 %collective-permute-start.39 = (bf16[320,512]{1,0:T(8,128)(2,1)S(1)}, bf16[320,512]{1,0:T(8,128)(2,1)S(1)}, u32[]{:S(2)}, u32[]{:S(2)}) collective-permute-start(bf16[320,512]{1,0:T(8,128)(2,1)S(1)} %pad_maximum_fusion.7), channel_id=1, source_target_pairs={{0,2},{1,3},{2,0},{3,1},{4,6},{5,7},{6,4},{7,5},{8,10},{9,11},{10,... | collective-permute-start | bytes 983048 | tf_op jit(solution)/shard_map/ppermute | solution.py:98
  165.2 10.2 %collective-permute-start.37 = (bf16[144,512]{1,0:T(8,128)(2,1)S(1)}, bf16[144,512]{1,0:T(8,128)(2,1)S(1)}, u32[]{:S(2)}, u32[]{:S(2)}) collective-permute-start(bf16[144,512]{1,0:T(8,128)(2,1)S(1)} %pad_maximum_fusion.22), channel_id=1, source_target_pairs={{0,4},{1,5},{2,6},{3,7},{4,0},{5,1},{6,2},{7,3},{8,12},{9,13},{10,... | collective-permute-start | bytes 442376 | tf_op jit(solution)/shard_map/ppermute | solution.py:98
  168.6 7.1 %collective-permute-start.40 = (bf16[320,512]{1,0:T(8,128)(2,1)S(1)}, bf16[320,512]{1,0:T(8,128)(2,1)S(1)}, u32[]{:S(2)}, u32[]{:S(2)}) collective-permute-start(bf16[320,512]{1,0:T(8,128)(2,1)S(1)} %pad_maximum_fusion.8), channel_id=1, source_target_pairs={{0,1},{1,0},{2,3},{3,2},{4,5},{5,4},{6,7},{7,6},{8,9},{9,8},{10,11... | collective-permute-start | bytes 983048 | tf_op jit(solution)/shard_map/ppermute | solution.py:98
  170.2 7.1 %collective-permute-start.43 = (bf16[320,512]{1,0:T(8,128)(2,1)S(1)}, bf16[320,512]{1,0:T(8,128)(2,1)S(1)}, u32[]{:S(2)}, u32[]{:S(2)}) collective-permute-start(bf16[320,512]{1,0:T(8,128)(2,1)S(1)} %pad_maximum_fusion.10), channel_id=1, source_target_pairs={{0,16},{8,24},{16,0},{24,8},{1,17},{9,25},{17,1},{25,9},{2,18},{10... | collective-permute-start | bytes 983048 | tf_op jit(solution)/shard_map/ppermute | solution.py:98
  175.5 6.3 %collective-permute-start.42 = (bf16[128,512]{1,0:T(8,128)(2,1)S(1)}, bf16[128,512]{1,0:T(8,128)(2,1)S(1)}, u32[]{:S(2)}, u32[]{:S(2)}) collective-permute-start(bf16[128,512]{1,0:T(8,128)(2,1)S(1)} %pad_maximum_fusion.25), channel_id=1, source_target_pairs={{0,4},{1,5},{2,6},{3,7},{4,0},{5,1},{6,2},{7,3},{8,12},{9,13},{10,... | collective-permute-start | bytes 393224 | tf_op jit(solution)/shard_map/ppermute | solution.py:98
  181.9 6.4 %collective-permute-start.44 = (bf16[256,512]{1,0:T(8,128)(2,1)S(1)}, bf16[256,512]{1,0:T(8,128)(2,1)S(1)}, u32[]{:S(2)}, u32[]{:S(2)}) collective-permute-start(bf16[256,512]{1,0:T(8,128)(2,1)S(1)} %pad_maximum_fusion.14), channel_id=1, source_target_pairs={{0,2},{1,3},{2,0},{3,1},{4,6},{5,7},{6,4},{7,5},{8,10},{9,11},{10,... | collective-permute-start | bytes 786440 | tf_op jit(solution)/shard_map/ppermute | solution.py:98
  182.0 21.6 %collective-permute-start.41 = (bf16[640,512]{1,0:T(8,128)(2,1)S(1)}, bf16[640,512]{1,0:T(8,128)(2,1)S(1)}, u32[]{:S(2)}, u32[]{:S(2)}) collective-permute-start(bf16[640,512]{1,0:T(8,128)(2,1)S(1)} %pad_maximum_fusion.1), channel_id=1, source_target_pairs={{0,16},{8,24},{16,0},{24,8},{1,17},{9,25},{17,1},{25,9},{2,18},{10... | collective-permute-start | bytes 1966088 | tf_op jit(solution)/shard_map/ppermute | solution.py:98
  188.4 13.9 %collective-permute-start.47 = (bf16[256,512]{1,0:T(8,128)(2,1)S(1)}, bf16[256,512]{1,0:T(8,128)(2,1)S(1)}, u32[]{:S(2)}, u32[]{:S(2)}) collective-permute-start(bf16[256,512]{1,0:T(8,128)(2,1)S(1)} %pad_maximum_fusion.15), channel_id=1, source_target_pairs={{0,16},{8,24},{16,0},{24,8},{1,17},{9,25},{17,1},{25,9},{2,18},{10... | collective-permute-start | bytes 786440 | tf_op jit(solution)/shard_map/ppermute | solution.py:98
  189.5 13.0 %collective-permute-start.49 = (bf16[256,512]{1,0:T(8,128)(2,1)S(1)}, bf16[256,512]{1,0:T(8,128)(2,1)S(1)}, u32[]{:S(2)}, u32[]{:S(2)}) collective-permute-start(bf16[256,512]{1,0:T(8,128)(2,1)S(1)} %pad_maximum_fusion.17), channel_id=1, source_target_pairs={{0,1},{1,0},{2,3},{3,2},{4,5},{5,4},{6,7},{7,6},{8,9},{9,8},{10,11... | collective-permute-start | bytes 786440 | tf_op jit(solution)/shard_map/ppermute | solution.py:98
  190.1 20.6 %collective-permute-start.45 = (bf16[640,512]{1,0:T(8,128)(2,1)S(1)}, bf16[640,512]{1,0:T(8,128)(2,1)S(1)}, u32[]{:S(2)}, u32[]{:S(2)}) collective-permute-start(bf16[640,512]{1,0:T(8,128)(2,1)S(1)} %pad_maximum_fusion.2), channel_id=1, source_target_pairs={{0,1},{1,0},{2,3},{3,2},{4,5},{5,4},{6,7},{7,6},{8,9},{9,8},{10,11... | collective-permute-start | bytes 1966088 | tf_op jit(solution)/shard_map/ppermute | solution.py:98
  202.3 14.0 %collective-permute-start.48 = (bf16[512,512]{1,0:T(8,128)(2,1)S(1)}, bf16[512,512]{1,0:T(8,128)(2,1)S(1)}, u32[]{:S(2)}, u32[]{:S(2)}) collective-permute-start(bf16[512,512]{1,0:T(8,128)(2,1)S(1)} %pad_maximum_fusion.3), channel_id=1, source_target_pairs={{0,1},{1,0},{2,3},{3,2},{4,5},{5,4},{6,7},{7,6},{8,9},{9,8},{10,11... | collective-permute-start | bytes 1572872 | tf_op jit(solution)/shard_map/ppermute | solution.py:98
  202.5 13.9 %collective-permute-start.50 = (bf16[512,512]{1,0:T(8,128)(2,1)S(1)}, bf16[512,512]{1,0:T(8,128)(2,1)S(1)}, u32[]{:S(2)}, u32[]{:S(2)}) collective-permute-start(bf16[512,512]{1,0:T(8,128)(2,1)S(1)} %pad_maximum_fusion.4), channel_id=1, source_target_pairs={{0,16},{8,24},{16,0},{24,8},{1,17},{9,25},{17,1},{25,9},{2,18},{10... | collective-permute-start | bytes 1572872 | tf_op jit(solution)/shard_map/ppermute | solution.py:98
  210.8 15.6 %collective-permute-start.46 = (bf16[2560,512]{1,0:T(8,128)(2,1)S(1)}, bf16[2560,512]{1,0:T(8,128)(2,1)S(1)}, u32[]{:S(2)}, u32[]{:S(2)}) collective-permute-start(bf16[2560,512]{1,0:T(8,128)(2,1)S(1)} %constant_dynamic-update-slice_fusion.refs_0_), channel_id=1, source_target_pairs={{0,8},{8,0},{16,24},{24,16},{1,9},{9,1},{17,25},{25,17},{2,10},{10... | collective-permute-start | bytes 7864328 | tf_op jit(solution)/shard_map/ppermute | solution.py:98
  216.5 7.3 %collective-permute-start.51 = (bf16[2048,512]{1,0:T(8,128)(2,1)S(1)}, bf16[2048,512]{1,0:T(8,128)(2,1)S(1)}, u32[]{:S(2)}, u32[]{:S(2)}) collective-permute-start(bf16[2048,512]{1,0:T(8,128)(2,1)S(1)} %constant_dynamic-update-slice_fusion.10.refs_0_), channel_id=1, source_target_pairs={{0,8},{8,0},{16,24},{24,16},{1,9},{9,1},{17,25},{25,17},{2,10},{10... | collective-permute-start | bytes 6291464 | tf_op jit(solution)/shard_map/ppermute | solution.py:98
  (15 other events, 340.6 us)

commit v3 on v1

v3 whole, which is shorter than its diff:
```python
import functools

import jax
import jax.numpy as jnp
from jax import lax
from jax.experimental import pallas as pl
from jax.experimental.pallas import tpu as pltpu
from jax.sharding import PartitionSpec as P

HEADS = 8
HEAD_DIM = 64
LANES = 128
GROUPS = HEADS * HEAD_DIM // LANES
EPSILON = 1e-05
MASKED_OUT = -1e30
SCALE = HEAD_DIM ** (-0.5)
GELU_SCALE = 0.7978845608028654
GELU_CUBIC = 0.044715
SCATTER_BITS = 5
EXTRA_ROWS = 16
VMEM_SMALL = 28 * 1024 * 1024
VMEM_LARGE = 60 * 1024 * 1024
SHORT_ROW = 768
BYTES_MICROSECOND = 3_690_000

EVENTS = (
    "Wb", "Wa", "A1", "A0", "K", "V", "K", "A1", "V", "A0", "K", "TK", "V", "TV", "A1", "B0",
    "A0", "B1", "A1", "A0", "A1", "A0", "B0", "B1", "A1", "A0", "B0", "A1", "B1", "A0", "B0",
    "B1", "A1", "B0", "A0", "B1", "B0", "B1", "B0", "B1", "A1", "A0", "B0", "B1", "A0n", "A0f",
    "A1n", "A1f", "B0", "B0n", "B1", "B0f", "B1n", "B1f",
)

BF16 = jnp.bfloat16
F32 = jnp.float32


def dot(left, right):
    return jnp.dot(left, right, preferred_element_type=F32)


def dot_nt(left, right):
    return lax.dot_general(left, right, (((1,), (1,)), ((), ())), preferred_element_type=F32)


def dot_tn(left, right):
    return lax.dot_general(left, right, (((0,), (0,)), ((), ())), preferred_element_type=F32)


def normalize(values):
    average = jnp.mean(values, axis=-1, keepdims=True)
    centred = values - average
    variance = jnp.mean(centred * centred, axis=-1, keepdims=True)
    inverse_dev = lax.rsqrt(variance + EPSILON)
    return centred * inverse_dev, inverse_dev


def normalize_back(grad_normed, unit, inverse_dev, gain):
    grad_unit = grad_normed * gain
    first_mean = jnp.mean(grad_unit, axis=-1, keepdims=True)
    second_mean = jnp.mean(grad_unit * unit, axis=-1, keepdims=True)
    return inverse_dev * (grad_unit - first_mean - unit * second_mean)


class Plan:
    def __init__(self, mesh):
        self.n_rows = mesh.shape["rows"]
        self.n_seq = mesh.shape["seq"]
        rows = [("rows", 1 << i) for i in range(self.n_rows.bit_length() - 1)]
        seq = [("seq", 1 << i) for i in range(self.n_seq.bit_length() - 1)]
        kept = max(0, min(len(seq), SCATTER_BITS - len(rows)))
        self.seq_block = 1 << kept
        self.blocks = self.n_rows * self.seq_block
        core, others = rows[:1], rows[1:]
        low, high = seq[:1], seq[1:kept] if kept else []
        low = low[:kept]
        self.core = core[0]
        self.first = others + low
        self.second = low + others
        self.tail = high
        self.rest = seq[kept:]
        bits = [1 << i for i in range(len(seq))]
        self.key_order = bits[::-1]
        self.value_order = bits[:1] + bits[:0:-1]

    def mask(self, bit):
        axis, value = bit
        return value * self.seq_block if axis == "rows" else value

    def relative(self, order, position):
        result = 0
        for number, bit in enumerate(order):
            if position >> (len(order) - 1 - number) & 1:
                result |= self.mask(bit)
        return result

    def seq_relative(self, order, position):
        result = 0
        for number, bit in enumerate(order):
            if position >> number & 1:
                result |= bit
        return result

    def swap(self, array, bit):
        axis, value = bit
        size = self.n_rows if axis == "rows" else self.n_seq
        return lax.ppermute(array, axis, [(i, i ^ value) for i in range(size)])


def order_matrix(length, transposed):
    slots = length // 3
    rows = lax.broadcasted_iota(jnp.int32, (length, length), 1 if transposed else 0)
    columns = lax.broadcasted_iota(jnp.int32, (length, length), 0 if transposed else 1)
    tap = (rows >= slots).astype(jnp.int32) + (rows >= 2 * slots).astype(jnp.int32)
    return (columns == 3 * (rows - tap * slots) + tap).astype(BF16)


def window_masks(segment_column, slots):
    last = segment_column[2 * slots :]
    return [(segment_column[i * slots : (i + 1) * slots] == last).astype(F32) for i in range(3)]


def fetch_all(pairs, arrived):
    copies = [
        pltpu.make_async_copy(source, target, arrived.at[number])
        for number, (source, target) in enumerate(pairs)
    ]
    for copy in copies:
        copy.start()

    def ready(number):
        copies[number].wait()
        return pairs[number][1]

    return ready


class Order:
    def __init__(self):
        self.last = ()

    def call(
        self, kernel, name, outs, scratch=(), anywhere=(), out_anywhere=(), aliases=None,
        vmem=VMEM_SMALL, microseconds=0.3, token=0,
    ):
        def spec(number, places):
            return pl.BlockSpec(memory_space=pl.ANY if number in places else pltpu.VMEM)

        def run(*operands):
            count, last = len(operands), self.last

            def without_last(*refs):
                kernel(*refs[:count], *refs[count + len(last) :])

            operands = [
                pltpu.with_memory_space_constraint(operand, pltpu.HBM)
                if number in anywhere and not aliases
                else operand
                for number, operand in enumerate(operands)
            ]
            results = pl.pallas_call(
                without_last,
                name=name,
                out_shape=[
                    pltpu.HBM(shape, dtype)
                    if number in out_anywhere
                    else jax.ShapeDtypeStruct(shape, dtype)
                    for number, (shape, dtype) in enumerate(outs)
                ],
                in_specs=[spec(number, anywhere) for number in range(count)]
                + [pl.BlockSpec(memory_space=pl.ANY)] * len(last),
                out_specs=[spec(number, out_anywhere) for number in range(len(outs))],
                scratch_shapes=list(scratch),
                input_output_aliases=aliases or {},
                compiler_params=pltpu.CompilerParams(vmem_limit_bytes=vmem),
                cost_estimate=pl.CostEstimate(
                    flops=int(microseconds * 1_150_000_000), bytes_accessed=int(microseconds * BYTES_MICROSECOND), transcendentals=0
                ),
            )(*operands, *last)
            self.last = (results[token],)
            return results

        return run

    def combine(self, name, inputs, outs, microseconds=0.3):
        width = inputs[0].shape[1]

        def kernel(*refs):
            sources, targets = refs[: len(inputs)], refs[len(inputs) :]
            for target, pieces in zip(targets, outs):
                offset = 0
                for number, start, rows, *other in pieces:
                    part = sources[number][start : start + rows, :]
                    if other:
                        added = sources[other[0]][other[1] : other[1] + rows, :]
                        part = (part.astype(F32) + added.astype(F32)).astype(BF16)
                    target[offset : offset + rows, :] = part
                    offset += rows

        shapes = [((sum(piece[2] for piece in pieces), width), BF16) for pieces in outs]
        return self.call(kernel, name, shapes, microseconds=microseconds)(*inputs)


def own_places(plan):
    seq = lax.axis_index("seq")
    return seq, lax.axis_index("rows") * plan.seq_block + lax.rem(seq, plan.seq_block)


def read_segments(order, segments, batch):
    length = order.shape[0]
    rows = [segments[b].astype(F32) for b in range(batch)]
    rows = jnp.concatenate(rows + [jnp.zeros((EXTRA_ROWS - batch, length), F32)], axis=0)
    columns = dot_nt(order, rows.astype(BF16))
    return rows, [columns[:, b : b + 1] for b in range(batch)]


def project_kernel(
    tokens_far, gain_far, segments_far, w_query, w_key, w_value, conv_key, conv_value,
    x_out, normed_out, query_out, key_out, value_out, segment_out, packed_key, packed_value,
    query_here, key_here, value_here, conv_key_here, conv_value_here, tokens, gain, segments,
    arrived,
):
    ready = fetch_all(
        [
            (tokens_far, tokens), (segments_far, segments), (gain_far, gain), (w_key, key_here), (conv_key, conv_key_here), (w_value, value_here),
            (conv_value, conv_value_here), (w_query, query_here),
        ],
        arrived,
    )
    batch, _, length, width = tokens.shape
    slots = length // 3
    order = order_matrix(length, False)
    for number in range(3):
        ready(number)
    rows = [dot(order, tokens[b, 0]) for b in range(batch)]
    segment_rows, segment_columns = read_segments(order, segments, batch)
    x = jnp.concatenate(rows, axis=0)
    x_out[...] = x
    for b in range(batch):
        segment_out[b] = segment_columns[b]
    last = lax.broadcasted_iota(jnp.int32, (length, width), 0)
    slot = lax.broadcasted_iota(jnp.int32, (length, width), 1)
    extra = dot(segment_rows.astype(BF16), (last == 3 * slot + 2).astype(BF16)).astype(BF16)
    unit, _ = normalize(x)
    normed = (unit * gain[...].astype(F32).reshape(1, width)).astype(BF16)

    normed_out[...] = normed
    for number, flat_out, packed_out in ((3, key_out, packed_key), (5, value_out, packed_value)):
        flat = dot(normed, ready(number)[...]).astype(BF16)
        flat_out[...] = flat
        taps = [[], [], []]
        for b in range(batch):
            masks = window_masks(segment_columns[b], slots)
            for i in range(3):
                start = b * length + i * slots
                part = flat[start : start + slots].astype(F32) * masks[i]
                taps[i].append(part.astype(BF16))
        conv = ready(number + 1)
        total = None
        for i in range(3):
            term = dot(jnp.concatenate(taps[i], axis=0), conv[i * width : (i + 1) * width, :])
            total = term if total is None else total + term
        packed_out[0 : batch * slots, :] = total.astype(BF16)
    packed_key[batch * slots :, :] = extra
    query_out[...] = dot(normed, ready(7)[...]).astype(BF16)


def layer_kernel(
    plan, short,
    x_in, cotangent, query_in, key_in, value_in, segment_column, gain_ffn,
    keys_near, keys_far, values_near, values_far, w_out, w_up, w_down,
    layer_out, d_hidden_out, normed_ffn_out, activated_out, d_expanded_out, cotangent_out,
    attended_out, d_branch_out, d_query_out, d_key_own, d_value_own,
    d_key_keep, d_key_send, d_value_keep, d_value_send, gain_grad,
    all_keys, all_values, all_extra, bias, statistics, prob_keep, expanded_sum, d_normed_sum,
    d_attended, *copied,
):
    batch, _, length, width = cotangent.shape
    slots = length // 3
    n_seq = plan.n_seq
    half = n_seq // 2
    total_slots = slots * n_seq
    own_place = lax.axis_index("seq")
    key_position = {plan.seq_relative(plan.key_order, p): p for p in range(n_seq)}
    packed_rows = batch * slots
    payload = packed_rows + EXTRA_ROWS
    copies = []

    def put(source, start, rows, target, lanes=slice(None)):
        if short:
            target[...] = source[start : start + rows, lanes]
            return
        copies.append(
            pltpu.make_async_copy(
                source.at[pl.ds(start, rows), lanes], target, copied[0].at[len(copies)]
            )
        )
        copies[-1].start()

    for p in range(n_seq):
        keys, values = (keys_near, values_near) if p < half else (keys_far, values_far)
        place = p % half
        q = key_position[plan.seq_relative(plan.value_order, p)]
        put(
            keys, place * payload + packed_rows, EXTRA_ROWS, all_extra.at[p], slice(0, LANES)
        )
        for b in range(batch):
            put(
                keys, place * payload + b * slots, slots,
                all_keys.at[b, pl.ds(p * slots, slots), :],
            )
            put(
                values, place * packed_rows + b * slots, slots,
                all_values.at[b, pl.ds(q * slots, slots), :],
            )
    for copy in copies:
        copy.wait()

    segment_rows = jnp.zeros((EXTRA_ROWS, total_slots), F32)
    slot_lane = lax.broadcasted_iota(jnp.int32, (1, total_slots), 1)
    slot_end = jnp.zeros((1, total_slots), jnp.int32)
    select_row = lax.broadcasted_iota(jnp.int32, (LANES, total_slots), 0)
    select_lane = lax.broadcasted_iota(jnp.int32, (LANES, total_slots), 1)
    for p in range(n_seq):
        selected = (select_lane == select_row + p * slots) & (select_row < slots)
        segment_rows += dot(all_extra[p], selected.astype(BF16))
        owner = plan.seq_relative(plan.key_order, p) ^ own_place
        here = (slot_lane >= p * slots) & (slot_lane < (p + 1) * slots)
        slot_end = jnp.where(here, length * owner - length * p + 3 * slot_lane + 2, slot_end)
    row = lax.broadcasted_iota(jnp.int32, (length, 1), 0)
    tap = (row >= slots).astype(jnp.int32) + (row >= 2 * slots).astype(jnp.int32)
    query_place = length * own_place + 3 * (row - tap * slots) + tap
    causal = slot_end <= query_place
    for b in range(batch):
        matching = segment_rows[b : b + 1, :] == segment_column[b]
        bias[b] = jnp.where(causal & matching, 0.0, MASKED_OUT)

    low_lane = lax.broadcasted_iota(jnp.int32, (length, LANES), 1) < HEAD_DIM

    def stacked(part):
        zero = jnp.zeros_like(part)
        return jnp.concatenate(
            [jnp.where(low_lane, part, zero), jnp.where(low_lane, zero, part)], axis=0
        )

    def twice(part):
        return jnp.concatenate([part, part], axis=0)

    def merged(part):
        return jnp.where(low_lane, part[:length], part[length:])

    def lanes_of(g):
        return pl.ds(pl.multiple_of(g * LANES, LANES), LANES)

    def place_of(number):
        b, g = number // GROUPS, number % GROUPS
        if short:
            return b, slice(b * length, (b + 1) * length), slice(g * LANES, (g + 1) * LANES)
        return b, pl.ds(pl.multiple_of(b * length, 16), length), lanes_of(g)

    def each(step):
        if short:
            for number in range(batch * GROUPS):
                step(number)
        else:
            lax.fori_loop(0, batch * GROUPS, lambda number, carry: (step(number), carry)[1], 0)

    def scaled_queries(rows, lanes):
        part = query_in[rows, lanes].astype(F32) * SCALE
        return stacked(part).astype(BF16)

    def attend(number):
        b, rows, lanes = place_of(number)
        queries = scaled_queries(rows, lanes)
        own_key = twice(key_in[rows, lanes].astype(F32))
        scores = dot_nt(queries, all_keys[b, :, lanes]) + twice(bias[b])
        own_score = jnp.sum(queries.astype(F32) * own_key, axis=-1, keepdims=True)
        top = jnp.maximum(own_score, jnp.max(scores, axis=-1, keepdims=True))
        raised = jnp.exp(scores - top)
        own_raised = jnp.exp(own_score - top)
        inverse = 1.0 / (own_raised + jnp.sum(raised, axis=-1, keepdims=True))
        prob = raised * inverse
        own_prob = own_raised * inverse
        if short:
            prob_keep[number] = prob
        statistics[number, :, 0:1] = own_prob
        statistics[number, :, 1:2] = top - jnp.log(inverse)
        result = dot(prob.astype(BF16), all_values[b, :, lanes])
        own_value = twice(value_in[rows, lanes].astype(F32))
        result += own_prob.astype(BF16).astype(F32) * own_value
        attended_out[rows, lanes] = merged(result).astype(BF16)

    each(attend)

    x = x_in[...]
    hidden = x + dot(attended_out[...], w_out[...])
    unit, inverse_dev = normalize(hidden)
    gain = gain_ffn[...].astype(F32).reshape(1, width)
    normed_ffn_out[...] = (unit * gain).astype(BF16)
    order = order_matrix(length, False)
    for b in range(batch):
        cotangent_out[b * length : (b + 1) * length, :] = dot(order, cotangent[b, 0]).astype(BF16)
    expanded_sum[...] = hidden
    d_normed_sum[...] = jnp.zeros_like(d_normed_sum)
    chunk = width
    total_width = w_up.shape[1]

    def feed(number, carry):
        columns = pl.ds(pl.multiple_of(number * chunk, chunk), chunk)
        expanded = dot(normed_ffn_out[...], w_up[:, columns])
        square = expanded * expanded
        curve = jnp.tanh(GELU_SCALE * expanded * (1.0 + GELU_CUBIC * square))
        activated = (0.5 * expanded * (1.0 + curve)).astype(BF16)
        activated_out[:, columns] = activated
        slope = 0.5 * (1.0 + curve) + 0.5 * expanded * (1.0 - curve * curve) * (
            GELU_SCALE * (1.0 + 3.0 * GELU_CUBIC * square)
        )
        expanded_sum[...] += dot(activated, w_down[columns, :])
        d_activated = dot_nt(cotangent_out[...], w_down[columns, :])
        d_expanded = (d_activated * slope).astype(BF16)
        d_expanded_out[:, columns] = d_expanded
        d_normed_sum[...] += dot_nt(d_expanded, w_up[:, columns])
        return carry

    lax.fori_loop(0, total_width // chunk, feed, 0, unroll=True)

    unorder = order_matrix(length, True)
    for b in range(batch):
        part = expanded_sum[b * length : (b + 1) * length, :].astype(BF16)
        layer_out[b, 0] = dot(unorder, part).astype(BF16)
    d_normed = d_normed_sum[...]
    gain_grad[...] = jnp.sum(d_normed * unit, axis=0, keepdims=True)
    d_hidden = cotangent_out[...].astype(F32) + normalize_back(d_normed, unit, inverse_dev, gain)
    d_hidden_out[...] = d_hidden
    d_branch = d_hidden.astype(BF16)
    d_branch_out[...] = d_branch
    d_attended[...] = dot_nt(d_branch, w_out[...]).astype(BF16)

    value_spot = [key_position[plan.seq_relative(plan.value_order, p)] for p in range(n_seq)]

    def attend_back(number):
        b, rows, lanes = place_of(number)
        queries = scaled_queries(rows, lanes)
        own_prob = statistics[number, :, 0:1]
        if short:
            prob = prob_keep[number]
        else:
            scores = dot_nt(queries, all_keys[b, :, lanes]) + twice(bias[b])
            prob = jnp.exp(scores - statistics[number, :, 1:2])
        grads = stacked(d_attended[rows, lanes])
        own_value = twice(value_in[rows, lanes].astype(F32))
        own_key = twice(key_in[rows, lanes].astype(F32))
        prob_grad = dot_nt(grads, all_values[b, :, lanes])
        own_prob_grad = jnp.sum(grads.astype(F32) * own_value, axis=-1, keepdims=True)
        delta = own_prob * own_prob_grad + jnp.sum(prob * prob_grad, axis=-1, keepdims=True)
        d_score = (prob * (prob_grad - delta)).astype(BF16)
        d_own = (own_prob * (own_prob_grad - delta)).astype(BF16).astype(F32)
        own_low = own_prob.astype(BF16).astype(F32)
        d_query = merged(dot(d_score, all_keys[b, :, lanes]) + d_own * own_key) * SCALE
        d_query_out[rows, lanes] = d_query.astype(BF16)
        d_key_own[rows, lanes] = merged(d_own * queries.astype(F32))
        d_value_own[rows, lanes] = merged(own_low * grads.astype(F32))
        key_sums = dot_tn(d_score, queries).astype(BF16)
        value_sums = dot_tn(prob.astype(BF16), grads).astype(BF16)
        for p in range(n_seq):
            spot = pl.ds(p % half * packed_rows + b * slots, slots)
            key_target, value_target = (
                (d_key_keep, d_value_keep) if p < half else (d_key_send, d_value_send)
            )
            key_target[spot, lanes] = key_sums[p * slots : (p + 1) * slots]
            q = value_spot[p]
            value_target[spot, lanes] = value_sums[q * slots : (q + 1) * slots]

    each(attend_back)


def spread(plan, place, order, parts, send, keep):
    half = plan.blocks // 2
    for target, core in ((send, 1), (keep, 0)):
        start = 0
        for p in range(half):
            block = plan.relative(order, core * half + p) ^ place
            for source, rows in parts:
                target[start : start + rows, :] = source[
                    pl.ds(pl.multiple_of(block * rows, 16), rows), :
                ]
                start += rows


def down_grad_kernel(
    plan, order, activated, cotangent, attended, d_branch, send, keep, down_rows, out_rows
):
    width = cotangent.shape[1]
    wide = activated.shape[1]
    for c in range(wide // width):
        columns = slice(c * width, (c + 1) * width)
        down_rows[columns, :] = dot_tn(activated[:, columns], cotangent[...]).astype(BF16)
    out_rows[...] = dot_tn(attended[...], d_branch[...]).astype(BF16)
    _, mine = own_places(plan)
    parts = ((down_rows, wide // plan.blocks), (out_rows, width // plan.blocks))
    spread(plan, mine, order, parts, send, keep)


def up_grad_kernel(
    plan, order, normed_ffn, d_expanded, normed, d_query, send, keep, up_rows, query_rows
):
    width = normed_ffn.shape[1]
    chunks = d_expanded.shape[1] // width
    for c in range(chunks):
        columns = slice(c * width, (c + 1) * width)
        up_rows[c] = dot_tn(normed_ffn[...], d_expanded[:, columns]).astype(BF16)
    query_rows[...] = dot_tn(normed[...], d_query[...]).astype(BF16)
    _, mine = own_places(plan)
    thin = width // plan.blocks
    parts = tuple((up_rows.at[c], thin) for c in range(chunks)) + ((query_rows, thin),)
    spread(plan, mine, order, parts, send, keep)


def conv_grads(
    plan, order, segment_column, d_packed, flat, own, conv, normed, conv_rows, flat_rows, send, keep
):
    batch, length, _ = segment_column.shape
    width = conv.shape[1]
    slots = length // 3
    masks = [window_masks(segment_column[b], slots) for b in range(batch)]
    back = d_packed[...]
    pieces = [[None] * 3 for _ in range(batch)]
    for i in range(3):
        taps = []
        from_tap = dot_nt(back, conv[i * width : (i + 1) * width, :])
        for b in range(batch):
            start = b * length + i * slots
            part = flat[start : start + slots, :].astype(F32) * masks[b][i]
            taps.append(part.astype(BF16))
            pieces[b][i] = from_tap[b * slots : (b + 1) * slots] * masks[b][i]
        window = jnp.concatenate(taps, axis=0)
        conv_rows[i * width : (i + 1) * width, :] = dot_tn(window, back).astype(BF16)
    whole = jnp.concatenate([piece for row in pieces for piece in row], axis=0)
    d_flat = (whole + own[...]).astype(BF16)
    flat_rows[...] = dot_tn(normed[...], d_flat).astype(BF16)
    _, mine = own_places(plan)
    parts = ((conv_rows, 3 * width // plan.blocks), (flat_rows, width // plan.blocks))
    spread(plan, mine, order, parts, send, keep)
    return d_flat


def key_grad_kernel(
    plan, order, segment_column, d_packed, flat, own, conv, normed,
    send, keep, d_flat_out, conv_rows, flat_rows,
):
    d_flat_out[...] = conv_grads(
        plan, order, segment_column, d_packed, flat, own, conv, normed, conv_rows, flat_rows,
        send, keep,
    )


def value_grad_kernel(
    plan, order, segment_column, d_packed, flat, own, conv, normed,
    x_in, gain, d_query, d_keys, d_hidden, gain_ffn_grad, w_query, w_key, w_value,
    send, keep, grad_tokens, conv_rows, flat_rows,
):
    batch, _, length, width = grad_tokens.shape
    d_values = conv_grads(
        plan, order, segment_column, d_packed, flat, own, conv, normed, conv_rows, flat_rows,
        send, keep,
    )
    d_normed = (
        dot_nt(d_query[...], w_query[...])
        + dot_nt(d_keys[...], w_key[...])
        + dot_nt(d_values, w_value[...])
    )
    unit, inverse_dev = normalize(x_in[...])
    gain_grad = jnp.sum(d_normed * unit, axis=0, keepdims=True)
    d_input = normalize_back(d_normed, unit, inverse_dev, gain[...].astype(F32).reshape(1, width))
    result = (d_hidden[...] + d_input).astype(BF16)
    unorder = order_matrix(length, True)
    for b in range(batch):
        part = result[b * length : (b + 1) * length, :]
        grad_tokens[b, 0] = dot(unorder, part).astype(BF16)
    row = lax.broadcasted_iota(jnp.int32, (EXTRA_ROWS, width), 0)
    gains = jnp.where(row == 0, gain_grad, jnp.where(row == 1, gain_ffn_grad[...], 0.0))
    send[send.shape[0] - EXTRA_ROWS :, :] = gains.astype(BF16)
    keep[keep.shape[0] - EXTRA_ROWS :, :] = gains.astype(BF16)


def finish_kernel(plan, layout, parts, core, count, *refs):
    blocks, refs = refs[0], refs[1 + core * count :]
    targets, (token, stage, sent) = refs[:count], refs[count:]
    token[...] = jnp.zeros_like(token)
    _, mine = own_places(plan)
    half = plan.blocks // 2
    copies = []
    start = 0
    for p in range(half):
        block = plan.relative(layout, core * half + p) ^ mine
        for rows, target, columns in parts:
            stage[start : start + rows, :] = blocks[start : start + rows, :].astype(F32)
            spot = pl.ds(pl.multiple_of(block * rows, 16), rows)
            copy = pltpu.make_async_copy(
                stage.at[pl.ds(start, rows), :],
                targets[target].at[spot, columns],
                sent.at[len(copies)],
            )
            copy.start()
            copies.append(copy)
            start += rows
    for copy in copies:
        copy.wait()


class RowGather:
    def __init__(self, plan, order, array, bits):
        self.plan, self.order, self.held, self.bits = plan, order, array, list(bits)

    def step(self):
        arrived = self.plan.swap(self.held, ("seq", self.bits.pop(0)))
        if not self.bits:
            return [self.held, arrived]
        rows = self.held.shape[0]
        self.held, = self.order.combine(
            "gather_row", [self.held, arrived], [[(0, 0, rows), (1, 0, rows)]]
        )


class RowScatter:
    def __init__(self, plan, order, keep, send, bits):
        self.plan, self.order, self.keep, self.send = plan, order, keep, send
        self.bits = list(bits)

    def step(self):
        if not self.bits:
            return
        arrived = self.plan.swap(self.send, ("seq", self.bits.pop()))
        rows = self.keep.shape[0]
        half = rows // 2
        outs = [(0, rows)] if not self.bits else [(0, half), (half, half)]
        self.keep, *send = self.order.combine(
            "scatter_row", [self.keep, arrived], [[(0, start, size, 1, start)] for start, size in outs]
        )
        self.send = send[0] if send else None


class Part:
    def __init__(self, plan, order, bits, send, keep, shapes, parts, extra=0):
        self.plan, self.order, self.bits, self.extra = plan, order, bits, extra
        self.send, self.keep = send, keep
        self.shapes, self.parts = shapes, parts
        self.done = 0

    def step(self):
        if self.done < len(self.bits):
            self.scatter(self.bits[self.done])
        else:
            self.gather(self.bits[2 * len(self.bits) - 1 - self.done])
        self.done += 1

    def scatter(self, bit):
        arrived = self.plan.swap(self.send, bit)
        extra = self.extra
        rows = self.keep.shape[0] - extra
        last = [(0, rows, extra, 1, rows)]
        if self.done < len(self.bits) - 1:
            half = rows // 2
            outs = [[(0, start, half, 1, start)] + (last if extra else []) for start in (0, half)]
            self.keep, self.send = self.order.combine("scatter", [self.keep, arrived], outs)
            return
        outs = [[(0, 0, rows, 1, 0)]] + ([last] if extra else [])
        self.held, *self.sums = self.order.combine("scatter", [self.keep, arrived], outs)
        for bit in self.plan.rest:
            arrays = [self.held] + self.sums
            arrived = [self.plan.swap(array, bit) for array in arrays]
            self.held, *self.sums = self.order.combine(
                "scatter_rest", arrays + arrived,
                [
                    [(i, 0, array.shape[0], i + len(arrays), 0)]
                    for i, array in enumerate(arrays)
                ],
            )

    def gather(self, bit):
        arrived = self.plan.swap(self.held, bit)
        if bit == self.plan.core:
            self.far = arrived
            return
        rows = self.held.shape[0]
        self.held, = self.order.combine(
            "gather", [self.held, arrived], [[(0, 0, rows), (1, 0, rows)]]
        )

    def finish(self, core, *targets):
        if core:
            self.gather(self.plan.core)
        blocks = self.far if core else self.held
        count = len(self.shapes)
        everywhere = tuple(range(count))
        copies = self.plan.blocks // 2 * len(self.parts)
        return self.order.call(
            functools.partial(finish_kernel, self.plan, self.bits, self.parts, core, count),
            "finish",
            [(shape, F32) for shape in self.shapes] + [((8, LANES), F32)],
            [pltpu.VMEM(blocks.shape, F32), pltpu.SemaphoreType.DMA((copies,))],
            anywhere=tuple(range(1, count + 1)) if core else (),
            out_anywhere=everywhere,
            aliases={1 + number: number for number in everywhere} if core else None,
            token=count,
        )(blocks, *targets)[:count]


def body(
    plan, tokens, segments, cotangent, gain_attn, w_query, w_key, w_value, conv_key, conv_value,
    w_out, gain_ffn, w_up, w_down,
):
    batch, _, length, width = tokens.shape
    slots = length // 3
    square = (width, width)
    positions = batch * length
    flat, flat32 = ((positions, width), BF16), ((positions, width), F32)
    square_here = pltpu.VMEM(square, BF16)
    conv_here = pltpu.VMEM(conv_key.shape, BF16)
    order = Order()
    x, normed, queries, key_rows, value_rows, segment_column, packed_key, packed_value = order.call(
        project_kernel,
        "project",
        [flat32] + [flat] * 4 + [((batch, length, 1), F32)]
        + [((batch * slots + EXTRA_ROWS, width), BF16), ((batch * slots, width), BF16)],
        scratch=[square_here] * 3 + [conv_here] * 2
        + [
            pltpu.VMEM(tokens.shape, BF16), pltpu.VMEM(gain_attn.shape, BF16),
            pltpu.VMEM(segments.shape, jnp.int32), pltpu.SemaphoreType.DMA((8,)),
        ],
        anywhere=tuple(range(8)),
        token=5,
    )(tokens, gain_attn, segments, w_query, w_key, w_value, conv_key, conv_value)

    steps = len(plan.key_order)
    keys = RowGather(plan, order, packed_key, plan.key_order)
    values = RowGather(plan, order, packed_value, plan.value_order)
    for number in range(steps - 1):
        for gather in (values, keys) if number == 0 else (keys, values):
            gather.step()

    total_slots = slots * plan.n_seq
    short = total_slots <= SHORT_ROW
    wide = ((positions, w_up.shape[1]), BF16)
    half_packed = ((batch * total_slots // 2, width), BF16)
    copied = [] if short else [pltpu.SemaphoreType.DMA((plan.n_seq * (1 + 2 * batch),))]
    (
        layer_out, d_hidden, normed_ffn, activated, d_expanded, cotangent_rows, attended, d_branch,
        d_query, d_key_own, d_value_own, *d_packed, gain_ffn_grad,
    ) = order.call(
        functools.partial(layer_kernel, plan, short),
        "layer",
        [(tokens.shape, BF16), flat32, flat, wide, wide, flat, flat, flat]
        + [flat, flat32, flat32] + [half_packed] * 4 + [((1, width), F32)],
        scratch=[
            pltpu.VMEM((batch, total_slots, width), BF16),
            pltpu.VMEM((batch, total_slots, width), BF16),
            pltpu.VMEM((plan.n_seq, EXTRA_ROWS, LANES), BF16),
            pltpu.VMEM((batch, length, total_slots), F32),
            pltpu.VMEM((batch * GROUPS, 2 * length, LANES), F32),
            pltpu.VMEM((batch * GROUPS if short else 1, 2 * length, total_slots), F32),
            pltpu.VMEM((positions, width), F32),
            pltpu.VMEM((positions, width), F32),
            pltpu.VMEM((positions, width), BF16),
        ]
        + copied,
        anywhere=() if short else (7, 8, 9, 10),
        vmem=VMEM_SMALL if short else VMEM_LARGE,
        token=-1,
    )(
        x, cotangent, queries, key_rows, value_rows, segment_column, gain_ffn,
        *keys.step(), *values.step(), w_out, w_up, w_down,
    )
    rows = [
        RowScatter(plan, order, d_packed[0], d_packed[1], plan.key_order),
        RowScatter(plan, order, d_packed[2], d_packed[3], plan.value_order),
    ]

    core = [plan.core]
    x_first, y_first = core + plan.first + plan.tail, core + plan.second + plan.tail
    bits = {"A0": y_first, "A1": x_first, "B0": y_first, "B1": x_first}
    half = plan.blocks // 2
    thin, down_block, conv_block = (
        rows // plan.blocks for rows in (width, w_down.shape[0], conv_key.shape[0])
    )
    chunks = w_up.shape[1] // width
    everything = slice(None)
    ups = [(thin, 0, slice(c * width, (c + 1) * width)) for c in range(chunks)]
    layouts = {
        "A0": ([w_down.shape, square], [(down_block, 0, everything), (thin, 1, everything)]),
        "A1": ([w_up.shape, square], ups + [(thin, 1, everything)]),
        "B0": ([conv_key.shape, square], [(conv_block, 0, everything), (thin, 1, everything)]),
        "B1": ([conv_value.shape, square], [(conv_block, 0, everything), (thin, 1, everything)]),
    }
    chains, results = {"K": rows[0], "V": rows[1]}, {}

    def make(name, kernel, outs, scratch, operands, extra=0):
        shapes, parts = layouts[name]
        total = half * sum(part[0] for part in parts) + extra
        send, keep, *others = order.call(
            functools.partial(kernel, plan, bits[name]),
            kernel.__name__,
            [((total, width), BF16)] * 2 + outs,
            scratch=scratch,
        )(*operands)
        chains[name] = Part(plan, order, bits[name], send, keep, shapes, parts, extra)
        return others

    wide_here = pltpu.VMEM(w_down.shape, BF16)
    for event in EVENTS:
        if event == "Wa":
            make(
                "A0", down_grad_kernel, [], [wide_here, square_here],
                (activated, cotangent_rows, attended, d_branch),
            )
        elif event == "Wb":
            make(
                "A1", up_grad_kernel, [],
                [pltpu.VMEM((chunks, width, width), BF16), square_here],
                (normed_ffn, d_expanded, normed, d_query),
            )
        elif event == "TK":
            while rows[0].bits:
                rows[0].step()
            d_keys, = make(
                "B0", key_grad_kernel, [flat], [conv_here, square_here],
                (segment_column, rows[0].keep, key_rows, d_key_own, conv_key, normed),
            )
        elif event == "TV":
            while rows[1].bits:
                rows[1].step()
            grad_tokens, = make(
                "B1", value_grad_kernel, [(tokens.shape, BF16)], [conv_here, square_here],
                (
                    segment_column, rows[1].keep, value_rows, d_value_own, conv_value, normed,
                    x, gain_attn, d_query, d_keys, d_hidden, gain_ffn_grad,
                    w_query, w_key, w_value,
                ),
                EXTRA_ROWS,
            )
        elif event[2:] == "n":
            results[event[:2]] = chains[event[:2]].finish(0)
        elif event[2:] == "f":
            results[event[:2]] = chains[event[:2]].finish(1, *results[event[:2]])
        else:
            chains[event].step()
    grad_down, grad_out = results["A0"]
    grad_up, grad_query = results["A1"]
    grad_conv_key, grad_key = results["B0"]
    grad_conv_value, grad_value = results["B1"]
    gains = chains["B1"].sums[0].astype(F32)
    return (
        layer_out, grad_tokens, gains[0], grad_query, grad_key, grad_value,
        grad_conv_key, grad_conv_value, grad_out, gains[1], grad_up, grad_down,
    )


def solution(mesh):
    packed = P(None, "rows", "seq", None)
    in_specs = (packed, P(None, "rows", "seq"), packed) + (P(),) * 10
    out_specs = (packed, packed) + (P(),) * 10
    return jax.shard_map(
        functools.partial(body, Plan(mesh)),
        mesh=mesh, in_specs=in_specs, out_specs=out_specs, check_vma=False,
    )
```

time: 277 us -> 200 us (0.72)
  waiting for transfers between devices: 150 us -> 96.3 us
  Pallas kernels: 58.4 us -> 43.2 us
  other arithmetic: 12.2 us -> 0 us
  starting transfers between devices: 46 us -> 57.5 us
  local copies, waits for them, and re-layouts: 8.42 us -> 1.11 us
    ppermute x40 -> x52, waiting for transfers between devices: 150 us -> 96.3 us  [swap(): return lax.ppermute(array, axis, [(i, i ^ value) for i in range(size)])]
    pallas_call x6 -> x60, Pallas kernels: 58.4 us -> 43.2 us  [run(): pl.pallas_call(without_last, name=name, out_shape=[pltpu.HBM(shape, dtype...]
    ppermute x40 -> x52, starting transfers between devices: 46 us -> 57.5 us  [swap(): return lax.ppermute(array, axis, [(i, i ^ value) for i in range(size)])]
    convert_element_type x19 -> x0, other arithmetic: 5.43 us -> none  [the longest x18 4.73 us: add(): return (left.astype(F32) + right.astype(F32)).astype(BF16)]
    concatenate x20 -> x0, other arithmetic: 4.1 us -> none  [the longest x4 3.71 us: gather_row(): held = jnp.concatenate([held, arrived], axis=0)]
  transfers between devices with their start and end apart: 40 -> 52, of which waited for: 26 -> 29; matrix products, arithmetic and copies ran while one was open for 4% -> 0% of each run, Pallas kernels for 6% -> 11%
where the time goes in v3:
time: 200 us
  waiting for transfers between devices  96.3 us (48%)
  starting transfers between devices  57.5 us (29%)
  Pallas kernels  43.2 us (22%)
    ppermute x52, waiting for transfers between devices, swap(): return lax.ppermute(array, axis, [(i, i ^ value) for i in range(size)])  96.3 us
    ppermute x52, starting transfers between devices, swap(): return lax.ppermute(array, axis, [(i, i ^ value) for i in range(size)])  57.5 us
    pallas_call x60, Pallas kernels, run(): pl.pallas_call(without_last, name=name, out_shape=[pltpu.HBM(shape, dtype...  43.2 us
  transfers between devices with their start and end apart: 52, of which 29 were waited for; matrix products, arithmetic and copies ran while one was open for 0% of the time, Pallas kernels for 11%

profile of v3, /device:TPU:0, one launch (start us, length us, event | category | flops | bytes accessed | tf_op | source)
XLA Modules:
  0.0 199.6 jit_solution(847783114367404547)
XLA Ops:
  0.6 3.3 %project.1 = (f32[288,512]{1,0:T(8,128)S(1)}, bf16[288,512]{1,0:T(8,128)(2,1)S(1)}, bf16[288,512]{1,0:T(8,128)(2,1)S(1)}, bf16[288,512]{1,0:T(8,128)(2,1)S(1)}, ...) custom-call(bf16[2,1,144,512]{3,2,1,0:T(8,128)(2,1)} %refs_0_.1, ...), custom_call_target="tpu_custom_call" | custom-call | flops 345000000 | bytes 1107000 | tf_op jit(solution)/shard_map/project/pallas_call | solution.py:160
  4.0 3.0 %collective-permute-start.1 = (bf16[96,512]{1,0:T(8,128)(2,1)S(1)}, bf16[96,512]{1,0:T(8,128)(2,1)S(1)}, u32[]{:S(2)}, u32[]{:S(2)}) collective-permute-start(bf16[96,512]{1,0:T(8,128)(2,1)S(1)} %get-tuple-element.117.refs_0_), channel_id=1, source_target_pairs={{0,1},{1,0},{2,3},{3,2},{4,5},{5,4},{6,7},{7,6},{8,9},{9,8},{10,11... | collective-permute-start | bytes 294920 | tf_op jit(solution)/shard_map/ppermute | solution.py:106
  7.0 2.6 %collective-permute-start = (bf16[112,512]{1,0:T(8,128)(2,1)S(1)}, bf16[112,512]{1,0:T(8,128)(2,1)S(1)}, u32[]{:S(2)}, u32[]{:S(2)}) collective-permute-start(bf16[112,512]{1,0:T(8,128)(2,1)S(1)} %get-tuple-element.116.refs_0_), channel_id=1, source_target_pairs={{0,4},{1,5},{2,6},{3,7},{4,0},{5,1},{6,2},{7,3},{8,12},{9,13},{10,... | collective-permute-start | bytes 344072 | tf_op jit(solution)/shard_map/ppermute | solution.py:106
  9.8 5.1 %collective-permute-done.refs_1_ = bf16[112,512]{1,0:T(8,128)(2,1)S(1)} collective-permute-done((bf16[112,512]{1,0:T(8,128)(2,1)S(1)}, bf16[112,512]{1,0:T(8,128)(2,1)S(1)}, u32[]{:S(2)}, u32[]{:S(2)}) %collective-permute-start) | collective-permute-done | bytes 114720 | tf_op jit(solution)/shard_map/ppermute | solution.py:106
  15.8 3.4 %collective-permute-start.4 = (bf16[192,512]{1,0:T(8,128)(2,1)S(1)}, bf16[192,512]{1,0:T(8,128)(2,1)S(1)}, u32[]{:S(2)}, u32[]{:S(2)}) collective-permute-start(bf16[192,512]{1,0:T(8,128)(2,1)S(1)} %gather_row.4.refs_2_.refs_0_), channel_id=1, source_target_pairs={{0,4},{1,5},{2,6},{3,7},{4,0},{5,1},{6,2},{7,3},{8,12},{9,13},{10,... | collective-permute-start | bytes 589832 | tf_op jit(solution)/shard_map/ppermute | solution.py:106
  19.2 6.6 %collective-permute-done.2.refs_1_ = bf16[224,512]{1,0:T(8,128)(2,1)S(1)} collective-permute-done((bf16[224,512]{1,0:T(8,128)(2,1)S(1)}, bf16[224,512]{1,0:T(8,128)(2,1)S(1)}, u32[]{:S(2)}, u32[]{:S(2)}) %collective-permute-start.2) | collective-permute-done | bytes 229408 | tf_op jit(solution)/shard_map/ppermute | solution.py:106
  26.4 2.8 %collective-permute-start.5 = (bf16[384,512]{1,0:T(8,128)(2,1)S(1)}, bf16[384,512]{1,0:T(8,128)(2,1)S(1)}, u32[]{:S(2)}, u32[]{:S(2)}) collective-permute-start(bf16[384,512]{1,0:T(8,128)(2,1)S(1)} %gather_row.7.refs_9_.refs_14_), channel_id=1, source_target_pairs={{0,2},{1,3},{2,0},{3,1},{4,6},{5,7},{6,4},{7,5},{8,10},{9,11},{10,... | collective-permute-start | bytes 1179656 | tf_op jit(solution)/shard_map/ppermute | solution.py:106
  29.2 8.7 %collective-permute-done.5.refs_10_ = bf16[384,512]{1,0:T(8,128)(2,1)S(1)} collective-permute-done((bf16[384,512]{1,0:T(8,128)(2,1)S(1)}, bf16[384,512]{1,0:T(8,128)(2,1)S(1)}, u32[]{:S(2)}, u32[]{:S(2)}) %collective-permute-start.5) | collective-permute-done | bytes 393248 | tf_op jit(solution)/shard_map/ppermute | solution.py:106
  37.9 14.0 %layer.1 = (bf16[2,1,144,512]{3,2,1,0:T(8,128)(2,1)}, f32[288,512]{1,0:T(8,128)S(1)}, bf16[288,512]{1,0:T(8,128)(2,1)S(1)}, bf16[288,2048]{1,0:T(8,128)(2,1)S(1)...) custom-call(f32[288,512]{1,0:T(8,128)S(1)} %get-tuple-element.111.re, ...), custom_call_target="tpu_custom_call" | custom-call | flops 345000000 | bytes 1107000 | tf_op jit(solution)/shard_map/layer/pallas_call | solution.py:160
  51.9 1.8 up_grad_kernel.1
  53.7 1.8 down_grad_kernel.1
  59.1 1.7 collective-permute-start.6
  61.1 1.6 collective-permute-start.15
  62.7 7.9 %collective-permute-done.7.refs_1_ = bf16[384,512]{1,0:T(8,128)(2,1)S(1)} collective-permute-done((bf16[384,512]{1,0:T(8,128)(2,1)S(1)}, bf16[384,512]{1,0:T(8,128)(2,1)S(1)}, u32[]{:S(2)}, u32[]{:S(2)}) %collective-permute-start.7) | collective-permute-done | bytes 393248 | tf_op jit(solution)/shard_map/ppermute | solution.py:106
  70.7 1.8 collective-permute-start.12
  72.6 1.9 collective-permute-start.10
  74.4 3.3 %collective-permute-done.12.refs_1_ = bf16[192,512]{1,0:T(8,128)(2,1)S(1)} collective-permute-done((bf16[192,512]{1,0:T(8,128)(2,1)S(1)}, bf16[192,512]{1,0:T(8,128)(2,1)S(1)}, u32[]{:S(2)}, u32[]{:S(2)}) %collective-permute-start.12) | collective-permute-done | bytes 196640 | tf_op jit(solution)/shard_map/ppermute | solution.py:106
  77.8 2.5 %collective-permute-start.14 = (bf16[96,512]{1,0:T(8,128)(2,1)S(1)}, bf16[96,512]{1,0:T(8,128)(2,1)S(1)}, u32[]{:S(2)}, u32[]{:S(2)}) collective-permute-start(bf16[96,512]{1,0:T(8,128)(2,1)S(1)} %get-tuple-element.147), channel_id=1, source_target_pairs={{0,4},{1,5},{2,6},{3,7},{4,0},{5,1},{6,2},{7,3},{8,12},{9,13},{10,... | collective-permute-start | bytes 294920 | tf_op jit(solution)/shard_map/ppermute | solution.py:106
  80.5 4.8 %collective-permute-done.10.refs_1_ = bf16[192,512]{1,0:T(8,128)(2,1)S(1)} collective-permute-done((bf16[192,512]{1,0:T(8,128)(2,1)S(1)}, bf16[192,512]{1,0:T(8,128)(2,1)S(1)}, u32[]{:S(2)}, u32[]{:S(2)}) %collective-permute-start.10) | collective-permute-done | bytes 196640 | tf_op jit(solution)/shard_map/ppermute | solution.py:106
  88.4 1.7 collective-permute-done.13.refs_1_
  90.1 3.0 %value_grad_kernel.1 = (bf16[1040,512]{1,0:T(8,128)(2,1)S(1)}, bf16[1040,512]{1,0:T(8,128)(2,1)S(1)}, bf16[2,1,144,512]{3,2,1,0:T(8,128)(2,1)}) custom-call(f32[2,144,1]{2,1,0:T(8,128)S(1)} %get-tuple-element.115.refs_2_.refs_5_.refs_0_, bf16[96,512]{1,0:T(8,128)(2,1)S(1)} %scatter_row.11.refs_1_.refs_15_, ...), custom_call_target="tpu_custom_call" | custom-call | flops 345000000 | bytes 1107000 | tf_op jit(solution)/shard_map/value_grad_kernel/pallas_call | solution.py:160
  95.0 8.2 %collective-permute-done.19.refs_1_ = bf16[320,512]{1,0:T(8,128)(2,1)S(1)} collective-permute-done((bf16[320,512]{1,0:T(8,128)(2,1)S(1)}, bf16[320,512]{1,0:T(8,128)(2,1)S(1)}, u32[]{:S(2)}, u32[]{:S(2)}) %collective-permute-start.19) | collective-permute-done | bytes 327712 | tf_op jit(solution)/shard_map/ppermute | solution.py:106
  105.9 2.0 %collective-permute-start.22 = (bf16[160,512]{1,0:T(8,128)(2,1)S(1)}, bf16[160,512]{1,0:T(8,128)(2,1)S(1)}, u32[]{:S(2)}, u32[]{:S(2)}) collective-permute-start(bf16[160,512]{1,0:T(8,128)(2,1)S(1)} %get-tuple-element.167), channel_id=1, source_target_pairs={{0,2},{1,3},{2,0},{3,1},{4,6},{5,7},{6,4},{7,5},{8,10},{9,11},{10,... | collective-permute-start | bytes 491528 | tf_op jit(solution)/shard_map/ppermute | solution.py:106
  107.9 5.0 %collective-permute-done.23.refs_1_ = bf16[160,512]{1,0:T(8,128)(2,1)S(1)} collective-permute-done((bf16[160,512]{1,0:T(8,128)(2,1)S(1)}, bf16[160,512]{1,0:T(8,128)(2,1)S(1)}, u32[]{:S(2)}, u32[]{:S(2)}) %collective-permute-start.23) | collective-permute-done | bytes 163872 | tf_op jit(solution)/shard_map/ppermute | solution.py:106
  113.1 2.5 %collective-permute-done.22.refs_1_ = bf16[160,512]{1,0:T(8,128)(2,1)S(1)} collective-permute-done((bf16[160,512]{1,0:T(8,128)(2,1)S(1)}, bf16[160,512]{1,0:T(8,128)(2,1)S(1)}, u32[]{:S(2)}, u32[]{:S(2)}) %collective-permute-start.22) | collective-permute-done | bytes 163872 | tf_op jit(solution)/shard_map/ppermute | solution.py:106
  116.1 4.8 %collective-permute-done.25.refs_1_ = bf16[80,512]{1,0:T(8,128)(2,1)S(1)} collective-permute-done((bf16[80,512]{1,0:T(8,128)(2,1)S(1)}, bf16[80,512]{1,0:T(8,128)(2,1)S(1)}, u32[]{:S(2)}, u32[]{:S(2)}) %collective-permute-start.25) | collective-permute-done | bytes 81952 | tf_op jit(solution)/shard_map/ppermute | solution.py:106
  124.6 2.5 %collective-permute-start.30 = (bf16[80,512]{1,0:T(8,128)(2,1)S(1)}, bf16[80,512]{1,0:T(8,128)(2,1)S(1)}, u32[]{:S(2)}, u32[]{:S(2)}) collective-permute-start(bf16[80,512]{1,0:T(8,128)(2,1)S(1)} %scatter.31.refs_2_.refs_0_), channel_id=1, source_target_pairs={{0,4},{1,5},{2,6},{3,7},{4,0},{5,1},{6,2},{7,3},{8,12},{9,13},{10,... | collective-permute-start | bytes 245768 | tf_op jit(solution)/shard_map/ppermute | solution.py:106
  127.1 2.6 %collective-permute-done.27.refs_1_ = bf16[80,512]{1,0:T(8,128)(2,1)S(1)} collective-permute-done((bf16[80,512]{1,0:T(8,128)(2,1)S(1)}, bf16[80,512]{1,0:T(8,128)(2,1)S(1)}, u32[]{:S(2)}, u32[]{:S(2)}) %collective-permute-start.27) | collective-permute-done | bytes 81952 | tf_op jit(solution)/shard_map/ppermute | solution.py:106
  130.7 1.8 collective-permute-start.33
  132.5 2.8 %collective-permute-done.28.refs_1_ = bf16[160,512]{1,0:T(8,128)(2,1)S(1)} collective-permute-done((bf16[160,512]{1,0:T(8,128)(2,1)S(1)}, bf16[160,512]{1,0:T(8,128)(2,1)S(1)}, u32[]{:S(2)}, u32[]{:S(2)}) %collective-permute-start.28) | collective-permute-done | bytes 163872 | tf_op jit(solution)/shard_map/ppermute | solution.py:106
  139.8 3.6 %collective-permute-done.32.refs_1_ = bf16[128,512]{1,0:T(8,128)(2,1)S(1)} collective-permute-done((bf16[128,512]{1,0:T(8,128)(2,1)S(1)}, bf16[128,512]{1,0:T(8,128)(2,1)S(1)}, u32[]{:S(2)}, u32[]{:S(2)}) %collective-permute-start.32) | collective-permute-done | bytes 131104 | tf_op jit(solution)/shard_map/ppermute | solution.py:106
  145.1 1.8 collective-permute-start.38
  146.9 4.1 %collective-permute-done.36.refs_1_ = bf16[64,512]{1,0:T(8,128)(2,1)S(1)} collective-permute-done((bf16[64,512]{1,0:T(8,128)(2,1)S(1)}, bf16[64,512]{1,0:T(8,128)(2,1)S(1)}, u32[]{:S(2)}, u32[]{:S(2)}) %collective-permute-start.36) | collective-permute-done | bytes 65568 | tf_op jit(solution)/shard_map/ppermute | solution.py:106
  152.4 2.8 %collective-permute-start.40 = (bf16[64,512]{1,0:T(8,128)(2,1)S(1)}, bf16[64,512]{1,0:T(8,128)(2,1)S(1)}, u32[]{:S(2)}, u32[]{:S(2)}) collective-permute-start(bf16[64,512]{1,0:T(8,128)(2,1)S(1)} %scatter.38.refs_2_.refs_0_), channel_id=1, source_target_pairs={{0,4},{1,5},{2,6},{3,7},{4,0},{5,1},{6,2},{7,3},{8,12},{9,13},{10,... | collective-permute-start | bytes 196616 | tf_op jit(solution)/shard_map/ppermute | solution.py:106
  155.2 2.9 %collective-permute-done.34.refs_1_ = bf16[80,512]{1,0:T(8,128)(2,1)S(1)} collective-permute-done((bf16[80,512]{1,0:T(8,128)(2,1)S(1)}, bf16[80,512]{1,0:T(8,128)(2,1)S(1)}, u32[]{:S(2)}, u32[]{:S(2)}) %collective-permute-start.34) | collective-permute-done | bytes 81952 | tf_op jit(solution)/shard_map/ppermute | solution.py:106
  158.9 2.4 %collective-permute-start.42 = (bf16[128,512]{1,0:T(8,128)(2,1)S(1)}, bf16[128,512]{1,0:T(8,128)(2,1)S(1)}, u32[]{:S(2)}, u32[]{:S(2)}) collective-permute-start(bf16[128,512]{1,0:T(8,128)(2,1)S(1)} %gather.22.refs_2_.refs_0_), channel_id=1, source_target_pairs={{0,2},{1,3},{2,0},{3,1},{4,6},{5,7},{6,4},{7,5},{8,10},{9,11},{10,... | collective-permute-start | bytes 393224 | tf_op jit(solution)/shard_map/ppermute | solution.py:106
  161.3 2.4 %collective-permute-done.39.refs_1_ = bf16[64,512]{1,0:T(8,128)(2,1)S(1)} collective-permute-done((bf16[64,512]{1,0:T(8,128)(2,1)S(1)}, bf16[64,512]{1,0:T(8,128)(2,1)S(1)}, u32[]{:S(2)}, u32[]{:S(2)}) %collective-permute-start.39) | collective-permute-done | bytes 65568 | tf_op jit(solution)/shard_map/ppermute | solution.py:106
  164.9 3.8 %collective-permute-done.41.refs_1_ = bf16[128,512]{1,0:T(8,128)(2,1)S(1)} collective-permute-done((bf16[128,512]{1,0:T(8,128)(2,1)S(1)}, bf16[128,512]{1,0:T(8,128)(2,1)S(1)}, u32[]{:S(2)}, u32[]{:S(2)}) %collective-permute-start.41) | collective-permute-done | bytes 131104 | tf_op jit(solution)/shard_map/ppermute | solution.py:106
  172.0 5.9 %collective-permute-done.47.refs_1_ = bf16[256,512]{1,0:T(8,128)(2,1)S(1)} collective-permute-done((bf16[256,512]{1,0:T(8,128)(2,1)S(1)}, bf16[256,512]{1,0:T(8,128)(2,1)S(1)}, u32[]{:S(2)}, u32[]{:S(2)}) %collective-permute-start.47) | collective-permute-done | bytes 262176 | tf_op jit(solution)/shard_map/ppermute | solution.py:106
  178.9 1.6 collective-permute-start.50
  180.5 1.8 finish.8
  182.2 1.8 finish.9
  184.0 2.2 %finish.10 = (f32[512,2048]{1,0:T(8,128)}, f32[512,512]{1,0:T(8,128)}, f32[8,128]{1,0:T(8,128)S(1)}) custom-call(bf16[1280,512]{1,0:T(8,128)(2,1)S(1)} %gather.26.refs_2_.refs_0_, f32[8,128]{1,0:T(8,128)S(1)} %get-tuple-element.190.refs_1_), custom_call_target="tpu_custom_call" | custom-call | flops 345000000 | bytes 1107000 | tf_op jit(solution)/shard_map/finish/pallas_call | solution.py:160
  186.2 2.2 %finish.11 = (f32[512,2048]{1,0:T(8,128)}, f32[512,512]{1,0:T(8,128)}, f32[8,128]{1,0:T(8,128)S(1)}) custom-call(bf16[1280,512]{1,0:T(8,128)(2,1)S(1)} %collective-permute-done.43.refs_0_, f32[512,2048]{1,0:T(8,128)} %get-tuple-element.191.refs_1_, f32[512,512]{1,0:T(8,128)} %get-tuple-element.192.refs_2_, ...), custom_call_target="tpu_custom_call", output_to_operand_aliasing={{0}: (1, {}), {1}: (2, {})} | custom-call | flops 345000000 | bytes 1107000 | tf_op jit(solution)/shard_map/finish/pallas_call | solution.py:160
  188.4 2.6 %collective-permute-done.48.refs_1_ = bf16[512,512]{1,0:T(8,128)(2,1)S(1)} collective-permute-done((bf16[512,512]{1,0:T(8,128)(2,1)S(1)}, bf16[512,512]{1,0:T(8,128)(2,1)S(1)}, u32[]{:S(2)}, u32[]{:S(2)}) %collective-permute-start.48) | collective-permute-done | bytes 524320 | tf_op jit(solution)/shard_map/ppermute | solution.py:106
  191.2 1.6 finish.12
  195.6 1.6 finish.14
  197.2 2.2 %finish.15 = (f32[1536,512]{1,0:T(8,128)}, f32[512,512]{1,0:T(8,128)}, f32[8,128]{1,0:T(8,128)}) custom-call(bf16[1024,512]{1,0:T(8,128)(2,1)S(1)} %collective-permute-done.51.refs_0_, f32[1536,512]{1,0:T(8,128)} %get-tuple-element.201.refs_1_, f32[512,512]{1,0:T(8,128)} %get-tuple-element.202.refs_2_, ...), custom_call_target="tpu_custom_call", output_to_operand_aliasing={{0}: (1, {}), {1}: (2, {})} | custom-call | flops 345000000 | bytes 1107000 | tf_op jit(solution)/shard_map/finish/pallas_call | solution.py:160
  (139 shorter events, 35.4 us)
Async XLA Ops:
  4.0 5.8 %collective-permute-start.1 = (bf16[96,512]{1,0:T(8,128)(2,1)S(1)}, bf16[96,512]{1,0:T(8,128)(2,1)S(1)}, u32[]{:S(2)}, u32[]{:S(2)}) collective-permute-start(bf16[96,512]{1,0:T(8,128)(2,1)S(1)} %get-tuple-element.117.refs_0_), channel_id=1, source_target_pairs={{0,1},{1,0},{2,3},{3,2},{4,5},{5,4},{6,7},{7,6},{8,9},{9,8},{10,11... | collective-permute-start | bytes 294920 | tf_op jit(solution)/shard_map/ppermute | solution.py:106
  7.0 8.0 %collective-permute-start = (bf16[112,512]{1,0:T(8,128)(2,1)S(1)}, bf16[112,512]{1,0:T(8,128)(2,1)S(1)}, u32[]{:S(2)}, u32[]{:S(2)}) collective-permute-start(bf16[112,512]{1,0:T(8,128)(2,1)S(1)} %get-tuple-element.116.refs_0_), channel_id=1, source_target_pairs={{0,4},{1,5},{2,6},{3,7},{4,0},{5,1},{6,2},{7,3},{8,12},{9,13},{10,... | collective-permute-start | bytes 344072 | tf_op jit(solution)/shard_map/ppermute | solution.py:106
  15.0 10.7 %collective-permute-start.2 = (bf16[224,512]{1,0:T(8,128)(2,1)S(1)}, bf16[224,512]{1,0:T(8,128)(2,1)S(1)}, u32[]{:S(2)}, u32[]{:S(2)}) collective-permute-start(bf16[224,512]{1,0:T(8,128)(2,1)S(1)} %gather_row.5.refs_0_.refs_2_), channel_id=1, source_target_pairs={{0,2},{1,3},{2,0},{3,1},{4,6},{5,7},{6,4},{7,5},{8,10},{9,11},{10,... | collective-permute-start | bytes 688136 | tf_op jit(solution)/shard_map/ppermute | solution.py:106
  15.8 10.6 %collective-permute-start.4 = (bf16[192,512]{1,0:T(8,128)(2,1)S(1)}, bf16[192,512]{1,0:T(8,128)(2,1)S(1)}, u32[]{:S(2)}, u32[]{:S(2)}) collective-permute-start(bf16[192,512]{1,0:T(8,128)(2,1)S(1)} %gather_row.4.refs_2_.refs_0_), channel_id=1, source_target_pairs={{0,4},{1,5},{2,6},{3,7},{4,0},{5,1},{6,2},{7,3},{8,12},{9,13},{10,... | collective-permute-start | bytes 589832 | tf_op jit(solution)/shard_map/ppermute | solution.py:106
  25.8 12.0 %collective-permute-start.3 = (bf16[448,512]{1,0:T(8,128)(2,1)S(1)}, bf16[448,512]{1,0:T(8,128)(2,1)S(1)}, u32[]{:S(2)}, u32[]{:S(2)}) collective-permute-start(bf16[448,512]{1,0:T(8,128)(2,1)S(1)} %gather_row.6.refs_2_.refs_7_), channel_id=1, source_target_pairs={{0,1},{1,0},{2,3},{3,2},{4,5},{5,4},{6,7},{7,6},{8,9},{9,8},{10,11... | collective-permute-start | bytes 1376264 | tf_op jit(solution)/shard_map/ppermute | solution.py:106
  26.4 11.4 %collective-permute-start.5 = (bf16[384,512]{1,0:T(8,128)(2,1)S(1)}, bf16[384,512]{1,0:T(8,128)(2,1)S(1)}, u32[]{:S(2)}, u32[]{:S(2)}) collective-permute-start(bf16[384,512]{1,0:T(8,128)(2,1)S(1)} %gather_row.7.refs_9_.refs_14_), channel_id=1, source_target_pairs={{0,2},{1,3},{2,0},{3,1},{4,6},{5,7},{6,4},{7,5},{8,10},{9,11},{10,... | collective-permute-start | bytes 1179656 | tf_op jit(solution)/shard_map/ppermute | solution.py:106
  55.5 5.4 %collective-permute-start.8 = (bf16[1280,512]{1,0:T(8,128)(2,1)S(1)}, bf16[1280,512]{1,0:T(8,128)(2,1)S(1)}, u32[]{:S(2)}, u32[]{:S(2)}) collective-permute-start(bf16[1280,512]{1,0:T(8,128)(2,1)S(1)} %get-tuple-element.134.refs_2_), channel_id=1, source_target_pairs={{0,8},{8,0},{16,24},{24,16},{1,9},{9,1},{17,25},{25,17},{2,10},{10... | collective-permute-start | bytes 3932168 | tf_op jit(solution)/shard_map/ppermute | solution.py:106
  57.0 23.3 %collective-permute-start.11 = (bf16[640,512]{1,0:T(8,128)(2,1)S(1)}, bf16[640,512]{1,0:T(8,128)(2,1)S(1)}, u32[]{:S(2)}, u32[]{:S(2)}) collective-permute-start(bf16[640,512]{1,0:T(8,128)(2,1)S(1)} %get-tuple-element.141), channel_id=1, source_target_pairs={{0,16},{8,24},{16,0},{24,8},{1,17},{9,25},{17,1},{25,9},{2,18},{10... | collective-permute-start | bytes 1966088 | tf_op jit(solution)/shard_map/ppermute | solution.py:106
  58.6 12.0 %collective-permute-start.7 = (bf16[384,512]{1,0:T(8,128)(2,1)S(1)}, bf16[384,512]{1,0:T(8,128)(2,1)S(1)}, u32[]{:S(2)}, u32[]{:S(2)}) collective-permute-start(bf16[384,512]{1,0:T(8,128)(2,1)S(1)} %get-tuple-element.122), channel_id=1, source_target_pairs={{0,1},{1,0},{2,3},{3,2},{4,5},{5,4},{6,7},{7,6},{8,9},{9,8},{10,11... | collective-permute-start | bytes 1179656 | tf_op jit(solution)/shard_map/ppermute | solution.py:106
  59.1 13.4 %collective-permute-start.6 = (bf16[384,512]{1,0:T(8,128)(2,1)S(1)}, bf16[384,512]{1,0:T(8,128)(2,1)S(1)}, u32[]{:S(2)}, u32[]{:S(2)}) collective-permute-start(bf16[384,512]{1,0:T(8,128)(2,1)S(1)} %get-tuple-element.120), channel_id=1, source_target_pairs={{0,2},{1,3},{2,0},{3,1},{4,6},{5,7},{6,4},{7,5},{8,10},{9,11},{10,... | collective-permute-start | bytes 1179656 | tf_op jit(solution)/shard_map/ppermute | solution.py:106
  61.1 24.3 %collective-permute-start.15 = (bf16[640,512]{1,0:T(8,128)(2,1)S(1)}, bf16[640,512]{1,0:T(8,128)(2,1)S(1)}, u32[]{:S(2)}, u32[]{:S(2)}) collective-permute-start(bf16[640,512]{1,0:T(8,128)(2,1)S(1)} %get-tuple-element.148), channel_id=1, source_target_pairs={{0,1},{1,0},{2,3},{3,2},{4,5},{5,4},{6,7},{7,6},{8,9},{9,8},{10,11... | collective-permute-start | bytes 1966088 | tf_op jit(solution)/shard_map/ppermute | solution.py:106
  70.7 7.1 %collective-permute-start.12 = (bf16[192,512]{1,0:T(8,128)(2,1)S(1)}, bf16[192,512]{1,0:T(8,128)(2,1)S(1)}, u32[]{:S(2)}, u32[]{:S(2)}) collective-permute-start(bf16[192,512]{1,0:T(8,128)(2,1)S(1)} %get-tuple-element.142), channel_id=1, source_target_pairs={{0,2},{1,3},{2,0},{3,1},{4,6},{5,7},{6,4},{7,5},{8,10},{9,11},{10,... | collective-permute-start | bytes 589832 | tf_op jit(solution)/shard_map/ppermute | solution.py:106
  72.6 12.7 %collective-permute-start.10 = (bf16[192,512]{1,0:T(8,128)(2,1)S(1)}, bf16[192,512]{1,0:T(8,128)(2,1)S(1)}, u32[]{:S(2)}, u32[]{:S(2)}) collective-permute-start(bf16[192,512]{1,0:T(8,128)(2,1)S(1)} %get-tuple-element.140), channel_id=1, source_target_pairs={{0,4},{1,5},{2,6},{3,7},{4,0},{5,1},{6,2},{7,3},{8,12},{9,13},{10,... | collective-permute-start | bytes 589832 | tf_op jit(solution)/shard_map/ppermute | solution.py:106
  77.8 8.5 %collective-permute-start.14 = (bf16[96,512]{1,0:T(8,128)(2,1)S(1)}, bf16[96,512]{1,0:T(8,128)(2,1)S(1)}, u32[]{:S(2)}, u32[]{:S(2)}) collective-permute-start(bf16[96,512]{1,0:T(8,128)(2,1)S(1)} %get-tuple-element.147), channel_id=1, source_target_pairs={{0,4},{1,5},{2,6},{3,7},{4,0},{5,1},{6,2},{7,3},{8,12},{9,13},{10,... | collective-permute-start | bytes 294920 | tf_op jit(solution)/shard_map/ppermute | solution.py:106
  88.3 15.0 %collective-permute-start.18 = (bf16[1024,512]{1,0:T(8,128)(2,1)S(1)}, bf16[1024,512]{1,0:T(8,128)(2,1)S(1)}, u32[]{:S(2)}, u32[]{:S(2)}) collective-permute-start(bf16[1024,512]{1,0:T(8,128)(2,1)S(1)} %get-tuple-element.151.refs_2_), channel_id=1, source_target_pairs={{0,8},{8,0},{16,24},{24,16},{1,9},{9,1},{17,25},{25,17},{2,10},{10... | collective-permute-start | bytes 3145736 | tf_op jit(solution)/shard_map/ppermute | solution.py:106
  93.1 12.0 %collective-permute-start.16 = (bf16[1040,512]{1,0:T(8,128)(2,1)S(1)}, bf16[1040,512]{1,0:T(8,128)(2,1)S(1)}, u32[]{:S(2)}, u32[]{:S(2)}) collective-permute-start(bf16[1040,512]{1,0:T(8,128)(2,1)S(1)} %get-tuple-element.157.refs_2_), channel_id=1, source_target_pairs={{0,8},{8,0},{16,24},{24,16},{1,9},{9,1},{17,25},{25,17},{2,10},{10... | collective-permute-start | bytes 3194888 | tf_op jit(solution)/shard_map/ppermute | solution.py:106
  93.1 10.1 %collective-permute-start.19 = (bf16[320,512]{1,0:T(8,128)(2,1)S(1)}, bf16[320,512]{1,0:T(8,128)(2,1)S(1)}, u32[]{:S(2)}, u32[]{:S(2)}) collective-permute-start(bf16[320,512]{1,0:T(8,128)(2,1)S(1)} %get-tuple-element.160), channel_id=1, source_target_pairs={{0,1},{1,0},{2,3},{3,2},{4,5},{5,4},{6,7},{7,6},{8,9},{9,8},{10,11... | collective-permute-start | bytes 983048 | tf_op jit(solution)/shard_map/ppermute | solution.py:106
  94.4 10.5 %collective-permute-start.17 = (bf16[320,512]{1,0:T(8,128)(2,1)S(1)}, bf16[320,512]{1,0:T(8,128)(2,1)S(1)}, u32[]{:S(2)}, u32[]{:S(2)}) collective-permute-start(bf16[320,512]{1,0:T(8,128)(2,1)S(1)} %get-tuple-element.158), channel_id=1, source_target_pairs={{0,16},{8,24},{16,0},{24,8},{1,17},{9,25},{17,1},{25,9},{2,18},{10... | collective-permute-start | bytes 983048 | tf_op jit(solution)/shard_map/ppermute | solution.py:106
  103.5 18.3 %collective-permute-start.21 = (bf16[512,512]{1,0:T(8,128)(2,1)S(1)}, bf16[512,512]{1,0:T(8,128)(2,1)S(1)}, u32[]{:S(2)}, u32[]{:S(2)}) collective-permute-start(bf16[512,512]{1,0:T(8,128)(2,1)S(1)} %get-tuple-element.166), channel_id=1, source_target_pairs={{0,1},{1,0},{2,3},{3,2},{4,5},{5,4},{6,7},{7,6},{8,9},{9,8},{10,11... | collective-permute-start | bytes 1572872 | tf_op jit(solution)/shard_map/ppermute | solution.py:106
  105.3 18.2 %collective-permute-start.20 = (bf16[528,512]{1,0:T(8,128)(2,1)S(1)}, bf16[528,512]{1,0:T(8,128)(2,1)S(1)}, u32[]{:S(2)}, u32[]{:S(2)}) collective-permute-start(bf16[528,512]{1,0:T(8,128)(2,1)S(1)} %get-tuple-element.165), channel_id=1, source_target_pairs={{0,16},{8,24},{16,0},{24,8},{1,17},{9,25},{17,1},{25,9},{2,18},{10... | collective-permute-start | bytes 1622024 | tf_op jit(solution)/shard_map/ppermute | solution.py:106
  105.9 7.0 %collective-permute-start.23 = (bf16[160,512]{1,0:T(8,128)(2,1)S(1)}, bf16[160,512]{1,0:T(8,128)(2,1)S(1)}, u32[]{:S(2)}, u32[]{:S(2)}) collective-permute-start(bf16[160,512]{1,0:T(8,128)(2,1)S(1)} %get-tuple-element.168), channel_id=1, source_target_pairs={{0,2},{1,3},{2,0},{3,1},{4,6},{5,7},{6,4},{7,5},{8,10},{9,11},{10,... | collective-permute-start | bytes 491528 | tf_op jit(solution)/shard_map/ppermute | solution.py:106
  105.9 9.7 %collective-permute-start.22 = (bf16[160,512]{1,0:T(8,128)(2,1)S(1)}, bf16[160,512]{1,0:T(8,128)(2,1)S(1)}, u32[]{:S(2)}, u32[]{:S(2)}) collective-permute-start(bf16[160,512]{1,0:T(8,128)(2,1)S(1)} %get-tuple-element.167), channel_id=1, source_target_pairs={{0,2},{1,3},{2,0},{3,1},{4,6},{5,7},{6,4},{7,5},{8,10},{9,11},{10,... | collective-permute-start | bytes 491528 | tf_op jit(solution)/shard_map/ppermute | solution.py:106
  113.0 7.9 %collective-permute-start.25 = (bf16[80,512]{1,0:T(8,128)(2,1)S(1)}, bf16[80,512]{1,0:T(8,128)(2,1)S(1)}, u32[]{:S(2)}, u32[]{:S(2)}) collective-permute-start(bf16[80,512]{1,0:T(8,128)(2,1)S(1)} %get-tuple-element.172), channel_id=1, source_target_pairs={{0,4},{1,5},{2,6},{3,7},{4,0},{5,1},{6,2},{7,3},{8,12},{9,13},{10,... | collective-permute-start | bytes 245768 | tf_op jit(solution)/shard_map/ppermute | solution.py:106
  115.6 6.2 %collective-permute-start.24 = (bf16[80,512]{1,0:T(8,128)(2,1)S(1)}, bf16[80,512]{1,0:T(8,128)(2,1)S(1)}, u32[]{:S(2)}, u32[]{:S(2)}) collective-permute-start(bf16[80,512]{1,0:T(8,128)(2,1)S(1)} %get-tuple-element.171), channel_id=1, source_target_pairs={{0,4},{1,5},{2,6},{3,7},{4,0},{5,1},{6,2},{7,3},{8,12},{9,13},{10,... | collective-permute-start | bytes 245768 | tf_op jit(solution)/shard_map/ppermute | solution.py:106
  122.0 10.5 %collective-permute-start.29 = (bf16[256,512]{1,0:T(8,128)(2,1)S(1)}, bf16[256,512]{1,0:T(8,128)(2,1)S(1)}, u32[]{:S(2)}, u32[]{:S(2)}) collective-permute-start(bf16[256,512]{1,0:T(8,128)(2,1)S(1)} %get-tuple-element.176), channel_id=1, source_target_pairs={{0,16},{8,24},{16,0},{24,8},{1,17},{9,25},{17,1},{25,9},{2,18},{10... | collective-permute-start | bytes 786440 | tf_op jit(solution)/shard_map/ppermute | solution.py:106
  123.5 6.2 %collective-permute-start.27 = (bf16[80,512]{1,0:T(8,128)(2,1)S(1)}, bf16[80,512]{1,0:T(8,128)(2,1)S(1)}, u32[]{:S(2)}, u32[]{:S(2)}) collective-permute-start(bf16[80,512]{1,0:T(8,128)(2,1)S(1)} %scatter.30.refs_2_.refs_0_), channel_id=1, source_target_pairs={{0,4},{1,5},{2,6},{3,7},{4,0},{5,1},{6,2},{7,3},{8,12},{9,13},{10,... | collective-permute-start | bytes 245768 | tf_op jit(solution)/shard_map/ppermute | solution.py:106
  123.7 12.8 %collective-permute-start.26 = (bf16[272,512]{1,0:T(8,128)(2,1)S(1)}, bf16[272,512]{1,0:T(8,128)(2,1)S(1)}, u32[]{:S(2)}, u32[]{:S(2)}) collective-permute-start(bf16[272,512]{1,0:T(8,128)(2,1)S(1)} %get-tuple-element.175), channel_id=1, source_target_pairs={{0,1},{1,0},{2,3},{3,2},{4,5},{5,4},{6,7},{7,6},{8,9},{9,8},{10,11... | collective-permute-start | bytes 835592 | tf_op jit(solution)/shard_map/ppermute | solution.py:106
  124.6 6.0 %collective-permute-start.30 = (bf16[80,512]{1,0:T(8,128)(2,1)S(1)}, bf16[80,512]{1,0:T(8,128)(2,1)S(1)}, u32[]{:S(2)}, u32[]{:S(2)}) collective-permute-start(bf16[80,512]{1,0:T(8,128)(2,1)S(1)} %scatter.31.refs_2_.refs_0_), channel_id=1, source_target_pairs={{0,4},{1,5},{2,6},{3,7},{4,0},{5,1},{6,2},{7,3},{8,12},{9,13},{10,... | collective-permute-start | bytes 245768 | tf_op jit(solution)/shard_map/ppermute | solution.py:106
  129.8 5.6 %collective-permute-start.28 = (bf16[160,512]{1,0:T(8,128)(2,1)S(1)}, bf16[160,512]{1,0:T(8,128)(2,1)S(1)}, u32[]{:S(2)}, u32[]{:S(2)}) collective-permute-start(bf16[160,512]{1,0:T(8,128)(2,1)S(1)} %gather.16.refs_2_.refs_0_), channel_id=1, source_target_pairs={{0,2},{1,3},{2,0},{3,1},{4,6},{5,7},{6,4},{7,5},{8,10},{9,11},{10,... | collective-permute-start | bytes 491528 | tf_op jit(solution)/shard_map/ppermute | solution.py:106
  130.7 6.7 %collective-permute-start.33 = (bf16[160,512]{1,0:T(8,128)(2,1)S(1)}, bf16[160,512]{1,0:T(8,128)(2,1)S(1)}, u32[]{:S(2)}, u32[]{:S(2)}) collective-permute-start(bf16[160,512]{1,0:T(8,128)(2,1)S(1)} %gather.17.refs_2_.refs_0_), channel_id=1, source_target_pairs={{0,2},{1,3},{2,0},{3,1},{4,6},{5,7},{6,4},{7,5},{8,10},{9,11},{10,... | collective-permute-start | bytes 491528 | tf_op jit(solution)/shard_map/ppermute | solution.py:106
  135.4 9.6 %collective-permute-start.37 = (bf16[320,512]{1,0:T(8,128)(2,1)S(1)}, bf16[320,512]{1,0:T(8,128)(2,1)S(1)}, u32[]{:S(2)}, u32[]{:S(2)}) collective-permute-start(bf16[320,512]{1,0:T(8,128)(2,1)S(1)} %gather.18.refs_2_.refs_0_), channel_id=1, source_target_pairs={{0,1},{1,0},{2,3},{3,2},{4,5},{5,4},{6,7},{7,6},{8,9},{9,8},{10,11... | collective-permute-start | bytes 983048 | tf_op jit(solution)/shard_map/ppermute | solution.py:106
  137.4 13.6 %collective-permute-start.35 = (bf16[320,512]{1,0:T(8,128)(2,1)S(1)}, bf16[320,512]{1,0:T(8,128)(2,1)S(1)}, u32[]{:S(2)}, u32[]{:S(2)}) collective-permute-start(bf16[320,512]{1,0:T(8,128)(2,1)S(1)} %gather.19.refs_2_.refs_0_), channel_id=1, source_target_pairs={{0,16},{8,24},{16,0},{24,8},{1,17},{9,25},{17,1},{25,9},{2,18},{10... | collective-permute-start | bytes 983048 | tf_op jit(solution)/shard_map/ppermute | solution.py:106
  137.8 5.7 %collective-permute-start.32 = (bf16[128,512]{1,0:T(8,128)(2,1)S(1)}, bf16[128,512]{1,0:T(8,128)(2,1)S(1)}, u32[]{:S(2)}, u32[]{:S(2)}) collective-permute-start(bf16[128,512]{1,0:T(8,128)(2,1)S(1)} %get-tuple-element.180), channel_id=1, source_target_pairs={{0,2},{1,3},{2,0},{3,1},{4,6},{5,7},{6,4},{7,5},{8,10},{9,11},{10,... | collective-permute-start | bytes 393224 | tf_op jit(solution)/shard_map/ppermute | solution.py:106
  138.6 6.4 %collective-permute-start.31 = (bf16[144,512]{1,0:T(8,128)(2,1)S(1)}, bf16[144,512]{1,0:T(8,128)(2,1)S(1)}, u32[]{:S(2)}, u32[]{:S(2)}) collective-permute-start(bf16[144,512]{1,0:T(8,128)(2,1)S(1)} %get-tuple-element.179), channel_id=1, source_target_pairs={{0,2},{1,3},{2,0},{3,1},{4,6},{5,7},{6,4},{7,5},{8,10},{9,11},{10,... | collective-permute-start | bytes 442376 | tf_op jit(solution)/shard_map/ppermute | solution.py:106
  143.5 7.5 %collective-permute-start.36 = (bf16[64,512]{1,0:T(8,128)(2,1)S(1)}, bf16[64,512]{1,0:T(8,128)(2,1)S(1)}, u32[]{:S(2)}, u32[]{:S(2)}) collective-permute-start(bf16[64,512]{1,0:T(8,128)(2,1)S(1)} %get-tuple-element.184), channel_id=1, source_target_pairs={{0,4},{1,5},{2,6},{3,7},{4,0},{5,1},{6,2},{7,3},{8,12},{9,13},{10,... | collective-permute-start | bytes 196616 | tf_op jit(solution)/shard_map/ppermute | solution.py:106
  145.1 23.7 %collective-permute-start.38 = (bf16[640,512]{1,0:T(8,128)(2,1)S(1)}, bf16[640,512]{1,0:T(8,128)(2,1)S(1)}, u32[]{:S(2)}, u32[]{:S(2)}) collective-permute-start(bf16[640,512]{1,0:T(8,128)(2,1)S(1)} %gather.20.refs_2_.refs_0_), channel_id=1, source_target_pairs={{0,16},{8,24},{16,0},{24,8},{1,17},{9,25},{17,1},{25,9},{2,18},{10... | collective-permute-start | bytes 1966088 | tf_op jit(solution)/shard_map/ppermute | solution.py:106
  151.1 17.8 %collective-permute-start.44 = (bf16[640,512]{1,0:T(8,128)(2,1)S(1)}, bf16[640,512]{1,0:T(8,128)(2,1)S(1)}, u32[]{:S(2)}, u32[]{:S(2)}) collective-permute-start(bf16[640,512]{1,0:T(8,128)(2,1)S(1)} %gather.21.refs_2_.refs_0_), channel_id=1, source_target_pairs={{0,1},{1,0},{2,3},{3,2},{4,5},{5,4},{6,7},{7,6},{8,9},{9,8},{10,11... | collective-permute-start | bytes 1966088 | tf_op jit(solution)/shard_map/ppermute | solution.py:106
  152.3 5.8 %collective-permute-start.34 = (bf16[80,512]{1,0:T(8,128)(2,1)S(1)}, bf16[80,512]{1,0:T(8,128)(2,1)S(1)}, u32[]{:S(2)}, u32[]{:S(2)}) collective-permute-start(bf16[80,512]{1,0:T(8,128)(2,1)S(1)} %get-tuple-element.183), channel_id=1, source_target_pairs={{0,4},{1,5},{2,6},{3,7},{4,0},{5,1},{6,2},{7,3},{8,12},{9,13},{10,... | collective-permute-start | bytes 245768 | tf_op jit(solution)/shard_map/ppermute | solution.py:106
  152.4 6.4 %collective-permute-start.40 = (bf16[64,512]{1,0:T(8,128)(2,1)S(1)}, bf16[64,512]{1,0:T(8,128)(2,1)S(1)}, u32[]{:S(2)}, u32[]{:S(2)}) collective-permute-start(bf16[64,512]{1,0:T(8,128)(2,1)S(1)} %scatter.38.refs_2_.refs_0_), channel_id=1, source_target_pairs={{0,4},{1,5},{2,6},{3,7},{4,0},{5,1},{6,2},{7,3},{8,12},{9,13},{10,... | collective-permute-start | bytes 196616 | tf_op jit(solution)/shard_map/ppermute | solution.py:106
  158.1 5.6 %collective-permute-start.39 = (bf16[64,512]{1,0:T(8,128)(2,1)S(1)}, bf16[64,512]{1,0:T(8,128)(2,1)S(1)}, u32[]{:S(2)}, u32[]{:S(2)}) collective-permute-start(bf16[64,512]{1,0:T(8,128)(2,1)S(1)} %get-tuple-element.186.refs_2_.refs_0_), channel_id=1, source_target_pairs={{0,4},{1,5},{2,6},{3,7},{4,0},{5,1},{6,2},{7,3},{8,12},{9,13},{10,... | collective-permute-start | bytes 196616 | tf_op jit(solution)/shard_map/ppermute | solution.py:106
  158.9 6.1 %collective-permute-start.42 = (bf16[128,512]{1,0:T(8,128)(2,1)S(1)}, bf16[128,512]{1,0:T(8,128)(2,1)S(1)}, u32[]{:S(2)}, u32[]{:S(2)}) collective-permute-start(bf16[128,512]{1,0:T(8,128)(2,1)S(1)} %gather.22.refs_2_.refs_0_), channel_id=1, source_target_pairs={{0,2},{1,3},{2,0},{3,1},{4,6},{5,7},{6,4},{7,5},{8,10},{9,11},{10,... | collective-permute-start | bytes 393224 | tf_op jit(solution)/shard_map/ppermute | solution.py:106
  163.7 5.0 %collective-permute-start.41 = (bf16[128,512]{1,0:T(8,128)(2,1)S(1)}, bf16[128,512]{1,0:T(8,128)(2,1)S(1)}, u32[]{:S(2)}, u32[]{:S(2)}) collective-permute-start(bf16[128,512]{1,0:T(8,128)(2,1)S(1)} %gather.23.refs_2_.refs_0_), channel_id=1, source_target_pairs={{0,2},{1,3},{2,0},{3,1},{4,6},{5,7},{6,4},{7,5},{8,10},{9,11},{10,... | collective-permute-start | bytes 393224 | tf_op jit(solution)/shard_map/ppermute | solution.py:106
  169.0 13.2 %collective-permute-start.45 = (bf16[1280,512]{1,0:T(8,128)(2,1)S(1)}, bf16[1280,512]{1,0:T(8,128)(2,1)S(1)}, u32[]{:S(2)}, u32[]{:S(2)}) collective-permute-start(bf16[1280,512]{1,0:T(8,128)(2,1)S(1)} %gather.27.refs_2_.refs_0_), channel_id=1, source_target_pairs={{0,8},{8,0},{16,24},{24,16},{1,9},{9,1},{17,25},{25,17},{2,10},{10... | collective-permute-start | bytes 3932168 | tf_op jit(solution)/shard_map/ppermute | solution.py:106
  169.1 17.1 %collective-permute-start.43 = (bf16[1280,512]{1,0:T(8,128)(2,1)S(1)}, bf16[1280,512]{1,0:T(8,128)(2,1)S(1)}, u32[]{:S(2)}, u32[]{:S(2)}) collective-permute-start(bf16[1280,512]{1,0:T(8,128)(2,1)S(1)} %gather.26.refs_2_.refs_0_), channel_id=1, source_target_pairs={{0,8},{8,0},{16,24},{24,16},{1,9},{9,1},{17,25},{25,17},{2,10},{10... | collective-permute-start | bytes 3932168 | tf_op jit(solution)/shard_map/ppermute | solution.py:106
  169.6 8.3 %collective-permute-start.47 = (bf16[256,512]{1,0:T(8,128)(2,1)S(1)}, bf16[256,512]{1,0:T(8,128)(2,1)S(1)}, u32[]{:S(2)}, u32[]{:S(2)}) collective-permute-start(bf16[256,512]{1,0:T(8,128)(2,1)S(1)} %gather.24.refs_2_.refs_0_), channel_id=1, source_target_pairs={{0,16},{8,24},{16,0},{24,8},{1,17},{9,25},{17,1},{25,9},{2,18},{10... | collective-permute-start | bytes 786440 | tf_op jit(solution)/shard_map/ppermute | solution.py:106
  170.7 8.1 %collective-permute-start.46 = (bf16[256,512]{1,0:T(8,128)(2,1)S(1)}, bf16[256,512]{1,0:T(8,128)(2,1)S(1)}, u32[]{:S(2)}, u32[]{:S(2)}) collective-permute-start(bf16[256,512]{1,0:T(8,128)(2,1)S(1)} %gather.25.refs_2_.refs_0_), channel_id=1, source_target_pairs={{0,1},{1,0},{2,3},{3,2},{4,5},{5,4},{6,7},{7,6},{8,9},{9,8},{10,11... | collective-permute-start | bytes 786440 | tf_op jit(solution)/shard_map/ppermute | solution.py:106
  177.9 13.1 %collective-permute-start.48 = (bf16[512,512]{1,0:T(8,128)(2,1)S(1)}, bf16[512,512]{1,0:T(8,128)(2,1)S(1)}, u32[]{:S(2)}, u32[]{:S(2)}) collective-permute-start(bf16[512,512]{1,0:T(8,128)(2,1)S(1)} %gather.28.refs_2_.refs_0_), channel_id=1, source_target_pairs={{0,1},{1,0},{2,3},{3,2},{4,5},{5,4},{6,7},{7,6},{8,9},{9,8},{10,11... | collective-permute-start | bytes 1572872 | tf_op jit(solution)/shard_map/ppermute | solution.py:106
  178.9 13.9 %collective-permute-start.50 = (bf16[512,512]{1,0:T(8,128)(2,1)S(1)}, bf16[512,512]{1,0:T(8,128)(2,1)S(1)}, u32[]{:S(2)}, u32[]{:S(2)}) collective-permute-start(bf16[512,512]{1,0:T(8,128)(2,1)S(1)} %gather.29.refs_1_.refs_0_), channel_id=1, source_target_pairs={{0,16},{8,24},{16,0},{24,8},{1,17},{9,25},{17,1},{25,9},{2,18},{10... | collective-permute-start | bytes 1572872 | tf_op jit(solution)/shard_map/ppermute | solution.py:106
  (15 other events, 147.8 us)

commit v4 on v3

--- a/solution.py
+++ b/solution.py
@@ -19,15 +19,16 @@
 SCATTER_BITS = 5
 EXTRA_ROWS = 16
 VMEM_SMALL = 28 * 1024 * 1024
-VMEM_LARGE = 60 * 1024 * 1024
+VMEM_LARGE = 62 * 1024 * 1024
 SHORT_ROW = 768
 BYTES_MICROSECOND = 3_690_000
+EACH = 5
 
 EVENTS = (
-    "Wb", "Wa", "A1", "A0", "K", "V", "K", "A1", "V", "A0", "K", "TK", "V", "TV", "A1", "B0",
-    "A0", "B1", "A1", "A0", "A1", "A0", "B0", "B1", "A1", "A0", "B0", "A1", "B1", "A0", "B0",
-    "B1", "A1", "B0", "A0", "B1", "B0", "B1", "B0", "B1", "A1", "A0", "B0", "B1", "A0n", "A0f",
-    "A1n", "A1f", "B0", "B0n", "B1", "B0f", "B1n", "B1f",
+    "A1", "A0", "K", "V", "A1", "A0", "V", "K", "A1", "K", "TK", "V", "TV", "A0", "A1", "B0",
+    "B1", "A1", "A0", "B0", "B1", "A0", "A1", "B0", "A0", "A1", "B1", "A0", "B0", "B1", "A1",
+    "B0", "B1", "A0", "B0", "B1", "A1", "B0", "B1", "A0", "B0", "B1", "A0n", "A1n", "A1f", "A0f",
+    "B0", "B0n", "B1", "B0f", "B1n", "B1f",
 )
 
 BF16 = jnp.bfloat16
@@ -100,10 +101,11 @@
                 result |= bit
         return result
 
-    def swap(self, array, bit):
+    def swap(self, array, bit, name):
         axis, value = bit
         size = self.n_rows if axis == "rows" else self.n_seq
-        return lax.ppermute(array, axis, [(i, i ^ value) for i in range(size)])
+        with jax.named_scope(f"swap_{name}"):
+            return lax.ppermute(array, axis, [(i, i ^ value) for i in range(size)])
 
 
 def order_matrix(length, transposed):
@@ -140,7 +142,7 @@
 
     def call(
         self, kernel, name, outs, scratch=(), anywhere=(), out_anywhere=(), aliases=None,
-        vmem=VMEM_SMALL, microseconds=0.3, token=0,
+        vmem=VMEM_SMALL, microseconds=EACH, token=0,
     ):
         def spec(number, places):
             return pl.BlockSpec(memory_space=pl.ANY if number in places else pltpu.VMEM)
@@ -173,7 +175,7 @@
                 input_output_aliases=aliases or {},
                 compiler_params=pltpu.CompilerParams(vmem_limit_bytes=vmem),
                 cost_estimate=pl.CostEstimate(
-                    flops=int(microseconds * 1_150_000_000), bytes_accessed=int(microseconds * BYTES_MICROSECOND), transcendentals=0
+                    flops=1 + int(microseconds * 1_150_000_000), bytes_accessed=1 + int(microseconds * BYTES_MICROSECOND), transcendentals=0
                 ),
             )(*operands, *last)
             self.last = (results[token],)
@@ -181,7 +183,7 @@
 
         return run
 
-    def combine(self, name, inputs, outs, microseconds=0.3):
+    def combine(self, name, inputs, outs, microseconds=EACH):
         width = inputs[0].shape[1]
 
         def kernel(*refs):
@@ -265,14 +267,15 @@
 
 
 def layer_kernel(
-    plan, short,
-    x_in, cotangent, query_in, key_in, value_in, segment_column, gain_ffn,
+    plan, short, down_order, up_order,
+    x_in, normed_in, cotangent, query_in, key_in, value_in, segment_column, gain_ffn,
     keys_near, keys_far, values_near, values_far, w_out, w_up, w_down,
-    layer_out, d_hidden_out, normed_ffn_out, activated_out, d_expanded_out, cotangent_out,
-    attended_out, d_branch_out, d_query_out, d_key_own, d_value_own,
-    d_key_keep, d_key_send, d_value_keep, d_value_send, gain_grad,
+    layer_out, d_hidden_out, d_query_out, d_key_own, d_value_own,
+    d_key_keep, d_key_send, d_value_keep, d_value_send,
+    down_send, down_keep, up_send, up_keep, gain_grad,
     all_keys, all_values, all_extra, bias, statistics, prob_keep, expanded_sum, d_normed_sum,
-    d_attended, *copied,
+    d_attended, normed_ffn_out, activated_out, d_expanded_out, cotangent_out, attended_out,
+    d_branch_out, down_rows, up_rows, out_rows, query_rows, *copied,
 ):
     batch, _, length, width = cotangent.shape
     slots = length // 3
@@ -421,7 +424,7 @@
         d_normed_sum[...] += dot_nt(d_expanded, w_up[:, columns])
         return carry
 
-    lax.fori_loop(0, total_width // chunk, feed, 0, unroll=True)
+    lax.fori_loop(0, total_width // chunk, feed, 0, unroll=short)
 
     unorder = order_matrix(length, True)
     for b in range(batch):
@@ -472,6 +475,19 @@
 
     each(attend_back)
 
+    for c in range(total_width // chunk):
+        columns = slice(c * chunk, (c + 1) * chunk)
+        down_rows[columns, :] = dot_tn(activated_out[:, columns], cotangent_out[...]).astype(BF16)
+        up_rows[c] = dot_tn(normed_ffn_out[...], d_expanded_out[:, columns]).astype(BF16)
+    out_rows[...] = dot_tn(attended_out[...], d_branch_out[...]).astype(BF16)
+    query_rows[...] = dot_tn(normed_in[...], d_query_out[...]).astype(BF16)
+    _, mine = own_places(plan)
+    thin = width // plan.blocks
+    parts = ((down_rows, total_width // plan.blocks), (out_rows, thin))
+    spread(plan, mine, down_order, parts, down_send, down_keep)
+    parts = tuple((up_rows.at[c], thin) for c in range(total_width // chunk))
+    spread(plan, mine, up_order, parts + ((query_rows, thin),), up_send, up_keep)
+
 
 def spread(plan, place, order, parts, send, keep):
     half = plan.blocks // 2
@@ -484,35 +500,6 @@
                     pl.ds(pl.multiple_of(block * rows, 16), rows), :
                 ]
                 start += rows
-
-
-def down_grad_kernel(
-    plan, order, activated, cotangent, attended, d_branch, send, keep, down_rows, out_rows
-):
-    width = cotangent.shape[1]
-    wide = activated.shape[1]
-    for c in range(wide // width):
-        columns = slice(c * width, (c + 1) * width)
-        down_rows[columns, :] = dot_tn(activated[:, columns], cotangent[...]).astype(BF16)
-    out_rows[...] = dot_tn(attended[...], d_branch[...]).astype(BF16)
-    _, mine = own_places(plan)
-    parts = ((down_rows, wide // plan.blocks), (out_rows, width // plan.blocks))
-    spread(plan, mine, order, parts, send, keep)
-
-
-def up_grad_kernel(
-    plan, order, normed_ffn, d_expanded, normed, d_query, send, keep, up_rows, query_rows
-):
-    width = normed_ffn.shape[1]
-    chunks = d_expanded.shape[1] // width
-    for c in range(chunks):
-        columns = slice(c * width, (c + 1) * width)
-        up_rows[c] = dot_tn(normed_ffn[...], d_expanded[:, columns]).astype(BF16)
-    query_rows[...] = dot_tn(normed[...], d_query[...]).astype(BF16)
-    _, mine = own_places(plan)
-    thin = width // plan.blocks
-    parts = tuple((up_rows.at[c], thin) for c in range(chunks)) + ((query_rows, thin),)
-    spread(plan, mine, order, parts, send, keep)
 
 
 def conv_grads(
@@ -608,11 +595,12 @@
 
 
 class RowGather:
-    def __init__(self, plan, order, array, bits):
-        self.plan, self.order, self.held, self.bits = plan, order, array, list(bits)
+    def __init__(self, name, plan, order, array, bits):
+        self.name, self.plan, self.order = name, plan, order
+        self.held, self.bits = array, list(bits)
 
     def step(self):
-        arrived = self.plan.swap(self.held, ("seq", self.bits.pop(0)))
+        arrived = self.plan.swap(self.held, ("seq", self.bits.pop(0)), self.name)
         if not self.bits:
             return [self.held, arrived]
         rows = self.held.shape[0]
@@ -622,52 +610,57 @@
 
 
 class RowScatter:
-    def __init__(self, plan, order, keep, send, bits):
-        self.plan, self.order, self.keep, self.send = plan, order, keep, send
+    def __init__(self, name, plan, order, keep, send, bits):
+        self.name, self.plan, self.order, self.keep, self.send = name, plan, order, keep, send
         self.bits = list(bits)
 
-    def step(self):
+    def step(self, microseconds=EACH):
         if not self.bits:
             return
-        arrived = self.plan.swap(self.send, ("seq", self.bits.pop()))
+        arrived = self.plan.swap(self.send, ("seq", self.bits.pop()), self.name)
         rows = self.keep.shape[0]
         half = rows // 2
         outs = [(0, rows)] if not self.bits else [(0, half), (half, half)]
         self.keep, *send = self.order.combine(
-            "scatter_row", [self.keep, arrived], [[(0, start, size, 1, start)] for start, size in outs]
+            "scatter_row", [self.keep, arrived],
+            [[(0, start, size, 1, start)] for start, size in outs], microseconds,
         )
         self.send = send[0] if send else None
 
 
 class Part:
-    def __init__(self, plan, order, bits, send, keep, shapes, parts, extra=0):
-        self.plan, self.order, self.bits, self.extra = plan, order, bits, extra
+    def __init__(self, name, plan, order, bits, send, keep, shapes, parts, extra=0):
+        self.name, self.plan, self.order, self.bits, self.extra = name, plan, order, bits, extra
         self.send, self.keep = send, keep
         self.shapes, self.parts = shapes, parts
         self.done = 0
 
-    def step(self):
+    def step(self, microseconds):
         if self.done < len(self.bits):
-            self.scatter(self.bits[self.done])
+            self.scatter(self.bits[self.done], microseconds)
         else:
-            self.gather(self.bits[2 * len(self.bits) - 1 - self.done])
+            self.gather(self.bits[2 * len(self.bits) - 1 - self.done], microseconds)
         self.done += 1
 
-    def scatter(self, bit):
-        arrived = self.plan.swap(self.send, bit)
+    def scatter(self, bit, microseconds):
+        arrived = self.plan.swap(self.send, bit, self.name)
         extra = self.extra
         rows = self.keep.shape[0] - extra
         last = [(0, rows, extra, 1, rows)]
         if self.done < len(self.bits) - 1:
             half = rows // 2
             outs = [[(0, start, half, 1, start)] + (last if extra else []) for start in (0, half)]
-            self.keep, self.send = self.order.combine("scatter", [self.keep, arrived], outs)
+            self.keep, self.send = self.order.combine(
+                "scatter", [self.keep, arrived], outs, microseconds
+            )
             return
         outs = [[(0, 0, rows, 1, 0)]] + ([last] if extra else [])
-        self.held, *self.sums = self.order.combine("scatter", [self.keep, arrived], outs)
+        self.held, *self.sums = self.order.combine(
+            "scatter", [self.keep, arrived], outs, microseconds
+        )
         for bit in self.plan.rest:
             arrays = [self.held] + self.sums
-            arrived = [self.plan.swap(array, bit) for array in arrays]
+            arrived = [self.plan.swap(array, bit, self.name) for array in arrays]
             self.held, *self.sums = self.order.combine(
                 "scatter_rest", arrays + arrived,
                 [
@@ -676,14 +669,14 @@
                 ],
             )
 
-    def gather(self, bit):
-        arrived = self.plan.swap(self.held, bit)
+    def gather(self, bit, microseconds=EACH):
+        arrived = self.plan.swap(self.held, bit, self.name)
         if bit == self.plan.core:
             self.far = arrived
             return
         rows = self.held.shape[0]
         self.held, = self.order.combine(
-            "gather", [self.held, arrived], [[(0, 0, rows), (1, 0, rows)]]
+            "gather", [self.held, arrived], [[(0, 0, rows), (1, 0, rows)]], microseconds
         )
 
     def finish(self, core, *targets):
@@ -732,48 +725,11 @@
     )(tokens, gain_attn, segments, w_query, w_key, w_value, conv_key, conv_value)
 
     steps = len(plan.key_order)
-    keys = RowGather(plan, order, packed_key, plan.key_order)
-    values = RowGather(plan, order, packed_value, plan.value_order)
+    keys = RowGather("gather_keys", plan, order, packed_key, plan.key_order)
+    values = RowGather("gather_values", plan, order, packed_value, plan.value_order)
     for number in range(steps - 1):
-        for gather in (values, keys) if number == 0 else (keys, values):
-            gather.step()
-
-    total_slots = slots * plan.n_seq
-    short = total_slots <= SHORT_ROW
-    wide = ((positions, w_up.shape[1]), BF16)
-    half_packed = ((batch * total_slots // 2, width), BF16)
-    copied = [] if short else [pltpu.SemaphoreType.DMA((plan.n_seq * (1 + 2 * batch),))]
-    (
-        layer_out, d_hidden, normed_ffn, activated, d_expanded, cotangent_rows, attended, d_branch,
-        d_query, d_key_own, d_value_own, *d_packed, gain_ffn_grad,
-    ) = order.call(
-        functools.partial(layer_kernel, plan, short),
-        "layer",
-        [(tokens.shape, BF16), flat32, flat, wide, wide, flat, flat, flat]
-        + [flat, flat32, flat32] + [half_packed] * 4 + [((1, width), F32)],
-        scratch=[
-            pltpu.VMEM((batch, total_slots, width), BF16),
-            pltpu.VMEM((batch, total_slots, width), BF16),
-            pltpu.VMEM((plan.n_seq, EXTRA_ROWS, LANES), BF16),
-            pltpu.VMEM((batch, length, total_slots), F32),
-            pltpu.VMEM((batch * GROUPS, 2 * length, LANES), F32),
-            pltpu.VMEM((batch * GROUPS if short else 1, 2 * length, total_slots), F32),
-            pltpu.VMEM((positions, width), F32),
-            pltpu.VMEM((positions, width), F32),
-            pltpu.VMEM((positions, width), BF16),
-        ]
-        + copied,
-        anywhere=() if short else (7, 8, 9, 10),
-        vmem=VMEM_SMALL if short else VMEM_LARGE,
-        token=-1,
-    )(
-        x, cotangent, queries, key_rows, value_rows, segment_column, gain_ffn,
-        *keys.step(), *values.step(), w_out, w_up, w_down,
-    )
-    rows = [
-        RowScatter(plan, order, d_packed[0], d_packed[1], plan.key_order),
-        RowScatter(plan, order, d_packed[2], d_packed[3], plan.value_order),
-    ]
+        keys.step()
+        values.step()
 
     core = [plan.core]
     x_first, y_first = core + plan.first + plan.tail, core + plan.second + plan.tail
@@ -791,34 +747,65 @@
         "B0": ([conv_key.shape, square], [(conv_block, 0, everything), (thin, 1, everything)]),
         "B1": ([conv_value.shape, square], [(conv_block, 0, everything), (thin, 1, everything)]),
     }
+
+    def half_rows(name):
+        return half * sum(part[0] for part in layouts[name][1])
+
+    total_slots = slots * plan.n_seq
+    short = total_slots <= SHORT_ROW
+    half_packed = ((batch * total_slots // 2, width), BF16)
+    halves = [((half_rows(name), width), BF16) for name in ("A0", "A0", "A1", "A1")]
+    flat_here = pltpu.VMEM((positions, width), BF16)
+    wide_here = pltpu.VMEM((positions, w_up.shape[1]), BF16)
+    copied = [] if short else [pltpu.SemaphoreType.DMA((plan.n_seq * (1 + 2 * batch),))]
+    layer_out, d_hidden, d_query, d_key_own, d_value_own, *outs, gain_ffn_grad = order.call(
+        functools.partial(layer_kernel, plan, short, bits["A0"], bits["A1"]),
+        "layer",
+        [(tokens.shape, BF16), flat32, flat, flat32, flat32] + [half_packed] * 4 + halves
+        + [((1, width), F32)],
+        scratch=[
+            pltpu.VMEM((batch, total_slots, width), BF16),
+            pltpu.VMEM((batch, total_slots, width), BF16),
+            pltpu.VMEM((plan.n_seq, EXTRA_ROWS, LANES), BF16),
+            pltpu.VMEM((batch, length, total_slots), F32),
+            pltpu.VMEM((batch * GROUPS, 2 * length, LANES), F32),
+            pltpu.VMEM((batch * GROUPS, 2 * length, total_slots) if short else (1, 8, LANES), F32),
+            pltpu.VMEM((positions, width), F32),
+            pltpu.VMEM((positions, width), F32),
+            flat_here, flat_here, wide_here, wide_here, flat_here, flat_here, flat_here,
+            pltpu.VMEM(w_down.shape, BF16),
+            pltpu.VMEM((chunks, width, width), BF16),
+            square_here, square_here,
+        ]
+        + copied,
+        anywhere=() if short else (8, 9, 10, 11),
+        vmem=VMEM_SMALL if short else VMEM_LARGE,
+        token=-1,
+    )(
+        x, normed, cotangent, queries, key_rows, value_rows, segment_column, gain_ffn,
+        *keys.step(), *values.step(), w_out, w_up, w_down,
+    )
+    rows = [
+        RowScatter("K", plan, order, outs[0], outs[1], plan.key_order),
+        RowScatter("V", plan, order, outs[2], outs[3], plan.value_order),
+    ]
     chains, results = {"K": rows[0], "V": rows[1]}, {}
+    for name, (send, keep) in (("A0", outs[4:6]), ("A1", outs[6:8])):
+        chains[name] = Part(name, plan, order, bits[name], send, keep, *layouts[name])
 
     def make(name, kernel, outs, scratch, operands, extra=0):
-        shapes, parts = layouts[name]
-        total = half * sum(part[0] for part in parts) + extra
+        total = half_rows(name) + extra
         send, keep, *others = order.call(
             functools.partial(kernel, plan, bits[name]),
             kernel.__name__,
             [((total, width), BF16)] * 2 + outs,
             scratch=scratch,
         )(*operands)
-        chains[name] = Part(plan, order, bits[name], send, keep, shapes, parts, extra)
+        chains[name] = Part(name, plan, order, bits[name], send, keep, *layouts[name], extra)
         return others
 
-    wide_here = pltpu.VMEM(w_down.shape, BF16)
     for event in EVENTS:
-        if event == "Wa":
-            make(
-                "A0", down_grad_kernel, [], [wide_here, square_here],
-                (activated, cotangent_rows, attended, d_branch),
-            )
-        elif event == "Wb":
-            make(
-                "A1", up_grad_kernel, [],
-                [pltpu.VMEM((chunks, width, width), BF16), square_here],
-                (normed_ffn, d_expanded, normed, d_query),
-            )
-        elif event == "TK":
+        if event == "TK":
             while rows[0].bits:
                 rows[0].step()
             d_keys, = make(
@@ -842,7 +829,8 @@
         elif event[2:] == "f":
             results[event[:2]] = chains[event[:2]].finish(1, *results[event[:2]])
         else:
-            chains[event].step()
+            name, _, cost = event.partition(":")
+            chains[name].step(float(cost or EACH))
     grad_down, grad_out = results["A0"]
     grad_up, grad_query = results["A1"]
     grad_conv_key, grad_key = results["B0"]

time: 200 us -> 190 us (0.950)
  waiting for transfers between devices: 96.3 us -> 76.8 us
  starting transfers between devices: 57.5 us -> 65.3 us
  local copies, waits for them, and re-layouts: 1.11 us -> 3.67 us
    ppermute x52, waiting for transfers between devices: 96.3 us -> 76.8 us  [swap(): return lax.ppermute(array, axis, [(i, i ^ value) for i in range(size)])]
    ppermute x52, starting transfers between devices: 57.5 us -> 65.3 us  [swap(): return lax.ppermute(array, axis, [(i, i ^ value) for i in range(size)])]
    unnamed x22, local copies, waits for them, and re-layouts: 0.53 us -> 3.08 us
    pallas_call x60 -> x58, Pallas kernels: 43.2 us -> 42.5 us  [run(): pl.pallas_call(without_last, name=name, out_shape=[pltpu.HBM(shape, dtype...]
  transfers between devices with their start and end apart: 52 -> 52, of which waited for: 29 -> 23; matrix products, arithmetic and copies ran while one was open for 0% -> 0% of each run, Pallas kernels for 11% -> 11%
where the time goes in v4:
time: 190 us
  waiting for transfers between devices  76.8 us (40%)
  starting transfers between devices  65.3 us (34%)
  Pallas kernels  42.5 us (22%)
  local copies, waits for them, and re-layouts  3.67 us (2%)
    ppermute x52, waiting for transfers between devices, swap(): return lax.ppermute(array, axis, [(i, i ^ value) for i in range(size)])  76.8 us
    ppermute x52, starting transfers between devices, swap(): return lax.ppermute(array, axis, [(i, i ^ value) for i in range(size)])  65.3 us
    pallas_call x58, Pallas kernels, run(): pl.pallas_call(without_last, name=name, out_shape=[pltpu.HBM(shape, dtype...  42.5 us
  transfers between devices with their start and end apart: 52, of which 23 were waited for; matrix products, arithmetic and copies ran while one was open for 0% of the time, Pallas kernels for 11%

profile of v4, /device:TPU:0, one launch (start us, length us, event | category | flops | bytes accessed | tf_op | source)
XLA Modules:
  0.0 189.7 jit_solution(13488085113949654228)
XLA Ops:
  0.6 3.3 %project.1 = (f32[288,512]{1,0:T(8,128)S(1)}, bf16[288,512]{1,0:T(8,128)(2,1)S(1)}, bf16[288,512]{1,0:T(8,128)(2,1)S(1)}, bf16[288,512]{1,0:T(8,128)(2,1)S(1)}, ...) custom-call(bf16[2,1,144,512]{3,2,1,0:T(8,128)(2,1)} %refs_0_.1, ...), custom_call_target="tpu_custom_call" | custom-call | flops 5750000128 | bytes 18450000 | tf_op jit(solution)/shard_map/project/pallas_call | solution.py:162
  4.0 4.1 %collective-permute-start = (bf16[112,512]{1,0:T(8,128)(2,1)S(1)}, bf16[112,512]{1,0:T(8,128)(2,1)S(1)}, u32[]{:S(2)}, u32[]{:S(2)}) collective-permute-start(bf16[112,512]{1,0:T(8,128)(2,1)S(1)} %get-tuple-element.111.refs_0_), channel_id=1, source_target_pairs={{0,4},{1,5},{2,6},{3,7},{4,0},{5,1},{6,2},{7,3},{8,12},{9,13},{10,... | collective-permute-start | bytes 344072 | tf_op jit(solution)/shard_map/swap_gather_keys/ppermute | solution.py:108
  9.6 4.1 %collective-permute-done.refs_1_ = bf16[112,512]{1,0:T(8,128)(2,1)S(1)} collective-permute-done((bf16[112,512]{1,0:T(8,128)(2,1)S(1)}, bf16[112,512]{1,0:T(8,128)(2,1)S(1)}, u32[]{:S(2)}, u32[]{:S(2)}) %collective-permute-start) | collective-permute-done | bytes 114720 | tf_op jit(solution)/shard_map/swap_gather_keys/ppermute | solution.py:108
  14.5 3.4 %collective-permute-start.4 = (bf16[192,512]{1,0:T(8,128)(2,1)S(1)}, bf16[192,512]{1,0:T(8,128)(2,1)S(1)}, u32[]{:S(2)}, u32[]{:S(2)}) collective-permute-start(bf16[192,512]{1,0:T(8,128)(2,1)S(1)} %gather_row.5.refs_2_.refs_0_), channel_id=1, source_target_pairs={{0,4},{1,5},{2,6},{3,7},{4,0},{5,1},{6,2},{7,3},{8,12},{9,13},{10,... | collective-permute-start | bytes 589832 | tf_op jit(solution)/shard_map/swap_gather_values/ppermute | solution.py:108
  18.0 6.8 %collective-permute-done.1.refs_1_ = bf16[224,512]{1,0:T(8,128)(2,1)S(1)} collective-permute-done((bf16[224,512]{1,0:T(8,128)(2,1)S(1)}, bf16[224,512]{1,0:T(8,128)(2,1)S(1)}, u32[]{:S(2)}, u32[]{:S(2)}) %collective-permute-start.1) | collective-permute-done | bytes 229408 | tf_op jit(solution)/shard_map/swap_gather_keys/ppermute | solution.py:108
  26.3 1.7 collective-permute-start.5
  28.0 8.8 %collective-permute-done.5.refs_11_ = bf16[384,512]{1,0:T(8,128)(2,1)S(1)} collective-permute-done((bf16[384,512]{1,0:T(8,128)(2,1)S(1)}, bf16[384,512]{1,0:T(8,128)(2,1)S(1)}, u32[]{:S(2)}, u32[]{:S(2)}) %collective-permute-start.5) | collective-permute-done | bytes 393248 | tf_op jit(solution)/shard_map/swap_gather_values/ppermute | solution.py:108
  36.8 16.8 %layer.1 = (bf16[2,1,144,512]{3,2,1,0:T(8,128)(2,1)}, f32[288,512]{1,0:T(8,128)S(1)}, bf16[288,512]{1,0:T(8,128)(2,1)S(1)}, f32[288,512]{1,0:T(8,128)S(1)}, f32[...) custom-call(f32[288,512]{1,0:T(8,128)S(1)} %get-tuple-element.105.re, ...), custom_call_target="tpu_custom_call" | custom-call | flops 5750000128 | bytes 18450000 | tf_op jit(solution)/shard_map/layer/pallas_call | solution.py:162
  54.1 1.7 collective-permute-start.6
  58.8 1.6 collective-permute-start.11
  61.9 6.0 %collective-permute-done.7.refs_1_ = bf16[384,512]{1,0:T(8,128)(2,1)S(1)} collective-permute-done((bf16[384,512]{1,0:T(8,128)(2,1)S(1)}, bf16[384,512]{1,0:T(8,128)(2,1)S(1)}, u32[]{:S(2)}, u32[]{:S(2)}) %collective-permute-start.7) | collective-permute-done | bytes 393248 | tf_op jit(solution)/shard_map/swap_K/ppermute | solution.py:108
  68.1 1.8 collective-permute-start.10
  70.2 6.7 %collective-permute-done.12.refs_1_ = bf16[640,512]{1,0:T(8,128)(2,1)S(1)} collective-permute-done((bf16[640,512]{1,0:T(8,128)(2,1)S(1)}, bf16[640,512]{1,0:T(8,128)(2,1)S(1)}, u32[]{:S(2)}, u32[]{:S(2)}) %collective-permute-start.12) | collective-permute-done | bytes 655392 | tf_op jit(solution)/shard_map/swap_A1/ppermute | solution.py:108
  77.6 4.3 %collective-permute-done.11.refs_1_ = bf16[640,512]{1,0:T(8,128)(2,1)S(1)} collective-permute-done((bf16[640,512]{1,0:T(8,128)(2,1)S(1)}, bf16[640,512]{1,0:T(8,128)(2,1)S(1)}, u32[]{:S(2)}, u32[]{:S(2)}) %collective-permute-start.11) | collective-permute-done | bytes 655392 | tf_op jit(solution)/shard_map/swap_A0/ppermute | solution.py:108
  82.2 1.8 collective-permute-start.15
  87.0 1.6 collective-permute-done.16.refs_1_
  93.7 2.9 %value_grad_kernel.1 = (bf16[1040,512]{1,0:T(8,128)(2,1)S(1)}, bf16[1040,512]{1,0:T(8,128)(2,1)S(1)}, bf16[2,1,144,512]{3,2,1,0:T(8,128)(2,1)}) custom-call(f32[2,144,1]{2,1,0:T(8,128)S(1)} %get-tuple-element.110.refs_2_.refs_6_.refs_0_, bf16[96,512]{1,0:T(8,128)(2,1)S(1)} %scatter_row.11.refs_1_.refs_15_, ...), custom_call_target="tpu_custom_call" | custom-call | flops 5750000128 | bytes 18450000 | tf_op jit(solution)/shard_map/value_grad_kernel/pallas_call | solution.py:162
  96.8 1.8 collective-permute-start.23
  98.6 1.8 collective-permute-start.24
  100.7 1.6 collective-permute-start.22
  102.6 1.9 %collective-permute-done.24.refs_1_ = bf16[80,512]{1,0:T(8,128)(2,1)S(1)} collective-permute-done((bf16[80,512]{1,0:T(8,128)(2,1)S(1)}, bf16[80,512]{1,0:T(8,128)(2,1)S(1)}, u32[]{:S(2)}, u32[]{:S(2)}) %collective-permute-start.24) | collective-permute-done | bytes 81952 | tf_op jit(solution)/shard_map/swap_A1/ppermute | solution.py:108
  104.5 3.4 %collective-permute-start.26 = (bf16[80,512]{1,0:T(8,128)(2,1)S(1)}, bf16[80,512]{1,0:T(8,128)(2,1)S(1)}, u32[]{:S(2)}, u32[]{:S(2)}) collective-permute-start(bf16[80,512]{1,0:T(8,128)(2,1)S(1)} %scatter.29.refs_2_.refs_0_), channel_id=1, source_target_pairs={{0,4},{1,5},{2,6},{3,7},{4,0},{5,1},{6,2},{7,3},{8,12},{9,13},{10,... | collective-permute-start | bytes 245768 | tf_op jit(solution)/shard_map/swap_A1/ppermute | solution.py:108
  109.6 4.9 %collective-permute-done.22.refs_1_ = bf16[512,512]{1,0:T(8,128)(2,1)S(1)} collective-permute-done((bf16[512,512]{1,0:T(8,128)(2,1)S(1)}, bf16[512,512]{1,0:T(8,128)(2,1)S(1)}, u32[]{:S(2)}, u32[]{:S(2)}) %collective-permute-start.22) | collective-permute-done | bytes 524320 | tf_op jit(solution)/shard_map/swap_B0/ppermute | solution.py:108
  114.7 1.5 collective-permute-start.30
  116.2 6.9 %collective-permute-done.21.refs_1_ = bf16[528,512]{1,0:T(8,128)(2,1)S(1)} collective-permute-done((bf16[528,512]{1,0:T(8,128)(2,1)S(1)}, bf16[528,512]{1,0:T(8,128)(2,1)S(1)}, u32[]{:S(2)}, u32[]{:S(2)}) %collective-permute-start.21) | collective-permute-done | bytes 540704 | tf_op jit(solution)/shard_map/swap_B1/ppermute | solution.py:108
  123.5 2.1 %collective-permute-start.28 = (bf16[160,512]{1,0:T(8,128)(2,1)S(1)}, bf16[160,512]{1,0:T(8,128)(2,1)S(1)}, u32[]{:S(2)}, u32[]{:S(2)}) collective-permute-start(bf16[160,512]{1,0:T(8,128)(2,1)S(1)} %gather.16.refs_2_.refs_0_), channel_id=1, source_target_pairs={{0,2},{1,3},{2,0},{3,1},{4,6},{5,7},{6,4},{7,5},{8,10},{9,11},{10,... | collective-permute-start | bytes 491528 | tf_op jit(solution)/shard_map/swap_A1/ppermute | solution.py:108
  130.6 1.6 collective-permute-start.36
  132.2 1.9 %collective-permute-done.25.refs_1_ = bf16[272,512]{1,0:T(8,128)(2,1)S(1)} collective-permute-done((bf16[272,512]{1,0:T(8,128)(2,1)S(1)}, bf16[272,512]{1,0:T(8,128)(2,1)S(1)}, u32[]{:S(2)}, u32[]{:S(2)}) %collective-permute-start.25) | collective-permute-done | bytes 278560 | tf_op jit(solution)/shard_map/swap_B1/ppermute | solution.py:108
  134.3 3.0 %collective-permute-done.33.refs_1_ = bf16[160,512]{1,0:T(8,128)(2,1)S(1)} collective-permute-done((bf16[160,512]{1,0:T(8,128)(2,1)S(1)}, bf16[160,512]{1,0:T(8,128)(2,1)S(1)}, u32[]{:S(2)}, u32[]{:S(2)}) %collective-permute-start.33) | collective-permute-done | bytes 163872 | tf_op jit(solution)/shard_map/swap_A0/ppermute | solution.py:108
  137.3 1.6 collective-permute-start.40
  138.9 1.6 collective-permute-start.35
  143.0 2.5 %collective-permute-done.35.refs_1_ = bf16[64,512]{1,0:T(8,128)(2,1)S(1)} collective-permute-done((bf16[64,512]{1,0:T(8,128)(2,1)S(1)}, bf16[64,512]{1,0:T(8,128)(2,1)S(1)}, u32[]{:S(2)}, u32[]{:S(2)}) %collective-permute-start.35) | collective-permute-done | bytes 65568 | tf_op jit(solution)/shard_map/swap_B0/ppermute | solution.py:108
  146.1 2.8 %collective-permute-done.34.refs_1_ = bf16[80,512]{1,0:T(8,128)(2,1)S(1)} collective-permute-done((bf16[80,512]{1,0:T(8,128)(2,1)S(1)}, bf16[80,512]{1,0:T(8,128)(2,1)S(1)}, u32[]{:S(2)}, u32[]{:S(2)}) %collective-permute-start.34) | collective-permute-done | bytes 81952 | tf_op jit(solution)/shard_map/swap_B1/ppermute | solution.py:108
  149.8 1.6 collective-permute-start.42
  151.4 4.2 %collective-permute-start.44 = (bf16[128,512]{1,0:T(8,128)(2,1)S(1)}, bf16[128,512]{1,0:T(8,128)(2,1)S(1)}, u32[]{:S(2)}, u32[]{:S(2)}) collective-permute-start(bf16[128,512]{1,0:T(8,128)(2,1)S(1)} %gather.22.refs_2_.refs_0_), channel_id=1, source_target_pairs={{0,2},{1,3},{2,0},{3,1},{4,6},{5,7},{6,4},{7,5},{8,10},{9,11},{10,... | collective-permute-start | bytes 393224 | tf_op jit(solution)/shard_map/swap_B0/ppermute | solution.py:108
  156.4 2.3 %collective-permute-done.37.refs_1_ = bf16[640,512]{1,0:T(8,128)(2,1)S(1)} collective-permute-done((bf16[640,512]{1,0:T(8,128)(2,1)S(1)}, bf16[640,512]{1,0:T(8,128)(2,1)S(1)}, u32[]{:S(2)}, u32[]{:S(2)}) %collective-permute-start.37) | collective-permute-done | bytes 655392 | tf_op jit(solution)/shard_map/swap_A1/ppermute | solution.py:108
  162.2 5.4 %collective-permute-done.46.refs_1_ = bf16[256,512]{1,0:T(8,128)(2,1)S(1)} collective-permute-done((bf16[256,512]{1,0:T(8,128)(2,1)S(1)}, bf16[256,512]{1,0:T(8,128)(2,1)S(1)}, u32[]{:S(2)}, u32[]{:S(2)}) %collective-permute-start.46) | collective-permute-done | bytes 262176 | tf_op jit(solution)/shard_map/swap_B0/ppermute | solution.py:108
  167.7 1.6 collective-permute-start.47
  169.3 1.6 collective-permute-start.50
  170.9 1.8 finish.8
  172.6 2.2 %finish.9 = (f32[512,2048]{1,0:T(8,128)}, f32[512,512]{1,0:T(8,128)}, f32[8,128]{1,0:T(8,128)S(1)}) custom-call(bf16[1280,512]{1,0:T(8,128)(2,1)S(1)} %gather.24.refs_2_.refs_0_, f32[8,128]{1,0:T(8,128)S(1)} %get-tuple-element.175.refs_1_), custom_call_target="tpu_custom_call" | custom-call | flops 5750000128 | bytes 18450000 | tf_op jit(solution)/shard_map/finish/pallas_call | solution.py:162
  174.9 2.2 %finish.10 = (f32[512,2048]{1,0:T(8,128)}, f32[512,512]{1,0:T(8,128)}, f32[8,128]{1,0:T(8,128)S(1)}) custom-call(bf16[1280,512]{1,0:T(8,128)(2,1)S(1)} %collective-permute-done.41.refs_0_, f32[512,2048]{1,0:T(8,128)} %get-tuple-element.176.refs_1_, f32[512,512]{1,0:T(8,128)} %get-tuple-element.177.refs_2_, ...), custom_call_target="tpu_custom_call", output_to_operand_aliasing={{0}: (1, {}), {1}: (2, {})} | custom-call | flops 5750000128 | bytes 18450000 | tf_op jit(solution)/shard_map/finish/pallas_call | solution.py:162
  177.1 1.8 finish.11
  178.8 2.4 %collective-permute-done.47.refs_1_ = bf16[512,512]{1,0:T(8,128)(2,1)S(1)} collective-permute-done((bf16[512,512]{1,0:T(8,128)(2,1)S(1)}, bf16[512,512]{1,0:T(8,128)(2,1)S(1)}, u32[]{:S(2)}, u32[]{:S(2)}) %collective-permute-start.47) | collective-permute-done | bytes 524320 | tf_op jit(solution)/shard_map/swap_B0/ppermute | solution.py:108
  181.4 1.6 finish.12
  184.1 1.6 finish.13
  185.7 1.6 finish.14
  187.3 2.2 %finish.15 = (f32[1536,512]{1,0:T(8,128)}, f32[512,512]{1,0:T(8,128)}, f32[8,128]{1,0:T(8,128)}) custom-call(bf16[1024,512]{1,0:T(8,128)(2,1)S(1)} %collective-permute-done.51.refs_0_, f32[1536,512]{1,0:T(8,128)} %get-tuple-element.189.refs_1_, f32[512,512]{1,0:T(8,128)} %get-tuple-element.190.refs_2_, ...), custom_call_target="tpu_custom_call", output_to_operand_aliasing={{0}: (1, {}), {1}: (2, {})} | custom-call | flops 5750000128 | bytes 18450000 | tf_op jit(solution)/shard_map/finish/pallas_call | solution.py:162
  (137 shorter events, 35.7 us)
Async XLA Ops:
  4.0 9.7 %collective-permute-start = (bf16[112,512]{1,0:T(8,128)(2,1)S(1)}, bf16[112,512]{1,0:T(8,128)(2,1)S(1)}, u32[]{:S(2)}, u32[]{:S(2)}) collective-permute-start(bf16[112,512]{1,0:T(8,128)(2,1)S(1)} %get-tuple-element.111.refs_0_), channel_id=1, source_target_pairs={{0,4},{1,5},{2,6},{3,7},{4,0},{5,1},{6,2},{7,3},{8,12},{9,13},{10,... | collective-permute-start | bytes 344072 | tf_op jit(solution)/shard_map/swap_gather_keys/ppermute | solution.py:108
  8.1 6.4 %collective-permute-start.2 = (bf16[96,512]{1,0:T(8,128)(2,1)S(1)}, bf16[96,512]{1,0:T(8,128)(2,1)S(1)}, u32[]{:S(2)}, u32[]{:S(2)}) collective-permute-start(bf16[96,512]{1,0:T(8,128)(2,1)S(1)} %get-tuple-element.112.refs_0_), channel_id=1, source_target_pairs={{0,1},{1,0},{2,3},{3,2},{4,5},{5,4},{6,7},{7,6},{8,9},{9,8},{10,11... | collective-permute-start | bytes 294920 | tf_op jit(solution)/shard_map/swap_gather_values/ppermute | solution.py:108
  13.7 11.1 %collective-permute-start.1 = (bf16[224,512]{1,0:T(8,128)(2,1)S(1)}, bf16[224,512]{1,0:T(8,128)(2,1)S(1)}, u32[]{:S(2)}, u32[]{:S(2)}) collective-permute-start(bf16[224,512]{1,0:T(8,128)(2,1)S(1)} %gather_row.4.refs_2_.refs_0_), channel_id=1, source_target_pairs={{0,2},{1,3},{2,0},{3,1},{4,6},{5,7},{6,4},{7,5},{8,10},{9,11},{10,... | collective-permute-start | bytes 688136 | tf_op jit(solution)/shard_map/swap_gather_keys/ppermute | solution.py:108
  14.5 11.7 %collective-permute-start.4 = (bf16[192,512]{1,0:T(8,128)(2,1)S(1)}, bf16[192,512]{1,0:T(8,128)(2,1)S(1)}, u32[]{:S(2)}, u32[]{:S(2)}) collective-permute-start(bf16[192,512]{1,0:T(8,128)(2,1)S(1)} %gather_row.5.refs_2_.refs_0_), channel_id=1, source_target_pairs={{0,4},{1,5},{2,6},{3,7},{4,0},{5,1},{6,2},{7,3},{8,12},{9,13},{10,... | collective-permute-start | bytes 589832 | tf_op jit(solution)/shard_map/swap_gather_values/ppermute | solution.py:108
  24.9 11.9 %collective-permute-start.3 = (bf16[448,512]{1,0:T(8,128)(2,1)S(1)}, bf16[448,512]{1,0:T(8,128)(2,1)S(1)}, u32[]{:S(2)}, u32[]{:S(2)}) collective-permute-start(bf16[448,512]{1,0:T(8,128)(2,1)S(1)} %gather_row.6.refs_2_.refs_8_), channel_id=1, source_target_pairs={{0,1},{1,0},{2,3},{3,2},{4,5},{5,4},{6,7},{7,6},{8,9},{9,8},{10,11... | collective-permute-start | bytes 1376264 | tf_op jit(solution)/shard_map/swap_gather_keys/ppermute | solution.py:108
  26.3 10.5 %collective-permute-start.5 = (bf16[384,512]{1,0:T(8,128)(2,1)S(1)}, bf16[384,512]{1,0:T(8,128)(2,1)S(1)}, u32[]{:S(2)}, u32[]{:S(2)}) collective-permute-start(bf16[384,512]{1,0:T(8,128)(2,1)S(1)} %gather_row.7.refs_10_.refs_15_), channel_id=1, source_target_pairs={{0,2},{1,3},{2,0},{3,1},{4,6},{5,7},{6,4},{7,5},{8,10},{9,11},{10,... | collective-permute-start | bytes 1179656 | tf_op jit(solution)/shard_map/swap_gather_values/ppermute | solution.py:108
  54.1 13.9 %collective-permute-start.6 = (bf16[384,512]{1,0:T(8,128)(2,1)S(1)}, bf16[384,512]{1,0:T(8,128)(2,1)S(1)}, u32[]{:S(2)}, u32[]{:S(2)}) collective-permute-start(bf16[384,512]{1,0:T(8,128)(2,1)S(1)} %get-tuple-element.115), channel_id=1, source_target_pairs={{0,2},{1,3},{2,0},{3,1},{4,6},{5,7},{6,4},{7,5},{8,10},{9,11},{10,... | collective-permute-start | bytes 1179656 | tf_op jit(solution)/shard_map/swap_V/ppermute | solution.py:108
  55.8 12.0 %collective-permute-start.7 = (bf16[384,512]{1,0:T(8,128)(2,1)S(1)}, bf16[384,512]{1,0:T(8,128)(2,1)S(1)}, u32[]{:S(2)}, u32[]{:S(2)}) collective-permute-start(bf16[384,512]{1,0:T(8,128)(2,1)S(1)} %get-tuple-element.117), channel_id=1, source_target_pairs={{0,1},{1,0},{2,3},{3,2},{4,5},{5,4},{6,7},{7,6},{8,9},{9,8},{10,11... | collective-permute-start | bytes 1179656 | tf_op jit(solution)/shard_map/swap_K/ppermute | solution.py:108
  58.8 23.1 %collective-permute-start.11 = (bf16[640,512]{1,0:T(8,128)(2,1)S(1)}, bf16[640,512]{1,0:T(8,128)(2,1)S(1)}, u32[]{:S(2)}, u32[]{:S(2)}) collective-permute-start(bf16[640,512]{1,0:T(8,128)(2,1)S(1)} %get-tuple-element.128), channel_id=1, source_target_pairs={{0,1},{1,0},{2,3},{3,2},{4,5},{5,4},{6,7},{7,6},{8,9},{9,8},{10,11... | collective-permute-start | bytes 1966088 | tf_op jit(solution)/shard_map/swap_A0/ppermute | solution.py:108
  60.4 16.5 %collective-permute-start.12 = (bf16[640,512]{1,0:T(8,128)(2,1)S(1)}, bf16[640,512]{1,0:T(8,128)(2,1)S(1)}, u32[]{:S(2)}, u32[]{:S(2)}) collective-permute-start(bf16[640,512]{1,0:T(8,128)(2,1)S(1)} %get-tuple-element.129), channel_id=1, source_target_pairs={{0,16},{8,24},{16,0},{24,8},{1,17},{9,25},{17,1},{25,9},{2,18},{10... | collective-permute-start | bytes 1966088 | tf_op jit(solution)/shard_map/swap_A1/ppermute | solution.py:108
  68.1 14.0 %collective-permute-start.10 = (bf16[192,512]{1,0:T(8,128)(2,1)S(1)}, bf16[192,512]{1,0:T(8,128)(2,1)S(1)}, u32[]{:S(2)}, u32[]{:S(2)}) collective-permute-start(bf16[192,512]{1,0:T(8,128)(2,1)S(1)} %get-tuple-element.127), channel_id=1, source_target_pairs={{0,4},{1,5},{2,6},{3,7},{4,0},{5,1},{6,2},{7,3},{8,12},{9,13},{10,... | collective-permute-start | bytes 589832 | tf_op jit(solution)/shard_map/swap_V/ppermute | solution.py:108
  69.9 12.2 %collective-permute-start.14 = (bf16[192,512]{1,0:T(8,128)(2,1)S(1)}, bf16[192,512]{1,0:T(8,128)(2,1)S(1)}, u32[]{:S(2)}, u32[]{:S(2)}) collective-permute-start(bf16[192,512]{1,0:T(8,128)(2,1)S(1)} %get-tuple-element.134), channel_id=1, source_target_pairs={{0,2},{1,3},{2,0},{3,1},{4,6},{5,7},{6,4},{7,5},{8,10},{9,11},{10,... | collective-permute-start | bytes 589832 | tf_op jit(solution)/shard_map/swap_K/ppermute | solution.py:108
  77.0 11.7 %collective-permute-start.16 = (bf16[320,512]{1,0:T(8,128)(2,1)S(1)}, bf16[320,512]{1,0:T(8,128)(2,1)S(1)}, u32[]{:S(2)}, u32[]{:S(2)}) collective-permute-start(bf16[320,512]{1,0:T(8,128)(2,1)S(1)} %get-tuple-element.137), channel_id=1, source_target_pairs={{0,1},{1,0},{2,3},{3,2},{4,5},{5,4},{6,7},{7,6},{8,9},{9,8},{10,11... | collective-permute-start | bytes 983048 | tf_op jit(solution)/shard_map/swap_A1/ppermute | solution.py:108
  82.2 6.9 %collective-permute-start.15 = (bf16[96,512]{1,0:T(8,128)(2,1)S(1)}, bf16[96,512]{1,0:T(8,128)(2,1)S(1)}, u32[]{:S(2)}, u32[]{:S(2)}) collective-permute-start(bf16[96,512]{1,0:T(8,128)(2,1)S(1)} %get-tuple-element.136), channel_id=1, source_target_pairs={{0,4},{1,5},{2,6},{3,7},{4,0},{5,1},{6,2},{7,3},{8,12},{9,13},{10,... | collective-permute-start | bytes 294920 | tf_op jit(solution)/shard_map/swap_K/ppermute | solution.py:108
  84.0 8.0 %collective-permute-start.13 = (bf16[96,512]{1,0:T(8,128)(2,1)S(1)}, bf16[96,512]{1,0:T(8,128)(2,1)S(1)}, u32[]{:S(2)}, u32[]{:S(2)}) collective-permute-start(bf16[96,512]{1,0:T(8,128)(2,1)S(1)} %get-tuple-element.133), channel_id=1, source_target_pairs={{0,1},{1,0},{2,3},{3,2},{4,5},{5,4},{6,7},{7,6},{8,9},{9,8},{10,11... | collective-permute-start | bytes 294920 | tf_op jit(solution)/shard_map/swap_V/ppermute | solution.py:108
  85.5 11.2 %collective-permute-start.20 = (bf16[320,512]{1,0:T(8,128)(2,1)S(1)}, bf16[320,512]{1,0:T(8,128)(2,1)S(1)}, u32[]{:S(2)}, u32[]{:S(2)}) collective-permute-start(bf16[320,512]{1,0:T(8,128)(2,1)S(1)} %get-tuple-element.150), channel_id=1, source_target_pairs={{0,16},{8,24},{16,0},{24,8},{1,17},{9,25},{17,1},{25,9},{2,18},{10... | collective-permute-start | bytes 983048 | tf_op jit(solution)/shard_map/swap_A0/ppermute | solution.py:108
  88.8 9.8 %collective-permute-start.19 = (bf16[160,512]{1,0:T(8,128)(2,1)S(1)}, bf16[160,512]{1,0:T(8,128)(2,1)S(1)}, u32[]{:S(2)}, u32[]{:S(2)}) collective-permute-start(bf16[160,512]{1,0:T(8,128)(2,1)S(1)} %get-tuple-element.149), channel_id=1, source_target_pairs={{0,2},{1,3},{2,0},{3,1},{4,6},{5,7},{6,4},{7,5},{8,10},{9,11},{10,... | collective-permute-start | bytes 491528 | tf_op jit(solution)/shard_map/swap_A1/ppermute | solution.py:108
  92.0 8.5 %collective-permute-start.18 = (bf16[1024,512]{1,0:T(8,128)(2,1)S(1)}, bf16[1024,512]{1,0:T(8,128)(2,1)S(1)}, u32[]{:S(2)}, u32[]{:S(2)}) collective-permute-start(bf16[1024,512]{1,0:T(8,128)(2,1)S(1)} %get-tuple-element.140.refs_2_), channel_id=1, source_target_pairs={{0,8},{8,0},{16,24},{24,16},{1,9},{9,1},{17,25},{25,17},{2,10},{10... | collective-permute-start | bytes 3145736 | tf_op jit(solution)/shard_map/swap_B0/ppermute | solution.py:108
  96.7 5.6 %collective-permute-start.17 = (bf16[1040,512]{1,0:T(8,128)(2,1)S(1)}, bf16[1040,512]{1,0:T(8,128)(2,1)S(1)}, u32[]{:S(2)}, u32[]{:S(2)}) collective-permute-start(bf16[1040,512]{1,0:T(8,128)(2,1)S(1)} %get-tuple-element.147.refs_2_), channel_id=1, source_target_pairs={{0,8},{8,0},{16,24},{24,16},{1,9},{9,1},{17,25},{25,17},{2,10},{10... | collective-permute-start | bytes 3194888 | tf_op jit(solution)/shard_map/swap_B1/ppermute | solution.py:108
  96.8 12.7 %collective-permute-start.23 = (bf16[160,512]{1,0:T(8,128)(2,1)S(1)}, bf16[160,512]{1,0:T(8,128)(2,1)S(1)}, u32[]{:S(2)}, u32[]{:S(2)}) collective-permute-start(bf16[160,512]{1,0:T(8,128)(2,1)S(1)} %get-tuple-element.157), channel_id=1, source_target_pairs={{0,2},{1,3},{2,0},{3,1},{4,6},{5,7},{6,4},{7,5},{8,10},{9,11},{10,... | collective-permute-start | bytes 491528 | tf_op jit(solution)/shard_map/swap_A0/ppermute | solution.py:108
  98.6 5.8 %collective-permute-start.24 = (bf16[80,512]{1,0:T(8,128)(2,1)S(1)}, bf16[80,512]{1,0:T(8,128)(2,1)S(1)}, u32[]{:S(2)}, u32[]{:S(2)}) collective-permute-start(bf16[80,512]{1,0:T(8,128)(2,1)S(1)} %get-tuple-element.158), channel_id=1, source_target_pairs={{0,4},{1,5},{2,6},{3,7},{4,0},{5,1},{6,2},{7,3},{8,12},{9,13},{10,... | collective-permute-start | bytes 245768 | tf_op jit(solution)/shard_map/swap_A1/ppermute | solution.py:108
  100.7 13.8 %collective-permute-start.22 = (bf16[512,512]{1,0:T(8,128)(2,1)S(1)}, bf16[512,512]{1,0:T(8,128)(2,1)S(1)}, u32[]{:S(2)}, u32[]{:S(2)}) collective-permute-start(bf16[512,512]{1,0:T(8,128)(2,1)S(1)} %get-tuple-element.156), channel_id=1, source_target_pairs={{0,1},{1,0},{2,3},{3,2},{4,5},{5,4},{6,7},{7,6},{8,9},{9,8},{10,11... | collective-permute-start | bytes 1572872 | tf_op jit(solution)/shard_map/swap_B0/ppermute | solution.py:108
  104.5 18.9 %collective-permute-start.26 = (bf16[80,512]{1,0:T(8,128)(2,1)S(1)}, bf16[80,512]{1,0:T(8,128)(2,1)S(1)}, u32[]{:S(2)}, u32[]{:S(2)}) collective-permute-start(bf16[80,512]{1,0:T(8,128)(2,1)S(1)} %scatter.29.refs_2_.refs_0_), channel_id=1, source_target_pairs={{0,4},{1,5},{2,6},{3,7},{4,0},{5,1},{6,2},{7,3},{8,12},{9,13},{10,... | collective-permute-start | bytes 245768 | tf_op jit(solution)/shard_map/swap_A1/ppermute | solution.py:108
  107.9 15.2 %collective-permute-start.21 = (bf16[528,512]{1,0:T(8,128)(2,1)S(1)}, bf16[528,512]{1,0:T(8,128)(2,1)S(1)}, u32[]{:S(2)}, u32[]{:S(2)}) collective-permute-start(bf16[528,512]{1,0:T(8,128)(2,1)S(1)} %get-tuple-element.155), channel_id=1, source_target_pairs={{0,16},{8,24},{16,0},{24,8},{1,17},{9,25},{17,1},{25,9},{2,18},{10... | collective-permute-start | bytes 1622024 | tf_op jit(solution)/shard_map/swap_B1/ppermute | solution.py:108
  109.5 13.8 %collective-permute-start.27 = (bf16[80,512]{1,0:T(8,128)(2,1)S(1)}, bf16[80,512]{1,0:T(8,128)(2,1)S(1)}, u32[]{:S(2)}, u32[]{:S(2)}) collective-permute-start(bf16[80,512]{1,0:T(8,128)(2,1)S(1)} %get-tuple-element.163), channel_id=1, source_target_pairs={{0,4},{1,5},{2,6},{3,7},{4,0},{5,1},{6,2},{7,3},{8,12},{9,13},{10,... | collective-permute-start | bytes 245768 | tf_op jit(solution)/shard_map/swap_A0/ppermute | solution.py:108
  114.7 12.5 %collective-permute-start.30 = (bf16[256,512]{1,0:T(8,128)(2,1)S(1)}, bf16[256,512]{1,0:T(8,128)(2,1)S(1)}, u32[]{:S(2)}, u32[]{:S(2)}) collective-permute-start(bf16[256,512]{1,0:T(8,128)(2,1)S(1)} %get-tuple-element.164), channel_id=1, source_target_pairs={{0,16},{8,24},{16,0},{24,8},{1,17},{9,25},{17,1},{25,9},{2,18},{10... | collective-permute-start | bytes 786440 | tf_op jit(solution)/shard_map/swap_B0/ppermute | solution.py:108
  123.3 5.5 %collective-permute-start.29 = (bf16[80,512]{1,0:T(8,128)(2,1)S(1)}, bf16[80,512]{1,0:T(8,128)(2,1)S(1)}, u32[]{:S(2)}, u32[]{:S(2)}) collective-permute-start(bf16[80,512]{1,0:T(8,128)(2,1)S(1)} %scatter.33.refs_2_.refs_0_), channel_id=1, source_target_pairs={{0,4},{1,5},{2,6},{3,7},{4,0},{5,1},{6,2},{7,3},{8,12},{9,13},{10,... | collective-permute-start | bytes 245768 | tf_op jit(solution)/shard_map/swap_A0/ppermute | solution.py:108
  123.5 7.1 %collective-permute-start.28 = (bf16[160,512]{1,0:T(8,128)(2,1)S(1)}, bf16[160,512]{1,0:T(8,128)(2,1)S(1)}, u32[]{:S(2)}, u32[]{:S(2)}) collective-permute-start(bf16[160,512]{1,0:T(8,128)(2,1)S(1)} %gather.16.refs_2_.refs_0_), channel_id=1, source_target_pairs={{0,2},{1,3},{2,0},{3,1},{4,6},{5,7},{6,4},{7,5},{8,10},{9,11},{10,... | collective-permute-start | bytes 491528 | tf_op jit(solution)/shard_map/swap_A1/ppermute | solution.py:108
  125.5 8.6 %collective-permute-start.25 = (bf16[272,512]{1,0:T(8,128)(2,1)S(1)}, bf16[272,512]{1,0:T(8,128)(2,1)S(1)}, u32[]{:S(2)}, u32[]{:S(2)}) collective-permute-start(bf16[272,512]{1,0:T(8,128)(2,1)S(1)} %get-tuple-element.162), channel_id=1, source_target_pairs={{0,1},{1,0},{2,3},{3,2},{4,5},{5,4},{6,7},{7,6},{8,9},{9,8},{10,11... | collective-permute-start | bytes 835592 | tf_op jit(solution)/shard_map/swap_B1/ppermute | solution.py:108
  127.2 11.6 %collective-permute-start.32 = (bf16[128,512]{1,0:T(8,128)(2,1)S(1)}, bf16[128,512]{1,0:T(8,128)(2,1)S(1)}, u32[]{:S(2)}, u32[]{:S(2)}) collective-permute-start(bf16[128,512]{1,0:T(8,128)(2,1)S(1)} %get-tuple-element.168), channel_id=1, source_target_pairs={{0,2},{1,3},{2,0},{3,1},{4,6},{5,7},{6,4},{7,5},{8,10},{9,11},{10,... | collective-permute-start | bytes 393224 | tf_op jit(solution)/shard_map/swap_B0/ppermute | solution.py:108
  128.9 8.4 %collective-permute-start.33 = (bf16[160,512]{1,0:T(8,128)(2,1)S(1)}, bf16[160,512]{1,0:T(8,128)(2,1)S(1)}, u32[]{:S(2)}, u32[]{:S(2)}) collective-permute-start(bf16[160,512]{1,0:T(8,128)(2,1)S(1)} %gather.17.refs_2_.refs_0_), channel_id=1, source_target_pairs={{0,2},{1,3},{2,0},{3,1},{4,6},{5,7},{6,4},{7,5},{8,10},{9,11},{10,... | collective-permute-start | bytes 491528 | tf_op jit(solution)/shard_map/swap_A0/ppermute | solution.py:108
  130.6 11.4 %collective-permute-start.36 = (bf16[320,512]{1,0:T(8,128)(2,1)S(1)}, bf16[320,512]{1,0:T(8,128)(2,1)S(1)}, u32[]{:S(2)}, u32[]{:S(2)}) collective-permute-start(bf16[320,512]{1,0:T(8,128)(2,1)S(1)} %gather.18.refs_2_.refs_0_), channel_id=1, source_target_pairs={{0,1},{1,0},{2,3},{3,2},{4,5},{5,4},{6,7},{7,6},{8,9},{9,8},{10,11... | collective-permute-start | bytes 983048 | tf_op jit(solution)/shard_map/swap_A1/ppermute | solution.py:108
  134.2 6.3 %collective-permute-start.31 = (bf16[144,512]{1,0:T(8,128)(2,1)S(1)}, bf16[144,512]{1,0:T(8,128)(2,1)S(1)}, u32[]{:S(2)}, u32[]{:S(2)}) collective-permute-start(bf16[144,512]{1,0:T(8,128)(2,1)S(1)} %get-tuple-element.167), channel_id=1, source_target_pairs={{0,2},{1,3},{2,0},{3,1},{4,6},{5,7},{6,4},{7,5},{8,10},{9,11},{10,... | collective-permute-start | bytes 442376 | tf_op jit(solution)/shard_map/swap_B1/ppermute | solution.py:108
  137.3 12.5 %collective-permute-start.40 = (bf16[320,512]{1,0:T(8,128)(2,1)S(1)}, bf16[320,512]{1,0:T(8,128)(2,1)S(1)}, u32[]{:S(2)}, u32[]{:S(2)}) collective-permute-start(bf16[320,512]{1,0:T(8,128)(2,1)S(1)} %gather.19.refs_2_.refs_0_), channel_id=1, source_target_pairs={{0,16},{8,24},{16,0},{24,8},{1,17},{9,25},{17,1},{25,9},{2,18},{10... | collective-permute-start | bytes 983048 | tf_op jit(solution)/shard_map/swap_A0/ppermute | solution.py:108
  138.9 6.7 %collective-permute-start.35 = (bf16[64,512]{1,0:T(8,128)(2,1)S(1)}, bf16[64,512]{1,0:T(8,128)(2,1)S(1)}, u32[]{:S(2)}, u32[]{:S(2)}) collective-permute-start(bf16[64,512]{1,0:T(8,128)(2,1)S(1)} %get-tuple-element.172), channel_id=1, source_target_pairs={{0,4},{1,5},{2,6},{3,7},{4,0},{5,1},{6,2},{7,3},{8,12},{9,13},{10,... | collective-permute-start | bytes 196616 | tf_op jit(solution)/shard_map/swap_B0/ppermute | solution.py:108
  140.5 8.4 %collective-permute-start.34 = (bf16[80,512]{1,0:T(8,128)(2,1)S(1)}, bf16[80,512]{1,0:T(8,128)(2,1)S(1)}, u32[]{:S(2)}, u32[]{:S(2)}) collective-permute-start(bf16[80,512]{1,0:T(8,128)(2,1)S(1)} %get-tuple-element.171), channel_id=1, source_target_pairs={{0,4},{1,5},{2,6},{3,7},{4,0},{5,1},{6,2},{7,3},{8,12},{9,13},{10,... | collective-permute-start | bytes 245768 | tf_op jit(solution)/shard_map/swap_B1/ppermute | solution.py:108
  142.0 16.7 %collective-permute-start.37 = (bf16[640,512]{1,0:T(8,128)(2,1)S(1)}, bf16[640,512]{1,0:T(8,128)(2,1)S(1)}, u32[]{:S(2)}, u32[]{:S(2)}) collective-permute-start(bf16[640,512]{1,0:T(8,128)(2,1)S(1)} %gather.20.refs_2_.refs_0_), channel_id=1, source_target_pairs={{0,16},{8,24},{16,0},{24,8},{1,17},{9,25},{17,1},{25,9},{2,18},{10... | collective-permute-start | bytes 1966088 | tf_op jit(solution)/shard_map/swap_A1/ppermute | solution.py:108
  145.6 5.9 %collective-permute-start.39 = (bf16[64,512]{1,0:T(8,128)(2,1)S(1)}, bf16[64,512]{1,0:T(8,128)(2,1)S(1)}, u32[]{:S(2)}, u32[]{:S(2)}) collective-permute-start(bf16[64,512]{1,0:T(8,128)(2,1)S(1)} %scatter.38.refs_2_.refs_0_), channel_id=1, source_target_pairs={{0,4},{1,5},{2,6},{3,7},{4,0},{5,1},{6,2},{7,3},{8,12},{9,13},{10,... | collective-permute-start | bytes 196616 | tf_op jit(solution)/shard_map/swap_B0/ppermute | solution.py:108
  148.9 6.8 %collective-permute-start.38 = (bf16[64,512]{1,0:T(8,128)(2,1)S(1)}, bf16[64,512]{1,0:T(8,128)(2,1)S(1)}, u32[]{:S(2)}, u32[]{:S(2)}) collective-permute-start(bf16[64,512]{1,0:T(8,128)(2,1)S(1)} %get-tuple-element.174.refs_2_.refs_0_), channel_id=1, source_target_pairs={{0,4},{1,5},{2,6},{3,7},{4,0},{5,1},{6,2},{7,3},{8,12},{9,13},{10,... | collective-permute-start | bytes 196616 | tf_op jit(solution)/shard_map/swap_B1/ppermute | solution.py:108
  149.8 12.2 %collective-permute-start.42 = (bf16[640,512]{1,0:T(8,128)(2,1)S(1)}, bf16[640,512]{1,0:T(8,128)(2,1)S(1)}, u32[]{:S(2)}, u32[]{:S(2)}) collective-permute-start(bf16[640,512]{1,0:T(8,128)(2,1)S(1)} %gather.21.refs_2_.refs_0_), channel_id=1, source_target_pairs={{0,1},{1,0},{2,3},{3,2},{4,5},{5,4},{6,7},{7,6},{8,9},{9,8},{10,11... | collective-permute-start | bytes 1966088 | tf_op jit(solution)/shard_map/swap_A0/ppermute | solution.py:108
  151.4 7.4 %collective-permute-start.44 = (bf16[128,512]{1,0:T(8,128)(2,1)S(1)}, bf16[128,512]{1,0:T(8,128)(2,1)S(1)}, u32[]{:S(2)}, u32[]{:S(2)}) collective-permute-start(bf16[128,512]{1,0:T(8,128)(2,1)S(1)} %gather.22.refs_2_.refs_0_), channel_id=1, source_target_pairs={{0,2},{1,3},{2,0},{3,1},{4,6},{5,7},{6,4},{7,5},{8,10},{9,11},{10,... | collective-permute-start | bytes 393224 | tf_op jit(solution)/shard_map/swap_B0/ppermute | solution.py:108
  155.7 5.0 %collective-permute-start.43 = (bf16[128,512]{1,0:T(8,128)(2,1)S(1)}, bf16[128,512]{1,0:T(8,128)(2,1)S(1)}, u32[]{:S(2)}, u32[]{:S(2)}) collective-permute-start(bf16[128,512]{1,0:T(8,128)(2,1)S(1)} %gather.23.refs_2_.refs_0_), channel_id=1, source_target_pairs={{0,2},{1,3},{2,0},{3,1},{4,6},{5,7},{6,4},{7,5},{8,10},{9,11},{10,... | collective-permute-start | bytes 393224 | tf_op jit(solution)/shard_map/swap_B1/ppermute | solution.py:108
  158.8 16.1 %collective-permute-start.41 = (bf16[1280,512]{1,0:T(8,128)(2,1)S(1)}, bf16[1280,512]{1,0:T(8,128)(2,1)S(1)}, u32[]{:S(2)}, u32[]{:S(2)}) collective-permute-start(bf16[1280,512]{1,0:T(8,128)(2,1)S(1)} %gather.24.refs_2_.refs_0_), channel_id=1, source_target_pairs={{0,8},{8,0},{16,24},{24,16},{1,9},{9,1},{17,25},{25,17},{2,10},{10... | collective-permute-start | bytes 3932168 | tf_op jit(solution)/shard_map/swap_A1/ppermute | solution.py:108
  158.9 8.8 %collective-permute-start.46 = (bf16[256,512]{1,0:T(8,128)(2,1)S(1)}, bf16[256,512]{1,0:T(8,128)(2,1)S(1)}, u32[]{:S(2)}, u32[]{:S(2)}) collective-permute-start(bf16[256,512]{1,0:T(8,128)(2,1)S(1)} %gather.25.refs_2_.refs_0_), channel_id=1, source_target_pairs={{0,16},{8,24},{16,0},{24,8},{1,17},{9,25},{17,1},{25,9},{2,18},{10... | collective-permute-start | bytes 786440 | tf_op jit(solution)/shard_map/swap_B0/ppermute | solution.py:108
  160.7 8.5 %collective-permute-start.45 = (bf16[256,512]{1,0:T(8,128)(2,1)S(1)}, bf16[256,512]{1,0:T(8,128)(2,1)S(1)}, u32[]{:S(2)}, u32[]{:S(2)}) collective-permute-start(bf16[256,512]{1,0:T(8,128)(2,1)S(1)} %gather.26.refs_2_.refs_0_), channel_id=1, source_target_pairs={{0,1},{1,0},{2,3},{3,2},{4,5},{5,4},{6,7},{7,6},{8,9},{9,8},{10,11... | collective-permute-start | bytes 786440 | tf_op jit(solution)/shard_map/swap_B1/ppermute | solution.py:108
  162.2 14.9 %collective-permute-start.48 = (bf16[1280,512]{1,0:T(8,128)(2,1)S(1)}, bf16[1280,512]{1,0:T(8,128)(2,1)S(1)}, u32[]{:S(2)}, u32[]{:S(2)}) collective-permute-start(bf16[1280,512]{1,0:T(8,128)(2,1)S(1)} %gather.27.refs_2_.refs_0_), channel_id=1, source_target_pairs={{0,8},{8,0},{16,24},{24,16},{1,9},{9,1},{17,25},{25,17},{2,10},{10... | collective-permute-start | bytes 3932168 | tf_op jit(solution)/shard_map/swap_A0/ppermute | solution.py:108
  167.7 13.6 %collective-permute-start.47 = (bf16[512,512]{1,0:T(8,128)(2,1)S(1)}, bf16[512,512]{1,0:T(8,128)(2,1)S(1)}, u32[]{:S(2)}, u32[]{:S(2)}) collective-permute-start(bf16[512,512]{1,0:T(8,128)(2,1)S(1)} %gather.28.refs_2_.refs_0_), channel_id=1, source_target_pairs={{0,1},{1,0},{2,3},{3,2},{4,5},{5,4},{6,7},{7,6},{8,9},{9,8},{10,11... | collective-permute-start | bytes 1572872 | tf_op jit(solution)/shard_map/swap_B0/ppermute | solution.py:108
  169.3 13.7 %collective-permute-start.50 = (bf16[512,512]{1,0:T(8,128)(2,1)S(1)}, bf16[512,512]{1,0:T(8,128)(2,1)S(1)}, u32[]{:S(2)}, u32[]{:S(2)}) collective-permute-start(bf16[512,512]{1,0:T(8,128)(2,1)S(1)} %gather.29.refs_1_.refs_0_), channel_id=1, source_target_pairs={{0,16},{8,24},{16,0},{24,8},{1,17},{9,25},{17,1},{25,9},{2,18},{10... | collective-permute-start | bytes 1572872 | tf_op jit(solution)/shard_map/swap_B1/ppermute | solution.py:108
  (15 other events, 84.7 us)

commit v5 on v4

--- a/solution.py
+++ b/solution.py
@@ -25,10 +25,10 @@
 EACH = 5
 
 EVENTS = (
-    "A1", "A0", "K", "V", "A1", "A0", "V", "K", "A1", "K", "TK", "V", "TV", "A0", "A1", "B0",
-    "B1", "A1", "A0", "B0", "B1", "A0", "A1", "B0", "A0", "A1", "B1", "A0", "B0", "B1", "A1",
-    "B0", "B1", "A0", "B0", "B1", "A1", "B0", "B1", "A0", "B0", "B1", "A0n", "A1n", "A1f", "A0f",
-    "B0", "B0n", "B1", "B0f", "B1n", "B1f",
+    "A0", "A1", "K", "V", "A1", "A0", "V", "K", "A1", "K", "V", "TK", "TV", "T3", "A0", "A1",
+    "B2", "B1", "B0", "A0", "A1", "B1", "B2", "B0", "A0", "A1", "B1", "B2", "A0", "A1", "B0",
+    "B2", "B1", "A0", "A1", "B0", "B2", "B1", "A0", "B0", "B2", "B1", "B0", "A1", "B2", "B1",
+    "B0", "A0", "B2", "B0", "B1", "B2", "Af", "B0", "B1", "Bn", "Bf",
 )
 
 BF16 = jnp.bfloat16
@@ -218,7 +218,7 @@
 def project_kernel(
     tokens_far, gain_far, segments_far, w_query, w_key, w_value, conv_key, conv_value,
     x_out, normed_out, query_out, key_out, value_out, segment_out, packed_key, packed_value,
-    query_here, key_here, value_here, conv_key_here, conv_value_here, tokens, gain, segments,
+    conv_key_here, conv_value_here, query_here, key_here, value_here, tokens, gain, segments,
     arrived,
 ):
     ready = fetch_all(
@@ -473,13 +473,27 @@
             q = value_spot[p]
             value_target[spot, lanes] = value_sums[q * slots : (q + 1) * slots]
 
-    each(attend_back)
-
-    for c in range(total_width // chunk):
+    def weight_piece(number):
+        c = number // 2
         columns = slice(c * chunk, (c + 1) * chunk)
-        down_rows[columns, :] = dot_tn(activated_out[:, columns], cotangent_out[...]).astype(BF16)
-        up_rows[c] = dot_tn(normed_ffn_out[...], d_expanded_out[:, columns]).astype(BF16)
-    out_rows[...] = dot_tn(attended_out[...], d_branch_out[...]).astype(BF16)
+        if c == total_width // chunk:
+            out_rows[...] = dot_tn(attended_out[...], d_branch_out[...]).astype(BF16)
+        elif number % 2 == 0:
+            product = dot_tn(activated_out[:, columns], cotangent_out[...])
+            down_rows[columns, :] = product.astype(BF16)
+        else:
+            up_rows[c] = dot_tn(normed_ffn_out[...], d_expanded_out[:, columns]).astype(BF16)
+
+    pieces = list(range(2 * (total_width // chunk) + 1))
+
+    def attend_back_and_weigh(number):
+        attend_back(number)
+        if short and pieces:
+            weight_piece(pieces.pop(0))
+
+    each(attend_back_and_weigh)
+    while pieces:
+        weight_piece(pieces.pop(0))
     query_rows[...] = dot_tn(normed_in[...], d_query_out[...]).astype(BF16)
     _, mine = own_places(plan)
     thin = width // plan.blocks
@@ -502,58 +516,47 @@
                 start += rows
 
 
-def conv_grads(
-    plan, order, segment_column, d_packed, flat, own, conv, normed, conv_rows, flat_rows, send, keep
+def conv_grad_kernel(
+    plan, order, segment_column, d_packed, flat, own, conv, send, keep, d_flat_out, conv_rows
 ):
     batch, length, _ = segment_column.shape
     width = conv.shape[1]
     slots = length // 3
     masks = [window_masks(segment_column[b], slots) for b in range(batch)]
     back = d_packed[...]
-    pieces = [[None] * 3 for _ in range(batch)]
     for i in range(3):
         taps = []
-        from_tap = dot_nt(back, conv[i * width : (i + 1) * width, :])
         for b in range(batch):
             start = b * length + i * slots
             part = flat[start : start + slots, :].astype(F32) * masks[b][i]
             taps.append(part.astype(BF16))
-            pieces[b][i] = from_tap[b * slots : (b + 1) * slots] * masks[b][i]
         window = jnp.concatenate(taps, axis=0)
         conv_rows[i * width : (i + 1) * width, :] = dot_tn(window, back).astype(BF16)
-    whole = jnp.concatenate([piece for row in pieces for piece in row], axis=0)
-    d_flat = (whole + own[...]).astype(BF16)
-    flat_rows[...] = dot_tn(normed[...], d_flat).astype(BF16)
     _, mine = own_places(plan)
-    parts = ((conv_rows, 3 * width // plan.blocks), (flat_rows, width // plan.blocks))
-    spread(plan, mine, order, parts, send, keep)
-    return d_flat
-
-
-def key_grad_kernel(
-    plan, order, segment_column, d_packed, flat, own, conv, normed,
-    send, keep, d_flat_out, conv_rows, flat_rows,
-):
-    d_flat_out[...] = conv_grads(
-        plan, order, segment_column, d_packed, flat, own, conv, normed, conv_rows, flat_rows,
-        send, keep,
-    )
-
-
-def value_grad_kernel(
-    plan, order, segment_column, d_packed, flat, own, conv, normed,
-    x_in, gain, d_query, d_keys, d_hidden, gain_ffn_grad, w_query, w_key, w_value,
-    send, keep, grad_tokens, conv_rows, flat_rows,
+    spread(plan, mine, order, ((conv_rows, 3 * width // plan.blocks),), send, keep)
+    for i in range(3):
+        from_tap = dot_nt(back, conv[i * width : (i + 1) * width, :])
+        for b in range(batch):
+            start = b * length + i * slots
+            part = from_tap[b * slots : (b + 1) * slots] * masks[b][i]
+            d_flat_out[start : start + slots, :] = (part + own[start : start + slots, :]).astype(BF16)
+
+
+def tail_kernel(
+    plan, order, normed, x_in, gain, d_query, d_keys, d_values, d_hidden, gain_ffn_grad,
+    w_query, w_key, w_value,
+    send, keep, grad_tokens, key_rows, value_rows,
 ):
     batch, _, length, width = grad_tokens.shape
-    d_values = conv_grads(
-        plan, order, segment_column, d_packed, flat, own, conv, normed, conv_rows, flat_rows,
-        send, keep,
-    )
+    key_rows[...] = dot_tn(normed[...], d_keys[...]).astype(BF16)
+    value_rows[...] = dot_tn(normed[...], d_values[...]).astype(BF16)
+    _, mine = own_places(plan)
+    thin = width // plan.blocks
+    spread(plan, mine, order, ((key_rows, thin), (value_rows, thin)), send, keep)
     d_normed = (
         dot_nt(d_query[...], w_query[...])
         + dot_nt(d_keys[...], w_key[...])
-        + dot_nt(d_values, w_value[...])
+        + dot_nt(d_values[...], w_value[...])
     )
     unit, inverse_dev = normalize(x_in[...])
     gain_grad = jnp.sum(d_normed * unit, axis=0, keepdims=True)
@@ -569,29 +572,53 @@
     keep[keep.shape[0] - EXTRA_ROWS :, :] = gains.astype(BF16)
 
 
-def finish_kernel(plan, layout, parts, core, count, *refs):
-    blocks, refs = refs[0], refs[1 + core * count :]
-    targets, (token, stage, sent) = refs[:count], refs[count:]
+def finish_kernel(plan, items, count, aliased, *refs):
+    blocks, refs = refs[: len(items)], refs[len(items) + (count if aliased else 0) :]
+    targets, (token, sent, *stages) = refs[:count], refs[count:]
     token[...] = jnp.zeros_like(token)
     _, mine = own_places(plan)
     half = plan.blocks // 2
     copies = []
-    start = 0
-    for p in range(half):
-        block = plan.relative(layout, core * half + p) ^ mine
-        for rows, target, columns in parts:
-            stage[start : start + rows, :] = blocks[start : start + rows, :].astype(F32)
-            spot = pl.ds(pl.multiple_of(block * rows, 16), rows)
-            copy = pltpu.make_async_copy(
-                stage.at[pl.ds(start, rows), :],
-                targets[target].at[spot, columns],
-                sent.at[len(copies)],
-            )
-            copy.start()
-            copies.append(copy)
-            start += rows
+    for source, stage, (layout, parts, core) in zip(blocks, stages, items):
+        start = 0
+        for p in range(half):
+            block = plan.relative(layout, core * half + p) ^ mine
+            for rows, target, columns in parts:
+                stage[start : start + rows, :] = source[start : start + rows, :].astype(F32)
+                spot = pl.ds(pl.multiple_of(block * rows, 16), rows)
+                copy = pltpu.make_async_copy(
+                    stage.at[pl.ds(start, rows), :],
+                    targets[target].at[spot, columns],
+                    sent.at[len(copies)],
+                )
+                copy.start()
+                copies.append(copy)
+                start += rows
     for copy in copies:
         copy.wait()
+
+
+def finish(plan, order, name, chosen, cores, targets=()):
+    items, blocks, shapes = [], [], []
+    for part in chosen:
+        for core in cores:
+            parts = [(rows, len(shapes) + target, columns) for rows, target, columns in part.parts]
+            items.append((part.bits, parts, core))
+            blocks.append(part.far if core else part.held)
+        shapes += part.shapes
+    count = len(shapes)
+    everywhere = tuple(range(count))
+    copies = sum(plan.blocks // 2 * len(parts) for _, parts, _ in items)
+    return order.call(
+        functools.partial(finish_kernel, plan, items, count, bool(targets)),
+        name,
+        [(shape, F32) for shape in shapes] + [((8, LANES), F32)],
+        [pltpu.SemaphoreType.DMA((copies,))] + [pltpu.VMEM(array.shape, F32) for array in blocks],
+        anywhere=tuple(range(len(items), len(items) + count)) if targets else (),
+        out_anywhere=everywhere,
+        aliases={len(items) + number: number for number in everywhere} if targets else None,
+        token=count,
+    )(*blocks, *targets)[:count]
 
 
 class RowGather:
@@ -671,31 +698,12 @@
 
     def gather(self, bit, microseconds=EACH):
         arrived = self.plan.swap(self.held, bit, self.name)
-        if bit == self.plan.core:
-            self.far = arrived
-            return
         rows = self.held.shape[0]
         self.held, = self.order.combine(
             "gather", [self.held, arrived], [[(0, 0, rows), (1, 0, rows)]], microseconds
         )
-
-    def finish(self, core, *targets):
-        if core:
-            self.gather(self.plan.core)
-        blocks = self.far if core else self.held
-        count = len(self.shapes)
-        everywhere = tuple(range(count))
-        copies = self.plan.blocks // 2 * len(self.parts)
-        return self.order.call(
-            functools.partial(finish_kernel, self.plan, self.bits, self.parts, core, count),
-            "finish",
-            [(shape, F32) for shape in self.shapes] + [((8, LANES), F32)],
-            [pltpu.VMEM(blocks.shape, F32), pltpu.SemaphoreType.DMA((copies,))],
-            anywhere=tuple(range(1, count + 1)) if core else (),
-            out_anywhere=everywhere,
-            aliases={1 + number: number for number in everywhere} if core else None,
-            token=count,
-        )(blocks, *targets)[:count]
+        if self.done == 2 * len(self.bits) - 2:
+            self.far = self.plan.swap(self.held, self.plan.core, self.name)
 
 
 def body(
@@ -710,12 +718,17 @@
     square_here = pltpu.VMEM(square, BF16)
     conv_here = pltpu.VMEM(conv_key.shape, BF16)
     order = Order()
-    x, normed, queries, key_rows, value_rows, segment_column, packed_key, packed_value = order.call(
+    later = [conv_key, conv_value, w_query, w_key, w_value]
+    short = slots * plan.n_seq <= SHORT_ROW
+    (
+        x, normed, queries, key_rows, value_rows, segment_column, packed_key, packed_value, *here,
+    ) = order.call(
         project_kernel,
         "project",
         [flat32] + [flat] * 4 + [((batch, length, 1), F32)]
-        + [((batch * slots + EXTRA_ROWS, width), BF16), ((batch * slots, width), BF16)],
-        scratch=[square_here] * 3 + [conv_here] * 2
+        + [((batch * slots + EXTRA_ROWS, width), BF16), ((batch * slots, width), BF16)]
+        + ([(array.shape, BF16) for array in later] if short else []),
+        scratch=([] if short else [conv_here] * 2 + [square_here] * 3)
         + [
             pltpu.VMEM(tokens.shape, BF16), pltpu.VMEM(gain_attn.shape, BF16),
             pltpu.VMEM(segments.shape, jnp.int32), pltpu.SemaphoreType.DMA((8,)),
@@ -724,6 +737,7 @@
         token=5,
     )(tokens, gain_attn, segments, w_query, w_key, w_value, conv_key, conv_value)
 
+    later = here or later
     steps = len(plan.key_order)
     keys = RowGather("gather_keys", plan, order, packed_key, plan.key_order)
     values = RowGather("gather_values", plan, order, packed_value, plan.value_order)
@@ -733,7 +747,8 @@
 
     core = [plan.core]
     x_first, y_first = core + plan.first + plan.tail, core + plan.second + plan.tail
-    bits = {"A0": y_first, "A1": x_first, "B0": y_first, "B1": x_first}
+    z_first = core + plan.tail[:1] + plan.first + plan.tail[1:]
+    bits = {"A0": y_first, "A1": x_first, "B0": y_first, "B1": x_first, "B2": z_first}
     half = plan.blocks // 2
     thin, down_block, conv_block = (
         rows // plan.blocks for rows in (width, w_down.shape[0], conv_key.shape[0])
@@ -744,15 +759,15 @@
     layouts = {
         "A0": ([w_down.shape, square], [(down_block, 0, everything), (thin, 1, everything)]),
         "A1": ([w_up.shape, square], ups + [(thin, 1, everything)]),
-        "B0": ([conv_key.shape, square], [(conv_block, 0, everything), (thin, 1, everything)]),
-        "B1": ([conv_value.shape, square], [(conv_block, 0, everything), (thin, 1, everything)]),
+        "B0": ([conv_key.shape], [(conv_block, 0, everything)]),
+        "B1": ([conv_value.shape], [(conv_block, 0, everything)]),
+        "B2": ([square, square], [(thin, 0, everything), (thin, 1, everything)]),
     }
 
     def half_rows(name):
         return half * sum(part[0] for part in layouts[name][1])
 
     total_slots = slots * plan.n_seq
-    short = total_slots <= SHORT_ROW
     half_packed = ((batch * total_slots // 2, width), BF16)
     halves = [((half_rows(name), width), BF16) for name in ("A0", "A0", "A1", "A1")]
     flat_here = pltpu.VMEM((positions, width), BF16)
@@ -789,7 +804,7 @@
         RowScatter("K", plan, order, outs[0], outs[1], plan.key_order),
         RowScatter("V", plan, order, outs[2], outs[3], plan.value_order),
     ]
-    chains, results = {"K": rows[0], "V": rows[1]}, {}
+    chains, d_flats = {"K": rows[0], "V": rows[1]}, {}
     for name, (send, keep) in (("A0", outs[4:6]), ("A1", outs[6:8])):
         chains[name] = Part(name, plan, order, bits[name], send, keep, *layouts[name])
 
@@ -805,37 +820,40 @@
         return others
 
     for event in EVENTS:
-        if event == "TK":
-            while rows[0].bits:
-                rows[0].step()
-            d_keys, = make(
-                "B0", key_grad_kernel, [flat], [conv_here, square_here],
-                (segment_column, rows[0].keep, key_rows, d_key_own, conv_key, normed),
+        if event in ("TK", "TV"):
+            number = 0 if event == "TK" else 1
+            row = rows[number]
+            while row.bits:
+                row.step()
+            d_flat, = make(
+                f"B{number}", conv_grad_kernel, [flat], [conv_here],
+                (
+                    segment_column, row.keep, (key_rows, value_rows)[number],
+                    (d_key_own, d_value_own)[number], later[number],
+                ),
             )
-        elif event == "TV":
-            while rows[1].bits:
-                rows[1].step()
+            d_flats[event] = d_flat
+        elif event == "T3":
             grad_tokens, = make(
-                "B1", value_grad_kernel, [(tokens.shape, BF16)], [conv_here, square_here],
+                "B2", tail_kernel, [(tokens.shape, BF16)], [square_here, square_here],
                 (
-                    segment_column, rows[1].keep, value_rows, d_value_own, conv_value, normed,
-                    x, gain_attn, d_query, d_keys, d_hidden, gain_ffn_grad,
-                    w_query, w_key, w_value,
+                    normed, x, gain_attn, d_query, d_flats["TK"], d_flats["TV"], d_hidden,
+                    gain_ffn_grad, *later[2:],
                 ),
                 EXTRA_ROWS,
             )
-        elif event[2:] == "n":
-            results[event[:2]] = chains[event[:2]].finish(0)
-        elif event[2:] == "f":
-            results[event[:2]] = chains[event[:2]].finish(1, *results[event[:2]])
+        elif event == "Af":
+            grads = finish(plan, order, "finish", [chains["A0"], chains["A1"]], (0, 1))
+            grad_down, grad_out, grad_up, grad_query = grads
+        elif event in ("Bn", "Bf"):
+            chosen = [chains[name] for name in ("B0", "B1", "B2")]
+            previous = () if event == "Bn" else results
+            results = finish(plan, order, "finish", chosen, (int(event == "Bf"),), previous)
         else:
             name, _, cost = event.partition(":")
             chains[name].step(float(cost or EACH))
-    grad_down, grad_out = results["A0"]
-    grad_up, grad_query = results["A1"]
-    grad_conv_key, grad_key = results["B0"]
-    grad_conv_value, grad_value = results["B1"]
-    gains = chains["B1"].sums[0].astype(F32)
+    grad_conv_key, grad_conv_value, grad_key, grad_value = results
+    gains = chains["B2"].sums[0].astype(F32)
     return (
         layer_out, grad_tokens, gains[0], grad_query, grad_key, grad_value,
         grad_conv_key, grad_conv_value, grad_out, gains[1], grad_up, grad_down,

time: 190 us -> 183 us (0.963)
  waiting for transfers between devices: 76.8 us -> 60.8 us
  starting transfers between devices: 65.3 us -> 80.7 us
  local copies, waits for them, and re-layouts: 3.67 us -> 0.62 us
  Pallas kernels: 42.5 us -> 39.7 us
    ppermute x52 -> x62, waiting for transfers between devices: 76.8 us -> 60.8 us  [swap(): return lax.ppermute(array, axis, [(i, i ^ value) for i in range(size)])]
    ppermute x52 -> x62, starting transfers between devices: 65.3 us -> 80.7 us  [swap(): return lax.ppermute(array, axis, [(i, i ^ value) for i in range(size)])]
    unnamed x22 -> x12, local copies, waits for them, and re-layouts: 3.08 us -> 0.04 us
    pallas_call x58 -> x63, Pallas kernels: 42.5 us -> 39.7 us  [run(): pl.pallas_call(without_last, name=name, out_shape=[pltpu.HBM(shape, dtype...]
  transfers between devices with their start and end apart: 52 -> 62, of which waited for: 23 -> 24; matrix products, arithmetic and copies ran while one was open for 0% -> 0% of each run, Pallas kernels for 11% -> 9%
where the time goes in v5:
time: 183 us
  starting transfers between devices  80.7 us (44%)
  waiting for transfers between devices  60.8 us (33%)
  Pallas kernels  39.7 us (22%)
    ppermute x62, starting transfers between devices, swap(): return lax.ppermute(array, axis, [(i, i ^ value) for i in range(size)])  80.7 us
    ppermute x62, waiting for transfers between devices, swap(): return lax.ppermute(array, axis, [(i, i ^ value) for i in range(size)])  60.8 us
    pallas_call x63, Pallas kernels, run(): pl.pallas_call(without_last, name=name, out_shape=[pltpu.HBM(shape, dtype...  39.7 us
  transfers between devices with their start and end apart: 62, of which 24 were waited for; matrix products, arithmetic and copies ran while one was open for 0% of the time, Pallas kernels for 9%

profile of v5, /device:TPU:0, one launch (start us, length us, event | category | flops | bytes accessed | tf_op | source)
XLA Modules:
  0.0 183.1 jit_solution(290158302598603828)
XLA Ops:
  0.6 3.3 %project.1 = (f32[288,512]{1,0:T(8,128)S(1)}, bf16[288,512]{1,0:T(8,128)(2,1)S(1)}, bf16[288,512]{1,0:T(8,128)(2,1)S(1)}, bf16[288,512]{1,0:T(8,128)(2,1)S(1)}, ...) custom-call(bf16[2,1,144,512]{3,2,1,0:T(8,128)(2,1)} %refs_0_.1, ...), custom_call_target="tpu_custom_call" | custom-call | flops 5750000128 | bytes 18450000 | tf_op jit(solution)/shard_map/project/pallas_call | solution.py:162
  4.0 4.1 %collective-permute-start = (bf16[112,512]{1,0:T(8,128)(2,1)S(1)}, bf16[112,512]{1,0:T(8,128)(2,1)S(1)}, u32[]{:S(2)}, u32[]{:S(2)}) collective-permute-start(bf16[112,512]{1,0:T(8,128)(2,1)S(1)} %get-tuple-element.118.refs_0_), channel_id=1, source_target_pairs={{0,4},{1,5},{2,6},{3,7},{4,0},{5,1},{6,2},{7,3},{8,12},{9,13},{10,... | collective-permute-start | bytes 344072 | tf_op jit(solution)/shard_map/swap_gather_keys/ppermute | solution.py:108
  9.6 4.1 %collective-permute-done.refs_1_ = bf16[112,512]{1,0:T(8,128)(2,1)S(1)} collective-permute-done((bf16[112,512]{1,0:T(8,128)(2,1)S(1)}, bf16[112,512]{1,0:T(8,128)(2,1)S(1)}, u32[]{:S(2)}, u32[]{:S(2)}) %collective-permute-start) | collective-permute-done | bytes 114720 | tf_op jit(solution)/shard_map/swap_gather_keys/ppermute | solution.py:108
  14.5 3.4 %collective-permute-start.4 = (bf16[192,512]{1,0:T(8,128)(2,1)S(1)}, bf16[192,512]{1,0:T(8,128)(2,1)S(1)}, u32[]{:S(2)}, u32[]{:S(2)}) collective-permute-start(bf16[192,512]{1,0:T(8,128)(2,1)S(1)} %gather_row.5.refs_2_.refs_0_), channel_id=1, source_target_pairs={{0,4},{1,5},{2,6},{3,7},{4,0},{5,1},{6,2},{7,3},{8,12},{9,13},{10,... | collective-permute-start | bytes 589832 | tf_op jit(solution)/shard_map/swap_gather_values/ppermute | solution.py:108
  18.0 6.8 %collective-permute-done.1.refs_1_ = bf16[224,512]{1,0:T(8,128)(2,1)S(1)} collective-permute-done((bf16[224,512]{1,0:T(8,128)(2,1)S(1)}, bf16[224,512]{1,0:T(8,128)(2,1)S(1)}, u32[]{:S(2)}, u32[]{:S(2)}) %collective-permute-start.1) | collective-permute-done | bytes 229408 | tf_op jit(solution)/shard_map/swap_gather_keys/ppermute | solution.py:108
  26.2 1.7 collective-permute-start.5
  28.0 8.8 %collective-permute-done.5.refs_11_ = bf16[384,512]{1,0:T(8,128)(2,1)S(1)} collective-permute-done((bf16[384,512]{1,0:T(8,128)(2,1)S(1)}, bf16[384,512]{1,0:T(8,128)(2,1)S(1)}, u32[]{:S(2)}, u32[]{:S(2)}) %collective-permute-start.5) | collective-permute-done | bytes 393248 | tf_op jit(solution)/shard_map/swap_gather_values/ppermute | solution.py:108
  36.8 16.8 %layer.1 = (bf16[2,1,144,512]{3,2,1,0:T(8,128)(2,1)}, f32[288,512]{1,0:T(8,128)S(1)}, bf16[288,512]{1,0:T(8,128)(2,1)S(1)}, f32[288,512]{1,0:T(8,128)S(1)}, f32[...) custom-call(f32[288,512]{1,0:T(8,128)S(1)} %get-tuple-element.112.re, ...), custom_call_target="tpu_custom_call" | custom-call | flops 5750000128 | bytes 18450000 | tf_op jit(solution)/shard_map/layer/pallas_call | solution.py:162
  54.1 1.5 collective-permute-start.6
  55.7 1.8 collective-permute-start.10
  58.8 1.6 collective-permute-start.13
  61.9 4.2 %collective-permute-done.6.refs_1_ = bf16[384,512]{1,0:T(8,128)(2,1)S(1)} collective-permute-done((bf16[384,512]{1,0:T(8,128)(2,1)S(1)}, bf16[384,512]{1,0:T(8,128)(2,1)S(1)}, u32[]{:S(2)}, u32[]{:S(2)}) %collective-permute-start.6) | collective-permute-done | bytes 393248 | tf_op jit(solution)/shard_map/swap_K/ppermute | solution.py:108
  66.5 1.8 collective-permute-start.11
  68.3 1.7 collective-permute-start.9
  70.1 5.6 %collective-permute-done.13.refs_1_ = bf16[640,512]{1,0:T(8,128)(2,1)S(1)} collective-permute-done((bf16[640,512]{1,0:T(8,128)(2,1)S(1)}, bf16[640,512]{1,0:T(8,128)(2,1)S(1)}, u32[]{:S(2)}, u32[]{:S(2)}) %collective-permute-start.13) | collective-permute-done | bytes 655392 | tf_op jit(solution)/shard_map/swap_A1/ppermute | solution.py:108
  75.8 1.6 collective-permute-start.15
  77.4 2.7 %collective-permute-done.12.refs_1_ = bf16[640,512]{1,0:T(8,128)(2,1)S(1)} collective-permute-done((bf16[640,512]{1,0:T(8,128)(2,1)S(1)}, bf16[640,512]{1,0:T(8,128)(2,1)S(1)}, u32[]{:S(2)}, u32[]{:S(2)}) %collective-permute-start.12) | collective-permute-done | bytes 655392 | tf_op jit(solution)/shard_map/swap_A0/ppermute | solution.py:108
  80.4 1.8 %collective-permute-start.14 = (bf16[96,512]{1,0:T(8,128)(2,1)S(1)}, bf16[96,512]{1,0:T(8,128)(2,1)S(1)}, u32[]{:S(2)}, u32[]{:S(2)}) collective-permute-start(bf16[96,512]{1,0:T(8,128)(2,1)S(1)} %get-tuple-element.143), channel_id=1, source_target_pairs={{0,4},{1,5},{2,6},{3,7},{4,0},{5,1},{6,2},{7,3},{8,12},{9,13},{10,... | collective-permute-start | bytes 294920 | tf_op jit(solution)/shard_map/swap_K/ppermute | solution.py:108
  82.3 1.5 collective-permute-start.16
  85.3 1.9 %collective-permute-done.15.refs_1_ = bf16[320,512]{1,0:T(8,128)(2,1)S(1)} collective-permute-done((bf16[320,512]{1,0:T(8,128)(2,1)S(1)}, bf16[320,512]{1,0:T(8,128)(2,1)S(1)}, u32[]{:S(2)}, u32[]{:S(2)}) %collective-permute-start.15) | collective-permute-done | bytes 327712 | tf_op jit(solution)/shard_map/swap_A1/ppermute | solution.py:108
  87.3 1.8 collective-permute-start.18
  92.2 2.3 %tail_kernel.1 = (bf16[528,512]{1,0:T(8,128)(2,1)S(1)}, bf16[528,512]{1,0:T(8,128)(2,1)S(1)}, bf16[2,1,144,512]{3,2,1,0:T(8,128)(2,1)}) custom-call(bf16[288,512]{1,0:T(8,128)(2,1)S(1)} %get-tuple-element.113.refs_1_.refs_0_, f32[288,512]{1,0:T(8,128)S(1)} %get-tuple-element.112.refs_0_.refs_1_, bf16[512]{0:T(512)(128)(2,1)S(1)} %copy-done.5, ...), custom_call_target="tpu_custom_call" | custom-call | flops 5750000128 | bytes 18450000 | tf_op jit(solution)/shard_map/tail_kernel/pallas_call | solution.py:162
  95.7 1.8 %collective-permute-start.23 = (bf16[80,512]{1,0:T(8,128)(2,1)S(1)}, bf16[80,512]{1,0:T(8,128)(2,1)S(1)}, u32[]{:S(2)}, u32[]{:S(2)}) collective-permute-start(bf16[80,512]{1,0:T(8,128)(2,1)S(1)} %get-tuple-element.171), channel_id=1, source_target_pairs={{0,4},{1,5},{2,6},{3,7},{4,0},{5,1},{6,2},{7,3},{8,12},{9,13},{10,... | collective-permute-start | bytes 245768 | tf_op jit(solution)/shard_map/swap_A1/ppermute | solution.py:108
  99.0 1.6 collective-permute-start.22
  100.8 2.7 %collective-permute-done.24.refs_1_ = bf16[160,512]{1,0:T(8,128)(2,1)S(1)} collective-permute-done((bf16[160,512]{1,0:T(8,128)(2,1)S(1)}, bf16[160,512]{1,0:T(8,128)(2,1)S(1)}, u32[]{:S(2)}, u32[]{:S(2)}) %collective-permute-start.24) | collective-permute-done | bytes 163872 | tf_op jit(solution)/shard_map/swap_A0/ppermute | solution.py:108
  103.9 2.7 %collective-permute-start.28 = (bf16[80,512]{1,0:T(8,128)(2,1)S(1)}, bf16[80,512]{1,0:T(8,128)(2,1)S(1)}, u32[]{:S(2)}, u32[]{:S(2)}) collective-permute-start(bf16[80,512]{1,0:T(8,128)(2,1)S(1)} %scatter.36.refs_2_.refs_0_), channel_id=1, source_target_pairs={{0,4},{1,5},{2,6},{3,7},{4,0},{5,1},{6,2},{7,3},{8,12},{9,13},{10,... | collective-permute-start | bytes 245768 | tf_op jit(solution)/shard_map/swap_A1/ppermute | solution.py:108
  106.6 1.6 collective-permute-start.30
  108.1 1.6 collective-permute-done.22.refs_1_
  109.9 2.7 %collective-permute-done.20.refs_1_ = bf16[272,512]{1,0:T(8,128)(2,1)S(1)} collective-permute-done((bf16[272,512]{1,0:T(8,128)(2,1)S(1)}, bf16[272,512]{1,0:T(8,128)(2,1)S(1)}, u32[]{:S(2)}, u32[]{:S(2)}) %collective-permute-start.20) | collective-permute-done | bytes 278560 | tf_op jit(solution)/shard_map/swap_B2/ppermute | solution.py:108
  112.6 1.6 collective-permute-start.26
  117.3 2.3 %collective-permute-start.33 = (bf16[160,512]{1,0:T(8,128)(2,1)S(1)}, bf16[160,512]{1,0:T(8,128)(2,1)S(1)}, u32[]{:S(2)}, u32[]{:S(2)}) collective-permute-start(bf16[160,512]{1,0:T(8,128)(2,1)S(1)} %gather.20.refs_2_.refs_0_), channel_id=1, source_target_pairs={{0,2},{1,3},{2,0},{3,1},{4,6},{5,7},{6,4},{7,5},{8,10},{9,11},{10,... | collective-permute-start | bytes 491528 | tf_op jit(solution)/shard_map/swap_A1/ppermute | solution.py:108
  119.7 2.5 %collective-permute-start.32 = (bf16[192,512]{1,0:T(8,128)(2,1)S(1)}, bf16[192,512]{1,0:T(8,128)(2,1)S(1)}, u32[]{:S(2)}, u32[]{:S(2)}) collective-permute-start(bf16[192,512]{1,0:T(8,128)(2,1)S(1)} %get-tuple-element.186), channel_id=1, source_target_pairs={{0,16},{8,24},{16,0},{24,8},{1,17},{9,25},{17,1},{25,9},{2,18},{10... | collective-permute-start | bytes 589832 | tf_op jit(solution)/shard_map/swap_B0/ppermute | solution.py:108
  123.9 2.0 %collective-permute-start.38 = (bf16[160,512]{1,0:T(8,128)(2,1)S(1)}, bf16[160,512]{1,0:T(8,128)(2,1)S(1)}, u32[]{:S(2)}, u32[]{:S(2)}) collective-permute-start(bf16[160,512]{1,0:T(8,128)(2,1)S(1)} %gather.21.refs_2_.refs_0_), channel_id=1, source_target_pairs={{0,2},{1,3},{2,0},{3,1},{4,6},{5,7},{6,4},{7,5},{8,10},{9,11},{10,... | collective-permute-start | bytes 491528 | tf_op jit(solution)/shard_map/swap_A0/ppermute | solution.py:108
  126.6 1.9 %collective-permute-start.36 = (bf16[96,512]{1,0:T(8,128)(2,1)S(1)}, bf16[96,512]{1,0:T(8,128)(2,1)S(1)}, u32[]{:S(2)}, u32[]{:S(2)}) collective-permute-start(bf16[96,512]{1,0:T(8,128)(2,1)S(1)} %get-tuple-element.190), channel_id=1, source_target_pairs={{0,2},{1,3},{2,0},{3,1},{4,6},{5,7},{6,4},{7,5},{8,10},{9,11},{10,... | collective-permute-start | bytes 294920 | tf_op jit(solution)/shard_map/swap_B0/ppermute | solution.py:108
  129.7 1.9 %collective-permute-start.41 = (bf16[48,512]{1,0:T(8,128)(2,1)S(1)}, bf16[48,512]{1,0:T(8,128)(2,1)S(1)}, u32[]{:S(2)}, u32[]{:S(2)}) collective-permute-start(bf16[48,512]{1,0:T(8,128)(2,1)S(1)} %get-tuple-element.195), channel_id=1, source_target_pairs={{0,4},{1,5},{2,6},{3,7},{4,0},{5,1},{6,2},{7,3},{8,12},{9,13},{10,... | collective-permute-start | bytes 147464 | tf_op jit(solution)/shard_map/swap_B1/ppermute | solution.py:108
  131.6 2.7 %collective-permute-start.40 = (bf16[320,512]{1,0:T(8,128)(2,1)S(1)}, bf16[320,512]{1,0:T(8,128)(2,1)S(1)}, u32[]{:S(2)}, u32[]{:S(2)}) collective-permute-start(bf16[320,512]{1,0:T(8,128)(2,1)S(1)} %gather.23.refs_2_.refs_0_), channel_id=1, source_target_pairs={{0,16},{8,24},{16,0},{24,8},{1,17},{9,25},{17,1},{25,9},{2,18},{10... | collective-permute-start | bytes 983048 | tf_op jit(solution)/shard_map/swap_A0/ppermute | solution.py:108
  134.5 1.9 %collective-permute-start.46 = (bf16[32,512]{1,0:T(8,128)(2,1)S(1)}, bf16[32,512]{1,0:T(8,128)(2,1)S(1)}, u32[]{:S(2)}, u32[]{:S(2)}) collective-permute-start(bf16[32,512]{1,0:T(8,128)(2,1)S(1)} %get-tuple-element.196.refs_2_.refs_0_), channel_id=1, source_target_pairs={{0,4},{1,5},{2,6},{3,7},{4,0},{5,1},{6,2},{7,3},{8,12},{9,13},{10,... | collective-permute-start | bytes 98312 | tf_op jit(solution)/shard_map/swap_B2/ppermute | solution.py:108
  137.6 1.9 %collective-permute-start.43 = (bf16[48,512]{1,0:T(8,128)(2,1)S(1)}, bf16[48,512]{1,0:T(8,128)(2,1)S(1)}, u32[]{:S(2)}, u32[]{:S(2)}) collective-permute-start(bf16[48,512]{1,0:T(8,128)(2,1)S(1)} %get-tuple-element.197), channel_id=1, source_target_pairs={{0,4},{1,5},{2,6},{3,7},{4,0},{5,1},{6,2},{7,3},{8,12},{9,13},{10,... | collective-permute-start | bytes 147464 | tf_op jit(solution)/shard_map/swap_B0/ppermute | solution.py:108
  139.5 3.4 %collective-permute-done.40.refs_1_ = bf16[320,512]{1,0:T(8,128)(2,1)S(1)} collective-permute-done((bf16[320,512]{1,0:T(8,128)(2,1)S(1)}, bf16[320,512]{1,0:T(8,128)(2,1)S(1)}, u32[]{:S(2)}, u32[]{:S(2)}) %collective-permute-start.40) | collective-permute-done | bytes 327712 | tf_op jit(solution)/shard_map/swap_A0/ppermute | solution.py:108
  146.7 2.0 %collective-permute-start.48 = (bf16[96,512]{1,0:T(8,128)(2,1)S(1)}, bf16[96,512]{1,0:T(8,128)(2,1)S(1)}, u32[]{:S(2)}, u32[]{:S(2)}) collective-permute-start(bf16[96,512]{1,0:T(8,128)(2,1)S(1)} %gather.27.refs_2_.refs_0_), channel_id=1, source_target_pairs={{0,2},{1,3},{2,0},{3,1},{4,6},{5,7},{6,4},{7,5},{8,10},{9,11},{10,... | collective-permute-start | bytes 294920 | tf_op jit(solution)/shard_map/swap_B1/ppermute | solution.py:108
  150.2 4.0 %collective-permute-done.50.refs_1_ = bf16[640,512]{1,0:T(8,128)(2,1)S(1)} collective-permute-done((bf16[640,512]{1,0:T(8,128)(2,1)S(1)}, bf16[640,512]{1,0:T(8,128)(2,1)S(1)}, u32[]{:S(2)}, u32[]{:S(2)}) %collective-permute-start.50) | collective-permute-done | bytes 655392 | tf_op jit(solution)/shard_map/swap_A1/ppermute | solution.py:108
  155.5 1.5 collective-permute-start.53
  158.7 2.5 %collective-permute-done.53.refs_1_ = bf16[128,512]{1,0:T(8,128)(2,1)S(1)} collective-permute-done((bf16[128,512]{1,0:T(8,128)(2,1)S(1)}, bf16[128,512]{1,0:T(8,128)(2,1)S(1)}, u32[]{:S(2)}, u32[]{:S(2)}) %collective-permute-start.53) | collective-permute-done | bytes 131104 | tf_op jit(solution)/shard_map/swap_B2/ppermute | solution.py:108
  161.7 3.0 %collective-permute-done.56.refs_1_ = bf16[192,512]{1,0:T(8,128)(2,1)S(1)} collective-permute-done((bf16[192,512]{1,0:T(8,128)(2,1)S(1)}, bf16[192,512]{1,0:T(8,128)(2,1)S(1)}, u32[]{:S(2)}, u32[]{:S(2)}) %collective-permute-start.56) | collective-permute-done | bytes 196640 | tf_op jit(solution)/shard_map/swap_B0/ppermute | solution.py:108
  165.7 1.8 collective-permute-start.59
  167.7 5.8 %finish.3 = (f32[2048,512]{1,0:T(8,128)}, f32[512,512]{1,0:T(8,128)}, f32[512,2048]{1,0:T(8,128)}, f32[512,512]{1,0:T(8,128)}, f32[8,128]{1,0:T(8,128)S(1)}) custom-call(bf16[1280,512]{1,0:T(8,128)(2,1)S(1)} %gather.33.refs_2_.refs_0_, bf16[1280,512]{1,0:T(8,128)(2,1)S(1)} %collective-permute-done.51.refs_1_, bf16[1280,512]{1,0:T(8,128)(2,1)S(1)} %gather.29.refs_2_, ...), custom_call_target="tpu_custom_call" | custom-call | flops 5750000128 | bytes 18450000 | tf_op jit(solution)/shard_map/finish/pallas_call | solution.py:162
  176.8 2.6 %finish.4 = (f32[1536,512]{1,0:T(8,128)}, f32[1536,512]{1,0:T(8,128)}, f32[512,512]{1,0:T(8,128)}, f32[512,512]{1,0:T(8,128)}, f32[8,128]{1,0:T(8,128)S(1)}) custom-call(bf16[768,512]{1,0:T(8,128)(2,1)S(1)} %gather.38.refs_2_.refs_0_, bf16[768,512]{1,0:T(8,128)(2,1)S(1)} %gather.39.refs_1_.refs_3_, bf16[512,512]{1,0:T(8,128)(2,1)S(1)} %gather.37.refs_4_.refs_2_, ...), custom_call_target="tpu_custom_call" | custom-call | flops 5750000128 | bytes 18450000 | tf_op jit(solution)/shard_map/finish/pallas_call | solution.py:162
  179.8 3.2 %finish.5 = (f32[1536,512]{1,0:T(8,128)}, f32[1536,512]{1,0:T(8,128)}, f32[512,512]{1,0:T(8,128)}, f32[512,512]{1,0:T(8,128)}, f32[8,128]{1,0:T(8,128)}) custom-call(bf16[768,512]{1,0:T(8,128)(2,1)S(1)} %collective-permute-done.58.refs_0_, ...), custom_call_target="tpu_custom_call", output_to_operand_aliasing={{0}: (3, {}), {1}: (4, {}), {2}: (5, {}), {3}: (6, {})} | custom-call | flops 5750000128 | bytes 18450000 | tf_op jit(solution)/shard_map/finish/pallas_call | solution.py:162
  (152 shorter events, 37.7 us)
Async XLA Ops:
  4.0 9.7 %collective-permute-start = (bf16[112,512]{1,0:T(8,128)(2,1)S(1)}, bf16[112,512]{1,0:T(8,128)(2,1)S(1)}, u32[]{:S(2)}, u32[]{:S(2)}) collective-permute-start(bf16[112,512]{1,0:T(8,128)(2,1)S(1)} %get-tuple-element.118.refs_0_), channel_id=1, source_target_pairs={{0,4},{1,5},{2,6},{3,7},{4,0},{5,1},{6,2},{7,3},{8,12},{9,13},{10,... | collective-permute-start | bytes 344072 | tf_op jit(solution)/shard_map/swap_gather_keys/ppermute | solution.py:108
  13.7 11.1 %collective-permute-start.1 = (bf16[224,512]{1,0:T(8,128)(2,1)S(1)}, bf16[224,512]{1,0:T(8,128)(2,1)S(1)}, u32[]{:S(2)}, u32[]{:S(2)}) collective-permute-start(bf16[224,512]{1,0:T(8,128)(2,1)S(1)} %gather_row.4.refs_2_.refs_0_), channel_id=1, source_target_pairs={{0,2},{1,3},{2,0},{3,1},{4,6},{5,7},{6,4},{7,5},{8,10},{9,11},{10,... | collective-permute-start | bytes 688136 | tf_op jit(solution)/shard_map/swap_gather_keys/ppermute | solution.py:108
  14.5 11.7 %collective-permute-start.4 = (bf16[192,512]{1,0:T(8,128)(2,1)S(1)}, bf16[192,512]{1,0:T(8,128)(2,1)S(1)}, u32[]{:S(2)}, u32[]{:S(2)}) collective-permute-start(bf16[192,512]{1,0:T(8,128)(2,1)S(1)} %gather_row.5.refs_2_.refs_0_), channel_id=1, source_target_pairs={{0,4},{1,5},{2,6},{3,7},{4,0},{5,1},{6,2},{7,3},{8,12},{9,13},{10,... | collective-permute-start | bytes 589832 | tf_op jit(solution)/shard_map/swap_gather_values/ppermute | solution.py:108
  24.9 11.9 %collective-permute-start.3 = (bf16[448,512]{1,0:T(8,128)(2,1)S(1)}, bf16[448,512]{1,0:T(8,128)(2,1)S(1)}, u32[]{:S(2)}, u32[]{:S(2)}) collective-permute-start(bf16[448,512]{1,0:T(8,128)(2,1)S(1)} %gather_row.6.refs_2_.refs_8_), channel_id=1, source_target_pairs={{0,1},{1,0},{2,3},{3,2},{4,5},{5,4},{6,7},{7,6},{8,9},{9,8},{10,11... | collective-permute-start | bytes 1376264 | tf_op jit(solution)/shard_map/swap_gather_keys/ppermute | solution.py:108
  26.2 10.5 %collective-permute-start.5 = (bf16[384,512]{1,0:T(8,128)(2,1)S(1)}, bf16[384,512]{1,0:T(8,128)(2,1)S(1)}, u32[]{:S(2)}, u32[]{:S(2)}) collective-permute-start(bf16[384,512]{1,0:T(8,128)(2,1)S(1)} %gather_row.7.refs_10_.refs_15_), channel_id=1, source_target_pairs={{0,2},{1,3},{2,0},{3,1},{4,6},{5,7},{6,4},{7,5},{8,10},{9,11},{10,... | collective-permute-start | bytes 1179656 | tf_op jit(solution)/shard_map/swap_gather_values/ppermute | solution.py:108
  54.1 12.0 %collective-permute-start.6 = (bf16[384,512]{1,0:T(8,128)(2,1)S(1)}, bf16[384,512]{1,0:T(8,128)(2,1)S(1)}, u32[]{:S(2)}, u32[]{:S(2)}) collective-permute-start(bf16[384,512]{1,0:T(8,128)(2,1)S(1)} %get-tuple-element.123), channel_id=1, source_target_pairs={{0,1},{1,0},{2,3},{3,2},{4,5},{5,4},{6,7},{7,6},{8,9},{9,8},{10,11... | collective-permute-start | bytes 1179656 | tf_op jit(solution)/shard_map/swap_K/ppermute | solution.py:108
  55.7 10.8 %collective-permute-start.10 = (bf16[384,512]{1,0:T(8,128)(2,1)S(1)}, bf16[384,512]{1,0:T(8,128)(2,1)S(1)}, u32[]{:S(2)}, u32[]{:S(2)}) collective-permute-start(bf16[384,512]{1,0:T(8,128)(2,1)S(1)} %get-tuple-element.134), channel_id=1, source_target_pairs={{0,2},{1,3},{2,0},{3,1},{4,6},{5,7},{6,4},{7,5},{8,10},{9,11},{10,... | collective-permute-start | bytes 1179656 | tf_op jit(solution)/shard_map/swap_V/ppermute | solution.py:108
  58.8 16.8 %collective-permute-start.13 = (bf16[640,512]{1,0:T(8,128)(2,1)S(1)}, bf16[640,512]{1,0:T(8,128)(2,1)S(1)}, u32[]{:S(2)}, u32[]{:S(2)}) collective-permute-start(bf16[640,512]{1,0:T(8,128)(2,1)S(1)} %get-tuple-element.138), channel_id=1, source_target_pairs={{0,16},{8,24},{16,0},{24,8},{1,17},{9,25},{17,1},{25,9},{2,18},{10... | collective-permute-start | bytes 1966088 | tf_op jit(solution)/shard_map/swap_A1/ppermute | solution.py:108
  60.4 19.8 %collective-permute-start.12 = (bf16[640,512]{1,0:T(8,128)(2,1)S(1)}, bf16[640,512]{1,0:T(8,128)(2,1)S(1)}, u32[]{:S(2)}, u32[]{:S(2)}) collective-permute-start(bf16[640,512]{1,0:T(8,128)(2,1)S(1)} %get-tuple-element.137), channel_id=1, source_target_pairs={{0,1},{1,0},{2,3},{3,2},{4,5},{5,4},{6,7},{7,6},{8,9},{9,8},{10,11... | collective-permute-start | bytes 1966088 | tf_op jit(solution)/shard_map/swap_A0/ppermute | solution.py:108
  66.5 13.8 %collective-permute-start.11 = (bf16[192,512]{1,0:T(8,128)(2,1)S(1)}, bf16[192,512]{1,0:T(8,128)(2,1)S(1)}, u32[]{:S(2)}, u32[]{:S(2)}) collective-permute-start(bf16[192,512]{1,0:T(8,128)(2,1)S(1)} %get-tuple-element.136), channel_id=1, source_target_pairs={{0,4},{1,5},{2,6},{3,7},{4,0},{5,1},{6,2},{7,3},{8,12},{9,13},{10,... | collective-permute-start | bytes 589832 | tf_op jit(solution)/shard_map/swap_V/ppermute | solution.py:108
  68.3 12.0 %collective-permute-start.9 = (bf16[192,512]{1,0:T(8,128)(2,1)S(1)}, bf16[192,512]{1,0:T(8,128)(2,1)S(1)}, u32[]{:S(2)}, u32[]{:S(2)}) collective-permute-start(bf16[192,512]{1,0:T(8,128)(2,1)S(1)} %get-tuple-element.132), channel_id=1, source_target_pairs={{0,2},{1,3},{2,0},{3,1},{4,6},{5,7},{6,4},{7,5},{8,10},{9,11},{10,... | collective-permute-start | bytes 589832 | tf_op jit(solution)/shard_map/swap_K/ppermute | solution.py:108
  75.8 11.4 %collective-permute-start.15 = (bf16[320,512]{1,0:T(8,128)(2,1)S(1)}, bf16[320,512]{1,0:T(8,128)(2,1)S(1)}, u32[]{:S(2)}, u32[]{:S(2)}) collective-permute-start(bf16[320,512]{1,0:T(8,128)(2,1)S(1)} %get-tuple-element.144), channel_id=1, source_target_pairs={{0,1},{1,0},{2,3},{3,2},{4,5},{5,4},{6,7},{7,6},{8,9},{9,8},{10,11... | collective-permute-start | bytes 983048 | tf_op jit(solution)/shard_map/swap_A1/ppermute | solution.py:108
  80.4 8.6 %collective-permute-start.14 = (bf16[96,512]{1,0:T(8,128)(2,1)S(1)}, bf16[96,512]{1,0:T(8,128)(2,1)S(1)}, u32[]{:S(2)}, u32[]{:S(2)}) collective-permute-start(bf16[96,512]{1,0:T(8,128)(2,1)S(1)} %get-tuple-element.143), channel_id=1, source_target_pairs={{0,4},{1,5},{2,6},{3,7},{4,0},{5,1},{6,2},{7,3},{8,12},{9,13},{10,... | collective-permute-start | bytes 294920 | tf_op jit(solution)/shard_map/swap_K/ppermute | solution.py:108
  82.3 6.8 %collective-permute-start.16 = (bf16[96,512]{1,0:T(8,128)(2,1)S(1)}, bf16[96,512]{1,0:T(8,128)(2,1)S(1)}, u32[]{:S(2)}, u32[]{:S(2)}) collective-permute-start(bf16[96,512]{1,0:T(8,128)(2,1)S(1)} %get-tuple-element.148), channel_id=1, source_target_pairs={{0,1},{1,0},{2,3},{3,2},{4,5},{5,4},{6,7},{7,6},{8,9},{9,8},{10,11... | collective-permute-start | bytes 294920 | tf_op jit(solution)/shard_map/swap_V/ppermute | solution.py:108
  83.8 10.8 %collective-permute-start.19 = (bf16[320,512]{1,0:T(8,128)(2,1)S(1)}, bf16[320,512]{1,0:T(8,128)(2,1)S(1)}, u32[]{:S(2)}, u32[]{:S(2)}) collective-permute-start(bf16[320,512]{1,0:T(8,128)(2,1)S(1)} %get-tuple-element.163), channel_id=1, source_target_pairs={{0,16},{8,24},{16,0},{24,8},{1,17},{9,25},{17,1},{25,9},{2,18},{10... | collective-permute-start | bytes 983048 | tf_op jit(solution)/shard_map/swap_A0/ppermute | solution.py:108
  87.3 8.4 %collective-permute-start.18 = (bf16[160,512]{1,0:T(8,128)(2,1)S(1)}, bf16[160,512]{1,0:T(8,128)(2,1)S(1)}, u32[]{:S(2)}, u32[]{:S(2)}) collective-permute-start(bf16[160,512]{1,0:T(8,128)(2,1)S(1)} %get-tuple-element.162), channel_id=1, source_target_pairs={{0,2},{1,3},{2,0},{3,1},{4,6},{5,7},{6,4},{7,5},{8,10},{9,11},{10,... | collective-permute-start | bytes 491528 | tf_op jit(solution)/shard_map/swap_A1/ppermute | solution.py:108
  90.4 10.2 %collective-permute-start.25 = (bf16[768,512]{1,0:T(8,128)(2,1)S(1)}, bf16[768,512]{1,0:T(8,128)(2,1)S(1)}, u32[]{:S(2)}, u32[]{:S(2)}) collective-permute-start(bf16[768,512]{1,0:T(8,128)(2,1)S(1)} %get-tuple-element.152.refs_5_), channel_id=1, source_target_pairs={{0,8},{8,0},{16,24},{24,16},{1,9},{9,1},{17,25},{25,17},{2,10},{10... | collective-permute-start | bytes 2359304 | tf_op jit(solution)/shard_map/swap_B0/ppermute | solution.py:108
  91.7 7.2 %collective-permute-start.21 = (bf16[768,512]{1,0:T(8,128)(2,1)S(1)}, bf16[768,512]{1,0:T(8,128)(2,1)S(1)}, u32[]{:S(2)}, u32[]{:S(2)}) collective-permute-start(bf16[768,512]{1,0:T(8,128)(2,1)S(1)} %get-tuple-element.158.refs_11_), channel_id=1, source_target_pairs={{0,8},{8,0},{16,24},{24,16},{1,9},{9,1},{17,25},{25,17},{2,10},{10... | collective-permute-start | bytes 2359304 | tf_op jit(solution)/shard_map/swap_B1/ppermute | solution.py:108
  94.7 8.8 %collective-permute-start.24 = (bf16[160,512]{1,0:T(8,128)(2,1)S(1)}, bf16[160,512]{1,0:T(8,128)(2,1)S(1)}, u32[]{:S(2)}, u32[]{:S(2)}) collective-permute-start(bf16[160,512]{1,0:T(8,128)(2,1)S(1)} %get-tuple-element.172), channel_id=1, source_target_pairs={{0,2},{1,3},{2,0},{3,1},{4,6},{5,7},{6,4},{7,5},{8,10},{9,11},{10,... | collective-permute-start | bytes 491528 | tf_op jit(solution)/shard_map/swap_A0/ppermute | solution.py:108
  95.7 8.1 %collective-permute-start.23 = (bf16[80,512]{1,0:T(8,128)(2,1)S(1)}, bf16[80,512]{1,0:T(8,128)(2,1)S(1)}, u32[]{:S(2)}, u32[]{:S(2)}) collective-permute-start(bf16[80,512]{1,0:T(8,128)(2,1)S(1)} %get-tuple-element.171), channel_id=1, source_target_pairs={{0,4},{1,5},{2,6},{3,7},{4,0},{5,1},{6,2},{7,3},{8,12},{9,13},{10,... | collective-permute-start | bytes 245768 | tf_op jit(solution)/shard_map/swap_A1/ppermute | solution.py:108
  97.7 14.8 %collective-permute-start.20 = (bf16[272,512]{1,0:T(8,128)(2,1)S(1)}, bf16[272,512]{1,0:T(8,128)(2,1)S(1)}, u32[]{:S(2)}, u32[]{:S(2)}) collective-permute-start(bf16[272,512]{1,0:T(8,128)(2,1)S(1)} %get-tuple-element.167), channel_id=1, source_target_pairs={{0,2},{1,3},{2,0},{3,1},{4,6},{5,7},{6,4},{7,5},{8,10},{9,11},{10,... | collective-permute-start | bytes 835592 | tf_op jit(solution)/shard_map/swap_B2/ppermute | solution.py:108
  99.0 10.7 %collective-permute-start.22 = (bf16[384,512]{1,0:T(8,128)(2,1)S(1)}, bf16[384,512]{1,0:T(8,128)(2,1)S(1)}, u32[]{:S(2)}, u32[]{:S(2)}) collective-permute-start(bf16[384,512]{1,0:T(8,128)(2,1)S(1)} %get-tuple-element.170), channel_id=1, source_target_pairs={{0,16},{8,24},{16,0},{24,8},{1,17},{9,25},{17,1},{25,9},{2,18},{10... | collective-permute-start | bytes 1179656 | tf_op jit(solution)/shard_map/swap_B1/ppermute | solution.py:108
  103.5 13.0 %collective-permute-start.29 = (bf16[80,512]{1,0:T(8,128)(2,1)S(1)}, bf16[80,512]{1,0:T(8,128)(2,1)S(1)}, u32[]{:S(2)}, u32[]{:S(2)}) collective-permute-start(bf16[80,512]{1,0:T(8,128)(2,1)S(1)} %get-tuple-element.180), channel_id=1, source_target_pairs={{0,4},{1,5},{2,6},{3,7},{4,0},{5,1},{6,2},{7,3},{8,12},{9,13},{10,... | collective-permute-start | bytes 245768 | tf_op jit(solution)/shard_map/swap_A0/ppermute | solution.py:108
  103.9 13.4 %collective-permute-start.28 = (bf16[80,512]{1,0:T(8,128)(2,1)S(1)}, bf16[80,512]{1,0:T(8,128)(2,1)S(1)}, u32[]{:S(2)}, u32[]{:S(2)}) collective-permute-start(bf16[80,512]{1,0:T(8,128)(2,1)S(1)} %scatter.36.refs_2_.refs_0_), channel_id=1, source_target_pairs={{0,4},{1,5},{2,6},{3,7},{4,0},{5,1},{6,2},{7,3},{8,12},{9,13},{10,... | collective-permute-start | bytes 245768 | tf_op jit(solution)/shard_map/swap_A1/ppermute | solution.py:108
  106.6 9.8 %collective-permute-start.30 = (bf16[384,512]{1,0:T(8,128)(2,1)S(1)}, bf16[384,512]{1,0:T(8,128)(2,1)S(1)}, u32[]{:S(2)}, u32[]{:S(2)}) collective-permute-start(bf16[384,512]{1,0:T(8,128)(2,1)S(1)} %get-tuple-element.181), channel_id=1, source_target_pairs={{0,1},{1,0},{2,3},{3,2},{4,5},{5,4},{6,7},{7,6},{8,9},{9,8},{10,11... | collective-permute-start | bytes 1179656 | tf_op jit(solution)/shard_map/swap_B0/ppermute | solution.py:108
  112.6 9.6 %collective-permute-start.26 = (bf16[144,512]{1,0:T(8,128)(2,1)S(1)}, bf16[144,512]{1,0:T(8,128)(2,1)S(1)}, u32[]{:S(2)}, u32[]{:S(2)}) collective-permute-start(bf16[144,512]{1,0:T(8,128)(2,1)S(1)} %get-tuple-element.178), channel_id=1, source_target_pairs={{0,16},{8,24},{16,0},{24,8},{1,17},{9,25},{17,1},{25,9},{2,18},{10... | collective-permute-start | bytes 442376 | tf_op jit(solution)/shard_map/swap_B2/ppermute | solution.py:108
  114.2 8.0 %collective-permute-start.27 = (bf16[192,512]{1,0:T(8,128)(2,1)S(1)}, bf16[192,512]{1,0:T(8,128)(2,1)S(1)}, u32[]{:S(2)}, u32[]{:S(2)}) collective-permute-start(bf16[192,512]{1,0:T(8,128)(2,1)S(1)} %get-tuple-element.179), channel_id=1, source_target_pairs={{0,1},{1,0},{2,3},{3,2},{4,5},{5,4},{6,7},{7,6},{8,9},{9,8},{10,11... | collective-permute-start | bytes 589832 | tf_op jit(solution)/shard_map/swap_B1/ppermute | solution.py:108
  116.6 7.3 %collective-permute-start.34 = (bf16[80,512]{1,0:T(8,128)(2,1)S(1)}, bf16[80,512]{1,0:T(8,128)(2,1)S(1)}, u32[]{:S(2)}, u32[]{:S(2)}) collective-permute-start(bf16[80,512]{1,0:T(8,128)(2,1)S(1)} %scatter.40.refs_2_.refs_0_), channel_id=1, source_target_pairs={{0,4},{1,5},{2,6},{3,7},{4,0},{5,1},{6,2},{7,3},{8,12},{9,13},{10,... | collective-permute-start | bytes 245768 | tf_op jit(solution)/shard_map/swap_A0/ppermute | solution.py:108
  117.3 8.6 %collective-permute-start.33 = (bf16[160,512]{1,0:T(8,128)(2,1)S(1)}, bf16[160,512]{1,0:T(8,128)(2,1)S(1)}, u32[]{:S(2)}, u32[]{:S(2)}) collective-permute-start(bf16[160,512]{1,0:T(8,128)(2,1)S(1)} %gather.20.refs_2_.refs_0_), channel_id=1, source_target_pairs={{0,2},{1,3},{2,0},{3,1},{4,6},{5,7},{6,4},{7,5},{8,10},{9,11},{10,... | collective-permute-start | bytes 491528 | tf_op jit(solution)/shard_map/swap_A1/ppermute | solution.py:108
  119.7 6.9 %collective-permute-start.32 = (bf16[192,512]{1,0:T(8,128)(2,1)S(1)}, bf16[192,512]{1,0:T(8,128)(2,1)S(1)}, u32[]{:S(2)}, u32[]{:S(2)}) collective-permute-start(bf16[192,512]{1,0:T(8,128)(2,1)S(1)} %get-tuple-element.186), channel_id=1, source_target_pairs={{0,16},{8,24},{16,0},{24,8},{1,17},{9,25},{17,1},{25,9},{2,18},{10... | collective-permute-start | bytes 589832 | tf_op jit(solution)/shard_map/swap_B0/ppermute | solution.py:108
  123.9 7.7 %collective-permute-start.38 = (bf16[160,512]{1,0:T(8,128)(2,1)S(1)}, bf16[160,512]{1,0:T(8,128)(2,1)S(1)}, u32[]{:S(2)}, u32[]{:S(2)}) collective-permute-start(bf16[160,512]{1,0:T(8,128)(2,1)S(1)} %gather.21.refs_2_.refs_0_), channel_id=1, source_target_pairs={{0,2},{1,3},{2,0},{3,1},{4,6},{5,7},{6,4},{7,5},{8,10},{9,11},{10,... | collective-permute-start | bytes 491528 | tf_op jit(solution)/shard_map/swap_A0/ppermute | solution.py:108
  125.9 8.4 %collective-permute-start.37 = (bf16[320,512]{1,0:T(8,128)(2,1)S(1)}, bf16[320,512]{1,0:T(8,128)(2,1)S(1)}, u32[]{:S(2)}, u32[]{:S(2)}) collective-permute-start(bf16[320,512]{1,0:T(8,128)(2,1)S(1)} %gather.22.refs_2_.refs_0_), channel_id=1, source_target_pairs={{0,1},{1,0},{2,3},{3,2},{4,5},{5,4},{6,7},{7,6},{8,9},{9,8},{10,11... | collective-permute-start | bytes 983048 | tf_op jit(solution)/shard_map/swap_A1/ppermute | solution.py:108
  126.6 7.8 %collective-permute-start.36 = (bf16[96,512]{1,0:T(8,128)(2,1)S(1)}, bf16[96,512]{1,0:T(8,128)(2,1)S(1)}, u32[]{:S(2)}, u32[]{:S(2)}) collective-permute-start(bf16[96,512]{1,0:T(8,128)(2,1)S(1)} %get-tuple-element.190), channel_id=1, source_target_pairs={{0,2},{1,3},{2,0},{3,1},{4,6},{5,7},{6,4},{7,5},{8,10},{9,11},{10,... | collective-permute-start | bytes 294920 | tf_op jit(solution)/shard_map/swap_B0/ppermute | solution.py:108
  131.6 11.3 %collective-permute-start.40 = (bf16[320,512]{1,0:T(8,128)(2,1)S(1)}, bf16[320,512]{1,0:T(8,128)(2,1)S(1)}, u32[]{:S(2)}, u32[]{:S(2)}) collective-permute-start(bf16[320,512]{1,0:T(8,128)(2,1)S(1)} %gather.23.refs_2_.refs_0_), channel_id=1, source_target_pairs={{0,16},{8,24},{16,0},{24,8},{1,17},{9,25},{17,1},{25,9},{2,18},{10... | collective-permute-start | bytes 983048 | tf_op jit(solution)/shard_map/swap_A0/ppermute | solution.py:108
  134.3 19.8 %collective-permute-start.50 = (bf16[640,512]{1,0:T(8,128)(2,1)S(1)}, bf16[640,512]{1,0:T(8,128)(2,1)S(1)}, u32[]{:S(2)}, u32[]{:S(2)}) collective-permute-start(bf16[640,512]{1,0:T(8,128)(2,1)S(1)} %gather.24.refs_2_.refs_0_), channel_id=1, source_target_pairs={{0,16},{8,24},{16,0},{24,8},{1,17},{9,25},{17,1},{25,9},{2,18},{10... | collective-permute-start | bytes 1966088 | tf_op jit(solution)/shard_map/swap_A1/ppermute | solution.py:108
  134.5 11.0 %collective-permute-start.46 = (bf16[32,512]{1,0:T(8,128)(2,1)S(1)}, bf16[32,512]{1,0:T(8,128)(2,1)S(1)}, u32[]{:S(2)}, u32[]{:S(2)}) collective-permute-start(bf16[32,512]{1,0:T(8,128)(2,1)S(1)} %get-tuple-element.196.refs_2_.refs_0_), channel_id=1, source_target_pairs={{0,4},{1,5},{2,6},{3,7},{4,0},{5,1},{6,2},{7,3},{8,12},{9,13},{10,... | collective-permute-start | bytes 98312 | tf_op jit(solution)/shard_map/swap_B2/ppermute | solution.py:108
  136.5 10.2 %collective-permute-start.45 = (bf16[48,512]{1,0:T(8,128)(2,1)S(1)}, bf16[48,512]{1,0:T(8,128)(2,1)S(1)}, u32[]{:S(2)}, u32[]{:S(2)}) collective-permute-start(bf16[48,512]{1,0:T(8,128)(2,1)S(1)} %scatter.48.refs_2_.refs_0_), channel_id=1, source_target_pairs={{0,4},{1,5},{2,6},{3,7},{4,0},{5,1},{6,2},{7,3},{8,12},{9,13},{10,... | collective-permute-start | bytes 147464 | tf_op jit(solution)/shard_map/swap_B1/ppermute | solution.py:108
  137.6 7.0 %collective-permute-start.43 = (bf16[48,512]{1,0:T(8,128)(2,1)S(1)}, bf16[48,512]{1,0:T(8,128)(2,1)S(1)}, u32[]{:S(2)}, u32[]{:S(2)}) collective-permute-start(bf16[48,512]{1,0:T(8,128)(2,1)S(1)} %get-tuple-element.197), channel_id=1, source_target_pairs={{0,4},{1,5},{2,6},{3,7},{4,0},{5,1},{6,2},{7,3},{8,12},{9,13},{10,... | collective-permute-start | bytes 147464 | tf_op jit(solution)/shard_map/swap_B0/ppermute | solution.py:108
  143.0 15.6 %collective-permute-start.42 = (bf16[640,512]{1,0:T(8,128)(2,1)S(1)}, bf16[640,512]{1,0:T(8,128)(2,1)S(1)}, u32[]{:S(2)}, u32[]{:S(2)}) collective-permute-start(bf16[640,512]{1,0:T(8,128)(2,1)S(1)} %gather.25.refs_2_.refs_0_), channel_id=1, source_target_pairs={{0,1},{1,0},{2,3},{3,2},{4,5},{5,4},{6,7},{7,6},{8,9},{9,8},{10,11... | collective-permute-start | bytes 1966088 | tf_op jit(solution)/shard_map/swap_A0/ppermute | solution.py:108
  145.5 10.0 %collective-permute-start.49 = (bf16[64,512]{1,0:T(8,128)(2,1)S(1)}, bf16[64,512]{1,0:T(8,128)(2,1)S(1)}, u32[]{:S(2)}, u32[]{:S(2)}) collective-permute-start(bf16[64,512]{1,0:T(8,128)(2,1)S(1)} %gather.26.refs_2_.refs_0_), channel_id=1, source_target_pairs={{0,1},{1,0},{2,3},{3,2},{4,5},{5,4},{6,7},{7,6},{8,9},{9,8},{10,11... | collective-permute-start | bytes 196616 | tf_op jit(solution)/shard_map/swap_B2/ppermute | solution.py:108
  146.7 10.3 %collective-permute-start.48 = (bf16[96,512]{1,0:T(8,128)(2,1)S(1)}, bf16[96,512]{1,0:T(8,128)(2,1)S(1)}, u32[]{:S(2)}, u32[]{:S(2)}) collective-permute-start(bf16[96,512]{1,0:T(8,128)(2,1)S(1)} %gather.27.refs_2_.refs_0_), channel_id=1, source_target_pairs={{0,2},{1,3},{2,0},{3,1},{4,6},{5,7},{6,4},{7,5},{8,10},{9,11},{10,... | collective-permute-start | bytes 294920 | tf_op jit(solution)/shard_map/swap_B1/ppermute | solution.py:108
  150.0 7.9 %collective-permute-start.47 = (bf16[96,512]{1,0:T(8,128)(2,1)S(1)}, bf16[96,512]{1,0:T(8,128)(2,1)S(1)}, u32[]{:S(2)}, u32[]{:S(2)}) collective-permute-start(bf16[96,512]{1,0:T(8,128)(2,1)S(1)} %gather.28.refs_2_.refs_0_), channel_id=1, source_target_pairs={{0,2},{1,3},{2,0},{3,1},{4,6},{5,7},{6,4},{7,5},{8,10},{9,11},{10,... | collective-permute-start | bytes 294920 | tf_op jit(solution)/shard_map/swap_B0/ppermute | solution.py:108
  154.2 13.5 %collective-permute-start.52 = (bf16[1280,512]{1,0:T(8,128)(2,1)S(1)}, bf16[1280,512]{1,0:T(8,128)(2,1)S(1)}, u32[]{:S(2)}, u32[]{:S(2)}) collective-permute-start(bf16[1280,512]{1,0:T(8,128)(2,1)S(1)} %gather.29.refs_2_), channel_id=1, source_target_pairs={{0,8},{8,0},{16,24},{24,16},{1,9},{9,1},{17,25},{25,17},{2,10},{10... | collective-permute-start | bytes 3932168 | tf_op jit(solution)/shard_map/swap_A1/ppermute | solution.py:108
  157.1 8.6 %collective-permute-start.55 = (bf16[192,512]{1,0:T(8,128)(2,1)S(1)}, bf16[192,512]{1,0:T(8,128)(2,1)S(1)}, u32[]{:S(2)}, u32[]{:S(2)}) collective-permute-start(bf16[192,512]{1,0:T(8,128)(2,1)S(1)} %gather.31.refs_2_.refs_0_), channel_id=1, source_target_pairs={{0,1},{1,0},{2,3},{3,2},{4,5},{5,4},{6,7},{7,6},{8,9},{9,8},{10,11... | collective-permute-start | bytes 589832 | tf_op jit(solution)/shard_map/swap_B1/ppermute | solution.py:108
  158.0 6.8 %collective-permute-start.56 = (bf16[192,512]{1,0:T(8,128)(2,1)S(1)}, bf16[192,512]{1,0:T(8,128)(2,1)S(1)}, u32[]{:S(2)}, u32[]{:S(2)}) collective-permute-start(bf16[192,512]{1,0:T(8,128)(2,1)S(1)} %gather.32.refs_2_.refs_0_), channel_id=1, source_target_pairs={{0,16},{8,24},{16,0},{24,8},{1,17},{9,25},{17,1},{25,9},{2,18},{10... | collective-permute-start | bytes 589832 | tf_op jit(solution)/shard_map/swap_B0/ppermute | solution.py:108
  158.6 9.1 %collective-permute-start.51 = (bf16[1280,512]{1,0:T(8,128)(2,1)S(1)}, bf16[1280,512]{1,0:T(8,128)(2,1)S(1)}, u32[]{:S(2)}, u32[]{:S(2)}) collective-permute-start(bf16[1280,512]{1,0:T(8,128)(2,1)S(1)} %gather.33.refs_2_.refs_0_), channel_id=1, source_target_pairs={{0,8},{8,0},{16,24},{24,16},{1,9},{9,1},{17,25},{25,17},{2,10},{10... | collective-permute-start | bytes 3932168 | tf_op jit(solution)/shard_map/swap_A0/ppermute | solution.py:108
  164.8 10.1 %collective-permute-start.57 = (bf16[384,512]{1,0:T(8,128)(2,1)S(1)}, bf16[384,512]{1,0:T(8,128)(2,1)S(1)}, u32[]{:S(2)}, u32[]{:S(2)}) collective-permute-start(bf16[384,512]{1,0:T(8,128)(2,1)S(1)} %gather.35.refs_2_.refs_0_), channel_id=1, source_target_pairs={{0,1},{1,0},{2,3},{3,2},{4,5},{5,4},{6,7},{7,6},{8,9},{9,8},{10,11... | collective-permute-start | bytes 1179656 | tf_op jit(solution)/shard_map/swap_B0/ppermute | solution.py:108
  165.7 9.8 %collective-permute-start.59 = (bf16[384,512]{1,0:T(8,128)(2,1)S(1)}, bf16[384,512]{1,0:T(8,128)(2,1)S(1)}, u32[]{:S(2)}, u32[]{:S(2)}) collective-permute-start(bf16[384,512]{1,0:T(8,128)(2,1)S(1)} %gather.36.refs_2_.refs_0_), channel_id=1, source_target_pairs={{0,16},{8,24},{16,0},{24,8},{1,17},{9,25},{17,1},{25,9},{2,18},{10... | collective-permute-start | bytes 1179656 | tf_op jit(solution)/shard_map/swap_B1/ppermute | solution.py:108
  (20 other events, 133.4 us)

commit v6 on v5

--- a/solution.py
+++ b/solution.py
@@ -25,10 +25,10 @@
 EACH = 5
 
 EVENTS = (
-    "A0", "A1", "K", "V", "A1", "A0", "V", "K", "A1", "K", "V", "TK", "TV", "T3", "A0", "A1",
-    "B2", "B1", "B0", "A0", "A1", "B1", "B2", "B0", "A0", "A1", "B1", "B2", "A0", "A1", "B0",
-    "B2", "B1", "A0", "A1", "B0", "B2", "B1", "A0", "B0", "B2", "B1", "B0", "A1", "B2", "B1",
-    "B0", "A0", "B2", "B0", "B1", "B2", "Af", "B0", "B1", "Bn", "Bf",
+    "A0", "A1", "K", "V", "V:0", "K:0", "A1:0", "A0", "K", "V", "TK", "TV", "T3", "B0", "B1",
+    "A0", "A1", "B2", "A0", "A1", "B1", "B0", "B2", "A1", "A0", "A1", "B1", "B2", "A0", "A1",
+    "B0", "B2", "B1", "A0", "A1", "B0", "B2", "B1", "A0", "B0", "B2", "B1", "B0", "A1", "B2",
+    "B1", "B0", "A0", "B2", "B0", "B1", "B2", "Af", "B0", "B1", "Bn", "Bf",
 )
 
 BF16 = jnp.bfloat16
@@ -572,10 +572,14 @@
     keep[keep.shape[0] - EXTRA_ROWS :, :] = gains.astype(BF16)
 
 
-def finish_kernel(plan, items, count, aliased, *refs):
-    blocks, refs = refs[: len(items)], refs[len(items) + (count if aliased else 0) :]
-    targets, (token, sent, *stages) = refs[:count], refs[count:]
+def finish_kernel(plan, items, count, aliased, n_gains, *refs):
+    blocks, refs = refs[: len(items)], refs[len(items) :]
+    gains, refs = refs[: min(n_gains, 1)], refs[min(n_gains, 1) + (count if aliased else 0) :]
+    targets, token, refs = refs[:count], refs[count], refs[count + 1 :]
+    gain_targets, (sent, *stages) = refs[:n_gains], refs[n_gains:]
     token[...] = jnp.zeros_like(token)
+    for row, target in enumerate(gain_targets):
+        target[...] = gains[0][...].astype(F32)[row : row + 1, :].reshape(-1)
     _, mine = own_places(plan)
     half = plan.blocks // 2
     copies = []
@@ -598,7 +602,7 @@
         copy.wait()
 
 
-def finish(plan, order, name, chosen, cores, targets=()):
+def finish(plan, order, name, chosen, cores, targets=(), gains=()):
     items, blocks, shapes = [], [], []
     for part in chosen:
         for core in cores:
@@ -609,16 +613,19 @@
     count = len(shapes)
     everywhere = tuple(range(count))
     copies = sum(plan.blocks // 2 * len(parts) for _, parts, _ in items)
-    return order.call(
-        functools.partial(finish_kernel, plan, items, count, bool(targets)),
+    n_gains = 2 * len(gains)
+    results = order.call(
+        functools.partial(finish_kernel, plan, items, count, bool(targets), n_gains),
         name,
-        [(shape, F32) for shape in shapes] + [((8, LANES), F32)],
+        [(shape, F32) for shape in shapes] + [((8, LANES), F32)]
+        + [((array.shape[1],), F32) for array in gains] * 2,
         [pltpu.SemaphoreType.DMA((copies,))] + [pltpu.VMEM(array.shape, F32) for array in blocks],
         anywhere=tuple(range(len(items), len(items) + count)) if targets else (),
         out_anywhere=everywhere,
         aliases={len(items) + number: number for number in everywhere} if targets else None,
         token=count,
-    )(*blocks, *targets)[:count]
+    )(*blocks, *gains, *targets)
+    return results[:count], results[count + 1 :]
 
 
 class RowGather:
@@ -843,17 +850,18 @@
                 EXTRA_ROWS,
             )
         elif event == "Af":
-            grads = finish(plan, order, "finish", [chains["A0"], chains["A1"]], (0, 1))
+            grads, gains = finish(
+                plan, order, "finish", [chains["A0"], chains["A1"]], (0, 1), (), chains["B2"].sums
+            )
             grad_down, grad_out, grad_up, grad_query = grads
         elif event in ("Bn", "Bf"):
             chosen = [chains[name] for name in ("B0", "B1", "B2")]
             previous = () if event == "Bn" else results
-            results = finish(plan, order, "finish", chosen, (int(event == "Bf"),), previous)
+            results, _ = finish(plan, order, "finish", chosen, (int(event == "Bf"),), previous)
         else:
             name, _, cost = event.partition(":")
             chains[name].step(float(cost or EACH))
     grad_conv_key, grad_conv_value, grad_key, grad_value = results
-    gains = chains["B2"].sums[0].astype(F32)
     return (
         layer_out, grad_tokens, gains[0], grad_query, grad_key, grad_value,
         grad_conv_key, grad_conv_value, grad_out, gains[1], grad_up, grad_down,

time: 183 us -> 180 us (0.984)
  starting transfers between devices: 80.7 us -> 74.3 us
  waiting for transfers between devices: 60.8 us -> 63.6 us
    ppermute x62, starting transfers between devices: 80.7 us -> 74.3 us  [swap(): return lax.ppermute(array, axis, [(i, i ^ value) for i in range(size)])]
    ppermute x62, waiting for transfers between devices: 60.8 us -> 63.6 us  [swap(): return lax.ppermute(array, axis, [(i, i ^ value) for i in range(size)])]
  transfers between devices with their start and end apart: 62 -> 62, of which waited for: 24 -> 22; matrix products, arithmetic and copies ran while one was open for 0% -> 0% of each run, Pallas kernels for 9% -> 9%
where the time goes in v6:
time: 180 us
  starting transfers between devices  74.3 us (41%)
  waiting for transfers between devices  63.6 us (35%)
  Pallas kernels  40.3 us (22%)
    ppermute x62, starting transfers between devices, swap(): return lax.ppermute(array, axis, [(i, i ^ value) for i in range(size)])  74.3 us
    ppermute x62, waiting for transfers between devices, swap(): return lax.ppermute(array, axis, [(i, i ^ value) for i in range(size)])  63.6 us
    pallas_call x63, Pallas kernels, run(): pl.pallas_call(without_last, name=name, out_shape=[pltpu.HBM(shape, dtype...  40.3 us
  transfers between devices with their start and end apart: 62, of which 22 were waited for; matrix products, arithmetic and copies ran while one was open for 0% of the time, Pallas kernels for 9%

profile of v6, /device:TPU:0, one launch (start us, length us, event | category | flops | bytes accessed | tf_op | source)
XLA Modules:
  0.0 179.6 jit_solution(16449335014487841730)
XLA Ops:
  0.6 3.3 %project.1 = (f32[288,512]{1,0:T(8,128)S(1)}, bf16[288,512]{1,0:T(8,128)(2,1)S(1)}, bf16[288,512]{1,0:T(8,128)(2,1)S(1)}, bf16[288,512]{1,0:T(8,128)(2,1)S(1)}, ...) custom-call(bf16[2,1,144,512]{3,2,1,0:T(8,128)(2,1)} %refs_0_.1, ...), custom_call_target="tpu_custom_call" | custom-call | flops 5750000128 | bytes 18450000 | tf_op jit(solution)/shard_map/project/pallas_call | solution.py:162
  4.0 4.1 %collective-permute-start = (bf16[112,512]{1,0:T(8,128)(2,1)S(1)}, bf16[112,512]{1,0:T(8,128)(2,1)S(1)}, u32[]{:S(2)}, u32[]{:S(2)}) collective-permute-start(bf16[112,512]{1,0:T(8,128)(2,1)S(1)} %get-tuple-element.120.refs_0_), channel_id=1, source_target_pairs={{0,4},{1,5},{2,6},{3,7},{4,0},{5,1},{6,2},{7,3},{8,12},{9,13},{10,... | collective-permute-start | bytes 344072 | tf_op jit(solution)/shard_map/swap_gather_keys/ppermute | solution.py:108
  8.1 1.5 collective-permute-start.2
  9.6 4.1 %collective-permute-done.refs_1_ = bf16[112,512]{1,0:T(8,128)(2,1)S(1)} collective-permute-done((bf16[112,512]{1,0:T(8,128)(2,1)S(1)}, bf16[112,512]{1,0:T(8,128)(2,1)S(1)}, u32[]{:S(2)}, u32[]{:S(2)}) %collective-permute-start) | collective-permute-done | bytes 114720 | tf_op jit(solution)/shard_map/swap_gather_keys/ppermute | solution.py:108
  14.5 3.4 %collective-permute-start.4 = (bf16[192,512]{1,0:T(8,128)(2,1)S(1)}, bf16[192,512]{1,0:T(8,128)(2,1)S(1)}, u32[]{:S(2)}, u32[]{:S(2)}) collective-permute-start(bf16[192,512]{1,0:T(8,128)(2,1)S(1)} %gather_row.5.refs_2_.refs_0_), channel_id=1, source_target_pairs={{0,4},{1,5},{2,6},{3,7},{4,0},{5,1},{6,2},{7,3},{8,12},{9,13},{10,... | collective-permute-start | bytes 589832 | tf_op jit(solution)/shard_map/swap_gather_values/ppermute | solution.py:108
  18.0 6.8 %collective-permute-done.1.refs_1_ = bf16[224,512]{1,0:T(8,128)(2,1)S(1)} collective-permute-done((bf16[224,512]{1,0:T(8,128)(2,1)S(1)}, bf16[224,512]{1,0:T(8,128)(2,1)S(1)}, u32[]{:S(2)}, u32[]{:S(2)}) %collective-permute-start.1) | collective-permute-done | bytes 229408 | tf_op jit(solution)/shard_map/swap_gather_keys/ppermute | solution.py:108
  26.2 1.7 collective-permute-start.5
  28.0 8.8 %collective-permute-done.5.refs_11_ = bf16[384,512]{1,0:T(8,128)(2,1)S(1)} collective-permute-done((bf16[384,512]{1,0:T(8,128)(2,1)S(1)}, bf16[384,512]{1,0:T(8,128)(2,1)S(1)}, u32[]{:S(2)}, u32[]{:S(2)}) %collective-permute-start.5) | collective-permute-done | bytes 393248 | tf_op jit(solution)/shard_map/swap_gather_values/ppermute | solution.py:108
  36.8 16.8 %layer.1 = (bf16[2,1,144,512]{3,2,1,0:T(8,128)(2,1)}, f32[288,512]{1,0:T(8,128)S(1)}, bf16[288,512]{1,0:T(8,128)(2,1)S(1)}, f32[288,512]{1,0:T(8,128)S(1)}, f32[...) custom-call(f32[288,512]{1,0:T(8,128)S(1)} %get-tuple-element.114.re, ...), custom_call_target="tpu_custom_call" | custom-call | flops 5750000128 | bytes 18450000 | tf_op jit(solution)/shard_map/layer/pallas_call | solution.py:162
  54.1 1.5 collective-permute-start.6
  55.7 1.8 collective-permute-start.10
  58.8 1.6 collective-permute-start.14
  60.4 1.5 collective-permute-start.13
  61.9 4.2 %collective-permute-done.6.refs_1_ = bf16[384,512]{1,0:T(8,128)(2,1)S(1)} collective-permute-done((bf16[384,512]{1,0:T(8,128)(2,1)S(1)}, bf16[384,512]{1,0:T(8,128)(2,1)S(1)}, u32[]{:S(2)}, u32[]{:S(2)}) %collective-permute-start.6) | collective-permute-done | bytes 393248 | tf_op jit(solution)/shard_map/swap_K/ppermute | solution.py:108
  66.5 1.8 %collective-permute-start.11 = (bf16[192,512]{1,0:T(8,128)(2,1)S(1)}, bf16[192,512]{1,0:T(8,128)(2,1)S(1)}, u32[]{:S(2)}, u32[]{:S(2)}) collective-permute-start(bf16[192,512]{1,0:T(8,128)(2,1)S(1)} %get-tuple-element.138), channel_id=1, source_target_pairs={{0,4},{1,5},{2,6},{3,7},{4,0},{5,1},{6,2},{7,3},{8,12},{9,13},{10,... | collective-permute-start | bytes 589832 | tf_op jit(solution)/shard_map/swap_V/ppermute | solution.py:108
  68.4 1.7 collective-permute-start.9
  70.1 7.3 %collective-permute-done.11.refs_1_ = bf16[192,512]{1,0:T(8,128)(2,1)S(1)} collective-permute-done((bf16[192,512]{1,0:T(8,128)(2,1)S(1)}, bf16[192,512]{1,0:T(8,128)(2,1)S(1)}, u32[]{:S(2)}, u32[]{:S(2)}) %collective-permute-start.11) | collective-permute-done | bytes 196640 | tf_op jit(solution)/shard_map/swap_V/ppermute | solution.py:108
  80.3 1.5 collective-permute-start.16
  81.9 2.8 %collective-permute-done.12.refs_1_ = bf16[96,512]{1,0:T(8,128)(2,1)S(1)} collective-permute-done((bf16[96,512]{1,0:T(8,128)(2,1)S(1)}, bf16[96,512]{1,0:T(8,128)(2,1)S(1)}, u32[]{:S(2)}, u32[]{:S(2)}) %collective-permute-start.12) | collective-permute-done | bytes 98336 | tf_op jit(solution)/shard_map/swap_K/ppermute | solution.py:108
  87.9 2.3 %tail_kernel.1 = (bf16[528,512]{1,0:T(8,128)(2,1)S(1)}, bf16[528,512]{1,0:T(8,128)(2,1)S(1)}, bf16[2,1,144,512]{3,2,1,0:T(8,128)(2,1)}) custom-call(bf16[288,512]{1,0:T(8,128)(2,1)S(1)} %get-tuple-element.115.refs_1_.refs_0_, f32[288,512]{1,0:T(8,128)S(1)} %get-tuple-element.114.refs_0_.refs_1_, bf16[512]{0:T(512)(128)(2,1)S(1)} %copy-done.5, ...), custom_call_target="tpu_custom_call" | custom-call | flops 5750000128 | bytes 18450000 | tf_op jit(solution)/shard_map/tail_kernel/pallas_call | solution.py:162
  90.8 1.4 collective-permute-start.23
  93.1 1.4 collective-permute-start.25
  94.5 1.5 collective-permute-start.27
  96.3 5.1 %collective-permute-done.19.refs_1_ = bf16[160,512]{1,0:T(8,128)(2,1)S(1)} collective-permute-done((bf16[160,512]{1,0:T(8,128)(2,1)S(1)}, bf16[160,512]{1,0:T(8,128)(2,1)S(1)}, u32[]{:S(2)}, u32[]{:S(2)}) %collective-permute-start.19) | collective-permute-done | bytes 163872 | tf_op jit(solution)/shard_map/swap_A0/ppermute | solution.py:108
  102.4 2.1 %collective-permute-start.22 = (bf16[80,512]{1,0:T(8,128)(2,1)S(1)}, bf16[80,512]{1,0:T(8,128)(2,1)S(1)}, u32[]{:S(2)}, u32[]{:S(2)}) collective-permute-start(bf16[80,512]{1,0:T(8,128)(2,1)S(1)} %get-tuple-element.173), channel_id=1, source_target_pairs={{0,4},{1,5},{2,6},{3,7},{4,0},{5,1},{6,2},{7,3},{8,12},{9,13},{10,... | collective-permute-start | bytes 245768 | tf_op jit(solution)/shard_map/swap_A0/ppermute | solution.py:108
  106.1 4.0 %collective-permute-done.25.refs_1_ = bf16[272,512]{1,0:T(8,128)(2,1)S(1)} collective-permute-done((bf16[272,512]{1,0:T(8,128)(2,1)S(1)}, bf16[272,512]{1,0:T(8,128)(2,1)S(1)}, u32[]{:S(2)}, u32[]{:S(2)}) %collective-permute-start.25) | collective-permute-done | bytes 278560 | tf_op jit(solution)/shard_map/swap_B2/ppermute | solution.py:108
  111.4 1.8 %collective-permute-start.28 = (bf16[80,512]{1,0:T(8,128)(2,1)S(1)}, bf16[80,512]{1,0:T(8,128)(2,1)S(1)}, u32[]{:S(2)}, u32[]{:S(2)}) collective-permute-start(bf16[80,512]{1,0:T(8,128)(2,1)S(1)} %scatter.40.refs_2_.refs_0_), channel_id=1, source_target_pairs={{0,4},{1,5},{2,6},{3,7},{4,0},{5,1},{6,2},{7,3},{8,12},{9,13},{10,... | collective-permute-start | bytes 245768 | tf_op jit(solution)/shard_map/swap_A0/ppermute | solution.py:108
  113.2 1.5 collective-permute-start.29
  115.3 3.2 %collective-permute-done.31.refs_1_ = bf16[80,512]{1,0:T(8,128)(2,1)S(1)} collective-permute-done((bf16[80,512]{1,0:T(8,128)(2,1)S(1)}, bf16[80,512]{1,0:T(8,128)(2,1)S(1)}, u32[]{:S(2)}, u32[]{:S(2)}) %collective-permute-start.31) | collective-permute-done | bytes 81952 | tf_op jit(solution)/shard_map/swap_A1/ppermute | solution.py:108
  118.7 2.1 %collective-permute-start.33 = (bf16[96,512]{1,0:T(8,128)(2,1)S(1)}, bf16[96,512]{1,0:T(8,128)(2,1)S(1)}, u32[]{:S(2)}, u32[]{:S(2)}) collective-permute-start(bf16[96,512]{1,0:T(8,128)(2,1)S(1)} %get-tuple-element.187), channel_id=1, source_target_pairs={{0,2},{1,3},{2,0},{3,1},{4,6},{5,7},{6,4},{7,5},{8,10},{9,11},{10,... | collective-permute-start | bytes 294920 | tf_op jit(solution)/shard_map/swap_B1/ppermute | solution.py:108
  120.8 2.1 %collective-permute-start.34 = (bf16[80,512]{1,0:T(8,128)(2,1)S(1)}, bf16[80,512]{1,0:T(8,128)(2,1)S(1)}, u32[]{:S(2)}, u32[]{:S(2)}) collective-permute-start(bf16[80,512]{1,0:T(8,128)(2,1)S(1)} %get-tuple-element.188), channel_id=1, source_target_pairs={{0,1},{1,0},{2,3},{3,2},{4,5},{5,4},{6,7},{7,6},{8,9},{9,8},{10,11... | collective-permute-start | bytes 245768 | tf_op jit(solution)/shard_map/swap_B2/ppermute | solution.py:108
  123.0 2.4 %collective-permute-done.36.refs_1_ = bf16[160,512]{1,0:T(8,128)(2,1)S(1)} collective-permute-done((bf16[160,512]{1,0:T(8,128)(2,1)S(1)}, bf16[160,512]{1,0:T(8,128)(2,1)S(1)}, u32[]{:S(2)}, u32[]{:S(2)}) %collective-permute-start.36) | collective-permute-done | bytes 163872 | tf_op jit(solution)/shard_map/swap_A1/ppermute | solution.py:108
  125.4 2.9 %collective-permute-start.41 = (bf16[320,512]{1,0:T(8,128)(2,1)S(1)}, bf16[320,512]{1,0:T(8,128)(2,1)S(1)}, u32[]{:S(2)}, u32[]{:S(2)}) collective-permute-start(bf16[320,512]{1,0:T(8,128)(2,1)S(1)} %gather.22.refs_2_.refs_0_), channel_id=1, source_target_pairs={{0,1},{1,0},{2,3},{3,2},{4,5},{5,4},{6,7},{7,6},{8,9},{9,8},{10,11... | collective-permute-start | bytes 983048 | tf_op jit(solution)/shard_map/swap_A1/ppermute | solution.py:108
  128.5 2.0 %collective-permute-start.39 = (bf16[48,512]{1,0:T(8,128)(2,1)S(1)}, bf16[48,512]{1,0:T(8,128)(2,1)S(1)}, u32[]{:S(2)}, u32[]{:S(2)}) collective-permute-start(bf16[48,512]{1,0:T(8,128)(2,1)S(1)} %get-tuple-element.194), channel_id=1, source_target_pairs={{0,4},{1,5},{2,6},{3,7},{4,0},{5,1},{6,2},{7,3},{8,12},{9,13},{10,... | collective-permute-start | bytes 147464 | tf_op jit(solution)/shard_map/swap_B2/ppermute | solution.py:108
  131.6 1.8 collective-permute-start.37
  133.5 1.5 collective-permute-start.50
  136.2 1.5 collective-permute-done.38.refs_1_
  138.1 2.5 %collective-permute-start.43 = (bf16[48,512]{1,0:T(8,128)(2,1)S(1)}, bf16[48,512]{1,0:T(8,128)(2,1)S(1)}, u32[]{:S(2)}, u32[]{:S(2)}) collective-permute-start(bf16[48,512]{1,0:T(8,128)(2,1)S(1)} %get-tuple-element.198), channel_id=1, source_target_pairs={{0,4},{1,5},{2,6},{3,7},{4,0},{5,1},{6,2},{7,3},{8,12},{9,13},{10,... | collective-permute-start | bytes 147464 | tf_op jit(solution)/shard_map/swap_B0/ppermute | solution.py:108
  143.3 2.4 %collective-permute-start.44 = (bf16[48,512]{1,0:T(8,128)(2,1)S(1)}, bf16[48,512]{1,0:T(8,128)(2,1)S(1)}, u32[]{:S(2)}, u32[]{:S(2)}) collective-permute-start(bf16[48,512]{1,0:T(8,128)(2,1)S(1)} %scatter.49.refs_2_.refs_0_), channel_id=1, source_target_pairs={{0,4},{1,5},{2,6},{3,7},{4,0},{5,1},{6,2},{7,3},{8,12},{9,13},{10,... | collective-permute-start | bytes 147464 | tf_op jit(solution)/shard_map/swap_B0/ppermute | solution.py:108
  148.4 2.1 %collective-permute-start.47 = (bf16[96,512]{1,0:T(8,128)(2,1)S(1)}, bf16[96,512]{1,0:T(8,128)(2,1)S(1)}, u32[]{:S(2)}, u32[]{:S(2)}) collective-permute-start(bf16[96,512]{1,0:T(8,128)(2,1)S(1)} %gather.28.refs_2_.refs_0_), channel_id=1, source_target_pairs={{0,2},{1,3},{2,0},{3,1},{4,6},{5,7},{6,4},{7,5},{8,10},{9,11},{10,... | collective-permute-start | bytes 294920 | tf_op jit(solution)/shard_map/swap_B0/ppermute | solution.py:108
  150.7 2.6 %collective-permute-done.49.refs_1_ = bf16[64,512]{1,0:T(8,128)(2,1)S(1)} collective-permute-done((bf16[64,512]{1,0:T(8,128)(2,1)S(1)}, bf16[64,512]{1,0:T(8,128)(2,1)S(1)}, u32[]{:S(2)}, u32[]{:S(2)}) %collective-permute-start.49) | collective-permute-done | bytes 65568 | tf_op jit(solution)/shard_map/swap_B2/ppermute | solution.py:108
  153.3 1.6 collective-permute-start.53
  156.5 2.5 %collective-permute-done.53.refs_1_ = bf16[128,512]{1,0:T(8,128)(2,1)S(1)} collective-permute-done((bf16[128,512]{1,0:T(8,128)(2,1)S(1)}, bf16[128,512]{1,0:T(8,128)(2,1)S(1)}, u32[]{:S(2)}, u32[]{:S(2)}) %collective-permute-start.53) | collective-permute-done | bytes 131104 | tf_op jit(solution)/shard_map/swap_B2/ppermute | solution.py:108
  160.0 1.4 collective-permute-done.56.refs_1_
  163.5 1.9 %collective-permute-done.54.refs_1_ = bf16[256,512]{1,0:T(8,128)(2,1)S(1)} collective-permute-done((bf16[256,512]{1,0:T(8,128)(2,1)S(1)}, bf16[256,512]{1,0:T(8,128)(2,1)S(1)}, u32[]{:S(2)}, u32[]{:S(2)}) %collective-permute-start.54) | collective-permute-done | bytes 262176 | tf_op jit(solution)/shard_map/swap_B2/ppermute | solution.py:108
  165.5 6.4 %finish.3 = (f32[2048,512]{1,0:T(8,128)}, f32[512,512]{1,0:T(8,128)}, f32[512,2048]{1,0:T(8,128)}, f32[512,512]{1,0:T(8,128)}, f32[8,128]{1,0:T(8,128)S(1)}, /*index=5*/f32[512]{0:T(512)}, f32[512]{0:T(512)}) custom-call(bf16[1280,512]{1,0:T(8,128)(2,1)S(1)} %gather.33.refs_2_.refs_0_, bf16[1280,512]{1,0:T(8,128)(2,1)S(1)} %collective-permute-done.51.refs_1_, ...), custom_call_target="tpu_custom_call" | custom-call | flops 5750000128 | bytes 18450000 | tf_op jit(solution)/shard_map/finish/pallas_call | solution.py:162
  172.7 2.6 %finish.4 = (f32[1536,512]{1,0:T(8,128)}, f32[1536,512]{1,0:T(8,128)}, f32[512,512]{1,0:T(8,128)}, f32[512,512]{1,0:T(8,128)}, f32[8,128]{1,0:T(8,128)S(1)}) custom-call(bf16[768,512]{1,0:T(8,128)(2,1)S(1)} %gather.38.refs_2_.refs_0_, bf16[768,512]{1,0:T(8,128)(2,1)S(1)} %gather.39.refs_1_.refs_3_, bf16[512,512]{1,0:T(8,128)(2,1)S(1)} %gather.37.refs_5_.refs_2_, ...), custom_call_target="tpu_custom_call" | custom-call | flops 5750000128 | bytes 18450000 | tf_op jit(solution)/shard_map/finish/pallas_call | solution.py:162
  176.2 3.1 %finish.5 = (f32[1536,512]{1,0:T(8,128)}, f32[1536,512]{1,0:T(8,128)}, f32[512,512]{1,0:T(8,128)}, f32[512,512]{1,0:T(8,128)}, f32[8,128]{1,0:T(8,128)}) custom-call(bf16[768,512]{1,0:T(8,128)(2,1)S(1)} %collective-permute-done.58.refs_0_, ...), custom_call_target="tpu_custom_call", output_to_operand_aliasing={{0}: (3, {}), {1}: (4, {}), {2}: (5, {}), {3}: (6, {})} | custom-call | flops 5750000128 | bytes 18450000 | tf_op jit(solution)/shard_map/finish/pallas_call | solution.py:162
  (151 shorter events, 32.0 us)
Async XLA Ops:
  4.0 9.7 %collective-permute-start = (bf16[112,512]{1,0:T(8,128)(2,1)S(1)}, bf16[112,512]{1,0:T(8,128)(2,1)S(1)}, u32[]{:S(2)}, u32[]{:S(2)}) collective-permute-start(bf16[112,512]{1,0:T(8,128)(2,1)S(1)} %get-tuple-element.120.refs_0_), channel_id=1, source_target_pairs={{0,4},{1,5},{2,6},{3,7},{4,0},{5,1},{6,2},{7,3},{8,12},{9,13},{10,... | collective-permute-start | bytes 344072 | tf_op jit(solution)/shard_map/swap_gather_keys/ppermute | solution.py:108
  13.7 11.1 %collective-permute-start.1 = (bf16[224,512]{1,0:T(8,128)(2,1)S(1)}, bf16[224,512]{1,0:T(8,128)(2,1)S(1)}, u32[]{:S(2)}, u32[]{:S(2)}) collective-permute-start(bf16[224,512]{1,0:T(8,128)(2,1)S(1)} %gather_row.4.refs_2_.refs_0_), channel_id=1, source_target_pairs={{0,2},{1,3},{2,0},{3,1},{4,6},{5,7},{6,4},{7,5},{8,10},{9,11},{10,... | collective-permute-start | bytes 688136 | tf_op jit(solution)/shard_map/swap_gather_keys/ppermute | solution.py:108
  14.5 11.7 %collective-permute-start.4 = (bf16[192,512]{1,0:T(8,128)(2,1)S(1)}, bf16[192,512]{1,0:T(8,128)(2,1)S(1)}, u32[]{:S(2)}, u32[]{:S(2)}) collective-permute-start(bf16[192,512]{1,0:T(8,128)(2,1)S(1)} %gather_row.5.refs_2_.refs_0_), channel_id=1, source_target_pairs={{0,4},{1,5},{2,6},{3,7},{4,0},{5,1},{6,2},{7,3},{8,12},{9,13},{10,... | collective-permute-start | bytes 589832 | tf_op jit(solution)/shard_map/swap_gather_values/ppermute | solution.py:108
  24.9 11.9 %collective-permute-start.3 = (bf16[448,512]{1,0:T(8,128)(2,1)S(1)}, bf16[448,512]{1,0:T(8,128)(2,1)S(1)}, u32[]{:S(2)}, u32[]{:S(2)}) collective-permute-start(bf16[448,512]{1,0:T(8,128)(2,1)S(1)} %gather_row.6.refs_2_.refs_8_), channel_id=1, source_target_pairs={{0,1},{1,0},{2,3},{3,2},{4,5},{5,4},{6,7},{7,6},{8,9},{9,8},{10,11... | collective-permute-start | bytes 1376264 | tf_op jit(solution)/shard_map/swap_gather_keys/ppermute | solution.py:108
  26.2 10.5 %collective-permute-start.5 = (bf16[384,512]{1,0:T(8,128)(2,1)S(1)}, bf16[384,512]{1,0:T(8,128)(2,1)S(1)}, u32[]{:S(2)}, u32[]{:S(2)}) collective-permute-start(bf16[384,512]{1,0:T(8,128)(2,1)S(1)} %gather_row.7.refs_10_.refs_15_), channel_id=1, source_target_pairs={{0,2},{1,3},{2,0},{3,1},{4,6},{5,7},{6,4},{7,5},{8,10},{9,11},{10,... | collective-permute-start | bytes 1179656 | tf_op jit(solution)/shard_map/swap_gather_values/ppermute | solution.py:108
  54.1 12.0 %collective-permute-start.6 = (bf16[384,512]{1,0:T(8,128)(2,1)S(1)}, bf16[384,512]{1,0:T(8,128)(2,1)S(1)}, u32[]{:S(2)}, u32[]{:S(2)}) collective-permute-start(bf16[384,512]{1,0:T(8,128)(2,1)S(1)} %get-tuple-element.125), channel_id=1, source_target_pairs={{0,1},{1,0},{2,3},{3,2},{4,5},{5,4},{6,7},{7,6},{8,9},{9,8},{10,11... | collective-permute-start | bytes 1179656 | tf_op jit(solution)/shard_map/swap_K/ppermute | solution.py:108
  55.7 10.8 %collective-permute-start.10 = (bf16[384,512]{1,0:T(8,128)(2,1)S(1)}, bf16[384,512]{1,0:T(8,128)(2,1)S(1)}, u32[]{:S(2)}, u32[]{:S(2)}) collective-permute-start(bf16[384,512]{1,0:T(8,128)(2,1)S(1)} %get-tuple-element.136), channel_id=1, source_target_pairs={{0,2},{1,3},{2,0},{3,1},{4,6},{5,7},{6,4},{7,5},{8,10},{9,11},{10,... | collective-permute-start | bytes 1179656 | tf_op jit(solution)/shard_map/swap_V/ppermute | solution.py:108
  58.8 20.4 %collective-permute-start.14 = (bf16[640,512]{1,0:T(8,128)(2,1)S(1)}, bf16[640,512]{1,0:T(8,128)(2,1)S(1)}, u32[]{:S(2)}, u32[]{:S(2)}) collective-permute-start(bf16[640,512]{1,0:T(8,128)(2,1)S(1)} %get-tuple-element.143), channel_id=1, source_target_pairs={{0,16},{8,24},{16,0},{24,8},{1,17},{9,25},{17,1},{25,9},{2,18},{10... | collective-permute-start | bytes 1966088 | tf_op jit(solution)/shard_map/swap_A1/ppermute | solution.py:108
  60.4 19.8 %collective-permute-start.13 = (bf16[640,512]{1,0:T(8,128)(2,1)S(1)}, bf16[640,512]{1,0:T(8,128)(2,1)S(1)}, u32[]{:S(2)}, u32[]{:S(2)}) collective-permute-start(bf16[640,512]{1,0:T(8,128)(2,1)S(1)} %get-tuple-element.142), channel_id=1, source_target_pairs={{0,1},{1,0},{2,3},{3,2},{4,5},{5,4},{6,7},{7,6},{8,9},{9,8},{10,11... | collective-permute-start | bytes 1966088 | tf_op jit(solution)/shard_map/swap_A0/ppermute | solution.py:108
  66.5 10.8 %collective-permute-start.11 = (bf16[192,512]{1,0:T(8,128)(2,1)S(1)}, bf16[192,512]{1,0:T(8,128)(2,1)S(1)}, u32[]{:S(2)}, u32[]{:S(2)}) collective-permute-start(bf16[192,512]{1,0:T(8,128)(2,1)S(1)} %get-tuple-element.138), channel_id=1, source_target_pairs={{0,4},{1,5},{2,6},{3,7},{4,0},{5,1},{6,2},{7,3},{8,12},{9,13},{10,... | collective-permute-start | bytes 589832 | tf_op jit(solution)/shard_map/swap_V/ppermute | solution.py:108
  68.4 9.8 %collective-permute-start.9 = (bf16[192,512]{1,0:T(8,128)(2,1)S(1)}, bf16[192,512]{1,0:T(8,128)(2,1)S(1)}, u32[]{:S(2)}, u32[]{:S(2)}) collective-permute-start(bf16[192,512]{1,0:T(8,128)(2,1)S(1)} %get-tuple-element.134), channel_id=1, source_target_pairs={{0,2},{1,3},{2,0},{3,1},{4,6},{5,7},{6,4},{7,5},{8,10},{9,11},{10,... | collective-permute-start | bytes 589832 | tf_op jit(solution)/shard_map/swap_K/ppermute | solution.py:108
  77.4 7.3 %collective-permute-start.15 = (bf16[96,512]{1,0:T(8,128)(2,1)S(1)}, bf16[96,512]{1,0:T(8,128)(2,1)S(1)}, u32[]{:S(2)}, u32[]{:S(2)}) collective-permute-start(bf16[96,512]{1,0:T(8,128)(2,1)S(1)} %get-tuple-element.148), channel_id=1, source_target_pairs={{0,1},{1,0},{2,3},{3,2},{4,5},{5,4},{6,7},{7,6},{8,9},{9,8},{10,11... | collective-permute-start | bytes 294920 | tf_op jit(solution)/shard_map/swap_V/ppermute | solution.py:108
  78.2 6.5 %collective-permute-start.12 = (bf16[96,512]{1,0:T(8,128)(2,1)S(1)}, bf16[96,512]{1,0:T(8,128)(2,1)S(1)}, u32[]{:S(2)}, u32[]{:S(2)}) collective-permute-start(bf16[96,512]{1,0:T(8,128)(2,1)S(1)} %get-tuple-element.141), channel_id=1, source_target_pairs={{0,4},{1,5},{2,6},{3,7},{4,0},{5,1},{6,2},{7,3},{8,12},{9,13},{10,... | collective-permute-start | bytes 294920 | tf_op jit(solution)/shard_map/swap_K/ppermute | solution.py:108
  79.4 11.3 %collective-permute-start.21 = (bf16[320,512]{1,0:T(8,128)(2,1)S(1)}, bf16[320,512]{1,0:T(8,128)(2,1)S(1)}, u32[]{:S(2)}, u32[]{:S(2)}) collective-permute-start(bf16[320,512]{1,0:T(8,128)(2,1)S(1)} %get-tuple-element.169), channel_id=1, source_target_pairs={{0,1},{1,0},{2,3},{3,2},{4,5},{5,4},{6,7},{7,6},{8,9},{9,8},{10,11... | collective-permute-start | bytes 983048 | tf_op jit(solution)/shard_map/swap_A1/ppermute | solution.py:108
  80.3 10.3 %collective-permute-start.16 = (bf16[320,512]{1,0:T(8,128)(2,1)S(1)}, bf16[320,512]{1,0:T(8,128)(2,1)S(1)}, u32[]{:S(2)}, u32[]{:S(2)}) collective-permute-start(bf16[320,512]{1,0:T(8,128)(2,1)S(1)} %get-tuple-element.160), channel_id=1, source_target_pairs={{0,16},{8,24},{16,0},{24,8},{1,17},{9,25},{17,1},{25,9},{2,18},{10... | collective-permute-start | bytes 983048 | tf_op jit(solution)/shard_map/swap_A0/ppermute | solution.py:108
  90.8 10.6 %collective-permute-start.23 = (bf16[160,512]{1,0:T(8,128)(2,1)S(1)}, bf16[160,512]{1,0:T(8,128)(2,1)S(1)}, u32[]{:S(2)}, u32[]{:S(2)}) collective-permute-start(bf16[160,512]{1,0:T(8,128)(2,1)S(1)} %get-tuple-element.174), channel_id=1, source_target_pairs={{0,2},{1,3},{2,0},{3,1},{4,6},{5,7},{6,4},{7,5},{8,10},{9,11},{10,... | collective-permute-start | bytes 491528 | tf_op jit(solution)/shard_map/swap_A1/ppermute | solution.py:108
  92.3 9.1 %collective-permute-start.19 = (bf16[160,512]{1,0:T(8,128)(2,1)S(1)}, bf16[160,512]{1,0:T(8,128)(2,1)S(1)}, u32[]{:S(2)}, u32[]{:S(2)}) collective-permute-start(bf16[160,512]{1,0:T(8,128)(2,1)S(1)} %get-tuple-element.167), channel_id=1, source_target_pairs={{0,2},{1,3},{2,0},{3,1},{4,6},{5,7},{6,4},{7,5},{8,10},{9,11},{10,... | collective-permute-start | bytes 491528 | tf_op jit(solution)/shard_map/swap_A0/ppermute | solution.py:108
  93.1 17.0 %collective-permute-start.25 = (bf16[272,512]{1,0:T(8,128)(2,1)S(1)}, bf16[272,512]{1,0:T(8,128)(2,1)S(1)}, u32[]{:S(2)}, u32[]{:S(2)}) collective-permute-start(bf16[272,512]{1,0:T(8,128)(2,1)S(1)} %get-tuple-element.177), channel_id=1, source_target_pairs={{0,2},{1,3},{2,0},{3,1},{4,6},{5,7},{6,4},{7,5},{8,10},{9,11},{10,... | collective-permute-start | bytes 835592 | tf_op jit(solution)/shard_map/swap_B2/ppermute | solution.py:108
  94.5 10.0 %collective-permute-start.27 = (bf16[384,512]{1,0:T(8,128)(2,1)S(1)}, bf16[384,512]{1,0:T(8,128)(2,1)S(1)}, u32[]{:S(2)}, u32[]{:S(2)}) collective-permute-start(bf16[384,512]{1,0:T(8,128)(2,1)S(1)} %get-tuple-element.179), channel_id=1, source_target_pairs={{0,16},{8,24},{16,0},{24,8},{1,17},{9,25},{17,1},{25,9},{2,18},{10... | collective-permute-start | bytes 1179656 | tf_op jit(solution)/shard_map/swap_B1/ppermute | solution.py:108
  96.0 10.0 %collective-permute-start.26 = (bf16[384,512]{1,0:T(8,128)(2,1)S(1)}, bf16[384,512]{1,0:T(8,128)(2,1)S(1)}, u32[]{:S(2)}, u32[]{:S(2)}) collective-permute-start(bf16[384,512]{1,0:T(8,128)(2,1)S(1)} %get-tuple-element.178), channel_id=1, source_target_pairs={{0,1},{1,0},{2,3},{3,2},{4,5},{5,4},{6,7},{7,6},{8,9},{9,8},{10,11... | collective-permute-start | bytes 1179656 | tf_op jit(solution)/shard_map/swap_B0/ppermute | solution.py:108
  101.5 8.6 %collective-permute-start.24 = (bf16[80,512]{1,0:T(8,128)(2,1)S(1)}, bf16[80,512]{1,0:T(8,128)(2,1)S(1)}, u32[]{:S(2)}, u32[]{:S(2)}) collective-permute-start(bf16[80,512]{1,0:T(8,128)(2,1)S(1)} %get-tuple-element.176), channel_id=1, source_target_pairs={{0,4},{1,5},{2,6},{3,7},{4,0},{5,1},{6,2},{7,3},{8,12},{9,13},{10,... | collective-permute-start | bytes 245768 | tf_op jit(solution)/shard_map/swap_A1/ppermute | solution.py:108
  102.4 9.0 %collective-permute-start.22 = (bf16[80,512]{1,0:T(8,128)(2,1)S(1)}, bf16[80,512]{1,0:T(8,128)(2,1)S(1)}, u32[]{:S(2)}, u32[]{:S(2)}) collective-permute-start(bf16[80,512]{1,0:T(8,128)(2,1)S(1)} %get-tuple-element.173), channel_id=1, source_target_pairs={{0,4},{1,5},{2,6},{3,7},{4,0},{5,1},{6,2},{7,3},{8,12},{9,13},{10,... | collective-permute-start | bytes 245768 | tf_op jit(solution)/shard_map/swap_A0/ppermute | solution.py:108
  104.6 14.0 %collective-permute-start.30 = (bf16[192,512]{1,0:T(8,128)(2,1)S(1)}, bf16[192,512]{1,0:T(8,128)(2,1)S(1)}, u32[]{:S(2)}, u32[]{:S(2)}) collective-permute-start(bf16[192,512]{1,0:T(8,128)(2,1)S(1)} %get-tuple-element.184), channel_id=1, source_target_pairs={{0,1},{1,0},{2,3},{3,2},{4,5},{5,4},{6,7},{7,6},{8,9},{9,8},{10,11... | collective-permute-start | bytes 589832 | tf_op jit(solution)/shard_map/swap_B1/ppermute | solution.py:108
  110.2 8.3 %collective-permute-start.31 = (bf16[80,512]{1,0:T(8,128)(2,1)S(1)}, bf16[80,512]{1,0:T(8,128)(2,1)S(1)}, u32[]{:S(2)}, u32[]{:S(2)}) collective-permute-start(bf16[80,512]{1,0:T(8,128)(2,1)S(1)} %scatter.39.refs_2_.refs_0_), channel_id=1, source_target_pairs={{0,4},{1,5},{2,6},{3,7},{4,0},{5,1},{6,2},{7,3},{8,12},{9,13},{10,... | collective-permute-start | bytes 245768 | tf_op jit(solution)/shard_map/swap_A1/ppermute | solution.py:108
  111.4 11.4 %collective-permute-start.28 = (bf16[80,512]{1,0:T(8,128)(2,1)S(1)}, bf16[80,512]{1,0:T(8,128)(2,1)S(1)}, u32[]{:S(2)}, u32[]{:S(2)}) collective-permute-start(bf16[80,512]{1,0:T(8,128)(2,1)S(1)} %scatter.40.refs_2_.refs_0_), channel_id=1, source_target_pairs={{0,4},{1,5},{2,6},{3,7},{4,0},{5,1},{6,2},{7,3},{8,12},{9,13},{10,... | collective-permute-start | bytes 245768 | tf_op jit(solution)/shard_map/swap_A0/ppermute | solution.py:108
  113.2 7.5 %collective-permute-start.29 = (bf16[144,512]{1,0:T(8,128)(2,1)S(1)}, bf16[144,512]{1,0:T(8,128)(2,1)S(1)}, u32[]{:S(2)}, u32[]{:S(2)}) collective-permute-start(bf16[144,512]{1,0:T(8,128)(2,1)S(1)} %get-tuple-element.183), channel_id=1, source_target_pairs={{0,16},{8,24},{16,0},{24,8},{1,17},{9,25},{17,1},{25,9},{2,18},{10... | collective-permute-start | bytes 442376 | tf_op jit(solution)/shard_map/swap_B2/ppermute | solution.py:108
  114.8 13.6 %collective-permute-start.35 = (bf16[192,512]{1,0:T(8,128)(2,1)S(1)}, bf16[192,512]{1,0:T(8,128)(2,1)S(1)}, u32[]{:S(2)}, u32[]{:S(2)}) collective-permute-start(bf16[192,512]{1,0:T(8,128)(2,1)S(1)} %get-tuple-element.189), channel_id=1, source_target_pairs={{0,16},{8,24},{16,0},{24,8},{1,17},{9,25},{17,1},{25,9},{2,18},{10... | collective-permute-start | bytes 589832 | tf_op jit(solution)/shard_map/swap_B0/ppermute | solution.py:108
  118.5 6.9 %collective-permute-start.36 = (bf16[160,512]{1,0:T(8,128)(2,1)S(1)}, bf16[160,512]{1,0:T(8,128)(2,1)S(1)}, u32[]{:S(2)}, u32[]{:S(2)}) collective-permute-start(bf16[160,512]{1,0:T(8,128)(2,1)S(1)} %gather.20.refs_2_.refs_0_), channel_id=1, source_target_pairs={{0,2},{1,3},{2,0},{3,1},{4,6},{5,7},{6,4},{7,5},{8,10},{9,11},{10,... | collective-permute-start | bytes 491528 | tf_op jit(solution)/shard_map/swap_A1/ppermute | solution.py:108
  118.7 11.9 %collective-permute-start.33 = (bf16[96,512]{1,0:T(8,128)(2,1)S(1)}, bf16[96,512]{1,0:T(8,128)(2,1)S(1)}, u32[]{:S(2)}, u32[]{:S(2)}) collective-permute-start(bf16[96,512]{1,0:T(8,128)(2,1)S(1)} %get-tuple-element.187), channel_id=1, source_target_pairs={{0,2},{1,3},{2,0},{3,1},{4,6},{5,7},{6,4},{7,5},{8,10},{9,11},{10,... | collective-permute-start | bytes 294920 | tf_op jit(solution)/shard_map/swap_B1/ppermute | solution.py:108
  120.8 7.7 %collective-permute-start.34 = (bf16[80,512]{1,0:T(8,128)(2,1)S(1)}, bf16[80,512]{1,0:T(8,128)(2,1)S(1)}, u32[]{:S(2)}, u32[]{:S(2)}) collective-permute-start(bf16[80,512]{1,0:T(8,128)(2,1)S(1)} %get-tuple-element.188), channel_id=1, source_target_pairs={{0,1},{1,0},{2,3},{3,2},{4,5},{5,4},{6,7},{7,6},{8,9},{9,8},{10,11... | collective-permute-start | bytes 245768 | tf_op jit(solution)/shard_map/swap_B2/ppermute | solution.py:108
  122.9 8.7 %collective-permute-start.32 = (bf16[160,512]{1,0:T(8,128)(2,1)S(1)}, bf16[160,512]{1,0:T(8,128)(2,1)S(1)}, u32[]{:S(2)}, u32[]{:S(2)}) collective-permute-start(bf16[160,512]{1,0:T(8,128)(2,1)S(1)} %gather.21.refs_2_.refs_0_), channel_id=1, source_target_pairs={{0,2},{1,3},{2,0},{3,1},{4,6},{5,7},{6,4},{7,5},{8,10},{9,11},{10,... | collective-permute-start | bytes 491528 | tf_op jit(solution)/shard_map/swap_A0/ppermute | solution.py:108
  125.4 8.0 %collective-permute-start.41 = (bf16[320,512]{1,0:T(8,128)(2,1)S(1)}, bf16[320,512]{1,0:T(8,128)(2,1)S(1)}, u32[]{:S(2)}, u32[]{:S(2)}) collective-permute-start(bf16[320,512]{1,0:T(8,128)(2,1)S(1)} %gather.22.refs_2_.refs_0_), channel_id=1, source_target_pairs={{0,1},{1,0},{2,3},{3,2},{4,5},{5,4},{6,7},{7,6},{8,9},{9,8},{10,11... | collective-permute-start | bytes 983048 | tf_op jit(solution)/shard_map/swap_A1/ppermute | solution.py:108
  128.4 6.6 %collective-permute-start.40 = (bf16[96,512]{1,0:T(8,128)(2,1)S(1)}, bf16[96,512]{1,0:T(8,128)(2,1)S(1)}, u32[]{:S(2)}, u32[]{:S(2)}) collective-permute-start(bf16[96,512]{1,0:T(8,128)(2,1)S(1)} %get-tuple-element.195), channel_id=1, source_target_pairs={{0,2},{1,3},{2,0},{3,1},{4,6},{5,7},{6,4},{7,5},{8,10},{9,11},{10,... | collective-permute-start | bytes 294920 | tf_op jit(solution)/shard_map/swap_B0/ppermute | solution.py:108
  128.5 6.5 %collective-permute-start.39 = (bf16[48,512]{1,0:T(8,128)(2,1)S(1)}, bf16[48,512]{1,0:T(8,128)(2,1)S(1)}, u32[]{:S(2)}, u32[]{:S(2)}) collective-permute-start(bf16[48,512]{1,0:T(8,128)(2,1)S(1)} %get-tuple-element.194), channel_id=1, source_target_pairs={{0,4},{1,5},{2,6},{3,7},{4,0},{5,1},{6,2},{7,3},{8,12},{9,13},{10,... | collective-permute-start | bytes 147464 | tf_op jit(solution)/shard_map/swap_B2/ppermute | solution.py:108
  130.6 7.1 %collective-permute-start.38 = (bf16[48,512]{1,0:T(8,128)(2,1)S(1)}, bf16[48,512]{1,0:T(8,128)(2,1)S(1)}, u32[]{:S(2)}, u32[]{:S(2)}) collective-permute-start(bf16[48,512]{1,0:T(8,128)(2,1)S(1)} %get-tuple-element.193), channel_id=1, source_target_pairs={{0,4},{1,5},{2,6},{3,7},{4,0},{5,1},{6,2},{7,3},{8,12},{9,13},{10,... | collective-permute-start | bytes 147464 | tf_op jit(solution)/shard_map/swap_B1/ppermute | solution.py:108
  131.6 10.3 %collective-permute-start.37 = (bf16[320,512]{1,0:T(8,128)(2,1)S(1)}, bf16[320,512]{1,0:T(8,128)(2,1)S(1)}, u32[]{:S(2)}, u32[]{:S(2)}) collective-permute-start(bf16[320,512]{1,0:T(8,128)(2,1)S(1)} %gather.23.refs_2_.refs_0_), channel_id=1, source_target_pairs={{0,16},{8,24},{16,0},{24,8},{1,17},{9,25},{17,1},{25,9},{2,18},{10... | collective-permute-start | bytes 983048 | tf_op jit(solution)/shard_map/swap_A0/ppermute | solution.py:108
  133.5 17.0 %collective-permute-start.50 = (bf16[640,512]{1,0:T(8,128)(2,1)S(1)}, bf16[640,512]{1,0:T(8,128)(2,1)S(1)}, u32[]{:S(2)}, u32[]{:S(2)}) collective-permute-start(bf16[640,512]{1,0:T(8,128)(2,1)S(1)} %gather.24.refs_2_.refs_0_), channel_id=1, source_target_pairs={{0,16},{8,24},{16,0},{24,8},{1,17},{9,25},{17,1},{25,9},{2,18},{10... | collective-permute-start | bytes 1966088 | tf_op jit(solution)/shard_map/swap_A1/ppermute | solution.py:108
  135.1 10.7 %collective-permute-start.46 = (bf16[32,512]{1,0:T(8,128)(2,1)S(1)}, bf16[32,512]{1,0:T(8,128)(2,1)S(1)}, u32[]{:S(2)}, u32[]{:S(2)}) collective-permute-start(bf16[32,512]{1,0:T(8,128)(2,1)S(1)} %get-tuple-element.197.refs_2_.refs_0_), channel_id=1, source_target_pairs={{0,4},{1,5},{2,6},{3,7},{4,0},{5,1},{6,2},{7,3},{8,12},{9,13},{10,... | collective-permute-start | bytes 98312 | tf_op jit(solution)/shard_map/swap_B2/ppermute | solution.py:108
  137.7 9.2 %collective-permute-start.45 = (bf16[48,512]{1,0:T(8,128)(2,1)S(1)}, bf16[48,512]{1,0:T(8,128)(2,1)S(1)}, u32[]{:S(2)}, u32[]{:S(2)}) collective-permute-start(bf16[48,512]{1,0:T(8,128)(2,1)S(1)} %scatter.48.refs_2_.refs_0_), channel_id=1, source_target_pairs={{0,4},{1,5},{2,6},{3,7},{4,0},{5,1},{6,2},{7,3},{8,12},{9,13},{10,... | collective-permute-start | bytes 147464 | tf_op jit(solution)/shard_map/swap_B1/ppermute | solution.py:108
  142.0 14.3 %collective-permute-start.42 = (bf16[640,512]{1,0:T(8,128)(2,1)S(1)}, bf16[640,512]{1,0:T(8,128)(2,1)S(1)}, u32[]{:S(2)}, u32[]{:S(2)}) collective-permute-start(bf16[640,512]{1,0:T(8,128)(2,1)S(1)} %gather.25.refs_2_.refs_0_), channel_id=1, source_target_pairs={{0,1},{1,0},{2,3},{3,2},{4,5},{5,4},{6,7},{7,6},{8,9},{9,8},{10,11... | collective-permute-start | bytes 1966088 | tf_op jit(solution)/shard_map/swap_A0/ppermute | solution.py:108
  145.7 7.6 %collective-permute-start.49 = (bf16[64,512]{1,0:T(8,128)(2,1)S(1)}, bf16[64,512]{1,0:T(8,128)(2,1)S(1)}, u32[]{:S(2)}, u32[]{:S(2)}) collective-permute-start(bf16[64,512]{1,0:T(8,128)(2,1)S(1)} %gather.26.refs_2_.refs_0_), channel_id=1, source_target_pairs={{0,1},{1,0},{2,3},{3,2},{4,5},{5,4},{6,7},{7,6},{8,9},{9,8},{10,11... | collective-permute-start | bytes 196616 | tf_op jit(solution)/shard_map/swap_B2/ppermute | solution.py:108
  146.8 8.0 %collective-permute-start.48 = (bf16[96,512]{1,0:T(8,128)(2,1)S(1)}, bf16[96,512]{1,0:T(8,128)(2,1)S(1)}, u32[]{:S(2)}, u32[]{:S(2)}) collective-permute-start(bf16[96,512]{1,0:T(8,128)(2,1)S(1)} %gather.27.refs_2_.refs_0_), channel_id=1, source_target_pairs={{0,2},{1,3},{2,0},{3,1},{4,6},{5,7},{6,4},{7,5},{8,10},{9,11},{10,... | collective-permute-start | bytes 294920 | tf_op jit(solution)/shard_map/swap_B1/ppermute | solution.py:108
  148.4 7.3 %collective-permute-start.47 = (bf16[96,512]{1,0:T(8,128)(2,1)S(1)}, bf16[96,512]{1,0:T(8,128)(2,1)S(1)}, u32[]{:S(2)}, u32[]{:S(2)}) collective-permute-start(bf16[96,512]{1,0:T(8,128)(2,1)S(1)} %gather.28.refs_2_.refs_0_), channel_id=1, source_target_pairs={{0,2},{1,3},{2,0},{3,1},{4,6},{5,7},{6,4},{7,5},{8,10},{9,11},{10,... | collective-permute-start | bytes 294920 | tf_op jit(solution)/shard_map/swap_B0/ppermute | solution.py:108
  150.6 14.9 %collective-permute-start.52 = (bf16[1280,512]{1,0:T(8,128)(2,1)S(1)}, bf16[1280,512]{1,0:T(8,128)(2,1)S(1)}, u32[]{:S(2)}, u32[]{:S(2)}) collective-permute-start(bf16[1280,512]{1,0:T(8,128)(2,1)S(1)} %gather.29.refs_2_), channel_id=1, source_target_pairs={{0,8},{8,0},{16,24},{24,16},{1,9},{9,1},{17,25},{25,17},{2,10},{10... | collective-permute-start | bytes 3932168 | tf_op jit(solution)/shard_map/swap_A1/ppermute | solution.py:108
  154.9 7.9 %collective-permute-start.55 = (bf16[192,512]{1,0:T(8,128)(2,1)S(1)}, bf16[192,512]{1,0:T(8,128)(2,1)S(1)}, u32[]{:S(2)}, u32[]{:S(2)}) collective-permute-start(bf16[192,512]{1,0:T(8,128)(2,1)S(1)} %gather.31.refs_2_.refs_0_), channel_id=1, source_target_pairs={{0,1},{1,0},{2,3},{3,2},{4,5},{5,4},{6,7},{7,6},{8,9},{9,8},{10,11... | collective-permute-start | bytes 589832 | tf_op jit(solution)/shard_map/swap_B1/ppermute | solution.py:108
  156.4 9.1 %collective-permute-start.51 = (bf16[1280,512]{1,0:T(8,128)(2,1)S(1)}, bf16[1280,512]{1,0:T(8,128)(2,1)S(1)}, u32[]{:S(2)}, u32[]{:S(2)}) collective-permute-start(bf16[1280,512]{1,0:T(8,128)(2,1)S(1)} %gather.33.refs_2_.refs_0_), channel_id=1, source_target_pairs={{0,8},{8,0},{16,24},{24,16},{1,9},{9,1},{17,25},{25,17},{2,10},{10... | collective-permute-start | bytes 3932168 | tf_op jit(solution)/shard_map/swap_A0/ppermute | solution.py:108
  161.4 10.4 %collective-permute-start.57 = (bf16[384,512]{1,0:T(8,128)(2,1)S(1)}, bf16[384,512]{1,0:T(8,128)(2,1)S(1)}, u32[]{:S(2)}, u32[]{:S(2)}) collective-permute-start(bf16[384,512]{1,0:T(8,128)(2,1)S(1)} %gather.35.refs_2_.refs_0_), channel_id=1, source_target_pairs={{0,1},{1,0},{2,3},{3,2},{4,5},{5,4},{6,7},{7,6},{8,9},{9,8},{10,11... | collective-permute-start | bytes 1179656 | tf_op jit(solution)/shard_map/swap_B0/ppermute | solution.py:108
  162.9 9.1 %collective-permute-start.59 = (bf16[384,512]{1,0:T(8,128)(2,1)S(1)}, bf16[384,512]{1,0:T(8,128)(2,1)S(1)}, u32[]{:S(2)}, u32[]{:S(2)}) collective-permute-start(bf16[384,512]{1,0:T(8,128)(2,1)S(1)} %gather.36.refs_2_.refs_0_), channel_id=1, source_target_pairs={{0,16},{8,24},{16,0},{24,8},{1,17},{9,25},{17,1},{25,9},{2,18},{10... | collective-permute-start | bytes 1179656 | tf_op jit(solution)/shard_map/swap_B1/ppermute | solution.py:108
  (20 other events, 126.7 us)

commit v7 on v6

--- a/solution.py
+++ b/solution.py
@@ -604,8 +604,8 @@
 
 def finish(plan, order, name, chosen, cores, targets=(), gains=()):
     items, blocks, shapes = [], [], []
-    for part in chosen:
-        for core in cores:
+    for part, halves in zip(chosen, cores):
+        for core in halves:
             parts = [(rows, len(shapes) + target, columns) for rows, target, columns in part.parts]
             items.append((part.bits, parts, core))
             blocks.append(part.far if core else part.held)
@@ -851,13 +851,15 @@
             )
         elif event == "Af":
             grads, gains = finish(
-                plan, order, "finish", [chains["A0"], chains["A1"]], (0, 1), (), chains["B2"].sums
+                plan, order, "finish", [chains["A0"], chains["A1"]], [(0, 1)] * 2, (),
+                chains["B2"].sums,
             )
             grad_down, grad_out, grad_up, grad_query = grads
         elif event in ("Bn", "Bf"):
             chosen = [chains[name] for name in ("B0", "B1", "B2")]
             previous = () if event == "Bn" else results
-            results, _ = finish(plan, order, "finish", chosen, (int(event == "Bf"),), previous)
+            cores = [(0,), (0,), (0, 1)] if event == "Bn" else [(1,), (1,), ()]
+            results, _ = finish(plan, order, "finish", chosen, cores, previous)
         else:
             name, _, cost = event.partition(":")
             chains[name].step(float(cost or EACH))

time: 180 us -> 179 us (level)
  transfers between devices with their start and end apart: 62 -> 62, of which waited for: 22 -> 21; matrix products, arithmetic and copies ran while one was open for 0% -> 0% of each run, Pallas kernels for 9% -> 10%
where the time goes in v7:
time: 179 us
  starting transfers between devices  74.4 us (42%)
  waiting for transfers between devices  62.6 us (35%)
  Pallas kernels  40.2 us (22%)
    ppermute x62, starting transfers between devices, swap(): return lax.ppermute(array, axis, [(i, i ^ value) for i in range(size)])  74.4 us
    ppermute x62, waiting for transfers between devices, swap(): return lax.ppermute(array, axis, [(i, i ^ value) for i in range(size)])  62.6 us
    pallas_call x63, Pallas kernels, run(): pl.pallas_call(without_last, name=name, out_shape=[pltpu.HBM(shape, dtype...  40.2 us
  transfers between devices with their start and end apart: 62, of which 21 were waited for; matrix products, arithmetic and copies ran while one was open for 0% of the time, Pallas kernels for 10%

profile of v7, /device:TPU:0, one launch (start us, length us, event | category | flops | bytes accessed | tf_op | source)
XLA Modules:
  0.0 178.6 jit_solution(17882785660102514481)
XLA Ops:
  0.6 3.3 %project.1 = (f32[288,512]{1,0:T(8,128)S(1)}, bf16[288,512]{1,0:T(8,128)(2,1)S(1)}, bf16[288,512]{1,0:T(8,128)(2,1)S(1)}, bf16[288,512]{1,0:T(8,128)(2,1)S(1)}, ...) custom-call(bf16[2,1,144,512]{3,2,1,0:T(8,128)(2,1)} %refs_0_.1, ...), custom_call_target="tpu_custom_call" | custom-call | flops 5750000128 | bytes 18450000 | tf_op jit(solution)/shard_map/project/pallas_call | solution.py:162
  4.0 4.1 %collective-permute-start = (bf16[112,512]{1,0:T(8,128)(2,1)S(1)}, bf16[112,512]{1,0:T(8,128)(2,1)S(1)}, u32[]{:S(2)}, u32[]{:S(2)}) collective-permute-start(bf16[112,512]{1,0:T(8,128)(2,1)S(1)} %get-tuple-element.120.refs_0_), channel_id=1, source_target_pairs={{0,4},{1,5},{2,6},{3,7},{4,0},{5,1},{6,2},{7,3},{8,12},{9,13},{10,... | collective-permute-start | bytes 344072 | tf_op jit(solution)/shard_map/swap_gather_keys/ppermute | solution.py:108
  8.1 1.5 collective-permute-start.2
  9.6 4.1 %collective-permute-done.refs_1_ = bf16[112,512]{1,0:T(8,128)(2,1)S(1)} collective-permute-done((bf16[112,512]{1,0:T(8,128)(2,1)S(1)}, bf16[112,512]{1,0:T(8,128)(2,1)S(1)}, u32[]{:S(2)}, u32[]{:S(2)}) %collective-permute-start) | collective-permute-done | bytes 114720 | tf_op jit(solution)/shard_map/swap_gather_keys/ppermute | solution.py:108
  14.5 3.4 %collective-permute-start.4 = (bf16[192,512]{1,0:T(8,128)(2,1)S(1)}, bf16[192,512]{1,0:T(8,128)(2,1)S(1)}, u32[]{:S(2)}, u32[]{:S(2)}) collective-permute-start(bf16[192,512]{1,0:T(8,128)(2,1)S(1)} %gather_row.5.refs_2_.refs_0_), channel_id=1, source_target_pairs={{0,4},{1,5},{2,6},{3,7},{4,0},{5,1},{6,2},{7,3},{8,12},{9,13},{10,... | collective-permute-start | bytes 589832 | tf_op jit(solution)/shard_map/swap_gather_values/ppermute | solution.py:108
  18.0 6.8 %collective-permute-done.1.refs_1_ = bf16[224,512]{1,0:T(8,128)(2,1)S(1)} collective-permute-done((bf16[224,512]{1,0:T(8,128)(2,1)S(1)}, bf16[224,512]{1,0:T(8,128)(2,1)S(1)}, u32[]{:S(2)}, u32[]{:S(2)}) %collective-permute-start.1) | collective-permute-done | bytes 229408 | tf_op jit(solution)/shard_map/swap_gather_keys/ppermute | solution.py:108
  26.2 1.7 collective-permute-start.5
  28.0 8.8 %collective-permute-done.5.refs_11_ = bf16[384,512]{1,0:T(8,128)(2,1)S(1)} collective-permute-done((bf16[384,512]{1,0:T(8,128)(2,1)S(1)}, bf16[384,512]{1,0:T(8,128)(2,1)S(1)}, u32[]{:S(2)}, u32[]{:S(2)}) %collective-permute-start.5) | collective-permute-done | bytes 393248 | tf_op jit(solution)/shard_map/swap_gather_values/ppermute | solution.py:108
  36.8 16.8 %layer.1 = (bf16[2,1,144,512]{3,2,1,0:T(8,128)(2,1)}, f32[288,512]{1,0:T(8,128)S(1)}, bf16[288,512]{1,0:T(8,128)(2,1)S(1)}, f32[288,512]{1,0:T(8,128)S(1)}, f32[...) custom-call(f32[288,512]{1,0:T(8,128)S(1)} %get-tuple-element.114.re, ...), custom_call_target="tpu_custom_call" | custom-call | flops 5750000128 | bytes 18450000 | tf_op jit(solution)/shard_map/layer/pallas_call | solution.py:162
  54.1 1.5 collective-permute-start.6
  55.7 1.8 collective-permute-start.10
  58.8 1.6 collective-permute-start.14
  60.4 1.5 collective-permute-start.13
  61.9 4.2 %collective-permute-done.6.refs_1_ = bf16[384,512]{1,0:T(8,128)(2,1)S(1)} collective-permute-done((bf16[384,512]{1,0:T(8,128)(2,1)S(1)}, bf16[384,512]{1,0:T(8,128)(2,1)S(1)}, u32[]{:S(2)}, u32[]{:S(2)}) %collective-permute-start.6) | collective-permute-done | bytes 393248 | tf_op jit(solution)/shard_map/swap_K/ppermute | solution.py:108
  66.5 1.8 %collective-permute-start.11 = (bf16[192,512]{1,0:T(8,128)(2,1)S(1)}, bf16[192,512]{1,0:T(8,128)(2,1)S(1)}, u32[]{:S(2)}, u32[]{:S(2)}) collective-permute-start(bf16[192,512]{1,0:T(8,128)(2,1)S(1)} %get-tuple-element.138), channel_id=1, source_target_pairs={{0,4},{1,5},{2,6},{3,7},{4,0},{5,1},{6,2},{7,3},{8,12},{9,13},{10,... | collective-permute-start | bytes 589832 | tf_op jit(solution)/shard_map/swap_V/ppermute | solution.py:108
  68.4 1.7 collective-permute-start.9
  70.1 7.3 %collective-permute-done.11.refs_1_ = bf16[192,512]{1,0:T(8,128)(2,1)S(1)} collective-permute-done((bf16[192,512]{1,0:T(8,128)(2,1)S(1)}, bf16[192,512]{1,0:T(8,128)(2,1)S(1)}, u32[]{:S(2)}, u32[]{:S(2)}) %collective-permute-start.11) | collective-permute-done | bytes 196640 | tf_op jit(solution)/shard_map/swap_V/ppermute | solution.py:108
  80.3 1.5 collective-permute-start.16
  81.9 2.8 %collective-permute-done.12.refs_1_ = bf16[96,512]{1,0:T(8,128)(2,1)S(1)} collective-permute-done((bf16[96,512]{1,0:T(8,128)(2,1)S(1)}, bf16[96,512]{1,0:T(8,128)(2,1)S(1)}, u32[]{:S(2)}, u32[]{:S(2)}) %collective-permute-start.12) | collective-permute-done | bytes 98336 | tf_op jit(solution)/shard_map/swap_K/ppermute | solution.py:108
  87.9 2.3 %tail_kernel.1 = (bf16[528,512]{1,0:T(8,128)(2,1)S(1)}, bf16[528,512]{1,0:T(8,128)(2,1)S(1)}, bf16[2,1,144,512]{3,2,1,0:T(8,128)(2,1)}) custom-call(bf16[288,512]{1,0:T(8,128)(2,1)S(1)} %get-tuple-element.115.refs_1_.refs_0_, f32[288,512]{1,0:T(8,128)S(1)} %get-tuple-element.114.refs_0_.refs_1_, bf16[512]{0:T(512)(128)(2,1)S(1)} %copy-done.5, ...), custom_call_target="tpu_custom_call" | custom-call | flops 5750000128 | bytes 18450000 | tf_op jit(solution)/shard_map/tail_kernel/pallas_call | solution.py:162
  90.8 1.4 collective-permute-start.23
  93.1 1.4 collective-permute-start.25
  94.5 1.5 collective-permute-start.27
  96.3 5.1 %collective-permute-done.19.refs_1_ = bf16[160,512]{1,0:T(8,128)(2,1)S(1)} collective-permute-done((bf16[160,512]{1,0:T(8,128)(2,1)S(1)}, bf16[160,512]{1,0:T(8,128)(2,1)S(1)}, u32[]{:S(2)}, u32[]{:S(2)}) %collective-permute-start.19) | collective-permute-done | bytes 163872 | tf_op jit(solution)/shard_map/swap_A0/ppermute | solution.py:108
  102.4 2.1 %collective-permute-start.22 = (bf16[80,512]{1,0:T(8,128)(2,1)S(1)}, bf16[80,512]{1,0:T(8,128)(2,1)S(1)}, u32[]{:S(2)}, u32[]{:S(2)}) collective-permute-start(bf16[80,512]{1,0:T(8,128)(2,1)S(1)} %get-tuple-element.173), channel_id=1, source_target_pairs={{0,4},{1,5},{2,6},{3,7},{4,0},{5,1},{6,2},{7,3},{8,12},{9,13},{10,... | collective-permute-start | bytes 245768 | tf_op jit(solution)/shard_map/swap_A0/ppermute | solution.py:108
  106.1 4.0 %collective-permute-done.25.refs_1_ = bf16[272,512]{1,0:T(8,128)(2,1)S(1)} collective-permute-done((bf16[272,512]{1,0:T(8,128)(2,1)S(1)}, bf16[272,512]{1,0:T(8,128)(2,1)S(1)}, u32[]{:S(2)}, u32[]{:S(2)}) %collective-permute-start.25) | collective-permute-done | bytes 278560 | tf_op jit(solution)/shard_map/swap_B2/ppermute | solution.py:108
  111.4 1.8 %collective-permute-start.28 = (bf16[80,512]{1,0:T(8,128)(2,1)S(1)}, bf16[80,512]{1,0:T(8,128)(2,1)S(1)}, u32[]{:S(2)}, u32[]{:S(2)}) collective-permute-start(bf16[80,512]{1,0:T(8,128)(2,1)S(1)} %scatter.40.refs_2_.refs_0_), channel_id=1, source_target_pairs={{0,4},{1,5},{2,6},{3,7},{4,0},{5,1},{6,2},{7,3},{8,12},{9,13},{10,... | collective-permute-start | bytes 245768 | tf_op jit(solution)/shard_map/swap_A0/ppermute | solution.py:108
  113.2 1.5 collective-permute-start.29
  115.3 3.2 %collective-permute-done.31.refs_1_ = bf16[80,512]{1,0:T(8,128)(2,1)S(1)} collective-permute-done((bf16[80,512]{1,0:T(8,128)(2,1)S(1)}, bf16[80,512]{1,0:T(8,128)(2,1)S(1)}, u32[]{:S(2)}, u32[]{:S(2)}) %collective-permute-start.31) | collective-permute-done | bytes 81952 | tf_op jit(solution)/shard_map/swap_A1/ppermute | solution.py:108
  118.7 2.1 %collective-permute-start.33 = (bf16[96,512]{1,0:T(8,128)(2,1)S(1)}, bf16[96,512]{1,0:T(8,128)(2,1)S(1)}, u32[]{:S(2)}, u32[]{:S(2)}) collective-permute-start(bf16[96,512]{1,0:T(8,128)(2,1)S(1)} %get-tuple-element.187), channel_id=1, source_target_pairs={{0,2},{1,3},{2,0},{3,1},{4,6},{5,7},{6,4},{7,5},{8,10},{9,11},{10,... | collective-permute-start | bytes 294920 | tf_op jit(solution)/shard_map/swap_B1/ppermute | solution.py:108
  120.8 2.1 %collective-permute-start.34 = (bf16[80,512]{1,0:T(8,128)(2,1)S(1)}, bf16[80,512]{1,0:T(8,128)(2,1)S(1)}, u32[]{:S(2)}, u32[]{:S(2)}) collective-permute-start(bf16[80,512]{1,0:T(8,128)(2,1)S(1)} %get-tuple-element.188), channel_id=1, source_target_pairs={{0,1},{1,0},{2,3},{3,2},{4,5},{5,4},{6,7},{7,6},{8,9},{9,8},{10,11... | collective-permute-start | bytes 245768 | tf_op jit(solution)/shard_map/swap_B2/ppermute | solution.py:108
  123.0 2.4 %collective-permute-done.36.refs_1_ = bf16[160,512]{1,0:T(8,128)(2,1)S(1)} collective-permute-done((bf16[160,512]{1,0:T(8,128)(2,1)S(1)}, bf16[160,512]{1,0:T(8,128)(2,1)S(1)}, u32[]{:S(2)}, u32[]{:S(2)}) %collective-permute-start.36) | collective-permute-done | bytes 163872 | tf_op jit(solution)/shard_map/swap_A1/ppermute | solution.py:108
  125.4 2.9 %collective-permute-start.41 = (bf16[320,512]{1,0:T(8,128)(2,1)S(1)}, bf16[320,512]{1,0:T(8,128)(2,1)S(1)}, u32[]{:S(2)}, u32[]{:S(2)}) collective-permute-start(bf16[320,512]{1,0:T(8,128)(2,1)S(1)} %gather.22.refs_2_.refs_0_), channel_id=1, source_target_pairs={{0,1},{1,0},{2,3},{3,2},{4,5},{5,4},{6,7},{7,6},{8,9},{9,8},{10,11... | collective-permute-start | bytes 983048 | tf_op jit(solution)/shard_map/swap_A1/ppermute | solution.py:108
  128.5 2.0 %collective-permute-start.39 = (bf16[48,512]{1,0:T(8,128)(2,1)S(1)}, bf16[48,512]{1,0:T(8,128)(2,1)S(1)}, u32[]{:S(2)}, u32[]{:S(2)}) collective-permute-start(bf16[48,512]{1,0:T(8,128)(2,1)S(1)} %get-tuple-element.194), channel_id=1, source_target_pairs={{0,4},{1,5},{2,6},{3,7},{4,0},{5,1},{6,2},{7,3},{8,12},{9,13},{10,... | collective-permute-start | bytes 147464 | tf_op jit(solution)/shard_map/swap_B2/ppermute | solution.py:108
  131.6 1.8 collective-permute-start.37
  133.5 1.5 collective-permute-start.50
  136.2 1.5 collective-permute-done.38.refs_1_
  138.1 2.5 %collective-permute-start.43 = (bf16[48,512]{1,0:T(8,128)(2,1)S(1)}, bf16[48,512]{1,0:T(8,128)(2,1)S(1)}, u32[]{:S(2)}, u32[]{:S(2)}) collective-permute-start(bf16[48,512]{1,0:T(8,128)(2,1)S(1)} %get-tuple-element.198), channel_id=1, source_target_pairs={{0,4},{1,5},{2,6},{3,7},{4,0},{5,1},{6,2},{7,3},{8,12},{9,13},{10,... | collective-permute-start | bytes 147464 | tf_op jit(solution)/shard_map/swap_B0/ppermute | solution.py:108
  143.3 2.4 %collective-permute-start.44 = (bf16[48,512]{1,0:T(8,128)(2,1)S(1)}, bf16[48,512]{1,0:T(8,128)(2,1)S(1)}, u32[]{:S(2)}, u32[]{:S(2)}) collective-permute-start(bf16[48,512]{1,0:T(8,128)(2,1)S(1)} %scatter.49.refs_2_.refs_0_), channel_id=1, source_target_pairs={{0,4},{1,5},{2,6},{3,7},{4,0},{5,1},{6,2},{7,3},{8,12},{9,13},{10,... | collective-permute-start | bytes 147464 | tf_op jit(solution)/shard_map/swap_B0/ppermute | solution.py:108
  148.4 2.1 %collective-permute-start.47 = (bf16[96,512]{1,0:T(8,128)(2,1)S(1)}, bf16[96,512]{1,0:T(8,128)(2,1)S(1)}, u32[]{:S(2)}, u32[]{:S(2)}) collective-permute-start(bf16[96,512]{1,0:T(8,128)(2,1)S(1)} %gather.28.refs_2_.refs_0_), channel_id=1, source_target_pairs={{0,2},{1,3},{2,0},{3,1},{4,6},{5,7},{6,4},{7,5},{8,10},{9,11},{10,... | collective-permute-start | bytes 294920 | tf_op jit(solution)/shard_map/swap_B0/ppermute | solution.py:108
  150.7 2.6 %collective-permute-done.49.refs_1_ = bf16[64,512]{1,0:T(8,128)(2,1)S(1)} collective-permute-done((bf16[64,512]{1,0:T(8,128)(2,1)S(1)}, bf16[64,512]{1,0:T(8,128)(2,1)S(1)}, u32[]{:S(2)}, u32[]{:S(2)}) %collective-permute-start.49) | collective-permute-done | bytes 65568 | tf_op jit(solution)/shard_map/swap_B2/ppermute | solution.py:108
  153.3 1.6 collective-permute-start.53
  156.5 2.5 %collective-permute-done.53.refs_1_ = bf16[128,512]{1,0:T(8,128)(2,1)S(1)} collective-permute-done((bf16[128,512]{1,0:T(8,128)(2,1)S(1)}, bf16[128,512]{1,0:T(8,128)(2,1)S(1)}, u32[]{:S(2)}, u32[]{:S(2)}) %collective-permute-start.53) | collective-permute-done | bytes 131104 | tf_op jit(solution)/shard_map/swap_B2/ppermute | solution.py:108
  160.0 1.4 collective-permute-done.56.refs_1_
  163.5 1.9 %collective-permute-done.54.refs_1_ = bf16[256,512]{1,0:T(8,128)(2,1)S(1)} collective-permute-done((bf16[256,512]{1,0:T(8,128)(2,1)S(1)}, bf16[256,512]{1,0:T(8,128)(2,1)S(1)}, u32[]{:S(2)}, u32[]{:S(2)}) %collective-permute-start.54) | collective-permute-done | bytes 262176 | tf_op jit(solution)/shard_map/swap_B2/ppermute | solution.py:108
  165.5 6.4 %finish.3 = (f32[2048,512]{1,0:T(8,128)}, f32[512,512]{1,0:T(8,128)}, f32[512,2048]{1,0:T(8,128)}, f32[512,512]{1,0:T(8,128)}, f32[8,128]{1,0:T(8,128)S(1)}, /*index=5*/f32[512]{0:T(512)}, f32[512]{0:T(512)}) custom-call(bf16[1280,512]{1,0:T(8,128)(2,1)S(1)} %gather.33.refs_2_.refs_0_, bf16[1280,512]{1,0:T(8,128)(2,1)S(1)} %collective-permute-done.51.refs_1_, ...), custom_call_target="tpu_custom_call" | custom-call | flops 5750000128 | bytes 18450000 | tf_op jit(solution)/shard_map/finish/pallas_call | solution.py:162
  172.7 3.2 %finish.4 = (f32[1536,512]{1,0:T(8,128)}, f32[1536,512]{1,0:T(8,128)}, f32[512,512]{1,0:T(8,128)}, f32[512,512]{1,0:T(8,128)}, f32[8,128]{1,0:T(8,128)S(1)}) custom-call(bf16[768,512]{1,0:T(8,128)(2,1)S(1)} %gather.38.refs_2_.refs_0_, bf16[768,512]{1,0:T(8,128)(2,1)S(1)} %gather.39.refs_1_.refs_4_, bf16[512,512]{1,0:T(8,128)(2,1)S(1)} %gather.37.refs_5_.refs_2_, ...), custom_call_target="tpu_custom_call" | custom-call | flops 5750000128 | bytes 18450000 | tf_op jit(solution)/shard_map/finish/pallas_call | solution.py:162
  175.9 2.5 %finish.5 = (f32[1536,512]{1,0:T(8,128)}, f32[1536,512]{1,0:T(8,128)}, f32[512,512]{1,0:T(8,128)}, f32[512,512]{1,0:T(8,128)}, f32[8,128]{1,0:T(8,128)}) custom-call(bf16[768,512]{1,0:T(8,128)(2,1)S(1)} %collective-permute-done.58.refs_0_, ...), custom_call_target="tpu_custom_call", output_to_operand_aliasing={{0}: (2, {}), {1}: (3, {}), {2}: (4, {}), {3}: (5, {})} | custom-call | flops 5750000128 | bytes 18450000 | tf_op jit(solution)/shard_map/finish/pallas_call | solution.py:162
  (151 shorter events, 31.0 us)
Async XLA Ops:
  4.0 9.7 %collective-permute-start = (bf16[112,512]{1,0:T(8,128)(2,1)S(1)}, bf16[112,512]{1,0:T(8,128)(2,1)S(1)}, u32[]{:S(2)}, u32[]{:S(2)}) collective-permute-start(bf16[112,512]{1,0:T(8,128)(2,1)S(1)} %get-tuple-element.120.refs_0_), channel_id=1, source_target_pairs={{0,4},{1,5},{2,6},{3,7},{4,0},{5,1},{6,2},{7,3},{8,12},{9,13},{10,... | collective-permute-start | bytes 344072 | tf_op jit(solution)/shard_map/swap_gather_keys/ppermute | solution.py:108
  13.7 11.1 %collective-permute-start.1 = (bf16[224,512]{1,0:T(8,128)(2,1)S(1)}, bf16[224,512]{1,0:T(8,128)(2,1)S(1)}, u32[]{:S(2)}, u32[]{:S(2)}) collective-permute-start(bf16[224,512]{1,0:T(8,128)(2,1)S(1)} %gather_row.4.refs_2_.refs_0_), channel_id=1, source_target_pairs={{0,2},{1,3},{2,0},{3,1},{4,6},{5,7},{6,4},{7,5},{8,10},{9,11},{10,... | collective-permute-start | bytes 688136 | tf_op jit(solution)/shard_map/swap_gather_keys/ppermute | solution.py:108
  14.5 11.7 %collective-permute-start.4 = (bf16[192,512]{1,0:T(8,128)(2,1)S(1)}, bf16[192,512]{1,0:T(8,128)(2,1)S(1)}, u32[]{:S(2)}, u32[]{:S(2)}) collective-permute-start(bf16[192,512]{1,0:T(8,128)(2,1)S(1)} %gather_row.5.refs_2_.refs_0_), channel_id=1, source_target_pairs={{0,4},{1,5},{2,6},{3,7},{4,0},{5,1},{6,2},{7,3},{8,12},{9,13},{10,... | collective-permute-start | bytes 589832 | tf_op jit(solution)/shard_map/swap_gather_values/ppermute | solution.py:108
  24.9 11.9 %collective-permute-start.3 = (bf16[448,512]{1,0:T(8,128)(2,1)S(1)}, bf16[448,512]{1,0:T(8,128)(2,1)S(1)}, u32[]{:S(2)}, u32[]{:S(2)}) collective-permute-start(bf16[448,512]{1,0:T(8,128)(2,1)S(1)} %gather_row.6.refs_2_.refs_8_), channel_id=1, source_target_pairs={{0,1},{1,0},{2,3},{3,2},{4,5},{5,4},{6,7},{7,6},{8,9},{9,8},{10,11... | collective-permute-start | bytes 1376264 | tf_op jit(solution)/shard_map/swap_gather_keys/ppermute | solution.py:108
  26.2 10.5 %collective-permute-start.5 = (bf16[384,512]{1,0:T(8,128)(2,1)S(1)}, bf16[384,512]{1,0:T(8,128)(2,1)S(1)}, u32[]{:S(2)}, u32[]{:S(2)}) collective-permute-start(bf16[384,512]{1,0:T(8,128)(2,1)S(1)} %gather_row.7.refs_10_.refs_15_), channel_id=1, source_target_pairs={{0,2},{1,3},{2,0},{3,1},{4,6},{5,7},{6,4},{7,5},{8,10},{9,11},{10,... | collective-permute-start | bytes 1179656 | tf_op jit(solution)/shard_map/swap_gather_values/ppermute | solution.py:108
  54.1 12.0 %collective-permute-start.6 = (bf16[384,512]{1,0:T(8,128)(2,1)S(1)}, bf16[384,512]{1,0:T(8,128)(2,1)S(1)}, u32[]{:S(2)}, u32[]{:S(2)}) collective-permute-start(bf16[384,512]{1,0:T(8,128)(2,1)S(1)} %get-tuple-element.125), channel_id=1, source_target_pairs={{0,1},{1,0},{2,3},{3,2},{4,5},{5,4},{6,7},{7,6},{8,9},{9,8},{10,11... | collective-permute-start | bytes 1179656 | tf_op jit(solution)/shard_map/swap_K/ppermute | solution.py:108
  55.7 10.8 %collective-permute-start.10 = (bf16[384,512]{1,0:T(8,128)(2,1)S(1)}, bf16[384,512]{1,0:T(8,128)(2,1)S(1)}, u32[]{:S(2)}, u32[]{:S(2)}) collective-permute-start(bf16[384,512]{1,0:T(8,128)(2,1)S(1)} %get-tuple-element.136), channel_id=1, source_target_pairs={{0,2},{1,3},{2,0},{3,1},{4,6},{5,7},{6,4},{7,5},{8,10},{9,11},{10,... | collective-permute-start | bytes 1179656 | tf_op jit(solution)/shard_map/swap_V/ppermute | solution.py:108
  58.8 20.4 %collective-permute-start.14 = (bf16[640,512]{1,0:T(8,128)(2,1)S(1)}, bf16[640,512]{1,0:T(8,128)(2,1)S(1)}, u32[]{:S(2)}, u32[]{:S(2)}) collective-permute-start(bf16[640,512]{1,0:T(8,128)(2,1)S(1)} %get-tuple-element.143), channel_id=1, source_target_pairs={{0,16},{8,24},{16,0},{24,8},{1,17},{9,25},{17,1},{25,9},{2,18},{10... | collective-permute-start | bytes 1966088 | tf_op jit(solution)/shard_map/swap_A1/ppermute | solution.py:108
  60.4 19.8 %collective-permute-start.13 = (bf16[640,512]{1,0:T(8,128)(2,1)S(1)}, bf16[640,512]{1,0:T(8,128)(2,1)S(1)}, u32[]{:S(2)}, u32[]{:S(2)}) collective-permute-start(bf16[640,512]{1,0:T(8,128)(2,1)S(1)} %get-tuple-element.142), channel_id=1, source_target_pairs={{0,1},{1,0},{2,3},{3,2},{4,5},{5,4},{6,7},{7,6},{8,9},{9,8},{10,11... | collective-permute-start | bytes 1966088 | tf_op jit(solution)/shard_map/swap_A0/ppermute | solution.py:108
  66.5 10.8 %collective-permute-start.11 = (bf16[192,512]{1,0:T(8,128)(2,1)S(1)}, bf16[192,512]{1,0:T(8,128)(2,1)S(1)}, u32[]{:S(2)}, u32[]{:S(2)}) collective-permute-start(bf16[192,512]{1,0:T(8,128)(2,1)S(1)} %get-tuple-element.138), channel_id=1, source_target_pairs={{0,4},{1,5},{2,6},{3,7},{4,0},{5,1},{6,2},{7,3},{8,12},{9,13},{10,... | collective-permute-start | bytes 589832 | tf_op jit(solution)/shard_map/swap_V/ppermute | solution.py:108
  68.4 9.8 %collective-permute-start.9 = (bf16[192,512]{1,0:T(8,128)(2,1)S(1)}, bf16[192,512]{1,0:T(8,128)(2,1)S(1)}, u32[]{:S(2)}, u32[]{:S(2)}) collective-permute-start(bf16[192,512]{1,0:T(8,128)(2,1)S(1)} %get-tuple-element.134), channel_id=1, source_target_pairs={{0,2},{1,3},{2,0},{3,1},{4,6},{5,7},{6,4},{7,5},{8,10},{9,11},{10,... | collective-permute-start | bytes 589832 | tf_op jit(solution)/shard_map/swap_K/ppermute | solution.py:108
  77.4 7.3 %collective-permute-start.15 = (bf16[96,512]{1,0:T(8,128)(2,1)S(1)}, bf16[96,512]{1,0:T(8,128)(2,1)S(1)}, u32[]{:S(2)}, u32[]{:S(2)}) collective-permute-start(bf16[96,512]{1,0:T(8,128)(2,1)S(1)} %get-tuple-element.148), channel_id=1, source_target_pairs={{0,1},{1,0},{2,3},{3,2},{4,5},{5,4},{6,7},{7,6},{8,9},{9,8},{10,11... | collective-permute-start | bytes 294920 | tf_op jit(solution)/shard_map/swap_V/ppermute | solution.py:108
  79.4 11.3 %collective-permute-start.21 = (bf16[320,512]{1,0:T(8,128)(2,1)S(1)}, bf16[320,512]{1,0:T(8,128)(2,1)S(1)}, u32[]{:S(2)}, u32[]{:S(2)}) collective-permute-start(bf16[320,512]{1,0:T(8,128)(2,1)S(1)} %get-tuple-element.169), channel_id=1, source_target_pairs={{0,1},{1,0},{2,3},{3,2},{4,5},{5,4},{6,7},{7,6},{8,9},{9,8},{10,11... | collective-permute-start | bytes 983048 | tf_op jit(solution)/shard_map/swap_A1/ppermute | solution.py:108
  80.3 10.3 %collective-permute-start.16 = (bf16[320,512]{1,0:T(8,128)(2,1)S(1)}, bf16[320,512]{1,0:T(8,128)(2,1)S(1)}, u32[]{:S(2)}, u32[]{:S(2)}) collective-permute-start(bf16[320,512]{1,0:T(8,128)(2,1)S(1)} %get-tuple-element.160), channel_id=1, source_target_pairs={{0,16},{8,24},{16,0},{24,8},{1,17},{9,25},{17,1},{25,9},{2,18},{10... | collective-permute-start | bytes 983048 | tf_op jit(solution)/shard_map/swap_A0/ppermute | solution.py:108
  90.8 10.6 %collective-permute-start.23 = (bf16[160,512]{1,0:T(8,128)(2,1)S(1)}, bf16[160,512]{1,0:T(8,128)(2,1)S(1)}, u32[]{:S(2)}, u32[]{:S(2)}) collective-permute-start(bf16[160,512]{1,0:T(8,128)(2,1)S(1)} %get-tuple-element.174), channel_id=1, source_target_pairs={{0,2},{1,3},{2,0},{3,1},{4,6},{5,7},{6,4},{7,5},{8,10},{9,11},{10,... | collective-permute-start | bytes 491528 | tf_op jit(solution)/shard_map/swap_A1/ppermute | solution.py:108
  92.3 9.1 %collective-permute-start.19 = (bf16[160,512]{1,0:T(8,128)(2,1)S(1)}, bf16[160,512]{1,0:T(8,128)(2,1)S(1)}, u32[]{:S(2)}, u32[]{:S(2)}) collective-permute-start(bf16[160,512]{1,0:T(8,128)(2,1)S(1)} %get-tuple-element.167), channel_id=1, source_target_pairs={{0,2},{1,3},{2,0},{3,1},{4,6},{5,7},{6,4},{7,5},{8,10},{9,11},{10,... | collective-permute-start | bytes 491528 | tf_op jit(solution)/shard_map/swap_A0/ppermute | solution.py:108
  93.1 17.0 %collective-permute-start.25 = (bf16[272,512]{1,0:T(8,128)(2,1)S(1)}, bf16[272,512]{1,0:T(8,128)(2,1)S(1)}, u32[]{:S(2)}, u32[]{:S(2)}) collective-permute-start(bf16[272,512]{1,0:T(8,128)(2,1)S(1)} %get-tuple-element.177), channel_id=1, source_target_pairs={{0,2},{1,3},{2,0},{3,1},{4,6},{5,7},{6,4},{7,5},{8,10},{9,11},{10,... | collective-permute-start | bytes 835592 | tf_op jit(solution)/shard_map/swap_B2/ppermute | solution.py:108
  94.5 10.0 %collective-permute-start.27 = (bf16[384,512]{1,0:T(8,128)(2,1)S(1)}, bf16[384,512]{1,0:T(8,128)(2,1)S(1)}, u32[]{:S(2)}, u32[]{:S(2)}) collective-permute-start(bf16[384,512]{1,0:T(8,128)(2,1)S(1)} %get-tuple-element.179), channel_id=1, source_target_pairs={{0,16},{8,24},{16,0},{24,8},{1,17},{9,25},{17,1},{25,9},{2,18},{10... | collective-permute-start | bytes 1179656 | tf_op jit(solution)/shard_map/swap_B1/ppermute | solution.py:108
  96.0 10.0 %collective-permute-start.26 = (bf16[384,512]{1,0:T(8,128)(2,1)S(1)}, bf16[384,512]{1,0:T(8,128)(2,1)S(1)}, u32[]{:S(2)}, u32[]{:S(2)}) collective-permute-start(bf16[384,512]{1,0:T(8,128)(2,1)S(1)} %get-tuple-element.178), channel_id=1, source_target_pairs={{0,1},{1,0},{2,3},{3,2},{4,5},{5,4},{6,7},{7,6},{8,9},{9,8},{10,11... | collective-permute-start | bytes 1179656 | tf_op jit(solution)/shard_map/swap_B0/ppermute | solution.py:108
  101.5 8.6 %collective-permute-start.24 = (bf16[80,512]{1,0:T(8,128)(2,1)S(1)}, bf16[80,512]{1,0:T(8,128)(2,1)S(1)}, u32[]{:S(2)}, u32[]{:S(2)}) collective-permute-start(bf16[80,512]{1,0:T(8,128)(2,1)S(1)} %get-tuple-element.176), channel_id=1, source_target_pairs={{0,4},{1,5},{2,6},{3,7},{4,0},{5,1},{6,2},{7,3},{8,12},{9,13},{10,... | collective-permute-start | bytes 245768 | tf_op jit(solution)/shard_map/swap_A1/ppermute | solution.py:108
  102.4 9.0 %collective-permute-start.22 = (bf16[80,512]{1,0:T(8,128)(2,1)S(1)}, bf16[80,512]{1,0:T(8,128)(2,1)S(1)}, u32[]{:S(2)}, u32[]{:S(2)}) collective-permute-start(bf16[80,512]{1,0:T(8,128)(2,1)S(1)} %get-tuple-element.173), channel_id=1, source_target_pairs={{0,4},{1,5},{2,6},{3,7},{4,0},{5,1},{6,2},{7,3},{8,12},{9,13},{10,... | collective-permute-start | bytes 245768 | tf_op jit(solution)/shard_map/swap_A0/ppermute | solution.py:108
  104.6 14.0 %collective-permute-start.30 = (bf16[192,512]{1,0:T(8,128)(2,1)S(1)}, bf16[192,512]{1,0:T(8,128)(2,1)S(1)}, u32[]{:S(2)}, u32[]{:S(2)}) collective-permute-start(bf16[192,512]{1,0:T(8,128)(2,1)S(1)} %get-tuple-element.184), channel_id=1, source_target_pairs={{0,1},{1,0},{2,3},{3,2},{4,5},{5,4},{6,7},{7,6},{8,9},{9,8},{10,11... | collective-permute-start | bytes 589832 | tf_op jit(solution)/shard_map/swap_B1/ppermute | solution.py:108
  110.2 8.3 %collective-permute-start.31 = (bf16[80,512]{1,0:T(8,128)(2,1)S(1)}, bf16[80,512]{1,0:T(8,128)(2,1)S(1)}, u32[]{:S(2)}, u32[]{:S(2)}) collective-permute-start(bf16[80,512]{1,0:T(8,128)(2,1)S(1)} %scatter.39.refs_2_.refs_0_), channel_id=1, source_target_pairs={{0,4},{1,5},{2,6},{3,7},{4,0},{5,1},{6,2},{7,3},{8,12},{9,13},{10,... | collective-permute-start | bytes 245768 | tf_op jit(solution)/shard_map/swap_A1/ppermute | solution.py:108
  111.4 11.4 %collective-permute-start.28 = (bf16[80,512]{1,0:T(8,128)(2,1)S(1)}, bf16[80,512]{1,0:T(8,128)(2,1)S(1)}, u32[]{:S(2)}, u32[]{:S(2)}) collective-permute-start(bf16[80,512]{1,0:T(8,128)(2,1)S(1)} %scatter.40.refs_2_.refs_0_), channel_id=1, source_target_pairs={{0,4},{1,5},{2,6},{3,7},{4,0},{5,1},{6,2},{7,3},{8,12},{9,13},{10,... | collective-permute-start | bytes 245768 | tf_op jit(solution)/shard_map/swap_A0/ppermute | solution.py:108
  113.2 7.5 %collective-permute-start.29 = (bf16[144,512]{1,0:T(8,128)(2,1)S(1)}, bf16[144,512]{1,0:T(8,128)(2,1)S(1)}, u32[]{:S(2)}, u32[]{:S(2)}) collective-permute-start(bf16[144,512]{1,0:T(8,128)(2,1)S(1)} %get-tuple-element.183), channel_id=1, source_target_pairs={{0,16},{8,24},{16,0},{24,8},{1,17},{9,25},{17,1},{25,9},{2,18},{10... | collective-permute-start | bytes 442376 | tf_op jit(solution)/shard_map/swap_B2/ppermute | solution.py:108
  114.8 13.6 %collective-permute-start.35 = (bf16[192,512]{1,0:T(8,128)(2,1)S(1)}, bf16[192,512]{1,0:T(8,128)(2,1)S(1)}, u32[]{:S(2)}, u32[]{:S(2)}) collective-permute-start(bf16[192,512]{1,0:T(8,128)(2,1)S(1)} %get-tuple-element.189), channel_id=1, source_target_pairs={{0,16},{8,24},{16,0},{24,8},{1,17},{9,25},{17,1},{25,9},{2,18},{10... | collective-permute-start | bytes 589832 | tf_op jit(solution)/shard_map/swap_B0/ppermute | solution.py:108
  118.5 6.9 %collective-permute-start.36 = (bf16[160,512]{1,0:T(8,128)(2,1)S(1)}, bf16[160,512]{1,0:T(8,128)(2,1)S(1)}, u32[]{:S(2)}, u32[]{:S(2)}) collective-permute-start(bf16[160,512]{1,0:T(8,128)(2,1)S(1)} %gather.20.refs_2_.refs_0_), channel_id=1, source_target_pairs={{0,2},{1,3},{2,0},{3,1},{4,6},{5,7},{6,4},{7,5},{8,10},{9,11},{10,... | collective-permute-start | bytes 491528 | tf_op jit(solution)/shard_map/swap_A1/ppermute | solution.py:108
  118.7 11.9 %collective-permute-start.33 = (bf16[96,512]{1,0:T(8,128)(2,1)S(1)}, bf16[96,512]{1,0:T(8,128)(2,1)S(1)}, u32[]{:S(2)}, u32[]{:S(2)}) collective-permute-start(bf16[96,512]{1,0:T(8,128)(2,1)S(1)} %get-tuple-element.187), channel_id=1, source_target_pairs={{0,2},{1,3},{2,0},{3,1},{4,6},{5,7},{6,4},{7,5},{8,10},{9,11},{10,... | collective-permute-start | bytes 294920 | tf_op jit(solution)/shard_map/swap_B1/ppermute | solution.py:108
  120.8 7.7 %collective-permute-start.34 = (bf16[80,512]{1,0:T(8,128)(2,1)S(1)}, bf16[80,512]{1,0:T(8,128)(2,1)S(1)}, u32[]{:S(2)}, u32[]{:S(2)}) collective-permute-start(bf16[80,512]{1,0:T(8,128)(2,1)S(1)} %get-tuple-element.188), channel_id=1, source_target_pairs={{0,1},{1,0},{2,3},{3,2},{4,5},{5,4},{6,7},{7,6},{8,9},{9,8},{10,11... | collective-permute-start | bytes 245768 | tf_op jit(solution)/shard_map/swap_B2/ppermute | solution.py:108
  122.9 8.7 %collective-permute-start.32 = (bf16[160,512]{1,0:T(8,128)(2,1)S(1)}, bf16[160,512]{1,0:T(8,128)(2,1)S(1)}, u32[]{:S(2)}, u32[]{:S(2)}) collective-permute-start(bf16[160,512]{1,0:T(8,128)(2,1)S(1)} %gather.21.refs_2_.refs_0_), channel_id=1, source_target_pairs={{0,2},{1,3},{2,0},{3,1},{4,6},{5,7},{6,4},{7,5},{8,10},{9,11},{10,... | collective-permute-start | bytes 491528 | tf_op jit(solution)/shard_map/swap_A0/ppermute | solution.py:108
  125.4 8.0 %collective-permute-start.41 = (bf16[320,512]{1,0:T(8,128)(2,1)S(1)}, bf16[320,512]{1,0:T(8,128)(2,1)S(1)}, u32[]{:S(2)}, u32[]{:S(2)}) collective-permute-start(bf16[320,512]{1,0:T(8,128)(2,1)S(1)} %gather.22.refs_2_.refs_0_), channel_id=1, source_target_pairs={{0,1},{1,0},{2,3},{3,2},{4,5},{5,4},{6,7},{7,6},{8,9},{9,8},{10,11... | collective-permute-start | bytes 983048 | tf_op jit(solution)/shard_map/swap_A1/ppermute | solution.py:108
  128.4 6.6 %collective-permute-start.40 = (bf16[96,512]{1,0:T(8,128)(2,1)S(1)}, bf16[96,512]{1,0:T(8,128)(2,1)S(1)}, u32[]{:S(2)}, u32[]{:S(2)}) collective-permute-start(bf16[96,512]{1,0:T(8,128)(2,1)S(1)} %get-tuple-element.195), channel_id=1, source_target_pairs={{0,2},{1,3},{2,0},{3,1},{4,6},{5,7},{6,4},{7,5},{8,10},{9,11},{10,... | collective-permute-start | bytes 294920 | tf_op jit(solution)/shard_map/swap_B0/ppermute | solution.py:108
  128.5 6.5 %collective-permute-start.39 = (bf16[48,512]{1,0:T(8,128)(2,1)S(1)}, bf16[48,512]{1,0:T(8,128)(2,1)S(1)}, u32[]{:S(2)}, u32[]{:S(2)}) collective-permute-start(bf16[48,512]{1,0:T(8,128)(2,1)S(1)} %get-tuple-element.194), channel_id=1, source_target_pairs={{0,4},{1,5},{2,6},{3,7},{4,0},{5,1},{6,2},{7,3},{8,12},{9,13},{10,... | collective-permute-start | bytes 147464 | tf_op jit(solution)/shard_map/swap_B2/ppermute | solution.py:108
  130.6 7.1 %collective-permute-start.38 = (bf16[48,512]{1,0:T(8,128)(2,1)S(1)}, bf16[48,512]{1,0:T(8,128)(2,1)S(1)}, u32[]{:S(2)}, u32[]{:S(2)}) collective-permute-start(bf16[48,512]{1,0:T(8,128)(2,1)S(1)} %get-tuple-element.193), channel_id=1, source_target_pairs={{0,4},{1,5},{2,6},{3,7},{4,0},{5,1},{6,2},{7,3},{8,12},{9,13},{10,... | collective-permute-start | bytes 147464 | tf_op jit(solution)/shard_map/swap_B1/ppermute | solution.py:108
  131.6 10.3 %collective-permute-start.37 = (bf16[320,512]{1,0:T(8,128)(2,1)S(1)}, bf16[320,512]{1,0:T(8,128)(2,1)S(1)}, u32[]{:S(2)}, u32[]{:S(2)}) collective-permute-start(bf16[320,512]{1,0:T(8,128)(2,1)S(1)} %gather.23.refs_2_.refs_0_), channel_id=1, source_target_pairs={{0,16},{8,24},{16,0},{24,8},{1,17},{9,25},{17,1},{25,9},{2,18},{10... | collective-permute-start | bytes 983048 | tf_op jit(solution)/shard_map/swap_A0/ppermute | solution.py:108
  133.5 17.0 %collective-permute-start.50 = (bf16[640,512]{1,0:T(8,128)(2,1)S(1)}, bf16[640,512]{1,0:T(8,128)(2,1)S(1)}, u32[]{:S(2)}, u32[]{:S(2)}) collective-permute-start(bf16[640,512]{1,0:T(8,128)(2,1)S(1)} %gather.24.refs_2_.refs_0_), channel_id=1, source_target_pairs={{0,16},{8,24},{16,0},{24,8},{1,17},{9,25},{17,1},{25,9},{2,18},{10... | collective-permute-start | bytes 1966088 | tf_op jit(solution)/shard_map/swap_A1/ppermute | solution.py:108
  135.1 10.7 %collective-permute-start.46 = (bf16[32,512]{1,0:T(8,128)(2,1)S(1)}, bf16[32,512]{1,0:T(8,128)(2,1)S(1)}, u32[]{:S(2)}, u32[]{:S(2)}) collective-permute-start(bf16[32,512]{1,0:T(8,128)(2,1)S(1)} %get-tuple-element.197.refs_2_.refs_0_), channel_id=1, source_target_pairs={{0,4},{1,5},{2,6},{3,7},{4,0},{5,1},{6,2},{7,3},{8,12},{9,13},{10,... | collective-permute-start | bytes 98312 | tf_op jit(solution)/shard_map/swap_B2/ppermute | solution.py:108
  137.7 9.2 %collective-permute-start.45 = (bf16[48,512]{1,0:T(8,128)(2,1)S(1)}, bf16[48,512]{1,0:T(8,128)(2,1)S(1)}, u32[]{:S(2)}, u32[]{:S(2)}) collective-permute-start(bf16[48,512]{1,0:T(8,128)(2,1)S(1)} %scatter.48.refs_2_.refs_0_), channel_id=1, source_target_pairs={{0,4},{1,5},{2,6},{3,7},{4,0},{5,1},{6,2},{7,3},{8,12},{9,13},{10,... | collective-permute-start | bytes 147464 | tf_op jit(solution)/shard_map/swap_B1/ppermute | solution.py:108
  142.0 14.3 %collective-permute-start.42 = (bf16[640,512]{1,0:T(8,128)(2,1)S(1)}, bf16[640,512]{1,0:T(8,128)(2,1)S(1)}, u32[]{:S(2)}, u32[]{:S(2)}) collective-permute-start(bf16[640,512]{1,0:T(8,128)(2,1)S(1)} %gather.25.refs_2_.refs_0_), channel_id=1, source_target_pairs={{0,1},{1,0},{2,3},{3,2},{4,5},{5,4},{6,7},{7,6},{8,9},{9,8},{10,11... | collective-permute-start | bytes 1966088 | tf_op jit(solution)/shard_map/swap_A0/ppermute | solution.py:108
  145.7 7.6 %collective-permute-start.49 = (bf16[64,512]{1,0:T(8,128)(2,1)S(1)}, bf16[64,512]{1,0:T(8,128)(2,1)S(1)}, u32[]{:S(2)}, u32[]{:S(2)}) collective-permute-start(bf16[64,512]{1,0:T(8,128)(2,1)S(1)} %gather.26.refs_2_.refs_0_), channel_id=1, source_target_pairs={{0,1},{1,0},{2,3},{3,2},{4,5},{5,4},{6,7},{7,6},{8,9},{9,8},{10,11... | collective-permute-start | bytes 196616 | tf_op jit(solution)/shard_map/swap_B2/ppermute | solution.py:108
  146.8 8.0 %collective-permute-start.48 = (bf16[96,512]{1,0:T(8,128)(2,1)S(1)}, bf16[96,512]{1,0:T(8,128)(2,1)S(1)}, u32[]{:S(2)}, u32[]{:S(2)}) collective-permute-start(bf16[96,512]{1,0:T(8,128)(2,1)S(1)} %gather.27.refs_2_.refs_0_), channel_id=1, source_target_pairs={{0,2},{1,3},{2,0},{3,1},{4,6},{5,7},{6,4},{7,5},{8,10},{9,11},{10,... | collective-permute-start | bytes 294920 | tf_op jit(solution)/shard_map/swap_B1/ppermute | solution.py:108
  148.4 7.3 %collective-permute-start.47 = (bf16[96,512]{1,0:T(8,128)(2,1)S(1)}, bf16[96,512]{1,0:T(8,128)(2,1)S(1)}, u32[]{:S(2)}, u32[]{:S(2)}) collective-permute-start(bf16[96,512]{1,0:T(8,128)(2,1)S(1)} %gather.28.refs_2_.refs_0_), channel_id=1, source_target_pairs={{0,2},{1,3},{2,0},{3,1},{4,6},{5,7},{6,4},{7,5},{8,10},{9,11},{10,... | collective-permute-start | bytes 294920 | tf_op jit(solution)/shard_map/swap_B0/ppermute | solution.py:108
  150.6 14.9 %collective-permute-start.52 = (bf16[1280,512]{1,0:T(8,128)(2,1)S(1)}, bf16[1280,512]{1,0:T(8,128)(2,1)S(1)}, u32[]{:S(2)}, u32[]{:S(2)}) collective-permute-start(bf16[1280,512]{1,0:T(8,128)(2,1)S(1)} %gather.29.refs_2_), channel_id=1, source_target_pairs={{0,8},{8,0},{16,24},{24,16},{1,9},{9,1},{17,25},{25,17},{2,10},{10... | collective-permute-start | bytes 3932168 | tf_op jit(solution)/shard_map/swap_A1/ppermute | solution.py:108
  154.9 7.9 %collective-permute-start.55 = (bf16[192,512]{1,0:T(8,128)(2,1)S(1)}, bf16[192,512]{1,0:T(8,128)(2,1)S(1)}, u32[]{:S(2)}, u32[]{:S(2)}) collective-permute-start(bf16[192,512]{1,0:T(8,128)(2,1)S(1)} %gather.31.refs_2_.refs_0_), channel_id=1, source_target_pairs={{0,1},{1,0},{2,3},{3,2},{4,5},{5,4},{6,7},{7,6},{8,9},{9,8},{10,11... | collective-permute-start | bytes 589832 | tf_op jit(solution)/shard_map/swap_B1/ppermute | solution.py:108
  156.4 9.2 %collective-permute-start.51 = (bf16[1280,512]{1,0:T(8,128)(2,1)S(1)}, bf16[1280,512]{1,0:T(8,128)(2,1)S(1)}, u32[]{:S(2)}, u32[]{:S(2)}) collective-permute-start(bf16[1280,512]{1,0:T(8,128)(2,1)S(1)} %gather.33.refs_2_.refs_0_), channel_id=1, source_target_pairs={{0,8},{8,0},{16,24},{24,16},{1,9},{9,1},{17,25},{25,17},{2,10},{10... | collective-permute-start | bytes 3932168 | tf_op jit(solution)/shard_map/swap_A0/ppermute | solution.py:108
  161.4 10.5 %collective-permute-start.57 = (bf16[384,512]{1,0:T(8,128)(2,1)S(1)}, bf16[384,512]{1,0:T(8,128)(2,1)S(1)}, u32[]{:S(2)}, u32[]{:S(2)}) collective-permute-start(bf16[384,512]{1,0:T(8,128)(2,1)S(1)} %gather.35.refs_2_.refs_0_), channel_id=1, source_target_pairs={{0,1},{1,0},{2,3},{3,2},{4,5},{5,4},{6,7},{7,6},{8,9},{9,8},{10,11... | collective-permute-start | bytes 1179656 | tf_op jit(solution)/shard_map/swap_B0/ppermute | solution.py:108
  162.9 9.1 %collective-permute-start.59 = (bf16[384,512]{1,0:T(8,128)(2,1)S(1)}, bf16[384,512]{1,0:T(8,128)(2,1)S(1)}, u32[]{:S(2)}, u32[]{:S(2)}) collective-permute-start(bf16[384,512]{1,0:T(8,128)(2,1)S(1)} %gather.36.refs_2_.refs_0_), channel_id=1, source_target_pairs={{0,16},{8,24},{16,0},{24,8},{1,17},{9,25},{17,1},{25,9},{2,18},{10... | collective-permute-start | bytes 1179656 | tf_op jit(solution)/shard_map/swap_B1/ppermute | solution.py:108
  165.4 7.3 %collective-permute-start.61 = (bf16[512,512]{1,0:T(8,128)(2,1)S(1)}, bf16[512,512]{1,0:T(8,128)(2,1)S(1)}, u32[]{:S(2)}, u32[]{:S(2)}) collective-permute-start(bf16[512,512]{1,0:T(8,128)(2,1)S(1)} %gather.37.refs_5_.refs_2_), channel_id=1, source_target_pairs={{0,8},{8,0},{16,24},{24,16},{1,9},{9,1},{17,25},{25,17},{2,10},{10... | collective-permute-start | bytes 1572872 | tf_op jit(solution)/shard_map/swap_B2/ppermute | solution.py:108
  (20 other events, 128.2 us)
